TPU v7x, 32 devices: a whole 2x2x4 slice. The times are simulated.
32 devices in a mesh: cell: 2 (over core), panel: 2 (over x), sc: 8 (over z, y).
Axes of the slice: x: 2, y: 2, z: 4, core: 2. Of those that a mesh axis runs over, the one named last changes fastest.
Arguments:
- channel: bfloat16 [4, 256, 2, 1024, 128], P('cell', 'sc', None, 'panel'), may hold values from -0.1875 to 0.1875
- received: bfloat16 [4, 256, 2, 14, 1024], P('cell', 'sc', None, None, 'panel'), may hold values from -6 to 6
- noise_power: float32 [4], P('cell'), may hold values from 0.05 to 0.5
- user_count: int32 [4, 16], P('cell', 'sc'), may hold values from 32 to 128
- serving_cell: int32 [4, 128, 1], P('cell'), may hold values from 0 to 3; in each aligned block of 256 rows (0 to 255, 256 to 511, ..., all dimensions but the last counted through in order) at most 128 rows name the same one
Outputs:
- routed_symbols: bfloat16 [4, 256, 2, 14, 256], P('cell', 'sc')
Inputs may be any that keep to these rules, and one draw needn't show every extreme that they name: `serving_cell`: at most 128 user slots of one block of 2 consecutive cells name the same serving cell, and in every draw some serving cell is named exactly 128 times by one block.
All inputs are finite; a program needn't handle non-finite values.
Results may differ from a plain program's by a relative error of at most 0.0057.
Values may be sent and summed in bfloat16 or wider, within the bound.
No kernel may reach another device: no remote copies, remote signals or barrier semaphores. Data moves between devices by JAX's collectives and lax.ppermute only.
A program may use at most 128 MiB of HBM per device.

v0:
```python
import jax
import jax.numpy as jnp
from jax import lax
from jax.sharding import PartitionSpec as P

GRP = 16
ITERS = 2


def with_halo(block, sides, width):
    for axis, dim in sides:
        count = lax.axis_size(axis)
        forward = [(i, i + 1) for i in range(count - 1)]
        backward = [(target, source) for source, target in forward]
        low = lax.ppermute(
            lax.slice_in_dim(block, block.shape[dim] - width, None, axis=dim), axis, forward
        )
        high = lax.ppermute(lax.slice_in_dim(block, 0, width, axis=dim), axis, backward)
        block = jnp.concatenate([low, block, high], axis=dim)
    return block


def adjoint_apply(matrix, vector):
    products = jnp.einsum("cfaku,cfbsk->cfabsu", matrix, vector, preferred_element_type=jnp.float32)
    return jnp.stack(
        (products[:, :, 0, 0] + products[:, :, 1, 1], products[:, :, 0, 1] - products[:, :, 1, 0]),
        axis=2,
    )


def apply_channel(matrix, vector):
    products = jnp.einsum("cfaku,cfbsu->cfabsk", matrix, vector, preferred_element_type=jnp.float32)
    return jnp.stack(
        (products[:, :, 0, 0] - products[:, :, 1, 1], products[:, :, 0, 1] + products[:, :, 1, 0]),
        axis=2,
    )


def user_sum(left, right):
    return jnp.sum(left * right, axis=(2, 4))


def widen(values):
    return values[:, :, None, :, None]


def body(channel, received, noise_power, user_count, serving_cell):
    cells, band, _, antennas, users = channel.shape
    padded = with_halo(channel, (("sc", 1),), 1)
    total = band * lax.axis_size("sc")
    index = lax.axis_index("sc") * band + lax.iota(jnp.int32, band)
    weight = jnp.where((index == 0) | (index == total - 1), 0.75, 1.0).astype(jnp.float32)
    lower = padded[:, :-2].astype(jnp.float32)
    middle = padded[:, 1:-1].astype(jnp.float32)
    upper = padded[:, 2:].astype(jnp.float32)
    smooth = (0.25 * lower + 0.5 * middle + 0.25 * upper) / weight[None, :, None, None, None]
    counts = jnp.repeat(user_count, GRP, axis=1)
    active = (lax.iota(jnp.int32, users)[None, None, :] < counts[:, :, None]).astype(jnp.float32)
    smoothed = (smooth * active[:, :, None, None, :]).astype(jnp.bfloat16)
    partial_sums = adjoint_apply(smoothed, received)
    noise = noise_power[:, None, None, None, None]
    matched = lax.psum(partial_sums, "panel")
    estimate = jnp.zeros_like(matched)
    residual = matched
    direction = matched
    norm_now = user_sum(residual, residual)
    for iteration in range(ITERS):
        column_image = apply_channel(smoothed, direction.astype(jnp.bfloat16)).astype(jnp.bfloat16)
        image = lax.psum(adjoint_apply(smoothed, column_image), "panel") + noise * direction
        alpha = norm_now / user_sum(direction, image)
        estimate = estimate + widen(alpha) * direction
        residual = residual - widen(alpha) * image
        norm_next = user_sum(residual, residual)
        direction = residual + widen(norm_next / norm_now) * direction
        norm_now = norm_next
    detected = estimate.astype(jnp.bfloat16)
    n_cell = lax.axis_size("cell")
    capacity = 2 * users // n_cell
    slot_count = n_cell * capacity
    keys = serving_cell[:, :, 0].reshape(-1)
    position = lax.iota(jnp.int32, cells * users)
    earlier = (keys[:, None] == keys[None, :]) & (position[None, :] < position[:, None])
    rank = jnp.sum(earlier.astype(jnp.int32), axis=1)
    target = keys % cells * slot_count + keys // cells * capacity + rank
    onehot = (target[:, None] == lax.iota(jnp.int32, cells * slot_count)[None, :]).astype(
        jnp.bfloat16
    )
    onehot = onehot.reshape(cells, users, cells * slot_count)
    outgoing = jnp.einsum("cfasu,cut->tasf", detected, onehot, preferred_element_type=jnp.float32)
    outgoing = outgoing.astype(jnp.bfloat16).reshape(cells, slot_count, 2, detected.shape[3], band)
    return lax.all_to_all(
        lax.all_to_all(outgoing, "cell", split_axis=1, concat_axis=1, tiled=True),
        "sc",
        split_axis=1,
        concat_axis=4,
        tiled=True,
    )


def solution(mesh):
    return jax.shard_map(
        body,
        mesh=mesh,
        in_specs=(
            P("cell", "sc", None, "panel", None),
            P("cell", "sc", None, None, "panel"),
            P("cell"),
            P("cell", "sc"),
            P("cell", None, None),
        ),
        out_specs=P("cell", "sc", None, None, None),
        check_vma=False,
    )
```

profile of v0, /device:TPU:0, one launch (start us, length us, event | category | flops | bytes accessed | tf_op | source)
XLA Modules:
  0.0 341.5 jit_solution(16876711183547523585)
XLA Ops:
  8.7 4.9 %collective-permute-start = (bf16[2,1,2,512,128]{4,3,2,1,0:T(8,128)(2,1)}, bf16[2,1,2,512,128]{4,3,2,1,0:T(8,128)(2,1)S(1)}, u32[]{:S(2)}, u32[]{:S(2)}) collective-permute-start(bf16[2,1,2,512,128]{4,3,2,1,0:T(8,128)(2,1)} %get-tuple-element.7), channel_id=1, source_target_pairs={{0,1},{1,2},{2,3},{3,4},{4,5},{5,6},{6,7},{8,9},{9,10},{10,11},{11... | collective-permute-start | bytes 1572872 | tf_op jit(solution)/shard_map/ppermute | solution.py:15
  15.9 20.5 %collective-permute-done = bf16[2,1,2,512,128]{4,3,2,1,0:T(8,128)(2,1)S(1)} collective-permute-done((bf16[2,1,2,512,128]{4,3,2,1,0:T(8,128)(2,1)}, bf16[2,1,2,512,128]{4,3,2,1,0:T(8,128)(2,1)S(1)}, u32[]{:S(2)}, u32[]{:S(2)}) %collective-permute-start) | collective-permute-done | bytes 524320 | tf_op jit(solution)/shard_map/ppermute | solution.py:15
  36.3 26.0 %multiply_convert_fusion = bf16[2,32,2,512,128]{4,3,2,1,0:T(8,128)(2,1)} fusion(bf16[2,32,2,512,128]{4,3,2,1,0:T(8,128)(2,1)} %param.5, bf16[2,1,2,512,128]{4,3,2,1,0:T(8,128)(2,1)S(1)} %collective-permute-done.1, bf16[2,1,2,512,128]{4,3,2,1,0:T(8,128)(2,1)S(1)} %collective-permute-done, f32[2,32,128]{2,1,0:T(8,128)S(1)} %fusion.44, f32[32]{0:T(128)S(1)} %or_select_fusion), kind=kLoop, calls=%fused_computation | loop fusion | flops 109051904 | bytes 34635904 | tf_op jit(solution)/shard_map/convert_element_type | solution.py:59
  62.3 7.0 %fusion = f32[2,32,2,128,2,14]{3,5,4,2,1,0:T(8,128)S(1)} fusion(bf16[2,32,2,512,128]{4,3,2,1,0:T(8,128)(2,1)} %multiply_convert_fusion, bf16[2,32,2,14,512,1]{4,2,3,1,0,5:T(2,128)(2,1)S(1)} %bitcast.136), kind=kOutput, calls=%fused_computation.3 | convolution fusion | flops 469762048 | bytes 20447232 | tf_op jit(solution)/shard_map/cfaku,cfbsk->cfabsu/dot_general | solution.py:24
  71.9 39.2 %all-reduce.4.cloned.1.call-done = f32[2,32,2,14,128]{4,1,3,2,0:T(8,128)} async-done(((f32[2,32,2,14,128]{4,1,3,2,0:T(8,128)}), f32[2,32,2,14,128]{4,1,3,2,0:T(8,128)}) %all-reduce.4.cloned.1.call-update) | async-done | bytes 917520 | tf_op jit(solution)/shard_map/psum | solution.py:62
  112.3 14.8 %fusion.10 = f32[2,32,2,2,14,512]{5,4,2,3,1,0:T(8,128)} fusion(bf16[2,32,2,512,128]{4,3,2,1,0:T(8,128)(2,1)} %multiply_convert_fusion, bf16[2,32,2,14,128,1]{4,1,3,2,0,5:T(8,128)(2,1)S(1)} %convert_bitcast_fusion.1), kind=kOutput, calls=%fused_computation.13 | convolution fusion | flops 469762048 | bytes 24576000 | tf_op jit(solution)/shard_map/cfaku,cfbsu->cfabsk/dot_general | solution.py:32
  127.1 2.6 fusion.26
  129.7 2.6 fusion.27
  132.4 8.2 %fusion.6 = f32[2,32,2,14,2,128]{5,3,4,2,1,0:T(8,128)S(1)} fusion(bf16[2,32,2,512,128]{4,3,2,1,0:T(8,128)(2,1)} %multiply_convert_fusion, bf16[2,32,1,14,512]{4,3,1,0,2:T(8,128)(2,1)S(1)} %fusion.27, bf16[2,32,1,14,512]{4,3,1,0,2:T(8,128)(2,1)S(1)} %fusion.26), kind=kOutput, calls=%fused_computation.9 | convolution fusion | flops 470679552 | bytes 20447232 | tf_op jit(solution)/shard_map/cfaku,cfbsk->cfabsu/dot_general | solution.py:24
  143.1 37.1 %all-reduce.6.cloned.1.call-done = f32[2,32,2,14,128]{4,1,3,2,0:T(8,128)} async-done(((f32[2,32,2,14,128]{4,1,3,2,0:T(8,128)}), f32[2,32,2,14,128]{4,1,3,2,0:T(8,128)}) %all-reduce.6.cloned.1.call-update) | async-done | bytes 917520 | tf_op jit(solution)/shard_map/psum | solution.py:69
  185.0 14.8 %fusion.13 = f32[2,32,2,2,14,512]{5,4,2,3,1,0:T(8,128)} fusion(bf16[2,32,2,512,128]{4,3,2,1,0:T(8,128)(2,1)} %multiply_convert_fusion, bf16[2,32,2,14,128,1]{4,1,3,2,0,5:T(8,128)(2,1)S(1)} %convert_bitcast_fusion), kind=kOutput, calls=%fused_computation.14 | convolution fusion | flops 469762048 | bytes 24576000 | tf_op jit(solution)/shard_map/cfaku,cfbsu->cfabsk/dot_general | solution.py:32
  199.8 2.6 fusion.28
  205.1 8.2 %fusion.2 = f32[2,32,2,14,2,128]{5,3,4,2,1,0:T(8,128)S(1)} fusion(bf16[2,32,2,512,128]{4,3,2,1,0:T(8,128)(2,1)} %multiply_convert_fusion, bf16[2,32,1,14,512]{4,3,1,0,2:T(8,128)(2,1)S(1)} %fusion.29, bf16[2,32,1,14,512]{4,3,1,0,2:T(8,128)(2,1)S(1)} %fusion.28), kind=kOutput, calls=%fused_computation.5 | convolution fusion | flops 470679552 | bytes 20447232 | tf_op jit(solution)/shard_map/cfaku,cfbsk->cfabsu/dot_general | solution.py:24
  215.8 37.1 %all-reduce.8.cloned.1.call-done = f32[2,32,2,14,128]{4,1,3,2,0:T(8,128)} async-done(((f32[2,32,2,14,128]{4,1,3,2,0:T(8,128)}), f32[2,32,2,14,128]{4,1,3,2,0:T(8,128)}) %all-reduce.8.cloned.1.call-update) | async-done | bytes 917520 | tf_op jit(solution)/shard_map/psum | solution.py:69
  255.6 7.0 %copy.85 = bf16[2,256,2,14,32]{4,2,3,0,1:T(2,128)(2,1)} copy(bf16[2,256,2,14,32]{1,0,4,3,2:T(2,128)(2,1)S(1)} %reshape.282) | data formatting | bytes 1835008 | tf_op jit(solution)/shard_map/reshape | solution.py:90
  262.6 5.1 %reshape.291 = bf16[2,2,114688]{2,1,0:T(2,128)(2,1)S(1)} reshape(bf16[256,2,14,2,32]{4,3,2,1,0:T(2,128)(2,1)} %bitcast.138) | data formatting | bytes 1835008
  267.7 4.5 %all_to_all.23 = bf16[2,2,114688]{2,1,0:T(2,128)(2,1)S(1)} all-to-all(bf16[2,2,114688]{2,1,0:T(2,128)(2,1)S(1)} %reshape.291), channel_id=1, replica_groups=mesh['cell'=2,'panel'=2,'sc'=8] {'cell'}, dimensions={0} | all-to-all | bytes 1835008 | tf_op jit(solution)/shard_map/all_to_all | solution.py:92
  272.2 3.0 reshape.292
  275.2 6.3 %bitcast_bitcast_fusion = bf16[256,2,14,2,32]{4,3,2,1,0:T(2,128)(2,1)} fusion(bf16[256,2,14,2,32]{4,3,2,1,0:T(2,128)(2,1)} %reshape.292), kind=kLoop, calls=%fused_computation.88 | loop fusion | bytes 1835008
  281.5 5.0 %reshape.293 = bf16[8,2,28672]{2,1,0:T(2,128)(2,1)S(1)} reshape(bf16[256,2,14,2,32]{4,3,2,1,0:T(2,128)(2,1)} %bitcast_bitcast_fusion) | data formatting | bytes 1835008
  286.5 29.3 %all_to_all.24 = bf16[8,2,28672]{2,1,0:T(2,128)(2,1)} all-to-all(bf16[8,2,28672]{2,1,0:T(2,128)(2,1)S(1)} %reshape.293), channel_id=1, replica_groups=mesh['cell'=2,'panel'=2,'sc'=8] {'sc'}, dimensions={0} | all-to-all | bytes 1835008 | tf_op jit(solution)/shard_map/all_to_all | solution.py:91
  315.8 4.8 %reshape.294 = bf16[256,2,14,2,32]{4,3,2,1,0:T(2,128)(2,1)} reshape(bf16[8,2,28672]{2,1,0:T(2,128)(2,1)} %all_to_all.24) | data formatting | bytes 1835008
  320.6 8.1 %copy.86 = bf16[2,32,2,14,8,32]{5,4,2,3,1,0:T(8,128)(2,1)} copy(bf16[2,32,2,14,8,32]{5,2,3,0,1,4:T(2,128)(2,1)} %bitcast.137) | data formatting | bytes 1835008 | tf_op jit(solution)/shard_map/all_to_all | solution.py:91
  328.7 6.2 %all_to_all.20 = bf16[2,32,2,14,256]{4,2,3,1,0:T(2,128)(2,1)} reshape(bf16[2,32,2,14,8,32]{5,4,2,3,1,0:T(8,128)(2,1)} %copy.86) | data formatting | bytes 1835008 | tf_op jit(solution)/shard_map/all_to_all | solution.py:91
  (47 shorter events, 23.2 us)
Async XLA Ops:
  6.5 55.8 %copy-start = (bf16[2,32,2,14,512]{4,2,3,1,0:T(2,128)(2,1)S(1)}, bf16[2,32,2,14,512]{4,2,3,1,0:T(2,128)(2,1)}, u32[]{:S(2)}) copy-start(bf16[2,32,2,14,512]{4,2,3,1,0:T(2,128)(2,1)} %param.6) | copy-start | bytes 5505028
  6.5 104.5 %all-reduce.4.cloned.1.call-start = ((), (), s32[]{:S(2)}) async-start(), calls=%async_computation.2 | async-start | bytes 1835008 | tf_op jit(solution)/shard_map/psum | solution.py:62
  8.7 27.6 %collective-permute-start = (bf16[2,1,2,512,128]{4,3,2,1,0:T(8,128)(2,1)}, bf16[2,1,2,512,128]{4,3,2,1,0:T(8,128)(2,1)S(1)}, u32[]{:S(2)}, u32[]{:S(2)}) collective-permute-start(bf16[2,1,2,512,128]{4,3,2,1,0:T(8,128)(2,1)} %get-tuple-element.7), channel_id=1, source_target_pairs={{0,1},{1,2},{2,3},{3,4},{4,5},{5,6},{6,7},{8,9},{9,10},{10,11},{11... | collective-permute-start | bytes 1572872 | tf_op jit(solution)/shard_map/ppermute | solution.py:15
  13.6 22.7 %collective-permute-start.1 = (bf16[2,1,2,512,128]{4,3,2,1,0:T(8,128)(2,1)S(1)}, bf16[2,1,2,512,128]{4,3,2,1,0:T(8,128)(2,1)S(1)}, u32[]{:S(2)}, u32[]{:S(2)}) collective-permute-start(bf16[2,1,2,512,128]{4,3,2,1,0:T(8,128)(2,1)S(1)} %get-tuple-element.8), channel_id=1, source_target_pairs={{1,0},{2,1},{3,2},{4,3},{5,4},{6,5},{7,6},{9,8},{10,9},{11,10},{12... | collective-permute-start | bytes 1572872 | tf_op jit(solution)/shard_map/ppermute | solution.py:18
  71.6 108.6 %all-reduce.6.cloned.1.call-start = ((), (), s32[]{:S(2)}) async-start(), calls=%async_computation.3 | async-start | bytes 1835008 | tf_op jit(solution)/shard_map/psum | solution.py:69
  140.6 39.6 %copy-start.2 = (f32[2,32,2,14,128]{4,1,3,2,0:T(8,128)S(1)}, f32[2,32,2,14,128]{4,1,3,2,0:T(8,128)}, u32[]{:S(2)}) copy-start(f32[2,32,2,14,128]{4,1,3,2,0:T(8,128)} %all-reduce.4.cloned.1.call-done) | copy-start | bytes 2752516
  140.6 39.6 %copy-start.5 = (f32[2]{0:T(128)S(1)}, f32[2]{0:T(128)}, u32[]{:S(2)}) copy-start(f32[2]{0:T(128)} %param.7) | copy-start | bytes 28
  142.8 110.1 %all-reduce.8.cloned.1.call-start = ((), (), s32[]{:S(2)}) async-start(), calls=%async_computation.4 | async-start | bytes 1835008 | tf_op jit(solution)/shard_map/psum | solution.py:69
  213.3 2.3 copy-start.4
  213.3 39.6 %copy-start.3 = (f32[2,32,2,14,128]{4,1,3,2,0:T(8,128)S(1)}, f32[2,32,2,14,128]{4,1,3,2,0:T(8,128)}, u32[]{:S(2)}) copy-start(f32[2,32,2,14,128]{4,1,3,2,0:T(8,128)} %all-reduce.6.cloned.1.call-done) | copy-start | bytes 2752516
  286.5 48.4 %copy-start.1 = (bf16[2,32,2,14,512]{4,2,3,1,0:T(2,128)(2,1)S(1)}, bf16[2,32,2,14,512]{4,2,3,1,0:T(2,128)(2,1)}, u32[]{:S(2)}) copy-start(bf16[2,32,2,14,512]{4,2,3,1,0:T(2,128)(2,1)} %param.6) | copy-start | bytes 5505028
Sparse Core Ops, SparseCore 0:
  71.7 39.2 all-reduce.3
  143.0 37.1 all-reduce.5
  215.7 37.1 all-reduce.7
where the time goes:
time: 342 us; the launch traced here: 341 us
  waiting for transfers between devices  134 us (39%)
  matrix products  53.8 us (16%)
  local copies, waits for them, and re-layouts  52 us (15%)
  other arithmetic  48 us (14%)
  blocking collectives  33.7 us (10%)
  between operations  13.3 us (4%)
  starting transfers between devices  6.67 us (2%)
    psum x2, waiting for transfers between devices, body(): lax.psum(adjoint_apply(smoothed, column_image), 'panel') + noise * direction  74.2 us
    psum x1, waiting for transfers between devices, body(): matched = lax.psum(partial_sums, 'panel')  39.2 us
    dot_general x2, matrix products, apply_channel(): jnp.einsum('cfaku,cfbsu->cfabsk', matrix, vector, preferred_element_type=...  29.7 us
    all_to_all x1, blocking collectives, body(): lax.all_to_all(lax.all_to_all(outgoing, 'cell', split_axis=1, concat_axis...  29.3 us
    convert_element_type x1, other arithmetic, body(): smoothed = (smooth * active[:, :, None, None, :]).astype(jnp.bfloat16)  26 us
    unnamed x17, local copies, waits for them, and re-layouts  24.2 us
    dot_general x3, matrix products, adjoint_apply(): jnp.einsum('cfaku,cfbsk->cfabsu', matrix, vector, preferred_element_type=...  23.4 us
    ppermute x1, waiting for transfers between devices, with_halo(): lax.ppermute(lax.slice_in_dim(block, block.shape[dim] - width, None, axis...  20.5 us
  transfers between devices with their start and end apart: 5, of which 4 were waited for; matrix products, arithmetic and copies ran while one was open for 0% of the time, Pallas kernels for 0%

commit v1 on v0

v1 whole, which is shorter than its diff:
```python
import jax
import jax.numpy as jnp
from jax import lax
from jax.experimental import pallas as pl
from jax.experimental.pallas import tpu as pltpu
from jax.sharding import PartitionSpec as P

F32, BF16 = jnp.float32, jnp.bfloat16
SPAD = 16
VMEM_LIMIT = 40 << 20
CHUNKS = (3, 6, 6)
SWAP = [(0, 1), (1, 0)]

SMEM_SPEC = pl.BlockSpec(memory_space=pltpu.SMEM)
VMEM_SPEC = pl.BlockSpec(memory_space=pltpu.VMEM)
ANY_SPEC = pl.BlockSpec(memory_space=pl.ANY)


def prepare(below, here, above, samples, factor, mat, lhs):
    antennas, users = here.shape[1:]
    symbols = samples.shape[0]
    slab = 128
    for k in range(2):
        first = 2 * users + SPAD * k
        lhs[first : first + symbols, :] = samples[:, k, :]
        for row in range(0, antennas, slab):
            rows = pl.ds(row, slab)
            outer = below[k, rows, :].astype(F32) + above[k, rows, :].astype(F32)
            smooth = outer * 0.25 + here[k, rows, :].astype(F32) * 0.5
            value = (smooth * factor).astype(BF16)
            mat[rows, k * users : (k + 1) * users] = value
            lhs[k * users : (k + 1) * users, rows] = value.T


def gram(mat, lhs, out, users):
    product = jnp.dot(lhs[...], mat[...], preferred_element_type=F32)
    row = lax.broadcasted_iota(jnp.int32, (users, users), 0)
    col = lax.broadcasted_iota(jnp.int32, (users, users), 1)
    real = product[:users, :users] + product[users : 2 * users, users:]
    imag = product[:users, users:] - product[users : 2 * users, :users]
    out[:users, :] = jnp.where(row <= col, real, imag).astype(out.dtype)
    low, high = product[2 * users : 2 * users + SPAD], product[2 * users + SPAD :]
    out[users : users + SPAD, :] = (low[:, :users] + high[:, users:]).astype(out.dtype)
    out[users + SPAD :, :] = (high[:, :users] - low[:, users:]).astype(out.dtype)


def work_buffers(antennas, users):
    return [
        pltpu.VMEM((antennas, 2 * users), BF16),
        pltpu.VMEM((2 * users + 2 * SPAD, antennas), BF16),
    ]


def inner_gram(place, counts, channel, received, peer, first, number, dtype):
    cells, band, _, antennas, users = channel.shape
    symbols = received.shape[2]
    group = band // counts.shape[1]
    half = band // 2
    items = cells * number

    def kernel(place_ref, count_ref, chan, samp, out, win, ybuf, mat_a, lhs_a, mat_b, lhs_b, wsem, ysem):
        side = 1 - place_ref[0] if peer else place_ref[0]
        start = 1 + side * (half - 1) + first

        def fetch(c, i):
            return pltpu.make_async_copy(chan.at[c, start - 1 + i], win.at[c, i], wsem.at[c, i])

        def fetch_samples(c):
            return pltpu.make_async_copy(samp.at[c, pl.ds(start, number)], ybuf.at[c], ysem.at[c])

        for c in range(cells):
            fetch_samples(c).start()
            for i in range(number + 2):
                fetch(c, i).start()
        lhs_a[...] = jnp.zeros_like(lhs_a)
        lhs_b[...] = jnp.zeros_like(lhs_b)
        lane = lax.broadcasted_iota(jnp.int32, (1, users), 1)

        def wait(item):
            c, i = item // number, item % number

            @pl.when(item < items)
            def _():
                @pl.when(i == 0)
                def _():
                    fetch_samples(c).wait()
                    fetch(c, 0).wait()
                    fetch(c, 1).wait()

                fetch(c, i + 2).wait()

        def ready(item, mat, lhs):
            item = jnp.minimum(item, items - 1)
            c, i = item // number, item % number
            factor = (lane < count_ref[c, (start + i) // group]).astype(F32)
            prepare(win.at[c, i], win.at[c, i + 1], win.at[c, i + 2], ybuf.at[c, i], factor, mat, lhs)

        def multiply(item, mat, lhs):
            item = jnp.minimum(item, items - 1)
            gram(mat, lhs, out.at[item // number, item % number], users)

        wait(0)
        ready(0, mat_a, lhs_a)

        def step(t, carry):
            wait(2 * t + 1)
            wait(2 * t + 2)
            ready(2 * t + 1, mat_b, lhs_b)
            multiply(2 * t, mat_a, lhs_a)
            ready(2 * t + 2, mat_a, lhs_a)
            multiply(2 * t + 1, mat_b, lhs_b)
            return carry

        lax.fori_loop(0, (items + 1) // 2, step, 0)

    rows = users + 2 * SPAD
    return pl.pallas_call(
        kernel,
        in_specs=[SMEM_SPEC, SMEM_SPEC, ANY_SPEC, ANY_SPEC],
        out_specs=VMEM_SPEC,
        out_shape=jax.ShapeDtypeStruct((cells, number, rows, users), dtype),
        scratch_shapes=[
            pltpu.VMEM((cells, number + 2, 2, antennas, users), BF16),
            pltpu.VMEM((cells, number, symbols, 2, antennas), BF16),
            *work_buffers(antennas, users),
            *work_buffers(antennas, users),
            pltpu.SemaphoreType.DMA((cells, number + 2)),
            pltpu.SemaphoreType.DMA((cells,)),
        ],
        compiler_params=pltpu.CompilerParams(vmem_limit_bytes=VMEM_LIMIT),
        cost_estimate=pl.CostEstimate(
            flops=items * 4 * antennas * users * 2 * (users + SPAD),
            bytes_accessed=cells * (number + 2) * 4 * antennas * users,
            transcendentals=0,
        ),
    )(place, counts, channel, received)


def edge_gram(place, counts, channel, received, low, high):
    cells, band, _, antennas, users = channel.shape
    symbols = received.shape[2]
    group = band // counts.shape[1]

    def kernel(place_ref, count_ref, chan, samp, low_ref, high_ref, out_peer, out_own, win, ybuf, mat_a, lhs_a, mat_b, lhs_b, wsem, ysem):
        def sources(c):
            return (
                (low_ref.at[c, 0], chan.at[c, 0], chan.at[c, 1], samp.at[c, 0]),
                (chan.at[c, band - 2], chan.at[c, band - 1], high_ref.at[c, 0], samp.at[c, band - 1]),
            )

        copies = []
        for c in range(cells):
            for e in range(2):
                *blocks, samples = sources(c)[e]
                for i, block in enumerate(blocks):
                    copies.append(pltpu.make_async_copy(block, win.at[e, c, i], wsem.at[e, c, i]))
                copies.append(pltpu.make_async_copy(samples, ybuf.at[e, c], ysem.at[e, c]))
        for copy in copies:
            copy.start()
        lhs_a[...] = jnp.zeros_like(lhs_a)
        lhs_b[...] = jnp.zeros_like(lhs_b)
        lane = lax.broadcasted_iota(jnp.int32, (1, users), 1)
        for copy in copies:
            copy.wait()
        own = place_ref[0]

        def ready(e, c, mat, lhs):
            weight = jnp.where(place_ref[1 + e] == 1, 0.75, 1.0)
            count = count_ref[c, e * (band - 1) // group]
            factor = (lane < count).astype(F32) / jnp.full((1, users), weight, F32)
            prepare(win.at[e, c, 0], win.at[e, c, 1], win.at[e, c, 2], ybuf.at[e, c], factor, mat, lhs)

        for out, e in ((out_peer, 1 - own), (out_own, own)):
            for c in range(cells):
                mat, lhs = ((mat_a, lhs_a), (mat_b, lhs_b))[c % 2]
                ready(e, c, mat, lhs)
                gram(mat, lhs, out.at[c], users)

    rows = users + 2 * SPAD
    return pl.pallas_call(
        kernel,
        in_specs=[SMEM_SPEC, SMEM_SPEC, ANY_SPEC, ANY_SPEC, ANY_SPEC, ANY_SPEC],
        out_specs=[VMEM_SPEC, VMEM_SPEC],
        out_shape=[
            jax.ShapeDtypeStruct((cells, rows, users), BF16),
            jax.ShapeDtypeStruct((cells, rows, users), F32),
        ],
        scratch_shapes=[
            pltpu.VMEM((2, cells, 3, 2, antennas, users), BF16),
            pltpu.VMEM((2, cells, symbols, 2, antennas), BF16),
            *work_buffers(antennas, users),
            *work_buffers(antennas, users),
            pltpu.SemaphoreType.DMA((2, cells, 3)),
            pltpu.SemaphoreType.DMA((2, cells)),
        ],
        compiler_params=pltpu.CompilerParams(vmem_limit_bytes=VMEM_LIMIT),
        cost_estimate=pl.CostEstimate(
            flops=2 * cells * 4 * antennas * users * 2 * (users + SPAD),
            bytes_accessed=2 * cells * 12 * antennas * users,
            transcendentals=0,
        ),
    )(place, counts, channel, received, low, high)


def conjugate_gradient(sums, noise, users):
    row = lax.broadcasted_iota(jnp.int32, (users, users), 0)
    col = lax.broadcasted_iota(jnp.int32, (users, users), 1)
    upper = row <= col
    grams = []
    for value in sums:
        packed = value[:users]
        turned = packed.T
        real = jnp.where(upper, packed, turned)
        imag = jnp.where(row == col, 0.0, jnp.where(upper, -turned, packed))
        grams.append(jnp.concatenate([real, imag], axis=1).astype(BF16))

    def apply(matrix, vector):
        product = jnp.dot(vector.astype(BF16), matrix, preferred_element_type=F32)
        low, high = product[:SPAD], product[SPAD:]
        image = jnp.concatenate([low[:, :users] + high[:, users:], high[:, :users] - low[:, users:]], axis=0)
        return image + noise * vector

    def user_sum(left, right):
        total = jnp.sum(left * right, axis=1, keepdims=True)
        total = total[:SPAD] + total[SPAD:]
        return jnp.concatenate([total, total], axis=0)

    direction = [value[users:] for value in sums]
    norm = [user_sum(d, d) for d in direction]
    image = [apply(g, d) for g, d in zip(grams, direction)]
    alpha = [n / user_sum(d, i) for n, d, i in zip(norm, direction, image)]
    estimate = [a * d for a, d in zip(alpha, direction)]
    residual = [d - a * i for d, a, i in zip(direction, alpha, image)]
    norm_next = [user_sum(r, r) for r in residual]
    direction = [r + (m / n) * d for r, m, n, d in zip(residual, norm_next, norm, direction)]
    image = [apply(g, d) for g, d in zip(grams, direction)]
    alpha = [n / user_sum(d, i) for n, d, i in zip(norm_next, direction, image)]
    return [e + a * d for e, a, d in zip(estimate, alpha, direction)]


def inner_detect(place, noise_power, own, peers):
    cells, inner, rows, users = own.shape
    half = inner + 1
    batch = 3

    def kernel(place_ref, noise_ref, own_ref, *refs):
        *peer_refs, out = refs
        shift = 1 - place_ref[0]
        start = 0
        for peer_ref in peer_refs:
            number = peer_ref.shape[1]

            def step(t, carry, start=start, peer_ref=peer_ref, number=number):
                steps = number // batch
                c, base = t // steps, t % steps * batch
                sums = [own_ref[c, start + base + i] + peer_ref[c, base + i].astype(F32) for i in range(batch)]
                for i, value in enumerate(conjugate_gradient(sums, noise_ref[c], users)):
                    out[c, pl.ds(start + base + i + shift, 2 * SPAD, stride=half), :] = value
                return carry

            lax.fori_loop(0, cells * (number // batch), step, 0)
            start += number

    return pl.pallas_call(
        kernel,
        in_specs=[SMEM_SPEC, SMEM_SPEC, VMEM_SPEC] + [VMEM_SPEC] * len(peers),
        out_specs=VMEM_SPEC,
        out_shape=jax.ShapeDtypeStruct((cells, 2 * SPAD * half, users), F32),
        compiler_params=pltpu.CompilerParams(vmem_limit_bytes=VMEM_LIMIT),
        cost_estimate=pl.CostEstimate(
            flops=cells * inner * 2 * 2 * 2 * SPAD * users * 2 * users,
            bytes_accessed=cells * inner * rows * users * 6,
            transcendentals=0,
        ),
    )(place, noise_power, own, *peers)


def edge_detect(place, noise_power, own, peer, inner, onehot, symbols, rounds):
    cells, rows, users = own.shape
    half = inner.shape[1] // (2 * SPAD)
    width = onehot.shape[1] // rounds
    keep = symbols * half

    def kernel(place_ref, noise_ref, own_ref, peer_ref, inner_ref, hot_ref, *refs):
        *outs, state = refs
        state[...] = inner_ref[...]
        spot = place_ref[0] * (half - 1)
        for c in range(cells):
            (value,) = conjugate_gradient([own_ref[c] + peer_ref[c].astype(F32)], noise_ref[c], users)
            state[c, pl.ds(spot, 2 * SPAD, stride=half), :] = value
        blocks = [
            state[c, k * SPAD * half : k * SPAD * half + keep, :].astype(BF16) for k in range(2) for c in range(cells)
        ]
        lhs = jnp.concatenate(blocks, axis=1)
        placed = jnp.dot(lhs, hot_ref[...], preferred_element_type=F32).astype(BF16)
        for i, out in enumerate(outs):
            out[...] = placed[:, i * width : (i + 1) * width]

    return pl.pallas_call(
        kernel,
        in_specs=[SMEM_SPEC, SMEM_SPEC] + [VMEM_SPEC] * 4,
        out_specs=[VMEM_SPEC] * rounds,
        out_shape=[jax.ShapeDtypeStruct((keep, width), BF16)] * rounds,
        scratch_shapes=[pltpu.VMEM(inner.shape, F32)],
        compiler_params=pltpu.CompilerParams(vmem_limit_bytes=VMEM_LIMIT),
        cost_estimate=pl.CostEstimate(
            flops=2 * keep * onehot.shape[0] * onehot.shape[1], bytes_accessed=4 * inner.size, transcendentals=0
        ),
    )(place, noise_power, own, peer, inner, onehot)


def assemble(place, mine, theirs, sources, cells, per_device, symbols, half):
    total = len(sources) * 2 * half
    lanes = mine[0].shape[2]
    slots = cells * per_device

    def kernel(place_ref, source_ref, *refs):
        mine_refs, theirs_refs = refs[: len(mine)], refs[len(mine) : 2 * len(mine)]
        out, gathered, turned = refs[2 * len(mine) :]
        for side, group in ((place_ref[0], mine_refs), (1 - place_ref[0], theirs_refs)):
            number = 0
            for ref in group:
                for i in range(ref.shape[0]):
                    start = pl.multiple_of(source_ref[number] * (2 * half) + side * half, half)
                    for s in range(symbols):
                        gathered[s, pl.ds(start, half), :] = ref[i, s * half : (s + 1) * half, :]
                    number += 1
        for s in range(symbols):
            value = gathered[s].T.astype(F32)
            for k in range(2):
                for part in range(total // 128):
                    piece = value[k * slots : (k + 1) * slots, part * 128 : (part + 1) * 128]
                    turned[part, pl.ds(2 * s + k, slots, stride=2 * SPAD), :] = piece
        for slot in range(slots):
            for part in range(total // 128):
                value = turned[part, slot * 2 * SPAD : (slot + 1) * 2 * SPAD, :].astype(BF16)
                out[slot // per_device, slot % per_device, :, :, part * 128 : (part + 1) * 128] = value[
                    : 2 * symbols
                ].reshape(symbols, 2, 128)

    return pl.pallas_call(
        kernel,
        in_specs=[SMEM_SPEC, SMEM_SPEC] + [VMEM_SPEC] * (2 * len(mine)),
        out_specs=VMEM_SPEC,
        out_shape=jax.ShapeDtypeStruct((cells, per_device, symbols, 2, total), BF16),
        scratch_shapes=[
            pltpu.VMEM((symbols, total, lanes), BF16),
            pltpu.VMEM((total // 128, slots * 2 * SPAD, 128), F32),
        ],
        compiler_params=pltpu.CompilerParams(vmem_limit_bytes=VMEM_LIMIT),
    )(place, sources, *mine, *theirs)


def body(channel, received, noise_power, user_count, serving_cell):
    cells, band, _, antennas, users = channel.shape
    symbols = received.shape[3]
    half = band // 2
    n_sc, n_cell = lax.axis_size("sc"), lax.axis_size("cell")
    panel, sc, cell = lax.axis_index("panel"), lax.axis_index("sc"), lax.axis_index("cell")

    upward = [(i, i + 1) for i in range(n_sc - 1)]
    downward = [(i + 1, i) for i in range(n_sc - 1)]
    low = lax.ppermute(channel[:, band - 1 :], "sc", upward)
    high = lax.ppermute(channel[:, :1], "sc", downward)

    place = jnp.stack([panel, (sc == 0).astype(jnp.int32), (sc == n_sc - 1).astype(jnp.int32)]).astype(jnp.int32)
    samples = jnp.transpose(received, (0, 1, 3, 2, 4))

    peers, first = [], 0
    for number in CHUNKS:
        outgoing = inner_gram(place, user_count, channel, samples, True, first, number, BF16)
        peers.append(lax.ppermute(outgoing, "panel", SWAP))
        first += number
    own = inner_gram(place, user_count, channel, samples, False, 0, half - 1, F32)
    edge_out, edge_own = edge_gram(place, user_count, channel, samples, low, high)
    edge_peer = lax.ppermute(edge_out, "panel", SWAP)
    inner = inner_detect(place, noise_power, own, peers)

    capacity = cells * users // n_cell
    per_device = n_cell * capacity // n_sc
    reach = capacity // per_device
    rounds = n_cell * reach
    keys = serving_cell[:, :, 0].reshape(-1)
    position = lax.iota(jnp.int32, cells * users)
    earlier = (keys[:, None] == keys[None, :]) & (position[None, :] < position[:, None])
    rank = jnp.sum(earlier.astype(jnp.int32), axis=1)
    turn = (keys // cells - sc // reach) % n_cell * reach + (rank // per_device - sc % reach) % reach
    column = (turn * 2 * cells + keys % cells) * per_device + rank % per_device
    column = jnp.concatenate([column, column + cells * per_device])
    width = 2 * cells * per_device
    onehot = (column[:, None] == lax.iota(jnp.int32, rounds * width)[None, :]).astype(BF16)

    messages = edge_detect(place, noise_power, edge_own, edge_peer, inner, onehot, symbols, rounds)
    arrived, sources = [], []
    for a in range(n_cell):
        for b in range(reach):
            pairs = [
                (s * n_sc + j, (j // reach + a) % n_cell * n_sc + s * reach + (j % reach + b) % reach)
                for s in range(n_cell)
                for j in range(n_sc)
            ]
            arrived.append(lax.ppermute(messages[a * reach + b], ("cell", "sc"), pairs))
            sources.append((cell - a) % n_cell * reach + (sc % reach - b) % reach)
    sources = jnp.stack(sources).astype(jnp.int32)
    groups = [arrived[: rounds // 2], arrived[rounds // 2 :]]
    mine = [jnp.stack(group) for group in groups]
    theirs = [lax.ppermute(group, "panel", SWAP) for group in mine]
    routed = assemble(place, mine, theirs, sources, cells, per_device, symbols, half)
    return jnp.transpose(routed, (0, 1, 3, 2, 4))


def solution(mesh):
    return jax.shard_map(
        body,
        mesh=mesh,
        in_specs=(
            P("cell", "sc", None, "panel", None),
            P("cell", "sc", None, None, "panel"),
            P("cell"),
            P("cell", "sc"),
            P("cell", None, None),
        ),
        out_specs=P("cell", "sc", None, None, None),
        check_vma=False,
    )
```

time: 342 us -> 93.3 us (0.27)
  waiting for transfers between devices: 134 us -> 9.3 us
  matrix products: 53.8 us -> 0 us
  Pallas kernels: 0 us -> 50 us
  local copies, waits for them, and re-layouts: 52 us -> 3.18 us
  other arithmetic: 48 us -> 0.59 us
  blocking collectives: 33.7 us -> 0 us
  starting transfers between devices: 6.67 us -> 29.8 us
  between operations: 13.3 us -> 0.24 us
    psum x3 -> x0, waiting for transfers between devices: 113 us -> none  [the longest x2 74.2 us: body(): lax.psum(adjoint_apply(smoothed, column_image), 'panel') + noise * direction]
    dot_general x6 -> x0, matrix products: 53.8 us -> none  [the longest x2 29.7 us: apply_channel(): jnp.einsum('cfaku,cfbsu->cfabsk', matrix, vector, preferred_element_type=...]
    pallas_call x0 -> x8, Pallas kernels: none -> 50 us  [the longest x4 30.6 us: inner_gram(): pl.pallas_call(kernel, in_specs=[SMEM_SPEC, SMEM_SPEC, ANY_SPEC, ANY_SPEC...]
    all_to_all x2 -> x0, blocking collectives: 33.7 us -> none  [the longest x1 29.3 us: body(): lax.all_to_all(lax.all_to_all(outgoing, 'cell', split_axis=1, concat_axis...]
    convert_element_type x4 -> x1, other arithmetic: 28.9 us -> 0.24 us  [body(): (column[:, None] == lax.iota(jnp.int32, rounds * width)[None, :]).astype(...]
    ppermute x2 -> x16, starting transfers between devices: 6.18 us -> 29.8 us  [the longest x8 16.1 us: body(): arrived.append(lax.ppermute(messages[a * reach + b], ('cell', 'sc'), pairs))]
    unnamed x17 -> x10, local copies, waits for them, and re-layouts: 24.2 us -> 0.7 us
    all_to_all x2 -> x0, local copies, waits for them, and re-layouts: 14.3 us -> none  [body(): lax.all_to_all(lax.all_to_all(outgoing, 'cell', split_axis=1, concat_axis...]
  transfers between devices with their start and end apart: 5 -> 16, of which waited for: 4 -> 6; matrix products, arithmetic and copies ran while one was open for 0% -> 1% of each run, Pallas kernels for 0% -> 47%
where the time goes in v1:
time: 93.3 us; the launch traced here: 93.1 us
  Pallas kernels  50 us (54%)
  starting transfers between devices  29.8 us (32%)
  waiting for transfers between devices  9.3 us (10%)
  local copies, waits for them, and re-layouts  3.18 us (3%)
    pallas_call x4, Pallas kernels, inner_gram(): pl.pallas_call(kernel, in_specs=[SMEM_SPEC, SMEM_SPEC, ANY_SPEC, ANY_SPEC...  30.6 us
    ppermute x8, starting transfers between devices, body(): arrived.append(lax.ppermute(messages[a * reach + b], ('cell', 'sc'), pairs))  16.1 us
    pallas_call x1, Pallas kernels, inner_detect(): pl.pallas_call(kernel, in_specs=[SMEM_SPEC, SMEM_SPEC, VMEM_SPEC] + [VMEM...  9.99 us
    ppermute x2, waiting for transfers between devices, body(): theirs = [lax.ppermute(group, 'panel', SWAP) for group in mine]  6.14 us
    ppermute x1, starting transfers between devices, body(): low = lax.ppermute(channel[:, band - 1:], 'sc', upward)  4.89 us
    pallas_call x1, Pallas kernels, assemble(): pl.pallas_call(kernel, in_specs=[SMEM_SPEC, SMEM_SPEC] + [VMEM_SPEC] * (2...  4.04 us
    ppermute x3, starting transfers between devices, body(): peers.append(lax.ppermute(outgoing, 'panel', SWAP))  3.71 us
    pallas_call x1, Pallas kernels, edge_gram(): pl.pallas_call(kernel, in_specs=[SMEM_SPEC, SMEM_SPEC, ANY_SPEC, ANY_SPEC...  3.62 us
  transfers between devices with their start and end apart: 16, of which 6 were waited for; matrix products, arithmetic and copies ran while one was open for 1% of the time, Pallas kernels for 47%

profile of v1, /device:TPU:0, one launch (start us, length us, event | category | flops | bytes accessed | tf_op | source)
XLA Modules:
  0.0 93.1 jit_solution(12797686984530596764)
XLA Ops:
  0.0 2.4 %fusion.9 = (bf16[2,1,2,512,128]{4,3,2,1,0:T(8,128)(2,1)}, bf16[2,1,2,512,128]{4,3,2,1,0:T(8,128)(2,1)}) fusion(bf16[2,32,2,512,128]{4,3,2,1,0:T(8,128)(2,1)} %chan.9), kind=kLoop, calls=%fused_computation.32 | loop fusion | bytes 2097152 | tf_op jit(solution)/shard_map/slice | solution.py:364
  2.4 4.9 %collective-permute-start = (bf16[2,1,2,512,128]{4,3,2,1,0:T(8,128)(2,1)}, bf16[2,1,2,512,128]{4,3,2,1,0:T(8,128)(2,1)S(1)}, u32[]{:S(2)}, u32[]{:S(2)}) collective-permute-start(bf16[2,1,2,512,128]{4,3,2,1,0:T(8,128)(2,1)} %get-tuple-element.28), channel_id=1, source_target_pairs={{0,1},{1,2},{2,3},{3,4},{4,5},{5,6},{6,7},{8,9},{9,10},{10,11},{11... | collective-permute-start | bytes 1572872 | tf_op jit(solution)/shard_map/ppermute | solution.py:363
  7.3 1.3 %collective-permute-start.1 = (bf16[2,1,2,512,128]{4,3,2,1,0:T(8,128)(2,1)}, bf16[2,1,2,512,128]{4,3,2,1,0:T(8,128)(2,1)S(1)}, u32[]{:S(2)}, u32[]{:S(2)}) collective-permute-start(bf16[2,1,2,512,128]{4,3,2,1,0:T(8,128)(2,1)} %get-tuple-element.27), channel_id=1, source_target_pairs={{1,0},{2,1},{3,2},{4,3},{5,4},{6,5},{7,6},{9,8},{10,9},{11,10},{12... | collective-permute-start | bytes 1572872 | tf_op jit(solution)/shard_map/ppermute | solution.py:364
  9.4 4.7 %shard_map.57 = bf16[2,3,160,128]{3,2,1,0:T(8,128)(2,1)} custom-call(s32[3]{0:T(128)S(1)} %pad_add_fusion.1.place_ref, s32[2,2]{1,0:T(2,128)S(1)} %copy-done.1, bf16[2,32,2,512,128]{4,3,2,1,0:T(8,128)(2,1)} %chan.9, bf16[2,32,14,2,512]{4,3,2,1,0:T(2,128)(2,1)S(1)} %bitcast.22), custom_call_target="tpu_custom_call" | custom-call | flops 452984832 | bytes 2621440 | tf_op jit(solution)/shard_map/pallas_call | solution.py:117
  14.1 1.6 %collective-permute-start.3 = (bf16[2,3,160,128]{3,2,1,0:T(8,128)(2,1)}, bf16[2,3,160,128]{3,2,1,0:T(8,128)(2,1)}, u32[]{:S(2)}, u32[]{:S(2)}) collective-permute-start(bf16[2,3,160,128]{3,2,1,0:T(8,128)(2,1)} %shard_map.57), channel_id=1, source_target_pairs={{0,8},{8,0},{1,9},{9,1},{2,10},{10,2},{3,11},{11,3},{4,12},{12,4},... | collective-permute-start | bytes 737288 | tf_op jit(solution)/shard_map/ppermute | solution.py:372
  15.7 6.9 %shard_map.58 = bf16[2,6,160,128]{3,2,1,0:T(8,128)(2,1)} custom-call(s32[3]{0:T(128)S(1)} %pad_add_fusion.1.place_ref, s32[2,2]{1,0:T(2,128)S(1)} %copy-done.1, bf16[2,32,2,512,128]{4,3,2,1,0:T(8,128)(2,1)} %chan.9, bf16[2,32,14,2,512]{4,3,2,1,0:T(2,128)(2,1)S(1)} %bitcast.23), custom_call_target="tpu_custom_call" | custom-call | flops 905969664 | bytes 4194304 | tf_op jit(solution)/shard_map/pallas_call | solution.py:117
  23.2 6.9 %shard_map.59 = bf16[2,6,160,128]{3,2,1,0:T(8,128)(2,1)} custom-call(s32[3]{0:T(128)S(1)} %pad_add_fusion.1.place_ref, s32[2,2]{1,0:T(2,128)S(1)} %copy-done.2, bf16[2,32,2,512,128]{4,3,2,1,0:T(8,128)(2,1)} %chan.9, bf16[2,32,14,2,512]{4,3,2,1,0:T(2,128)(2,1)S(1)} %bitcast.24), custom_call_target="tpu_custom_call" | custom-call | flops 905969664 | bytes 4194304 | tf_op jit(solution)/shard_map/pallas_call | solution.py:117
  30.1 1.6 %collective-permute-start.5 = (bf16[2,6,160,128]{3,2,1,0:T(8,128)(2,1)}, bf16[2,6,160,128]{3,2,1,0:T(8,128)(2,1)}, u32[]{:S(2)}, u32[]{:S(2)}) collective-permute-start(bf16[2,6,160,128]{3,2,1,0:T(8,128)(2,1)} %shard_map.59), channel_id=1, source_target_pairs={{0,8},{8,0},{1,9},{9,1},{2,10},{10,2},{3,11},{11,3},{4,12},{12,4},... | collective-permute-start | bytes 1474568 | tf_op jit(solution)/shard_map/ppermute | solution.py:372
  32.2 3.6 %shard_map.55 = (bf16[2,160,128]{2,1,0:T(8,128)(2,1)S(1)}, f32[2,160,128]{2,1,0:T(8,128)S(1)}) custom-call(s32[3]{0:T(128)S(1)} %pad_add_fusion.1.place_ref, s32[2,2]{1,0:T(2,128)S(1)} %copy-done.2, bf16[2,32,2,512,128]{4,3,2,1,0:T(8,128)(2,1)} %chan.9, bf16[2,32,14,2,512]{4,3,2,1,0:T(2,128)(2,1)S(1)} %bitcast.25, ...), custom_call_target="tpu_custom_call" | custom-call | flops 301989888 | bytes 3145728 | tf_op jit(solution)/shard_map/pallas_call | solution.py:180
  36.4 12.0 %shard_map.56.own_ref = f32[2,15,160,128]{3,2,1,0:T(8,128)S(1)} custom-call(s32[3]{0:T(128)S(1)} %pad_add_fusion.1.place_ref, s32[2,2]{1,0:T(2,128)S(1)} %copy-done.2, bf16[2,32,2,512,128]{4,3,2,1,0:T(8,128)(2,1)} %chan.9, bf16[2,32,14,2,512]{4,3,2,1,0:T(2,128)(2,1)S(1)} %bitcast.26), custom_call_target="tpu_custom_call" | custom-call | flops 2264924160 | bytes 8912896 | tf_op jit(solution)/shard_map/pallas_call | solution.py:117
  48.5 10.0 %shard_map.60.inner_ref = f32[2,512,128]{2,1,0:T(8,128)S(1)} custom-call(s32[3]{0:T(128)S(1)} %pad_add_fusion.1.place_ref, f32[2]{0:T(128)S(1)} %copy-done.3, f32[2,15,160,128]{3,2,1,0:T(8,128)S(1)} %shard_map.56.own_ref, bf16[2,3,160,128]{3,2,1,0:T(8,128)(2,1)} %collective-permute-done.3.refs_0_, ...), custom_call_target="tpu_custom_call" | custom-call | flops 125829120 | bytes 3686400 | tf_op jit(solution)/shard_map/pallas_call | solution.py:264
  58.5 1.8 %shard_map.61 = (bf16[224,128]{1,0:T(8,128)(2,1)S(1)}, bf16[224,128]{1,0:T(8,128)(2,1)S(1)}, bf16[224,128]{1,0:T(8,128)(2,1)S(1)}, bf16[224,128]{1,0:T(8,128)(2,...) custom-call(s32[3]{0:T(128)S(1)} %pad_add_fusion.1.place_ref, ...), custom_call_target="tpu_custom_call" | custom-call | flops 234881024 | bytes 524288 | tf_op jit(solution)/shard_map/pallas_call | solution.py:299
  60.3 3.7 %collective-permute-start.9 = (bf16[224,128]{1,0:T(8,128)(2,1)S(1)}, bf16[224,128]{1,0:T(8,128)(2,1)S(1)}, u32[]{:S(2)}, u32[]{:S(2)}) collective-permute-start(bf16[224,128]{1,0:T(8,128)(2,1)S(1)} %get-tuple-element.20), channel_id=1, source_target_pairs={{0,3},{1,0},{2,1},{3,2},{4,19},{5,16},{6,17},{7,18},{16,7},{17,4},... | collective-permute-start | bytes 172040 | tf_op jit(solution)/shard_map/ppermute | solution.py:402
  64.5 1.5 %collective-permute-start.7 = (bf16[224,128]{1,0:T(8,128)(2,1)S(1)}, bf16[224,128]{1,0:T(8,128)(2,1)S(1)}, u32[]{:S(2)}, u32[]{:S(2)}) collective-permute-start(bf16[224,128]{1,0:T(8,128)(2,1)S(1)} %get-tuple-element.18), channel_id=1, source_target_pairs={{0,1},{1,2},{2,3},{3,0},{4,17},{5,18},{6,19},{7,16},{16,5},{17,6},... | collective-permute-start | bytes 172040 | tf_op jit(solution)/shard_map/ppermute | solution.py:402
  66.6 6.1 %collective-permute-start.13 = (bf16[224,128]{1,0:T(8,128)(2,1)S(1)}, bf16[224,128]{1,0:T(8,128)(2,1)S(1)}, u32[]{:S(2)}, u32[]{:S(2)}) collective-permute-start(bf16[224,128]{1,0:T(8,128)(2,1)S(1)} %get-tuple-element.24), channel_id=1, source_target_pairs={{0,19},{1,16},{2,17},{3,18},{4,3},{5,0},{6,1},{7,2},{16,23},{17,20... | collective-permute-start | bytes 172040 | tf_op jit(solution)/shard_map/ppermute | solution.py:402
  72.7 2.7 %collective-permute-start.11 = (bf16[224,128]{1,0:T(8,128)(2,1)S(1)}, bf16[224,128]{1,0:T(8,128)(2,1)S(1)}, u32[]{:S(2)}, u32[]{:S(2)}) collective-permute-start(bf16[224,128]{1,0:T(8,128)(2,1)S(1)} %get-tuple-element.22), channel_id=1, source_target_pairs={{0,17},{1,18},{2,19},{3,16},{4,1},{5,2},{6,3},{7,0},{16,21},{17,22... | collective-permute-start | bytes 172040 | tf_op jit(solution)/shard_map/ppermute | solution.py:402
  75.5 1.0 %collective-permute-start.10 = (bf16[224,128]{1,0:T(8,128)(2,1)S(1)}, bf16[224,128]{1,0:T(8,128)(2,1)S(1)}, u32[]{:S(2)}, u32[]{:S(2)}) collective-permute-start(bf16[224,128]{1,0:T(8,128)(2,1)S(1)} %get-tuple-element.21), channel_id=1, source_target_pairs={{0,16},{1,17},{2,18},{3,19},{4,0},{5,1},{6,2},{7,3},{16,20},{17,21... | collective-permute-start | bytes 172040 | tf_op jit(solution)/shard_map/ppermute | solution.py:402
  76.5 1.6 %collective-permute-start.14 = (bf16[4,224,128]{2,1,0:T(8,128)(2,1)S(1)}, bf16[4,224,128]{2,1,0:T(8,128)(2,1)S(1)}, u32[]{:S(2)}, u32[]{:S(2)}) collective-permute-start(bf16[4,224,128]{2,1,0:T(8,128)(2,1)S(1)} %pad_maximum_fusion.refs_0_), channel_id=1, source_target_pairs={{0,8},{8,0},{1,9},{9,1},{2,10},{10,2},{3,11},{11,3},{4,12},{12,4},... | collective-permute-start | bytes 688136 | tf_op jit(solution)/shard_map/ppermute | solution.py:407
  78.4 0.9 collective-permute-done.12
  79.3 1.1 %collective-permute-done.11 = bf16[224,128]{1,0:T(8,128)(2,1)S(1)} collective-permute-done((bf16[224,128]{1,0:T(8,128)(2,1)S(1)}, bf16[224,128]{1,0:T(8,128)(2,1)S(1)}, u32[]{:S(2)}, u32[]{:S(2)}) %collective-permute-start.11) | collective-permute-done | bytes 57376 | tf_op jit(solution)/shard_map/ppermute | solution.py:402
  81.2 1.6 %collective-permute-start.15 = (bf16[4,224,128]{2,1,0:T(8,128)(2,1)S(1)}, bf16[4,224,128]{2,1,0:T(8,128)(2,1)S(1)}, u32[]{:S(2)}, u32[]{:S(2)}) collective-permute-start(bf16[4,224,128]{2,1,0:T(8,128)(2,1)S(1)} %pad_maximum_fusion.1.refs_1_), channel_id=1, source_target_pairs={{0,8},{8,0},{1,9},{9,1},{2,10},{10,2},{3,11},{11,3},{4,12},{12,4},... | collective-permute-start | bytes 688136 | tf_op jit(solution)/shard_map/ppermute | solution.py:407
  82.9 1.2 %collective-permute-done.14.refs_2_ = bf16[4,224,128]{2,1,0:T(8,128)(2,1)S(1)} collective-permute-done((bf16[4,224,128]{2,1,0:T(8,128)(2,1)S(1)}, bf16[4,224,128]{2,1,0:T(8,128)(2,1)S(1)}, u32[]{:S(2)}, u32[]{:S(2)}) %collective-permute-start.14) | collective-permute-done | bytes 229408 | tf_op jit(solution)/shard_map/ppermute | solution.py:407
  84.1 4.9 %collective-permute-done.15.refs_3_ = bf16[4,224,128]{2,1,0:T(8,128)(2,1)S(1)} collective-permute-done((bf16[4,224,128]{2,1,0:T(8,128)(2,1)S(1)}, bf16[4,224,128]{2,1,0:T(8,128)(2,1)S(1)}, u32[]{:S(2)}, u32[]{:S(2)}) %collective-permute-start.15) | collective-permute-done | bytes 229408 | tf_op jit(solution)/shard_map/ppermute | solution.py:407
  89.0 4.0 %shard_map.62 = bf16[2,32,14,2,256]{4,3,2,1,0:T(2,128)(2,1)} custom-call(s32[3]{0:T(128)S(1)} %pad_add_fusion.1.place_ref, s32[8]{0:T(128)S(1)} %stack.89.source_ref, bf16[4,224,128]{2,1,0:T(8,128)(2,1)S(1)} %pad_maximum_fusion.refs_0_, bf16[4,224,128]{2,1,0:T(8,128)(2,1)S(1)} %pad_maximum_fusion.1.refs_1_, ...), custom_call_target="tpu_custom_call" | custom-call | tf_op jit(solution)/shard_map/pallas_call | solution.py:341
  (35 shorter events, 4.9 us)
Async XLA Ops:
  0.0 8.7 %copy-start = (bf16[2,32,2,14,512]{4,2,3,1,0:T(2,128)(2,1)S(1)}, bf16[2,32,2,14,512]{4,2,3,1,0:T(2,128)(2,1)}, u32[]{:S(2)}) copy-start(bf16[2,32,2,14,512]{4,2,3,1,0:T(2,128)(2,1)} %param.6) | copy-start | bytes 5505028
  2.4 29.8 %collective-permute-start = (bf16[2,1,2,512,128]{4,3,2,1,0:T(8,128)(2,1)}, bf16[2,1,2,512,128]{4,3,2,1,0:T(8,128)(2,1)S(1)}, u32[]{:S(2)}, u32[]{:S(2)}) collective-permute-start(bf16[2,1,2,512,128]{4,3,2,1,0:T(8,128)(2,1)} %get-tuple-element.28), channel_id=1, source_target_pairs={{0,1},{1,2},{2,3},{3,4},{4,5},{5,6},{6,7},{8,9},{9,10},{10,11},{11... | collective-permute-start | bytes 1572872 | tf_op jit(solution)/shard_map/ppermute | solution.py:363
  7.3 24.9 %collective-permute-start.1 = (bf16[2,1,2,512,128]{4,3,2,1,0:T(8,128)(2,1)}, bf16[2,1,2,512,128]{4,3,2,1,0:T(8,128)(2,1)S(1)}, u32[]{:S(2)}, u32[]{:S(2)}) collective-permute-start(bf16[2,1,2,512,128]{4,3,2,1,0:T(8,128)(2,1)} %get-tuple-element.27), channel_id=1, source_target_pairs={{1,0},{2,1},{3,2},{4,3},{5,4},{6,5},{7,6},{9,8},{10,9},{11,10},{12... | collective-permute-start | bytes 1572872 | tf_op jit(solution)/shard_map/ppermute | solution.py:364
  8.7 0.7 copy-start.1
  14.1 9.1 %copy-start.2 = (s32[2,2]{1,0:T(2,128)S(1)}, s32[2,2]{1,0:T(2,128)}, u32[]{:S(2)}) copy-start(s32[2,2]{1,0:T(2,128)} %count_ref.9) | copy-start | bytes 52
  14.1 34.4 %collective-permute-start.3 = (bf16[2,3,160,128]{3,2,1,0:T(8,128)(2,1)}, bf16[2,3,160,128]{3,2,1,0:T(8,128)(2,1)}, u32[]{:S(2)}, u32[]{:S(2)}) collective-permute-start(bf16[2,3,160,128]{3,2,1,0:T(8,128)(2,1)} %shard_map.57), channel_id=1, source_target_pairs={{0,8},{8,0},{1,9},{9,1},{2,10},{10,2},{3,11},{11,3},{4,12},{12,4},... | collective-permute-start | bytes 737288 | tf_op jit(solution)/shard_map/ppermute | solution.py:372
  22.6 9.1 %copy-start.4 = (s32[2,128,1]{1,2,0:T(1,128)S(1)}, s32[2,128,1]{1,2,0:T(1,128)}, u32[]{:S(2)}) copy-start(s32[2,128,1]{1,2,0:T(1,128)} %param.9) | copy-start | bytes 3076
  22.6 25.9 %collective-permute-start.4 = (bf16[2,6,160,128]{3,2,1,0:T(8,128)(2,1)}, bf16[2,6,160,128]{3,2,1,0:T(8,128)(2,1)S(1)}, u32[]{:S(2)}, u32[]{:S(2)}) collective-permute-start(bf16[2,6,160,128]{3,2,1,0:T(8,128)(2,1)} %shard_map.58), channel_id=1, source_target_pairs={{0,8},{8,0},{1,9},{9,1},{2,10},{10,2},{3,11},{11,3},{4,12},{12,4},... | collective-permute-start | bytes 1474568 | tf_op jit(solution)/shard_map/ppermute | solution.py:372
  30.1 18.4 %collective-permute-start.5 = (bf16[2,6,160,128]{3,2,1,0:T(8,128)(2,1)}, bf16[2,6,160,128]{3,2,1,0:T(8,128)(2,1)}, u32[]{:S(2)}, u32[]{:S(2)}) collective-permute-start(bf16[2,6,160,128]{3,2,1,0:T(8,128)(2,1)} %shard_map.59), channel_id=1, source_target_pairs={{0,8},{8,0},{1,9},{9,1},{2,10},{10,2},{3,11},{11,3},{4,12},{12,4},... | collective-permute-start | bytes 1474568 | tf_op jit(solution)/shard_map/ppermute | solution.py:372
  35.8 12.7 %copy-start.3 = (f32[2]{0:T(128)S(1)}, f32[2]{0:T(128)}, u32[]{:S(2)}) copy-start(f32[2]{0:T(128)} %noise_ref.3) | copy-start | bytes 28
  35.8 22.7 %collective-permute-start.2 = (bf16[2,160,128]{2,1,0:T(8,128)(2,1)S(1)}, bf16[2,160,128]{2,1,0:T(8,128)(2,1)S(1)}, u32[]{:S(2)}, u32[]{:S(2)}) collective-permute-start(bf16[2,160,128]{2,1,0:T(8,128)(2,1)S(1)} %get-tuple-element.16), channel_id=1, source_target_pairs={{0,8},{8,0},{1,9},{9,1},{2,10},{10,2},{3,11},{11,3},{4,12},{12,4},... | collective-permute-start | bytes 245768 | tf_op jit(solution)/shard_map/ppermute | solution.py:376
  60.3 12.4 %collective-permute-start.9 = (bf16[224,128]{1,0:T(8,128)(2,1)S(1)}, bf16[224,128]{1,0:T(8,128)(2,1)S(1)}, u32[]{:S(2)}, u32[]{:S(2)}) collective-permute-start(bf16[224,128]{1,0:T(8,128)(2,1)S(1)} %get-tuple-element.20), channel_id=1, source_target_pairs={{0,3},{1,0},{2,1},{3,2},{4,19},{5,16},{6,17},{7,18},{16,7},{17,4},... | collective-permute-start | bytes 172040 | tf_op jit(solution)/shard_map/ppermute | solution.py:402
  64.0 8.8 %collective-permute-start.8 = (bf16[224,128]{1,0:T(8,128)(2,1)S(1)}, bf16[224,128]{1,0:T(8,128)(2,1)S(1)}, u32[]{:S(2)}, u32[]{:S(2)}) collective-permute-start(bf16[224,128]{1,0:T(8,128)(2,1)S(1)} %get-tuple-element.19), channel_id=1, source_target_pairs={{0,2},{1,3},{2,0},{3,1},{4,18},{5,19},{6,16},{7,17},{16,6},{17,7},... | collective-permute-start | bytes 172040 | tf_op jit(solution)/shard_map/ppermute | solution.py:402
  64.5 11.0 %collective-permute-start.7 = (bf16[224,128]{1,0:T(8,128)(2,1)S(1)}, bf16[224,128]{1,0:T(8,128)(2,1)S(1)}, u32[]{:S(2)}, u32[]{:S(2)}) collective-permute-start(bf16[224,128]{1,0:T(8,128)(2,1)S(1)} %get-tuple-element.18), channel_id=1, source_target_pairs={{0,1},{1,2},{2,3},{3,0},{4,17},{5,18},{6,19},{7,16},{16,5},{17,6},... | collective-permute-start | bytes 172040 | tf_op jit(solution)/shard_map/ppermute | solution.py:402
  65.9 10.5 %collective-permute-start.6 = (bf16[224,128]{1,0:T(8,128)(2,1)S(1)}, bf16[224,128]{1,0:T(8,128)(2,1)S(1)}, u32[]{:S(2)}, u32[]{:S(2)}) collective-permute-start(bf16[224,128]{1,0:T(8,128)(2,1)S(1)} %get-tuple-element.17), channel_id=1, source_target_pairs={{0,0},{1,1},{2,2},{3,3},{4,16},{5,17},{6,18},{7,19},{16,4},{17,5},... | collective-permute-start | bytes 172040 | tf_op jit(solution)/shard_map/ppermute | solution.py:402
  66.6 11.8 %collective-permute-start.13 = (bf16[224,128]{1,0:T(8,128)(2,1)S(1)}, bf16[224,128]{1,0:T(8,128)(2,1)S(1)}, u32[]{:S(2)}, u32[]{:S(2)}) collective-permute-start(bf16[224,128]{1,0:T(8,128)(2,1)S(1)} %get-tuple-element.24), channel_id=1, source_target_pairs={{0,19},{1,16},{2,17},{3,18},{4,3},{5,0},{6,1},{7,2},{16,23},{17,20... | collective-permute-start | bytes 172040 | tf_op jit(solution)/shard_map/ppermute | solution.py:402
  72.7 6.5 %collective-permute-start.12 = (bf16[224,128]{1,0:T(8,128)(2,1)S(1)}, bf16[224,128]{1,0:T(8,128)(2,1)S(1)}, u32[]{:S(2)}, u32[]{:S(2)}) collective-permute-start(bf16[224,128]{1,0:T(8,128)(2,1)S(1)} %get-tuple-element.23), channel_id=1, source_target_pairs={{0,18},{1,19},{2,16},{3,17},{4,2},{5,3},{6,0},{7,1},{16,22},{17,23... | collective-permute-start | bytes 172040 | tf_op jit(solution)/shard_map/ppermute | solution.py:402
  72.7 7.6 %collective-permute-start.11 = (bf16[224,128]{1,0:T(8,128)(2,1)S(1)}, bf16[224,128]{1,0:T(8,128)(2,1)S(1)}, u32[]{:S(2)}, u32[]{:S(2)}) collective-permute-start(bf16[224,128]{1,0:T(8,128)(2,1)S(1)} %get-tuple-element.22), channel_id=1, source_target_pairs={{0,17},{1,18},{2,19},{3,16},{4,1},{5,2},{6,3},{7,0},{16,21},{17,22... | collective-permute-start | bytes 172040 | tf_op jit(solution)/shard_map/ppermute | solution.py:402
  75.5 5.7 %collective-permute-start.10 = (bf16[224,128]{1,0:T(8,128)(2,1)S(1)}, bf16[224,128]{1,0:T(8,128)(2,1)S(1)}, u32[]{:S(2)}, u32[]{:S(2)}) collective-permute-start(bf16[224,128]{1,0:T(8,128)(2,1)S(1)} %get-tuple-element.21), channel_id=1, source_target_pairs={{0,16},{1,17},{2,18},{3,19},{4,0},{5,1},{6,2},{7,3},{16,20},{17,21... | collective-permute-start | bytes 172040 | tf_op jit(solution)/shard_map/ppermute | solution.py:402
  76.5 7.6 %collective-permute-start.14 = (bf16[4,224,128]{2,1,0:T(8,128)(2,1)S(1)}, bf16[4,224,128]{2,1,0:T(8,128)(2,1)S(1)}, u32[]{:S(2)}, u32[]{:S(2)}) collective-permute-start(bf16[4,224,128]{2,1,0:T(8,128)(2,1)S(1)} %pad_maximum_fusion.refs_0_), channel_id=1, source_target_pairs={{0,8},{8,0},{1,9},{9,1},{2,10},{10,2},{3,11},{11,3},{4,12},{12,4},... | collective-permute-start | bytes 688136 | tf_op jit(solution)/shard_map/ppermute | solution.py:407
  81.2 7.8 %collective-permute-start.15 = (bf16[4,224,128]{2,1,0:T(8,128)(2,1)S(1)}, bf16[4,224,128]{2,1,0:T(8,128)(2,1)S(1)}, u32[]{:S(2)}, u32[]{:S(2)}) collective-permute-start(bf16[4,224,128]{2,1,0:T(8,128)(2,1)S(1)} %pad_maximum_fusion.1.refs_1_), channel_id=1, source_target_pairs={{0,8},{8,0},{1,9},{9,1},{2,10},{10,2},{3,11},{11,3},{4,12},{12,4},... | collective-permute-start | bytes 688136 | tf_op jit(solution)/shard_map/ppermute | solution.py:407

commit v2 on v1

--- a/solution.py
+++ b/solution.py
@@ -8,7 +8,6 @@
 F32, BF16 = jnp.float32, jnp.bfloat16
 SPAD = 16
 VMEM_LIMIT = 40 << 20
-CHUNKS = (3, 6, 6)
 SWAP = [(0, 1), (1, 0)]
 
 SMEM_SPEC = pl.BlockSpec(memory_space=pltpu.SMEM)
@@ -16,7 +15,7 @@
 ANY_SPEC = pl.BlockSpec(memory_space=pl.ANY)
 
 
-def prepare(below, here, above, samples, factor, mat, lhs):
+def prepare(below, here, above, samples, stretch, mat, lhs):
     antennas, users = here.shape[1:]
     symbols = samples.shape[0]
     slab = 128
@@ -26,22 +25,26 @@
         for row in range(0, antennas, slab):
             rows = pl.ds(row, slab)
             outer = below[k, rows, :].astype(F32) + above[k, rows, :].astype(F32)
-            smooth = outer * 0.25 + here[k, rows, :].astype(F32) * 0.5
-            value = (smooth * factor).astype(BF16)
+            middle = here[k, rows, :]
+            value = outer + (middle + middle).astype(F32)
+            value = (value if stretch is None else value * stretch).astype(BF16)
             mat[rows, k * users : (k + 1) * users] = value
             lhs[k * users : (k + 1) * users, rows] = value.T
 
 
-def gram(mat, lhs, out, users):
+def gram(mat, lhs, out, count, users):
     product = jnp.dot(lhs[...], mat[...], preferred_element_type=F32)
     row = lax.broadcasted_iota(jnp.int32, (users, users), 0)
     col = lax.broadcasted_iota(jnp.int32, (users, users), 1)
     real = product[:users, :users] + product[users : 2 * users, users:]
     imag = product[:users, users:] - product[users : 2 * users, :users]
-    out[:users, :] = jnp.where(row <= col, real, imag).astype(out.dtype)
+    packed = jnp.where(row <= col, real, imag)
+    out[:users, :] = jnp.where(jnp.maximum(row, col) < count, packed * 0.0625, 0.0).astype(out.dtype)
+    lane = lax.broadcasted_iota(jnp.int32, (1, users), 1)
+    scale = jnp.where(lane < count, 0.25, 0.0)
     low, high = product[2 * users : 2 * users + SPAD], product[2 * users + SPAD :]
-    out[users : users + SPAD, :] = (low[:, :users] + high[:, users:]).astype(out.dtype)
-    out[users + SPAD :, :] = (high[:, :users] - low[:, users:]).astype(out.dtype)
+    out[users : users + SPAD, :] = ((low[:, :users] + high[:, users:]) * scale).astype(out.dtype)
+    out[users + SPAD :, :] = ((high[:, :users] - low[:, users:]) * scale).astype(out.dtype)
 
 
 def work_buffers(antennas, users):
@@ -69,12 +72,12 @@
             return pltpu.make_async_copy(samp.at[c, pl.ds(start, number)], ybuf.at[c], ysem.at[c])
 
         for c in range(cells):
-            fetch_samples(c).start()
             for i in range(number + 2):
                 fetch(c, i).start()
+                if i == min(2, number):
+                    fetch_samples(c).start()
         lhs_a[...] = jnp.zeros_like(lhs_a)
         lhs_b[...] = jnp.zeros_like(lhs_b)
-        lane = lax.broadcasted_iota(jnp.int32, (1, users), 1)
 
         def wait(item):
             c, i = item // number, item % number
@@ -92,12 +95,12 @@
         def ready(item, mat, lhs):
             item = jnp.minimum(item, items - 1)
             c, i = item // number, item % number
-            factor = (lane < count_ref[c, (start + i) // group]).astype(F32)
-            prepare(win.at[c, i], win.at[c, i + 1], win.at[c, i + 2], ybuf.at[c, i], factor, mat, lhs)
+            prepare(win.at[c, i], win.at[c, i + 1], win.at[c, i + 2], ybuf.at[c, i], None, mat, lhs)
 
         def multiply(item, mat, lhs):
             item = jnp.minimum(item, items - 1)
-            gram(mat, lhs, out.at[item // number, item % number], users)
+            c, i = item // number, item % number
+            gram(mat, lhs, out.at[c, i], count_ref[c, (start + i) // group], users)
 
         wait(0)
         ready(0, mat_a, lhs_a)
@@ -136,67 +139,64 @@
     )(place, counts, channel, received)
 
 
-def edge_gram(place, counts, channel, received, low, high):
+def edge_gram(place, counts, channel, received, low, high, peer, dtype):
     cells, band, _, antennas, users = channel.shape
     symbols = received.shape[2]
     group = band // counts.shape[1]
 
-    def kernel(place_ref, count_ref, chan, samp, low_ref, high_ref, out_peer, out_own, win, ybuf, mat_a, lhs_a, mat_b, lhs_b, wsem, ysem):
-        def sources(c):
-            return (
-                (low_ref.at[c, 0], chan.at[c, 0], chan.at[c, 1], samp.at[c, 0]),
-                (chan.at[c, band - 2], chan.at[c, band - 1], high_ref.at[c, 0], samp.at[c, band - 1]),
-            )
-
-        copies = []
-        for c in range(cells):
-            for e in range(2):
-                *blocks, samples = sources(c)[e]
-                for i, block in enumerate(blocks):
-                    copies.append(pltpu.make_async_copy(block, win.at[e, c, i], wsem.at[e, c, i]))
-                copies.append(pltpu.make_async_copy(samples, ybuf.at[e, c], ysem.at[e, c]))
-        for copy in copies:
-            copy.start()
+    def kernel(place_ref, count_ref, chan, samp, low_ref, high_ref, out, win, ybuf, mat_a, lhs_a, mat_b, lhs_b, wsem, ysem):
+        side = 1 - place_ref[0] if peer else place_ref[0]
+
+        def each_copy(act):
+            def run(e):
+                for c in range(cells):
+                    blocks = (
+                        (low_ref.at[c, 0], chan.at[c, 0], chan.at[c, 1]),
+                        (chan.at[c, band - 2], chan.at[c, band - 1], high_ref.at[c, 0]),
+                    )[e]
+                    for i, block in enumerate(blocks):
+                        act(pltpu.make_async_copy(block, win.at[c, i], wsem.at[c, i]))
+                    act(pltpu.make_async_copy(samp.at[c, e * (band - 1)], ybuf.at[c], ysem.at[c]))
+
+            @pl.when(side == 0)
+            def _():
+                run(0)
+
+            @pl.when(side == 1)
+            def _():
+                run(1)
+
+        each_copy(lambda copy: copy.start())
         lhs_a[...] = jnp.zeros_like(lhs_a)
         lhs_b[...] = jnp.zeros_like(lhs_b)
-        lane = lax.broadcasted_iota(jnp.int32, (1, users), 1)
-        for copy in copies:
-            copy.wait()
-        own = place_ref[0]
-
-        def ready(e, c, mat, lhs):
-            weight = jnp.where(place_ref[1 + e] == 1, 0.75, 1.0)
-            count = count_ref[c, e * (band - 1) // group]
-            factor = (lane < count).astype(F32) / jnp.full((1, users), weight, F32)
-            prepare(win.at[e, c, 0], win.at[e, c, 1], win.at[e, c, 2], ybuf.at[e, c], factor, mat, lhs)
-
-        for out, e in ((out_peer, 1 - own), (out_own, own)):
-            for c in range(cells):
-                mat, lhs = ((mat_a, lhs_a), (mat_b, lhs_b))[c % 2]
-                ready(e, c, mat, lhs)
-                gram(mat, lhs, out.at[c], users)
+        each_copy(lambda copy: copy.wait())
+        last = jnp.where(side == 0, place_ref[1], place_ref[2])
+        stretch = jnp.where(jnp.full((1, users), last, jnp.int32) == 1, 1 / 0.75, 1.0)
+        buffers = ((mat_a, lhs_a), (mat_b, lhs_b))
+        for c in range(cells):
+            mat, lhs = buffers[c % 2]
+            prepare(win.at[c, 0], win.at[c, 1], win.at[c, 2], ybuf.at[c], stretch, mat, lhs)
+        for c in range(cells):
+            gram(*buffers[c % 2], out.at[c], count_ref[c, side * (band - 1) // group], users)
 
     rows = users + 2 * SPAD
     return pl.pallas_call(
         kernel,
         in_specs=[SMEM_SPEC, SMEM_SPEC, ANY_SPEC, ANY_SPEC, ANY_SPEC, ANY_SPEC],
-        out_specs=[VMEM_SPEC, VMEM_SPEC],
-        out_shape=[
-            jax.ShapeDtypeStruct((cells, rows, users), BF16),
-            jax.ShapeDtypeStruct((cells, rows, users), F32),
-        ],
+        out_specs=VMEM_SPEC,
+        out_shape=jax.ShapeDtypeStruct((cells, rows, users), dtype),
         scratch_shapes=[
-            pltpu.VMEM((2, cells, 3, 2, antennas, users), BF16),
-            pltpu.VMEM((2, cells, symbols, 2, antennas), BF16),
+            pltpu.VMEM((cells, 3, 2, antennas, users), BF16),
+            pltpu.VMEM((cells, symbols, 2, antennas), BF16),
             *work_buffers(antennas, users),
             *work_buffers(antennas, users),
-            pltpu.SemaphoreType.DMA((2, cells, 3)),
-            pltpu.SemaphoreType.DMA((2, cells)),
+            pltpu.SemaphoreType.DMA((cells, 3)),
+            pltpu.SemaphoreType.DMA((cells,)),
         ],
         compiler_params=pltpu.CompilerParams(vmem_limit_bytes=VMEM_LIMIT),
         cost_estimate=pl.CostEstimate(
-            flops=2 * cells * 4 * antennas * users * 2 * (users + SPAD),
-            bytes_accessed=2 * cells * 12 * antennas * users,
+            flops=cells * 4 * antennas * users * 2 * (users + SPAD),
+            bytes_accessed=cells * 12 * antennas * users,
             transcendentals=0,
         ),
     )(place, counts, channel, received, low, high)
@@ -208,11 +208,11 @@
     upper = row <= col
     grams = []
     for value in sums:
-        packed = value[:users]
+        packed = value[:users].astype(BF16)
         turned = packed.T
         real = jnp.where(upper, packed, turned)
-        imag = jnp.where(row == col, 0.0, jnp.where(upper, -turned, packed))
-        grams.append(jnp.concatenate([real, imag], axis=1).astype(BF16))
+        imag = jnp.where(row == col, jnp.zeros_like(packed), jnp.where(upper, -turned, packed))
+        grams.append(jnp.concatenate([real, imag], axis=1))
 
     def apply(matrix, vector):
         product = jnp.dot(vector.astype(BF16), matrix, preferred_element_type=F32)
@@ -241,25 +241,21 @@
 def inner_detect(place, noise_power, own, peers):
     cells, inner, rows, users = own.shape
     half = inner + 1
-    batch = 3
 
     def kernel(place_ref, noise_ref, own_ref, *refs):
         *peer_refs, out = refs
         shift = 1 - place_ref[0]
-        start = 0
-        for peer_ref in peer_refs:
-            number = peer_ref.shape[1]
-
-            def step(t, carry, start=start, peer_ref=peer_ref, number=number):
-                steps = number // batch
-                c, base = t // steps, t % steps * batch
-                sums = [own_ref[c, start + base + i] + peer_ref[c, base + i].astype(F32) for i in range(batch)]
-                for i, value in enumerate(conjugate_gradient(sums, noise_ref[c], users)):
-                    out[c, pl.ds(start + base + i + shift, 2 * SPAD, stride=half), :] = value
-                return carry
-
-            lax.fori_loop(0, cells * (number // batch), step, 0)
-            start += number
+
+        def step(c, carry):
+            sums = []
+            for peer_ref in peer_refs:
+                for i in range(peer_ref.shape[1]):
+                    sums.append(own_ref[c, len(sums)] + peer_ref[c, i].astype(F32))
+            for i, value in enumerate(conjugate_gradient(sums, noise_ref[c], users)):
+                out[c, pl.ds(i + shift, 2 * SPAD, stride=half), :] = value
+            return carry
+
+        lax.fori_loop(0, cells, step, 0)
 
     return pl.pallas_call(
         kernel,
@@ -367,13 +363,14 @@
     samples = jnp.transpose(received, (0, 1, 3, 2, 4))
 
     peers, first = [], 0
-    for number in CHUNKS:
+    for number in (3, 6, half - 10):
         outgoing = inner_gram(place, user_count, channel, samples, True, first, number, BF16)
         peers.append(lax.ppermute(outgoing, "panel", SWAP))
         first += number
     own = inner_gram(place, user_count, channel, samples, False, 0, half - 1, F32)
-    edge_out, edge_own = edge_gram(place, user_count, channel, samples, low, high)
+    edge_out = edge_gram(place, user_count, channel, samples, low, high, True, BF16)
     edge_peer = lax.ppermute(edge_out, "panel", SWAP)
+    edge_own = edge_gram(place, user_count, channel, samples, low, high, False, F32)
     inner = inner_detect(place, noise_power, own, peers)
 
     capacity = cells * users // n_cell

time: 93.3 us -> 86.6 us (0.928)
  Pallas kernels: 50 us -> 42 us
  waiting for transfers between devices: 9.3 us -> 12.3 us
  starting transfers between devices: 29.8 us -> 28 us
    pallas_call x1, Pallas kernels: 9.99 us -> 3.73 us  [inner_detect(): pl.pallas_call(kernel, in_specs=[SMEM_SPEC, SMEM_SPEC, VMEM_SPEC] + [VMEM...]
    pallas_call x4, Pallas kernels: 30.6 us -> 27.4 us  [inner_gram(): pl.pallas_call(kernel, in_specs=[SMEM_SPEC, SMEM_SPEC, ANY_SPEC, ANY_SPEC...]
    ppermute x2, starting transfers between devices: 3.12 us -> 1.17 us  [body(): theirs = [lax.ppermute(group, 'panel', SWAP) for group in mine]]
    pallas_call x1 -> x2, Pallas kernels: 3.62 us -> 5.1 us  [edge_gram(): pl.pallas_call(kernel, in_specs=[SMEM_SPEC, SMEM_SPEC, ANY_SPEC, ANY_SPEC...]
    ppermute x3, waiting for transfers between devices: 0.01 us -> 1.06 us  [body(): peers.append(lax.ppermute(outgoing, 'panel', SWAP))]
    ppermute x2, waiting for transfers between devices: 6.14 us -> 7.12 us  [body(): theirs = [lax.ppermute(group, 'panel', SWAP) for group in mine]]
    ppermute x8, waiting for transfers between devices: 3.14 us -> 4.12 us  [body(): arrived.append(lax.ppermute(messages[a * reach + b], ('cell', 'sc'), pairs))]
  transfers between devices with their start and end apart: 16 -> 16, of which waited for: 6 -> 7; matrix products, arithmetic and copies ran while one was open for 1% -> 1% of each run, Pallas kernels for 47% -> 42%
where the time goes in v2:
time: 86.6 us; the launch traced here: 86.3 us
  Pallas kernels  42 us (48%)
  starting transfers between devices  28 us (32%)
  waiting for transfers between devices  12.3 us (14%)
  local copies, waits for them, and re-layouts  3.18 us (4%)
    pallas_call x4, Pallas kernels, inner_gram(): pl.pallas_call(kernel, in_specs=[SMEM_SPEC, SMEM_SPEC, ANY_SPEC, ANY_SPEC...  27.4 us
    ppermute x8, starting transfers between devices, body(): arrived.append(lax.ppermute(messages[a * reach + b], ('cell', 'sc'), pairs))  15.9 us
    ppermute x2, waiting for transfers between devices, body(): theirs = [lax.ppermute(group, 'panel', SWAP) for group in mine]  7.12 us
    pallas_call x2, Pallas kernels, edge_gram(): pl.pallas_call(kernel, in_specs=[SMEM_SPEC, SMEM_SPEC, ANY_SPEC, ANY_SPEC...  5.1 us
    ppermute x1, starting transfers between devices, body(): low = lax.ppermute(channel[:, band - 1:], 'sc', upward)  4.89 us
    ppermute x8, waiting for transfers between devices, body(): arrived.append(lax.ppermute(messages[a * reach + b], ('cell', 'sc'), pairs))  4.12 us
    pallas_call x1, Pallas kernels, assemble(): pl.pallas_call(kernel, in_specs=[SMEM_SPEC, SMEM_SPEC] + [VMEM_SPEC] * (2...  4.04 us
    pallas_call x1, Pallas kernels, inner_detect(): pl.pallas_call(kernel, in_specs=[SMEM_SPEC, SMEM_SPEC, VMEM_SPEC] + [VMEM...  3.73 us
  transfers between devices with their start and end apart: 16, of which 7 were waited for; matrix products, arithmetic and copies ran while one was open for 1% of the time, Pallas kernels for 42%

profile of v2, /device:TPU:0, one launch (start us, length us, event | category | flops | bytes accessed | tf_op | source)
XLA Modules:
  0.0 86.3 jit_solution(14021487997211439405)
XLA Ops:
  0.0 2.4 %fusion.9 = (bf16[2,1,2,512,128]{4,3,2,1,0:T(8,128)(2,1)}, bf16[2,1,2,512,128]{4,3,2,1,0:T(8,128)(2,1)}) fusion(bf16[2,32,2,512,128]{4,3,2,1,0:T(8,128)(2,1)} %chan.11), kind=kLoop, calls=%fused_computation.32 | loop fusion | bytes 2097152 | tf_op jit(solution)/shard_map/slice | solution.py:360
  2.4 4.9 %collective-permute-start = (bf16[2,1,2,512,128]{4,3,2,1,0:T(8,128)(2,1)}, bf16[2,1,2,512,128]{4,3,2,1,0:T(8,128)(2,1)S(1)}, u32[]{:S(2)}, u32[]{:S(2)}) collective-permute-start(bf16[2,1,2,512,128]{4,3,2,1,0:T(8,128)(2,1)} %get-tuple-element.24), channel_id=1, source_target_pairs={{0,1},{1,2},{2,3},{3,4},{4,5},{5,6},{6,7},{8,9},{9,10},{10,11},{11... | collective-permute-start | bytes 1572872 | tf_op jit(solution)/shard_map/ppermute | solution.py:359
  7.3 1.3 %collective-permute-start.1 = (bf16[2,1,2,512,128]{4,3,2,1,0:T(8,128)(2,1)}, bf16[2,1,2,512,128]{4,3,2,1,0:T(8,128)(2,1)S(1)}, u32[]{:S(2)}, u32[]{:S(2)}) collective-permute-start(bf16[2,1,2,512,128]{4,3,2,1,0:T(8,128)(2,1)} %get-tuple-element.23), channel_id=1, source_target_pairs={{1,0},{2,1},{3,2},{4,3},{5,4},{6,5},{7,6},{9,8},{10,9},{11,10},{12... | collective-permute-start | bytes 1572872 | tf_op jit(solution)/shard_map/ppermute | solution.py:360
  9.4 4.4 %shard_map.58 = bf16[2,3,160,128]{3,2,1,0:T(8,128)(2,1)} custom-call(s32[3]{0:T(128)S(1)} %pad_add_fusion.1.place_ref, s32[2,2]{1,0:T(2,128)S(1)} %copy-done.1, bf16[2,32,2,512,128]{4,3,2,1,0:T(8,128)(2,1)} %chan.11, bf16[2,32,14,2,512]{4,3,2,1,0:T(2,128)(2,1)S(1)} %bitcast.22), custom_call_target="tpu_custom_call" | custom-call | flops 452984832 | bytes 2621440 | tf_op jit(solution)/shard_map/pallas_call | solution.py:120
  13.7 1.6 %collective-permute-start.3 = (bf16[2,3,160,128]{3,2,1,0:T(8,128)(2,1)}, bf16[2,3,160,128]{3,2,1,0:T(8,128)(2,1)}, u32[]{:S(2)}, u32[]{:S(2)}) collective-permute-start(bf16[2,3,160,128]{3,2,1,0:T(8,128)(2,1)} %shard_map.58), channel_id=1, source_target_pairs={{0,8},{8,0},{1,9},{9,1},{2,10},{10,2},{3,11},{11,3},{4,12},{12,4},... | collective-permute-start | bytes 737288 | tf_op jit(solution)/shard_map/ppermute | solution.py:368
  15.3 6.2 %shard_map.59 = bf16[2,6,160,128]{3,2,1,0:T(8,128)(2,1)} custom-call(s32[3]{0:T(128)S(1)} %pad_add_fusion.1.place_ref, s32[2,2]{1,0:T(2,128)S(1)} %copy-done.1, bf16[2,32,2,512,128]{4,3,2,1,0:T(8,128)(2,1)} %chan.11, bf16[2,32,14,2,512]{4,3,2,1,0:T(2,128)(2,1)S(1)} %bitcast.23), custom_call_target="tpu_custom_call" | custom-call | flops 905969664 | bytes 4194304 | tf_op jit(solution)/shard_map/pallas_call | solution.py:120
  22.1 6.2 %shard_map.60 = bf16[2,6,160,128]{3,2,1,0:T(8,128)(2,1)} custom-call(s32[3]{0:T(128)S(1)} %pad_add_fusion.1.place_ref, s32[2,2]{1,0:T(2,128)S(1)} %copy-done.2, bf16[2,32,2,512,128]{4,3,2,1,0:T(8,128)(2,1)} %chan.11, bf16[2,32,14,2,512]{4,3,2,1,0:T(2,128)(2,1)S(1)} %bitcast.24), custom_call_target="tpu_custom_call" | custom-call | flops 905969664 | bytes 4194304 | tf_op jit(solution)/shard_map/pallas_call | solution.py:120
  28.4 1.6 %collective-permute-start.5 = (bf16[2,6,160,128]{3,2,1,0:T(8,128)(2,1)}, bf16[2,6,160,128]{3,2,1,0:T(8,128)(2,1)}, u32[]{:S(2)}, u32[]{:S(2)}) collective-permute-start(bf16[2,6,160,128]{3,2,1,0:T(8,128)(2,1)} %shard_map.60), channel_id=1, source_target_pairs={{0,8},{8,0},{1,9},{9,1},{2,10},{10,2},{3,11},{11,3},{4,12},{12,4},... | collective-permute-start | bytes 1474568 | tf_op jit(solution)/shard_map/ppermute | solution.py:368
  30.4 2.5 %shard_map.56 = bf16[2,160,128]{2,1,0:T(8,128)(2,1)S(1)} custom-call(s32[3]{0:T(128)S(1)} %pad_add_fusion.1.place_ref, s32[2,2]{1,0:T(2,128)S(1)} %copy-done.2, bf16[2,32,2,512,128]{4,3,2,1,0:T(8,128)(2,1)} %chan.11, bf16[2,32,14,2,512]{4,3,2,1,0:T(2,128)(2,1)S(1)} %bitcast.25, bf16[2,1,2,512,128]{4,3,2,1,0:T(8,128)(2,1)S(1)} %collective-permute-done.low_ref, ...), custom_call_target="tpu_custom_call" | custom-call | flops 150994944 | bytes 1572864 | tf_op jit(solution)/shard_map/pallas_call | solution.py:183
  33.0 1.1 %collective-permute-start.2 = (bf16[2,160,128]{2,1,0:T(8,128)(2,1)S(1)}, bf16[2,160,128]{2,1,0:T(8,128)(2,1)S(1)}, u32[]{:S(2)}, u32[]{:S(2)}) collective-permute-start(bf16[2,160,128]{2,1,0:T(8,128)(2,1)S(1)} %shard_map.56), channel_id=1, source_target_pairs={{0,8},{8,0},{1,9},{9,1},{2,10},{10,2},{3,11},{11,3},{4,12},{12,4},... | collective-permute-start | bytes 245768 | tf_op jit(solution)/shard_map/ppermute | solution.py:372
  34.1 10.5 %shard_map.57.own_ref = f32[2,15,160,128]{3,2,1,0:T(8,128)S(1)} custom-call(s32[3]{0:T(128)S(1)} %pad_add_fusion.1.place_ref, s32[2,2]{1,0:T(2,128)S(1)} %copy-done.2, bf16[2,32,2,512,128]{4,3,2,1,0:T(8,128)(2,1)} %chan.11, bf16[2,32,14,2,512]{4,3,2,1,0:T(2,128)(2,1)S(1)} %bitcast.26), custom_call_target="tpu_custom_call" | custom-call | flops 2264924160 | bytes 8912896 | tf_op jit(solution)/shard_map/pallas_call | solution.py:120
  44.7 1.1 %collective-permute-done.5.refs_2_ = bf16[2,6,160,128]{3,2,1,0:T(8,128)(2,1)} collective-permute-done((bf16[2,6,160,128]{3,2,1,0:T(8,128)(2,1)}, bf16[2,6,160,128]{3,2,1,0:T(8,128)(2,1)}, u32[]{:S(2)}, u32[]{:S(2)}) %collective-permute-start.5) | collective-permute-done | bytes 491552 | tf_op jit(solution)/shard_map/ppermute | solution.py:368
  45.7 3.7 %shard_map.61.inner_ref = f32[2,512,128]{2,1,0:T(8,128)S(1)} custom-call(s32[3]{0:T(128)S(1)} %pad_add_fusion.1.place_ref, f32[2]{0:T(128)S(1)} %copy-done.3, f32[2,15,160,128]{3,2,1,0:T(8,128)S(1)} %shard_map.57.own_ref, bf16[2,3,160,128]{3,2,1,0:T(8,128)(2,1)} %collective-permute-done.3.refs_0_, ...), custom_call_target="tpu_custom_call" | custom-call | flops 125829120 | bytes 3686400 | tf_op jit(solution)/shard_map/pallas_call | solution.py:260
  49.5 2.6 %shard_map.55.own_ref = f32[2,160,128]{2,1,0:T(8,128)S(1)} custom-call(s32[3]{0:T(128)S(1)} %pad_add_fusion.1.place_ref, s32[2,2]{1,0:T(2,128)S(1)} %copy-done.2, bf16[2,32,2,512,128]{4,3,2,1,0:T(8,128)(2,1)} %chan.11, bf16[2,32,14,2,512]{4,3,2,1,0:T(2,128)(2,1)S(1)} %bitcast.27, bf16[2,1,2,512,128]{4,3,2,1,0:T(8,128)(2,1)S(1)} %collective-permute-done.low_ref, ...), custom_call_target="tpu_custom_call" | custom-call | flops 150994944 | bytes 1572864 | tf_op jit(solution)/shard_map/pallas_call | solution.py:183
  52.1 1.7 %shard_map.62 = (bf16[224,128]{1,0:T(8,128)(2,1)S(1)}, bf16[224,128]{1,0:T(8,128)(2,1)S(1)}, bf16[224,128]{1,0:T(8,128)(2,1)S(1)}, bf16[224,128]{1,0:T(8,128)(2,...) custom-call(s32[3]{0:T(128)S(1)} %pad_add_fusion.1.place_ref, ...), custom_call_target="tpu_custom_call" | custom-call | flops 234881024 | bytes 524288 | tf_op jit(solution)/shard_map/pallas_call | solution.py:295
  53.8 3.4 %collective-permute-start.9 = (bf16[224,128]{1,0:T(8,128)(2,1)S(1)}, bf16[224,128]{1,0:T(8,128)(2,1)S(1)}, u32[]{:S(2)}, u32[]{:S(2)}) collective-permute-start(bf16[224,128]{1,0:T(8,128)(2,1)S(1)} %get-tuple-element.16), channel_id=1, source_target_pairs={{0,3},{1,0},{2,1},{3,2},{4,19},{5,16},{6,17},{7,18},{16,7},{17,4},... | collective-permute-start | bytes 172040 | tf_op jit(solution)/shard_map/ppermute | solution.py:399
  57.7 1.5 %collective-permute-start.7 = (bf16[224,128]{1,0:T(8,128)(2,1)S(1)}, bf16[224,128]{1,0:T(8,128)(2,1)S(1)}, u32[]{:S(2)}, u32[]{:S(2)}) collective-permute-start(bf16[224,128]{1,0:T(8,128)(2,1)S(1)} %get-tuple-element.14), channel_id=1, source_target_pairs={{0,1},{1,2},{2,3},{3,0},{4,17},{5,18},{6,19},{7,16},{16,5},{17,6},... | collective-permute-start | bytes 172040 | tf_op jit(solution)/shard_map/ppermute | solution.py:399
  59.8 6.1 %collective-permute-start.13 = (bf16[224,128]{1,0:T(8,128)(2,1)S(1)}, bf16[224,128]{1,0:T(8,128)(2,1)S(1)}, u32[]{:S(2)}, u32[]{:S(2)}) collective-permute-start(bf16[224,128]{1,0:T(8,128)(2,1)S(1)} %get-tuple-element.20), channel_id=1, source_target_pairs={{0,19},{1,16},{2,17},{3,18},{4,3},{5,0},{6,1},{7,2},{16,23},{17,20... | collective-permute-start | bytes 172040 | tf_op jit(solution)/shard_map/ppermute | solution.py:399
  66.0 2.7 %collective-permute-start.11 = (bf16[224,128]{1,0:T(8,128)(2,1)S(1)}, bf16[224,128]{1,0:T(8,128)(2,1)S(1)}, u32[]{:S(2)}, u32[]{:S(2)}) collective-permute-start(bf16[224,128]{1,0:T(8,128)(2,1)S(1)} %get-tuple-element.18), channel_id=1, source_target_pairs={{0,17},{1,18},{2,19},{3,16},{4,1},{5,2},{6,3},{7,0},{16,21},{17,22... | collective-permute-start | bytes 172040 | tf_op jit(solution)/shard_map/ppermute | solution.py:399
  70.3 1.3 %collective-permute-done.13 = bf16[224,128]{1,0:T(8,128)(2,1)S(1)} collective-permute-done((bf16[224,128]{1,0:T(8,128)(2,1)S(1)}, bf16[224,128]{1,0:T(8,128)(2,1)S(1)}, u32[]{:S(2)}, u32[]{:S(2)}) %collective-permute-start.13) | collective-permute-done | bytes 57376 | tf_op jit(solution)/shard_map/ppermute | solution.py:399
  72.5 1.1 %collective-permute-done.11 = bf16[224,128]{1,0:T(8,128)(2,1)S(1)} collective-permute-done((bf16[224,128]{1,0:T(8,128)(2,1)S(1)}, bf16[224,128]{1,0:T(8,128)(2,1)S(1)}, u32[]{:S(2)}, u32[]{:S(2)}) %collective-permute-start.11) | collective-permute-done | bytes 57376 | tf_op jit(solution)/shard_map/ppermute | solution.py:399
  75.1 2.2 %collective-permute-done.14.refs_2_ = bf16[4,224,128]{2,1,0:T(8,128)(2,1)S(1)} collective-permute-done((bf16[4,224,128]{2,1,0:T(8,128)(2,1)S(1)}, bf16[4,224,128]{2,1,0:T(8,128)(2,1)S(1)}, u32[]{:S(2)}, u32[]{:S(2)}) %collective-permute-start.14) | collective-permute-done | bytes 229408 | tf_op jit(solution)/shard_map/ppermute | solution.py:404
  77.3 4.9 %collective-permute-done.15.refs_3_ = bf16[4,224,128]{2,1,0:T(8,128)(2,1)S(1)} collective-permute-done((bf16[4,224,128]{2,1,0:T(8,128)(2,1)S(1)}, bf16[4,224,128]{2,1,0:T(8,128)(2,1)S(1)}, u32[]{:S(2)}, u32[]{:S(2)}) %collective-permute-start.15) | collective-permute-done | bytes 229408 | tf_op jit(solution)/shard_map/ppermute | solution.py:404
  82.2 4.0 %shard_map.63 = bf16[2,32,14,2,256]{4,3,2,1,0:T(2,128)(2,1)} custom-call(s32[3]{0:T(128)S(1)} %pad_add_fusion.1.place_ref, s32[8]{0:T(128)S(1)} %stack.89.source_ref, bf16[4,224,128]{2,1,0:T(8,128)(2,1)S(1)} %pad_maximum_fusion.refs_0_, bf16[4,224,128]{2,1,0:T(8,128)(2,1)S(1)} %pad_maximum_fusion.1.refs_1_, ...), custom_call_target="tpu_custom_call" | custom-call | tf_op jit(solution)/shard_map/pallas_call | solution.py:337
  (36 shorter events, 7.1 us)
Async XLA Ops:
  0.0 8.7 %copy-start = (bf16[2,32,2,14,512]{4,2,3,1,0:T(2,128)(2,1)S(1)}, bf16[2,32,2,14,512]{4,2,3,1,0:T(2,128)(2,1)}, u32[]{:S(2)}) copy-start(bf16[2,32,2,14,512]{4,2,3,1,0:T(2,128)(2,1)} %param.6) | copy-start | bytes 5505028
  2.4 28.0 %collective-permute-start = (bf16[2,1,2,512,128]{4,3,2,1,0:T(8,128)(2,1)}, bf16[2,1,2,512,128]{4,3,2,1,0:T(8,128)(2,1)S(1)}, u32[]{:S(2)}, u32[]{:S(2)}) collective-permute-start(bf16[2,1,2,512,128]{4,3,2,1,0:T(8,128)(2,1)} %get-tuple-element.24), channel_id=1, source_target_pairs={{0,1},{1,2},{2,3},{3,4},{4,5},{5,6},{6,7},{8,9},{9,10},{10,11},{11... | collective-permute-start | bytes 1572872 | tf_op jit(solution)/shard_map/ppermute | solution.py:359
  7.3 23.1 %collective-permute-start.1 = (bf16[2,1,2,512,128]{4,3,2,1,0:T(8,128)(2,1)}, bf16[2,1,2,512,128]{4,3,2,1,0:T(8,128)(2,1)S(1)}, u32[]{:S(2)}, u32[]{:S(2)}) collective-permute-start(bf16[2,1,2,512,128]{4,3,2,1,0:T(8,128)(2,1)} %get-tuple-element.23), channel_id=1, source_target_pairs={{1,0},{2,1},{3,2},{4,3},{5,4},{6,5},{7,6},{9,8},{10,9},{11,10},{12... | collective-permute-start | bytes 1572872 | tf_op jit(solution)/shard_map/ppermute | solution.py:360
  8.7 0.7 copy-start.1
  13.7 8.4 %copy-start.2 = (s32[2,2]{1,0:T(2,128)S(1)}, s32[2,2]{1,0:T(2,128)}, u32[]{:S(2)}) copy-start(s32[2,2]{1,0:T(2,128)} %count_ref.11) | copy-start | bytes 52
  13.7 30.9 %collective-permute-start.3 = (bf16[2,3,160,128]{3,2,1,0:T(8,128)(2,1)}, bf16[2,3,160,128]{3,2,1,0:T(8,128)(2,1)}, u32[]{:S(2)}, u32[]{:S(2)}) collective-permute-start(bf16[2,3,160,128]{3,2,1,0:T(8,128)(2,1)} %shard_map.58), channel_id=1, source_target_pairs={{0,8},{8,0},{1,9},{9,1},{2,10},{10,2},{3,11},{11,3},{4,12},{12,4},... | collective-permute-start | bytes 737288 | tf_op jit(solution)/shard_map/ppermute | solution.py:368
  21.5 8.4 %copy-start.4 = (s32[2,128,1]{1,2,0:T(1,128)S(1)}, s32[2,128,1]{1,2,0:T(1,128)}, u32[]{:S(2)}) copy-start(s32[2,128,1]{1,2,0:T(1,128)} %param.9) | copy-start | bytes 3076
  21.5 23.1 %collective-permute-start.4 = (bf16[2,6,160,128]{3,2,1,0:T(8,128)(2,1)}, bf16[2,6,160,128]{3,2,1,0:T(8,128)(2,1)S(1)}, u32[]{:S(2)}, u32[]{:S(2)}) collective-permute-start(bf16[2,6,160,128]{3,2,1,0:T(8,128)(2,1)} %shard_map.59), channel_id=1, source_target_pairs={{0,8},{8,0},{1,9},{9,1},{2,10},{10,2},{3,11},{11,3},{4,12},{12,4},... | collective-permute-start | bytes 1474568 | tf_op jit(solution)/shard_map/ppermute | solution.py:368
  28.4 17.4 %collective-permute-start.5 = (bf16[2,6,160,128]{3,2,1,0:T(8,128)(2,1)}, bf16[2,6,160,128]{3,2,1,0:T(8,128)(2,1)}, u32[]{:S(2)}, u32[]{:S(2)}) collective-permute-start(bf16[2,6,160,128]{3,2,1,0:T(8,128)(2,1)} %shard_map.60), channel_id=1, source_target_pairs={{0,8},{8,0},{1,9},{9,1},{2,10},{10,2},{3,11},{11,3},{4,12},{12,4},... | collective-permute-start | bytes 1474568 | tf_op jit(solution)/shard_map/ppermute | solution.py:368
  33.0 12.7 %copy-start.3 = (f32[2]{0:T(128)S(1)}, f32[2]{0:T(128)}, u32[]{:S(2)}) copy-start(f32[2]{0:T(128)} %noise_ref.3) | copy-start | bytes 28
  33.0 19.0 %collective-permute-start.2 = (bf16[2,160,128]{2,1,0:T(8,128)(2,1)S(1)}, bf16[2,160,128]{2,1,0:T(8,128)(2,1)S(1)}, u32[]{:S(2)}, u32[]{:S(2)}) collective-permute-start(bf16[2,160,128]{2,1,0:T(8,128)(2,1)S(1)} %shard_map.56), channel_id=1, source_target_pairs={{0,8},{8,0},{1,9},{9,1},{2,10},{10,2},{3,11},{11,3},{4,12},{12,4},... | collective-permute-start | bytes 245768 | tf_op jit(solution)/shard_map/ppermute | solution.py:372
  53.8 12.1 %collective-permute-start.9 = (bf16[224,128]{1,0:T(8,128)(2,1)S(1)}, bf16[224,128]{1,0:T(8,128)(2,1)S(1)}, u32[]{:S(2)}, u32[]{:S(2)}) collective-permute-start(bf16[224,128]{1,0:T(8,128)(2,1)S(1)} %get-tuple-element.16), channel_id=1, source_target_pairs={{0,3},{1,0},{2,1},{3,2},{4,19},{5,16},{6,17},{7,18},{16,7},{17,4},... | collective-permute-start | bytes 172040 | tf_op jit(solution)/shard_map/ppermute | solution.py:399
  57.2 8.8 %collective-permute-start.8 = (bf16[224,128]{1,0:T(8,128)(2,1)S(1)}, bf16[224,128]{1,0:T(8,128)(2,1)S(1)}, u32[]{:S(2)}, u32[]{:S(2)}) collective-permute-start(bf16[224,128]{1,0:T(8,128)(2,1)S(1)} %get-tuple-element.15), channel_id=1, source_target_pairs={{0,2},{1,3},{2,0},{3,1},{4,18},{5,19},{6,16},{7,17},{16,6},{17,7},... | collective-permute-start | bytes 172040 | tf_op jit(solution)/shard_map/ppermute | solution.py:399
  57.7 11.0 %collective-permute-start.7 = (bf16[224,128]{1,0:T(8,128)(2,1)S(1)}, bf16[224,128]{1,0:T(8,128)(2,1)S(1)}, u32[]{:S(2)}, u32[]{:S(2)}) collective-permute-start(bf16[224,128]{1,0:T(8,128)(2,1)S(1)} %get-tuple-element.14), channel_id=1, source_target_pairs={{0,1},{1,2},{2,3},{3,0},{4,17},{5,18},{6,19},{7,16},{16,5},{17,6},... | collective-permute-start | bytes 172040 | tf_op jit(solution)/shard_map/ppermute | solution.py:399
  59.2 10.5 %collective-permute-start.6 = (bf16[224,128]{1,0:T(8,128)(2,1)S(1)}, bf16[224,128]{1,0:T(8,128)(2,1)S(1)}, u32[]{:S(2)}, u32[]{:S(2)}) collective-permute-start(bf16[224,128]{1,0:T(8,128)(2,1)S(1)} %get-tuple-element.13), channel_id=1, source_target_pairs={{0,0},{1,1},{2,2},{3,3},{4,16},{5,17},{6,18},{7,19},{16,4},{17,5},... | collective-permute-start | bytes 172040 | tf_op jit(solution)/shard_map/ppermute | solution.py:399
  59.8 11.8 %collective-permute-start.13 = (bf16[224,128]{1,0:T(8,128)(2,1)S(1)}, bf16[224,128]{1,0:T(8,128)(2,1)S(1)}, u32[]{:S(2)}, u32[]{:S(2)}) collective-permute-start(bf16[224,128]{1,0:T(8,128)(2,1)S(1)} %get-tuple-element.20), channel_id=1, source_target_pairs={{0,19},{1,16},{2,17},{3,18},{4,3},{5,0},{6,1},{7,2},{16,23},{17,20... | collective-permute-start | bytes 172040 | tf_op jit(solution)/shard_map/ppermute | solution.py:399
  65.9 6.5 %collective-permute-start.12 = (bf16[224,128]{1,0:T(8,128)(2,1)S(1)}, bf16[224,128]{1,0:T(8,128)(2,1)S(1)}, u32[]{:S(2)}, u32[]{:S(2)}) collective-permute-start(bf16[224,128]{1,0:T(8,128)(2,1)S(1)} %get-tuple-element.19), channel_id=1, source_target_pairs={{0,18},{1,19},{2,16},{3,17},{4,2},{5,3},{6,0},{7,1},{16,22},{17,23... | collective-permute-start | bytes 172040 | tf_op jit(solution)/shard_map/ppermute | solution.py:399
  66.0 7.6 %collective-permute-start.11 = (bf16[224,128]{1,0:T(8,128)(2,1)S(1)}, bf16[224,128]{1,0:T(8,128)(2,1)S(1)}, u32[]{:S(2)}, u32[]{:S(2)}) collective-permute-start(bf16[224,128]{1,0:T(8,128)(2,1)S(1)} %get-tuple-element.18), channel_id=1, source_target_pairs={{0,17},{1,18},{2,19},{3,16},{4,1},{5,2},{6,3},{7,0},{16,21},{17,22... | collective-permute-start | bytes 172040 | tf_op jit(solution)/shard_map/ppermute | solution.py:399
  68.7 5.7 %collective-permute-start.10 = (bf16[224,128]{1,0:T(8,128)(2,1)S(1)}, bf16[224,128]{1,0:T(8,128)(2,1)S(1)}, u32[]{:S(2)}, u32[]{:S(2)}) collective-permute-start(bf16[224,128]{1,0:T(8,128)(2,1)S(1)} %get-tuple-element.17), channel_id=1, source_target_pairs={{0,16},{1,17},{2,18},{3,19},{4,0},{5,1},{6,2},{7,3},{16,20},{17,21... | collective-permute-start | bytes 172040 | tf_op jit(solution)/shard_map/ppermute | solution.py:399
  69.7 7.6 %collective-permute-start.14 = (bf16[4,224,128]{2,1,0:T(8,128)(2,1)S(1)}, bf16[4,224,128]{2,1,0:T(8,128)(2,1)S(1)}, u32[]{:S(2)}, u32[]{:S(2)}) collective-permute-start(bf16[4,224,128]{2,1,0:T(8,128)(2,1)S(1)} %pad_maximum_fusion.refs_0_), channel_id=1, source_target_pairs={{0,8},{8,0},{1,9},{9,1},{2,10},{10,2},{3,11},{11,3},{4,12},{12,4},... | collective-permute-start | bytes 688136 | tf_op jit(solution)/shard_map/ppermute | solution.py:404
  74.4 7.8 %collective-permute-start.15 = (bf16[4,224,128]{2,1,0:T(8,128)(2,1)S(1)}, bf16[4,224,128]{2,1,0:T(8,128)(2,1)S(1)}, u32[]{:S(2)}, u32[]{:S(2)}) collective-permute-start(bf16[4,224,128]{2,1,0:T(8,128)(2,1)S(1)} %pad_maximum_fusion.1.refs_1_), channel_id=1, source_target_pairs={{0,8},{8,0},{1,9},{9,1},{2,10},{10,2},{3,11},{11,3},{4,12},{12,4},... | collective-permute-start | bytes 688136 | tf_op jit(solution)/shard_map/ppermute | solution.py:404

commit v3 on v2

--- a/solution.py
+++ b/solution.py
@@ -6,22 +6,29 @@
 from jax.sharding import PartitionSpec as P
 
 F32, BF16 = jnp.float32, jnp.bfloat16
+GRP = 16
 SPAD = 16
 VMEM_LIMIT = 40 << 20
 SWAP = [(0, 1), (1, 0)]
 
 SMEM_SPEC = pl.BlockSpec(memory_space=pltpu.SMEM)
 VMEM_SPEC = pl.BlockSpec(memory_space=pltpu.VMEM)
-ANY_SPEC = pl.BlockSpec(memory_space=pl.ANY)
+HBM_SPEC = pl.BlockSpec(memory_space=pltpu.HBM)
+
+
+def cross(product, users):
+    left, right = product[:, :users], product[:, users:]
+    rows = product.shape[0]
+    even = lax.broadcasted_iota(jnp.int32, left.shape, 0) % 2 == 0
+    return left + jnp.where(even, pltpu.roll(right, rows - 1, 0), -pltpu.roll(right, 1, 0))
 
 
 def prepare(below, here, above, samples, stretch, mat, lhs):
     antennas, users = here.shape[1:]
     symbols = samples.shape[0]
     slab = 128
+    lhs[2 * users : 2 * (users + symbols), :] = samples[...].reshape(2 * symbols, antennas)
     for k in range(2):
-        first = 2 * users + SPAD * k
-        lhs[first : first + symbols, :] = samples[:, k, :]
         for row in range(0, antennas, slab):
             rows = pl.ds(row, slab)
             outer = below[k, rows, :].astype(F32) + above[k, rows, :].astype(F32)
@@ -42,9 +49,7 @@
     out[:users, :] = jnp.where(jnp.maximum(row, col) < count, packed * 0.0625, 0.0).astype(out.dtype)
     lane = lax.broadcasted_iota(jnp.int32, (1, users), 1)
     scale = jnp.where(lane < count, 0.25, 0.0)
-    low, high = product[2 * users : 2 * users + SPAD], product[2 * users + SPAD :]
-    out[users : users + SPAD, :] = ((low[:, :users] + high[:, users:]) * scale).astype(out.dtype)
-    out[users + SPAD :, :] = ((high[:, :users] - low[:, users:]) * scale).astype(out.dtype)
+    out[users:, :] = (cross(product[2 * users :], users) * scale).astype(out.dtype)
 
 
 def work_buffers(antennas, users):
@@ -54,15 +59,22 @@
     ]
 
 
-def inner_gram(place, counts, channel, received, peer, first, number, dtype):
+def inner_gram(control, channel, received, peer, first, number, dtype, halo=False):
     cells, band, _, antennas, users = channel.shape
     symbols = received.shape[2]
-    group = band // counts.shape[1]
+    group, groups = GRP, band // GRP
     half = band // 2
     items = cells * number
 
-    def kernel(place_ref, count_ref, chan, samp, out, win, ybuf, mat_a, lhs_a, mat_b, lhs_b, wsem, ysem):
-        side = 1 - place_ref[0] if peer else place_ref[0]
+    def kernel(control_ref, chan, samp, out, *refs):
+        ends, refs = (refs[:2], refs[2:]) if halo else ((), refs)
+        win, ybuf, mat_a, lhs_a, mat_b, lhs_b, wsem, ysem, esem = refs
+        edges = [
+            pltpu.make_async_copy(chan.at[c, i * (band - 1)], ends[i].at[c, 0], esem.at[c, i])
+            for c in range(cells)
+            for i in range(len(ends))
+        ]
+        side = 1 - control_ref[0] if peer else control_ref[0]
         start = 1 + side * (half - 1) + first
 
         def fetch(c, i):
@@ -76,6 +88,8 @@
                 fetch(c, i).start()
                 if i == min(2, number):
                     fetch_samples(c).start()
+        for copy in edges:
+            copy.start()
         lhs_a[...] = jnp.zeros_like(lhs_a)
         lhs_b[...] = jnp.zeros_like(lhs_b)
 
@@ -100,7 +114,7 @@
         def multiply(item, mat, lhs):
             item = jnp.minimum(item, items - 1)
             c, i = item // number, item % number
-            gram(mat, lhs, out.at[c, i], count_ref[c, (start + i) // group], users)
+            gram(mat, lhs, out.at[c, i], control_ref[3 + c * groups + (start + i) // group], users)
 
         wait(0)
         ready(0, mat_a, lhs_a)
@@ -115,13 +129,16 @@
             return carry
 
         lax.fori_loop(0, (items + 1) // 2, step, 0)
+        for copy in edges:
+            copy.wait()
 
     rows = users + 2 * SPAD
     return pl.pallas_call(
         kernel,
-        in_specs=[SMEM_SPEC, SMEM_SPEC, ANY_SPEC, ANY_SPEC],
-        out_specs=VMEM_SPEC,
-        out_shape=jax.ShapeDtypeStruct((cells, number, rows, users), dtype),
+        in_specs=[SMEM_SPEC, HBM_SPEC, HBM_SPEC],
+        out_specs=[VMEM_SPEC] + [HBM_SPEC] * (2 * halo),
+        out_shape=[jax.ShapeDtypeStruct((cells, number, rows, users), dtype)]
+        + [jax.ShapeDtypeStruct((cells, 1, 2, antennas, users), BF16)] * (2 * halo),
         scratch_shapes=[
             pltpu.VMEM((cells, number + 2, 2, antennas, users), BF16),
             pltpu.VMEM((cells, number, symbols, 2, antennas), BF16),
@@ -129,6 +146,7 @@
             *work_buffers(antennas, users),
             pltpu.SemaphoreType.DMA((cells, number + 2)),
             pltpu.SemaphoreType.DMA((cells,)),
+            pltpu.SemaphoreType.DMA((cells, 2)),
         ],
         compiler_params=pltpu.CompilerParams(vmem_limit_bytes=VMEM_LIMIT),
         cost_estimate=pl.CostEstimate(
@@ -136,70 +154,84 @@
             bytes_accessed=cells * (number + 2) * 4 * antennas * users,
             transcendentals=0,
         ),
-    )(place, counts, channel, received)
-
-
-def edge_gram(place, counts, channel, received, low, high, peer, dtype):
-    cells, band, _, antennas, users = channel.shape
-    symbols = received.shape[2]
-    group = band // counts.shape[1]
-
-    def kernel(place_ref, count_ref, chan, samp, low_ref, high_ref, out, win, ybuf, mat_a, lhs_a, mat_b, lhs_b, wsem, ysem):
-        side = 1 - place_ref[0] if peer else place_ref[0]
-
-        def each_copy(act):
-            def run(e):
-                for c in range(cells):
-                    blocks = (
-                        (low_ref.at[c, 0], chan.at[c, 0], chan.at[c, 1]),
-                        (chan.at[c, band - 2], chan.at[c, band - 1], high_ref.at[c, 0]),
-                    )[e]
-                    for i, block in enumerate(blocks):
-                        act(pltpu.make_async_copy(block, win.at[c, i], wsem.at[c, i]))
-                    act(pltpu.make_async_copy(samp.at[c, e * (band - 1)], ybuf.at[c], ysem.at[c]))
-
-            @pl.when(side == 0)
-            def _():
-                run(0)
-
-            @pl.when(side == 1)
-            def _():
-                run(1)
-
+    )(control, channel, received)
+
+
+def edge_scratch(cells, symbols, antennas, users):
+    return [
+        pltpu.VMEM((cells, 3, 2, antennas, users), BF16),
+        pltpu.VMEM((cells, symbols, 2, antennas), BF16),
+        *work_buffers(antennas, users),
+        *work_buffers(antennas, users),
+        pltpu.SemaphoreType.DMA((cells, 3)),
+        pltpu.SemaphoreType.DMA((cells,)),
+    ]
+
+
+def edge_work(side, control_ref, chan, samp, low_ref, high_ref, out, scratch):
+    win, ybuf, mat_a, lhs_a, mat_b, lhs_b, wsem, ysem = scratch
+    cells, band, _, _, users = chan.shape
+    groups = band // GRP
+    buffers = ((mat_a, lhs_a), (mat_b, lhs_b))
+
+    def each_copy(act):
+        def run(e):
+            for c in range(cells):
+                blocks = (
+                    (low_ref.at[c, 0], chan.at[c, 0], chan.at[c, 1]),
+                    (chan.at[c, band - 2], chan.at[c, band - 1], high_ref.at[c, 0]),
+                )[e]
+                for i, block in enumerate(blocks):
+                    act(pltpu.make_async_copy(block, win.at[c, i], wsem.at[c, i]))
+                act(pltpu.make_async_copy(samp.at[c, e * (band - 1)], ybuf.at[c], ysem.at[c]))
+
+        @pl.when(side == 0)
+        def _():
+            run(0)
+
+        @pl.when(side == 1)
+        def _():
+            run(1)
+
+    def fetch():
         each_copy(lambda copy: copy.start())
         lhs_a[...] = jnp.zeros_like(lhs_a)
         lhs_b[...] = jnp.zeros_like(lhs_b)
+
+    def work():
         each_copy(lambda copy: copy.wait())
-        last = jnp.where(side == 0, place_ref[1], place_ref[2])
+        last = jnp.where(side == 0, control_ref[1], control_ref[2])
         stretch = jnp.where(jnp.full((1, users), last, jnp.int32) == 1, 1 / 0.75, 1.0)
-        buffers = ((mat_a, lhs_a), (mat_b, lhs_b))
         for c in range(cells):
-            mat, lhs = buffers[c % 2]
-            prepare(win.at[c, 0], win.at[c, 1], win.at[c, 2], ybuf.at[c], stretch, mat, lhs)
+            prepare(win.at[c, 0], win.at[c, 1], win.at[c, 2], ybuf.at[c], stretch, *buffers[c % 2])
         for c in range(cells):
-            gram(*buffers[c % 2], out.at[c], count_ref[c, side * (band - 1) // group], users)
-
-    rows = users + 2 * SPAD
+            gram(*buffers[c % 2], out.at[c], control_ref[3 + c * groups + side * (band - 1) // GRP], users)
+
+    return fetch, work
+
+
+def edge_gram(control, channel, received, low, high):
+    cells, _, _, antennas, users = channel.shape
+    symbols = received.shape[2]
+
+    def kernel(control_ref, chan, samp, low_ref, high_ref, out, *scratch):
+        fetch, work = edge_work(1 - control_ref[0], control_ref, chan, samp, low_ref, high_ref, out, scratch)
+        fetch()
+        work()
+
     return pl.pallas_call(
         kernel,
-        in_specs=[SMEM_SPEC, SMEM_SPEC, ANY_SPEC, ANY_SPEC, ANY_SPEC, ANY_SPEC],
+        in_specs=[SMEM_SPEC] + [HBM_SPEC] * 4,
         out_specs=VMEM_SPEC,
-        out_shape=jax.ShapeDtypeStruct((cells, rows, users), dtype),
-        scratch_shapes=[
-            pltpu.VMEM((cells, 3, 2, antennas, users), BF16),
-            pltpu.VMEM((cells, symbols, 2, antennas), BF16),
-            *work_buffers(antennas, users),
-            *work_buffers(antennas, users),
-            pltpu.SemaphoreType.DMA((cells, 3)),
-            pltpu.SemaphoreType.DMA((cells,)),
-        ],
+        out_shape=jax.ShapeDtypeStruct((cells, users + 2 * SPAD, users), BF16),
+        scratch_shapes=edge_scratch(cells, symbols, antennas, users),
         compiler_params=pltpu.CompilerParams(vmem_limit_bytes=VMEM_LIMIT),
         cost_estimate=pl.CostEstimate(
             flops=cells * 4 * antennas * users * 2 * (users + SPAD),
             bytes_accessed=cells * 12 * antennas * users,
             transcendentals=0,
         ),
-    )(place, counts, channel, received, low, high)
+    )(control, channel, received, low, high)
 
 
 def conjugate_gradient(sums, noise, users):
@@ -216,14 +248,13 @@
 
     def apply(matrix, vector):
         product = jnp.dot(vector.astype(BF16), matrix, preferred_element_type=F32)
-        low, high = product[:SPAD], product[SPAD:]
-        image = jnp.concatenate([low[:, :users] + high[:, users:], high[:, :users] - low[:, users:]], axis=0)
-        return image + noise * vector
+        return cross(product, users) + noise * vector
 
     def user_sum(left, right):
-        total = jnp.sum(left * right, axis=1, keepdims=True)
-        total = total[:SPAD] + total[SPAD:]
-        return jnp.concatenate([total, total], axis=0)
+        total = left * right
+        even = lax.broadcasted_iota(jnp.int32, total.shape, 0) % 2 == 0
+        total = total + jnp.where(even, pltpu.roll(total, 2 * SPAD - 1, 0), pltpu.roll(total, 1, 0))
+        return jnp.sum(total, axis=1, keepdims=True)
 
     direction = [value[users:] for value in sums]
     norm = [user_sum(d, d) for d in direction]
@@ -238,13 +269,16 @@
     return [e + a * d for e, a, d in zip(estimate, alpha, direction)]
 
 
-def inner_detect(place, noise_power, own, peers):
+def inner_detect(control, noise_power, own, peers, channel, received, low, high):
     cells, inner, rows, users = own.shape
+    antennas, symbols = channel.shape[3], received.shape[2]
     half = inner + 1
 
-    def kernel(place_ref, noise_ref, own_ref, *refs):
-        *peer_refs, out = refs
-        shift = 1 - place_ref[0]
+    def kernel(control_ref, noise_ref, chan, samp, low_ref, high_ref, own_ref, *refs):
+        peer_refs, (out, edge_out), scratch = refs[: len(peers)], refs[len(peers) : len(peers) + 2], refs[len(peers) + 2 :]
+        fetch, work = edge_work(control_ref[0], control_ref, chan, samp, low_ref, high_ref, edge_out, scratch)
+        fetch()
+        shift = 1 - control_ref[0]
 
         def step(c, carry):
             sums = []
@@ -256,36 +290,44 @@
             return carry
 
         lax.fori_loop(0, cells, step, 0)
+        work()
 
     return pl.pallas_call(
         kernel,
-        in_specs=[SMEM_SPEC, SMEM_SPEC, VMEM_SPEC] + [VMEM_SPEC] * len(peers),
-        out_specs=VMEM_SPEC,
-        out_shape=jax.ShapeDtypeStruct((cells, 2 * SPAD * half, users), F32),
+        in_specs=[SMEM_SPEC, SMEM_SPEC] + [HBM_SPEC] * 4 + [VMEM_SPEC] * (1 + len(peers)),
+        out_specs=[VMEM_SPEC, VMEM_SPEC],
+        out_shape=[
+            jax.ShapeDtypeStruct((cells, 2 * SPAD * half, users), F32),
+            jax.ShapeDtypeStruct((cells, rows, users), F32),
+        ],
+        scratch_shapes=edge_scratch(cells, symbols, antennas, users),
         compiler_params=pltpu.CompilerParams(vmem_limit_bytes=VMEM_LIMIT),
         cost_estimate=pl.CostEstimate(
             flops=cells * inner * 2 * 2 * 2 * SPAD * users * 2 * users,
             bytes_accessed=cells * inner * rows * users * 6,
             transcendentals=0,
         ),
-    )(place, noise_power, own, *peers)
-
-
-def edge_detect(place, noise_power, own, peer, inner, onehot, symbols, rounds):
+    )(control, noise_power, channel, received, low, high, own, *peers)
+
+
+def edge_detect(control, noise_power, own, peer, inner, onehot, symbols, rounds):
     cells, rows, users = own.shape
     half = inner.shape[1] // (2 * SPAD)
     width = onehot.shape[1] // rounds
     keep = symbols * half
 
-    def kernel(place_ref, noise_ref, own_ref, peer_ref, inner_ref, hot_ref, *refs):
+    def kernel(control_ref, noise_ref, own_ref, peer_ref, inner_ref, hot_ref, *refs):
         *outs, state = refs
         state[...] = inner_ref[...]
-        spot = place_ref[0] * (half - 1)
+        spot = control_ref[0] * (half - 1)
         for c in range(cells):
             (value,) = conjugate_gradient([own_ref[c] + peer_ref[c].astype(F32)], noise_ref[c], users)
             state[c, pl.ds(spot, 2 * SPAD, stride=half), :] = value
+        values = state[...].astype(BF16)
         blocks = [
-            state[c, k * SPAD * half : k * SPAD * half + keep, :].astype(BF16) for k in range(2) for c in range(cells)
+            jnp.concatenate([values[c, (2 * s + k) * half : (2 * s + k + 1) * half] for s in range(symbols)], axis=0)
+            for k in range(2)
+            for c in range(cells)
         ]
         lhs = jnp.concatenate(blocks, axis=1)
         placed = jnp.dot(lhs, hot_ref[...], preferred_element_type=F32).astype(BF16)
@@ -302,18 +344,18 @@
         cost_estimate=pl.CostEstimate(
             flops=2 * keep * onehot.shape[0] * onehot.shape[1], bytes_accessed=4 * inner.size, transcendentals=0
         ),
-    )(place, noise_power, own, peer, inner, onehot)
-
-
-def assemble(place, mine, theirs, sources, cells, per_device, symbols, half):
+    )(control, noise_power, own, peer, inner, onehot)
+
+
+def assemble(control, mine, theirs, sources, cells, per_device, symbols, half):
     total = len(sources) * 2 * half
     lanes = mine[0].shape[2]
     slots = cells * per_device
 
-    def kernel(place_ref, source_ref, *refs):
+    def kernel(control_ref, source_ref, *refs):
         mine_refs, theirs_refs = refs[: len(mine)], refs[len(mine) : 2 * len(mine)]
         out, gathered, turned = refs[2 * len(mine) :]
-        for side, group in ((place_ref[0], mine_refs), (1 - place_ref[0], theirs_refs)):
+        for side, group in ((control_ref[0], mine_refs), (1 - control_ref[0], theirs_refs)):
             number = 0
             for ref in group:
                 for i in range(ref.shape[0]):
@@ -344,7 +386,7 @@
             pltpu.VMEM((total // 128, slots * 2 * SPAD, 128), F32),
         ],
         compiler_params=pltpu.CompilerParams(vmem_limit_bytes=VMEM_LIMIT),
-    )(place, sources, *mine, *theirs)
+    )(control, sources, *mine, *theirs)
 
 
 def body(channel, received, noise_power, user_count, serving_cell):
@@ -354,24 +396,21 @@
     n_sc, n_cell = lax.axis_size("sc"), lax.axis_size("cell")
     panel, sc, cell = lax.axis_index("panel"), lax.axis_index("sc"), lax.axis_index("cell")
 
-    upward = [(i, i + 1) for i in range(n_sc - 1)]
-    downward = [(i + 1, i) for i in range(n_sc - 1)]
-    low = lax.ppermute(channel[:, band - 1 :], "sc", upward)
-    high = lax.ppermute(channel[:, :1], "sc", downward)
-
-    place = jnp.stack([panel, (sc == 0).astype(jnp.int32), (sc == n_sc - 1).astype(jnp.int32)]).astype(jnp.int32)
+    ends = jnp.stack([panel, (sc == 0).astype(jnp.int32), (sc == n_sc - 1).astype(jnp.int32)])
+    control = jnp.concatenate([ends.astype(jnp.int32), user_count.reshape(-1)])
     samples = jnp.transpose(received, (0, 1, 3, 2, 4))
 
-    peers, first = [], 0
-    for number in (3, 6, half - 10):
-        outgoing = inner_gram(place, user_count, channel, samples, True, first, number, BF16)
-        peers.append(lax.ppermute(outgoing, "panel", SWAP))
-        first += number
-    own = inner_gram(place, user_count, channel, samples, False, 0, half - 1, F32)
-    edge_out = edge_gram(place, user_count, channel, samples, low, high, True, BF16)
-    edge_peer = lax.ppermute(edge_out, "panel", SWAP)
-    edge_own = edge_gram(place, user_count, channel, samples, low, high, False, F32)
-    inner = inner_detect(place, noise_power, own, peers)
+    inner = half - 1
+    count = inner // 2
+    outgoing, bottom, top = inner_gram(control, channel, samples, True, 0, count, BF16, halo=True)
+    peers = [lax.ppermute(outgoing, "panel", SWAP)]
+    low = lax.ppermute(top, "sc", [(i, i + 1) for i in range(n_sc - 1)])
+    high = lax.ppermute(bottom, "sc", [(i + 1, i) for i in range(n_sc - 1)])
+    (outgoing,) = inner_gram(control, channel, samples, True, count, inner - count, BF16)
+    peers.append(lax.ppermute(outgoing, "panel", SWAP))
+    (own,) = inner_gram(control, channel, samples, False, 0, inner, F32)
+    edge_peer = lax.ppermute(edge_gram(control, channel, samples, low, high), "panel", SWAP)
+    inner, edge_own = inner_detect(control, noise_power, own, peers, channel, samples, low, high)
 
     capacity = cells * users // n_cell
     per_device = n_cell * capacity // n_sc
@@ -387,9 +426,11 @@
     width = 2 * cells * per_device
     onehot = (column[:, None] == lax.iota(jnp.int32, rounds * width)[None, :]).astype(BF16)
 
-    messages = edge_detect(place, noise_power, edge_own, edge_peer, inner, onehot, symbols, rounds)
+    messages = edge_detect(control, noise_power, edge_own, edge_peer, inner, onehot, symbols, rounds)
     arrived, sources = [], []
     for a in range(n_cell):
+        if a == n_cell // 2:
+            messages, arrived = lax.optimization_barrier((messages, arrived))
         for b in range(reach):
             pairs = [
                 (s * n_sc + j, (j // reach + a) % n_cell * n_sc + s * reach + (j % reach + b) % reach)
@@ -402,7 +443,7 @@
     groups = [arrived[: rounds // 2], arrived[rounds // 2 :]]
     mine = [jnp.stack(group) for group in groups]
     theirs = [lax.ppermute(group, "panel", SWAP) for group in mine]
-    routed = assemble(place, mine, theirs, sources, cells, per_device, symbols, half)
+    routed = assemble(control, mine, theirs, sources, cells, per_device, symbols, half)
     return jnp.transpose(routed, (0, 1, 3, 2, 4))
 
 

time: 86.6 us -> 119 us (1.37)
  Pallas kernels: 42 us -> 62.6 us
  waiting for transfers between devices: 12.3 us -> 25.2 us
    pallas_call x7 -> x5, Pallas kernels: 36.2 us -> 57.1 us  [the longest x3 50.8 us: inner_gram(): pl.pallas_call(kernel, in_specs=[SMEM_SPEC, HBM_SPEC, HBM_SPEC], out_spec...]
    ppermute x3 -> x4, waiting for transfers between devices: 0.01 us -> 12.1 us  [the longest x1 12.1 us: body(): low = lax.ppermute(top, 'sc', [(i, i + 1) for i in range(n_sc - 1)])]
    ppermute x8, waiting for transfers between devices: 4.12 us -> 7.63 us  [body(): arrived.append(lax.ppermute(messages[a * reach + b], ('cell', 'sc'), pairs))]
    ppermute x3 -> x1, starting transfers between devices: 3.71 us -> 0.6 us  [body(): peers.append(lax.ppermute(outgoing, 'panel', SWAP))]
    slice x1 -> x0, local copies, waits for them, and re-layouts: 2.39 us -> none  [body(): high = lax.ppermute(channel[:, :1], 'sc', downward)]
    ppermute x3 -> x4, starting transfers between devices: 7.29 us -> 9.32 us  [the longest x1 4.9 us: body(): low = lax.ppermute(top, 'sc', [(i, i + 1) for i in range(n_sc - 1)])]
    ppermute x2, waiting for transfers between devices: 7.12 us -> 5.44 us  [body(): theirs = [lax.ppermute(group, 'panel', SWAP) for group in mine]]
  transfers between devices with their start and end apart: 16 -> 15, of which waited for: 7 -> 8; matrix products, arithmetic and copies ran while one was open for 1% -> 1% of each run, Pallas kernels for 42% -> 19%
where the time goes in v3:
time: 119 us
  Pallas kernels  62.6 us (53%)
  starting transfers between devices  27.7 us (23%)
  waiting for transfers between devices  25.2 us (21%)
  local copies, waits for them, and re-layouts  2.36 us (2%)
    pallas_call x3, Pallas kernels, inner_gram(): pl.pallas_call(kernel, in_specs=[SMEM_SPEC, HBM_SPEC, HBM_SPEC], out_spec...  50.8 us
    ppermute x8, starting transfers between devices, body(): arrived.append(lax.ppermute(messages[a * reach + b], ('cell', 'sc'), pairs))  16.6 us
    ppermute x1, waiting for transfers between devices, body(): low = lax.ppermute(top, 'sc', [(i, i + 1) for i in range(n_sc - 1)])  12.1 us
    ppermute x8, waiting for transfers between devices, body(): arrived.append(lax.ppermute(messages[a * reach + b], ('cell', 'sc'), pairs))  7.63 us
    ppermute x2, waiting for transfers between devices, body(): theirs = [lax.ppermute(group, 'panel', SWAP) for group in mine]  5.44 us
    ppermute x1, starting transfers between devices, body(): low = lax.ppermute(top, 'sc', [(i, i + 1) for i in range(n_sc - 1)])  4.9 us
    pallas_call x1, Pallas kernels, assemble(): pl.pallas_call(kernel, in_specs=[SMEM_SPEC, SMEM_SPEC] + [VMEM_SPEC] * (2...  4.04 us
    pallas_call x1, Pallas kernels, inner_detect(): pl.pallas_call(kernel, in_specs=[SMEM_SPEC, SMEM_SPEC] + [HBM_SPEC] * 4 +...  3.87 us
  transfers between devices with their start and end apart: 15, of which 8 were waited for; matrix products, arithmetic and copies ran while one was open for 1% of the time, Pallas kernels for 19%

profile of v3, /device:TPU:0, one launch (start us, length us, event | category | flops | bytes accessed | tf_op | source)
XLA Modules:
  0.0 118.7 jit_solution(3741244207369265377)
XLA Ops:
  0.8 1.5 %copy-done = bf16[2,32,2,14,512]{4,2,3,1,0:T(2,128)(2,1)S(1)} copy-done((bf16[2,32,2,14,512]{4,2,3,1,0:T(2,128)(2,1)S(1)}, bf16[2,32,2,14,512]{4,2,3,1,0:T(2,128)(2,1)}, u32[]{:S(2)}) %copy-start) | copy-done | bytes 1835032
  2.3 35.0 %shard_map.55 = (bf16[2,7,160,128]{3,2,1,0:T(8,128)(2,1)}, bf16[2,1,2,512,128]{4,3,2,1,0:T(8,128)(2,1)}, bf16[2,1,2,512,128]{4,3,2,1,0:T(8,128)(2,1)}) custom-call(s32[7]{0:T(128)S(1)} %pad_add_fusion.1.control_ref, bf16[2,32,2,512,128]{4,3,2,1,0:T(8,128)(2,1)} %chan.9, bf16[2,32,14,2,512]{4,3,2,1,0:T(2,128)(2,1)S(1)} %bitcast.22), custom_call_target="tpu_custom_call" | custom-call | flops 1056964608 | bytes 4718592 | tf_op jit(solution)/shard_map/pallas_call | solution.py:136
  37.4 4.9 %collective-permute-start = (bf16[2,1,2,512,128]{4,3,2,1,0:T(8,128)(2,1)}, bf16[2,1,2,512,128]{4,3,2,1,0:T(8,128)(2,1)S(1)}, u32[]{:S(2)}, u32[]{:S(2)}) collective-permute-start(bf16[2,1,2,512,128]{4,3,2,1,0:T(8,128)(2,1)} %get-tuple-element.26), channel_id=1, source_target_pairs={{0,1},{1,2},{2,3},{3,4},{4,5},{5,6},{6,7},{8,9},{9,10},{10,11},{11... | collective-permute-start | bytes 1572872 | tf_op jit(solution)/shard_map/ppermute | solution.py:407
  42.3 1.3 %collective-permute-start.1 = (bf16[2,1,2,512,128]{4,3,2,1,0:T(8,128)(2,1)}, bf16[2,1,2,512,128]{4,3,2,1,0:T(8,128)(2,1)S(1)}, u32[]{:S(2)}, u32[]{:S(2)}) collective-permute-start(bf16[2,1,2,512,128]{4,3,2,1,0:T(8,128)(2,1)} %get-tuple-element.27), channel_id=1, source_target_pairs={{1,0},{2,1},{3,2},{4,3},{5,4},{6,5},{7,6},{9,8},{10,9},{11,10},{12... | collective-permute-start | bytes 1572872 | tf_op jit(solution)/shard_map/ppermute | solution.py:408
  43.6 1.6 %collective-permute-start.2 = (bf16[2,7,160,128]{3,2,1,0:T(8,128)(2,1)}, bf16[2,7,160,128]{3,2,1,0:T(8,128)(2,1)}, u32[]{:S(2)}, u32[]{:S(2)}) collective-permute-start(bf16[2,7,160,128]{3,2,1,0:T(8,128)(2,1)} %get-tuple-element.28), channel_id=1, source_target_pairs={{0,8},{8,0},{1,9},{9,1},{2,10},{10,2},{3,11},{11,3},{4,12},{12,4},... | collective-permute-start | bytes 1720328 | tf_op jit(solution)/shard_map/ppermute | solution.py:406
  45.1 6.6 %shard_map.57 = bf16[2,8,160,128]{3,2,1,0:T(8,128)(2,1)} custom-call(s32[7]{0:T(128)S(1)} %pad_add_fusion.1.control_ref, bf16[2,32,2,512,128]{4,3,2,1,0:T(8,128)(2,1)} %chan.9, bf16[2,32,14,2,512]{4,3,2,1,0:T(2,128)(2,1)S(1)} %bitcast.23), custom_call_target="tpu_custom_call" | custom-call | flops 1207959552 | bytes 5242880 | tf_op jit(solution)/shard_map/pallas_call | solution.py:136
  52.8 12.1 %collective-permute-done.low_ref = bf16[2,1,2,512,128]{4,3,2,1,0:T(8,128)(2,1)S(1)} collective-permute-done((bf16[2,1,2,512,128]{4,3,2,1,0:T(8,128)(2,1)}, bf16[2,1,2,512,128]{4,3,2,1,0:T(8,128)(2,1)S(1)}, u32[]{:S(2)}, u32[]{:S(2)}) %collective-permute-start) | collective-permute-done | bytes 524320 | tf_op jit(solution)/shard_map/ppermute | solution.py:407
  65.0 2.4 %shard_map.59 = bf16[2,160,128]{2,1,0:T(8,128)(2,1)S(1)} custom-call(s32[7]{0:T(128)S(1)} %pad_add_fusion.1.control_ref, bf16[2,32,2,512,128]{4,3,2,1,0:T(8,128)(2,1)} %chan.9, bf16[2,32,14,2,512]{4,3,2,1,0:T(2,128)(2,1)S(1)} %bitcast.24, bf16[2,1,2,512,128]{4,3,2,1,0:T(8,128)(2,1)S(1)} %collective-permute-done.low_ref, ...), custom_call_target="tpu_custom_call" | custom-call | flops 150994944 | bytes 1572864 | tf_op jit(solution)/shard_map/pallas_call | solution.py:222
  67.4 1.6 %collective-permute-start.4 = (bf16[2,160,128]{2,1,0:T(8,128)(2,1)S(1)}, bf16[2,160,128]{2,1,0:T(8,128)(2,1)S(1)}, u32[]{:S(2)}, u32[]{:S(2)}) collective-permute-start(bf16[2,160,128]{2,1,0:T(8,128)(2,1)S(1)} %shard_map.59), channel_id=1, source_target_pairs={{0,8},{8,0},{1,9},{9,1},{2,10},{10,2},{3,11},{11,3},{4,12},{12,4},... | collective-permute-start | bytes 245768 | tf_op jit(solution)/shard_map/ppermute | solution.py:412
  69.0 9.2 %shard_map.56.own_ref = f32[2,15,160,128]{3,2,1,0:T(8,128)S(1)} custom-call(s32[7]{0:T(128)S(1)} %pad_add_fusion.1.control_ref, bf16[2,32,2,512,128]{4,3,2,1,0:T(8,128)(2,1)} %chan.9, bf16[2,32,14,2,512]{4,3,2,1,0:T(2,128)(2,1)S(1)} %bitcast.25), custom_call_target="tpu_custom_call" | custom-call | flops 2264924160 | bytes 8912896 | tf_op jit(solution)/shard_map/pallas_call | solution.py:136
  78.2 3.9 %shard_map.58 = (f32[2,512,128]{2,1,0:T(8,128)S(1)}, f32[2,160,128]{2,1,0:T(8,128)S(1)}) custom-call(s32[7]{0:T(128)S(1)} %pad_add_fusion.1.control_ref, f32[2]{0:T(128)S(1)} %copy-done.2, bf16[2,32,2,512,128]{4,3,2,1,0:T(8,128)(2,1)} %chan.9, bf16[2,32,14,2,512]{4,3,2,1,0:T(2,128)(2,1)S(1)} %bitcast.26, ...), custom_call_target="tpu_custom_call" | custom-call | flops 125829120 | bytes 3686400 | tf_op jit(solution)/shard_map/pallas_call | solution.py:295
  82.1 1.5 %shard_map.60 = (bf16[224,128]{1,0:T(8,128)(2,1)S(1)}, bf16[224,128]{1,0:T(8,128)(2,1)S(1)}, bf16[224,128]{1,0:T(8,128)(2,1)S(1)}, bf16[224,128]{1,0:T(8,128)(2,...) custom-call(s32[7]{0:T(128)S(1)} %pad_add_fusion.1.control_ref, ...), custom_call_target="tpu_custom_call" | custom-call | flops 234881024 | bytes 524288 | tf_op jit(solution)/shard_map/pallas_call | solution.py:337
  84.3 2.4 %collective-permute-start.6 = (bf16[224,128]{1,0:T(8,128)(2,1)S(1)}, bf16[224,128]{1,0:T(8,128)(2,1)S(1)}, u32[]{:S(2)}, u32[]{:S(2)}) collective-permute-start(bf16[224,128]{1,0:T(8,128)(2,1)S(1)} %get-tuple-element.32), channel_id=1, source_target_pairs={{0,1},{1,2},{2,3},{3,0},{4,17},{5,18},{6,19},{7,16},{16,5},{17,6},... | collective-permute-start | bytes 172040 | tf_op jit(solution)/shard_map/ppermute | solution.py:440
  86.7 1.6 %collective-permute-start.7 = (bf16[224,128]{1,0:T(8,128)(2,1)S(1)}, bf16[224,128]{1,0:T(8,128)(2,1)S(1)}, u32[]{:S(2)}, u32[]{:S(2)}) collective-permute-start(bf16[224,128]{1,0:T(8,128)(2,1)S(1)} %get-tuple-element.33), channel_id=1, source_target_pairs={{0,2},{1,3},{2,0},{3,1},{4,18},{5,19},{6,16},{7,17},{16,6},{17,7},... | collective-permute-start | bytes 172040 | tf_op jit(solution)/shard_map/ppermute | solution.py:440
  88.3 2.3 %collective-permute-start.8 = (bf16[224,128]{1,0:T(8,128)(2,1)S(1)}, bf16[224,128]{1,0:T(8,128)(2,1)S(1)}, u32[]{:S(2)}, u32[]{:S(2)}) collective-permute-start(bf16[224,128]{1,0:T(8,128)(2,1)S(1)} %get-tuple-element.34), channel_id=1, source_target_pairs={{0,3},{1,0},{2,1},{3,2},{4,19},{5,16},{6,17},{7,18},{16,7},{17,4},... | collective-permute-start | bytes 172040 | tf_op jit(solution)/shard_map/ppermute | solution.py:440
  90.9 1.6 %collective-permute-done.8 = bf16[224,128]{1,0:T(8,128)(2,1)S(1)} collective-permute-done((bf16[224,128]{1,0:T(8,128)(2,1)S(1)}, bf16[224,128]{1,0:T(8,128)(2,1)S(1)}, u32[]{:S(2)}, u32[]{:S(2)}) %collective-permute-start.8) | collective-permute-done | bytes 57376 | tf_op jit(solution)/shard_map/ppermute | solution.py:440
  92.5 5.9 %collective-permute-start.12 = (bf16[224,128]{1,0:T(8,128)(2,1)S(1)}, bf16[224,128]{1,0:T(8,128)(2,1)S(1)}, u32[]{:S(2)}, u32[]{:S(2)}) collective-permute-start(bf16[224,128]{1,0:T(8,128)(2,1)S(1)} %get-tuple-element.46), channel_id=1, source_target_pairs={{0,19},{1,16},{2,17},{3,18},{4,3},{5,0},{6,1},{7,2},{16,23},{17,20... | collective-permute-start | bytes 172040 | tf_op jit(solution)/shard_map/ppermute | solution.py:440
  98.4 2.8 %collective-permute-start.10 = (bf16[224,128]{1,0:T(8,128)(2,1)S(1)}, bf16[224,128]{1,0:T(8,128)(2,1)S(1)}, u32[]{:S(2)}, u32[]{:S(2)}) collective-permute-start(bf16[224,128]{1,0:T(8,128)(2,1)S(1)} %get-tuple-element.44), channel_id=1, source_target_pairs={{0,17},{1,18},{2,19},{3,16},{4,1},{5,2},{6,3},{7,0},{16,21},{17,22... | collective-permute-start | bytes 172040 | tf_op jit(solution)/shard_map/ppermute | solution.py:440
  102.7 1.7 %collective-permute-done.11 = bf16[224,128]{1,0:T(8,128)(2,1)S(1)} collective-permute-done((bf16[224,128]{1,0:T(8,128)(2,1)S(1)}, bf16[224,128]{1,0:T(8,128)(2,1)S(1)}, u32[]{:S(2)}, u32[]{:S(2)}) %collective-permute-start.11) | collective-permute-done | bytes 57376 | tf_op jit(solution)/shard_map/ppermute | solution.py:440
  104.4 2.0 %collective-permute-done.10 = bf16[224,128]{1,0:T(8,128)(2,1)S(1)} collective-permute-done((bf16[224,128]{1,0:T(8,128)(2,1)S(1)}, bf16[224,128]{1,0:T(8,128)(2,1)S(1)}, u32[]{:S(2)}, u32[]{:S(2)}) %collective-permute-start.10) | collective-permute-done | bytes 57376 | tf_op jit(solution)/shard_map/ppermute | solution.py:440
  106.4 2.1 %collective-permute-done.9 = bf16[224,128]{1,0:T(8,128)(2,1)S(1)} collective-permute-done((bf16[224,128]{1,0:T(8,128)(2,1)S(1)}, bf16[224,128]{1,0:T(8,128)(2,1)S(1)}, u32[]{:S(2)}, u32[]{:S(2)}) %collective-permute-start.9) | collective-permute-done | bytes 57376 | tf_op jit(solution)/shard_map/ppermute | solution.py:440
  109.2 1.5 %collective-permute-done.13.refs_2_ = bf16[4,224,128]{2,1,0:T(8,128)(2,1)S(1)} collective-permute-done((bf16[4,224,128]{2,1,0:T(8,128)(2,1)S(1)}, bf16[4,224,128]{2,1,0:T(8,128)(2,1)S(1)}, u32[]{:S(2)}, u32[]{:S(2)}) %collective-permute-start.13) | collective-permute-done | bytes 229408 | tf_op jit(solution)/shard_map/ppermute | solution.py:445
  110.7 4.0 %collective-permute-done.14.refs_3_ = bf16[4,224,128]{2,1,0:T(8,128)(2,1)S(1)} collective-permute-done((bf16[4,224,128]{2,1,0:T(8,128)(2,1)S(1)}, bf16[4,224,128]{2,1,0:T(8,128)(2,1)S(1)}, u32[]{:S(2)}, u32[]{:S(2)}) %collective-permute-start.14) | collective-permute-done | bytes 229408 | tf_op jit(solution)/shard_map/ppermute | solution.py:445
  114.6 4.0 %shard_map.61 = bf16[2,32,14,2,256]{4,3,2,1,0:T(2,128)(2,1)} custom-call(s32[7]{0:T(128)S(1)} %pad_add_fusion.1.control_ref, s32[8]{0:T(128)S(1)} %stack.85.source_ref, bf16[4,224,128]{2,1,0:T(8,128)(2,1)S(1)} %pad_maximum_fusion.refs_0_, bf16[4,224,128]{2,1,0:T(8,128)(2,1)S(1)} %pad_maximum_fusion.1.refs_1_, ...), custom_call_target="tpu_custom_call" | custom-call | tf_op jit(solution)/shard_map/pallas_call | solution.py:379
  (30 shorter events, 5.1 us)
Async XLA Ops:
  0.8 1.5 %copy-start = (bf16[2,32,2,14,512]{4,2,3,1,0:T(2,128)(2,1)S(1)}, bf16[2,32,2,14,512]{4,2,3,1,0:T(2,128)(2,1)}, u32[]{:S(2)}) copy-start(bf16[2,32,2,14,512]{4,2,3,1,0:T(2,128)(2,1)} %param.6) | copy-start | bytes 5505028
  37.4 27.6 %collective-permute-start = (bf16[2,1,2,512,128]{4,3,2,1,0:T(8,128)(2,1)}, bf16[2,1,2,512,128]{4,3,2,1,0:T(8,128)(2,1)S(1)}, u32[]{:S(2)}, u32[]{:S(2)}) collective-permute-start(bf16[2,1,2,512,128]{4,3,2,1,0:T(8,128)(2,1)} %get-tuple-element.26), channel_id=1, source_target_pairs={{0,1},{1,2},{2,3},{3,4},{4,5},{5,6},{6,7},{8,9},{9,10},{10,11},{11... | collective-permute-start | bytes 1572872 | tf_op jit(solution)/shard_map/ppermute | solution.py:407
  42.3 22.7 %collective-permute-start.1 = (bf16[2,1,2,512,128]{4,3,2,1,0:T(8,128)(2,1)}, bf16[2,1,2,512,128]{4,3,2,1,0:T(8,128)(2,1)S(1)}, u32[]{:S(2)}, u32[]{:S(2)}) collective-permute-start(bf16[2,1,2,512,128]{4,3,2,1,0:T(8,128)(2,1)} %get-tuple-element.27), channel_id=1, source_target_pairs={{1,0},{2,1},{3,2},{4,3},{5,4},{6,5},{7,6},{9,8},{10,9},{11,10},{12... | collective-permute-start | bytes 1572872 | tf_op jit(solution)/shard_map/ppermute | solution.py:408
  43.6 8.8 %copy-start.3 = (s32[2,128,1]{1,2,0:T(1,128)S(1)}, s32[2,128,1]{1,2,0:T(1,128)}, u32[]{:S(2)}) copy-start(s32[2,128,1]{1,2,0:T(1,128)} %param.9) | copy-start | bytes 3076
  43.6 34.6 %collective-permute-start.2 = (bf16[2,7,160,128]{3,2,1,0:T(8,128)(2,1)}, bf16[2,7,160,128]{3,2,1,0:T(8,128)(2,1)}, u32[]{:S(2)}, u32[]{:S(2)}) collective-permute-start(bf16[2,7,160,128]{3,2,1,0:T(8,128)(2,1)} %get-tuple-element.28), channel_id=1, source_target_pairs={{0,8},{8,0},{1,9},{9,1},{2,10},{10,2},{3,11},{11,3},{4,12},{12,4},... | collective-permute-start | bytes 1720328 | tf_op jit(solution)/shard_map/ppermute | solution.py:406
  45.1 19.8 %copy-start.1 = (bf16[2,32,2,14,512]{4,2,3,1,0:T(2,128)(2,1)S(1)}, bf16[2,32,2,14,512]{4,2,3,1,0:T(2,128)(2,1)}, u32[]{:S(2)}) copy-start(bf16[2,32,2,14,512]{4,2,3,1,0:T(2,128)(2,1)} %param.6) | copy-start | bytes 5505028
  51.7 26.4 %collective-permute-start.3 = (bf16[2,8,160,128]{3,2,1,0:T(8,128)(2,1)}, bf16[2,8,160,128]{3,2,1,0:T(8,128)(2,1)S(1)}, u32[]{:S(2)}, u32[]{:S(2)}) collective-permute-start(bf16[2,8,160,128]{3,2,1,0:T(8,128)(2,1)} %shard_map.57), channel_id=1, source_target_pairs={{0,8},{8,0},{1,9},{9,1},{2,10},{10,2},{3,11},{11,3},{4,12},{12,4},... | collective-permute-start | bytes 1966088 | tf_op jit(solution)/shard_map/ppermute | solution.py:410
  67.4 10.8 %copy-start.2 = (f32[2]{0:T(128)S(1)}, f32[2]{0:T(128)}, u32[]{:S(2)}) copy-start(f32[2]{0:T(128)} %noise_ref.3) | copy-start | bytes 28
  67.4 14.7 %collective-permute-start.4 = (bf16[2,160,128]{2,1,0:T(8,128)(2,1)S(1)}, bf16[2,160,128]{2,1,0:T(8,128)(2,1)S(1)}, u32[]{:S(2)}, u32[]{:S(2)}) collective-permute-start(bf16[2,160,128]{2,1,0:T(8,128)(2,1)S(1)} %shard_map.59), channel_id=1, source_target_pairs={{0,8},{8,0},{1,9},{9,1},{2,10},{10,2},{3,11},{11,3},{4,12},{12,4},... | collective-permute-start | bytes 245768 | tf_op jit(solution)/shard_map/ppermute | solution.py:412
  83.6 7.0 %collective-permute-start.5 = (bf16[224,128]{1,0:T(8,128)(2,1)S(1)}, bf16[224,128]{1,0:T(8,128)(2,1)S(1)}, u32[]{:S(2)}, u32[]{:S(2)}) collective-permute-start(bf16[224,128]{1,0:T(8,128)(2,1)S(1)} %get-tuple-element.31), channel_id=1, source_target_pairs={{0,0},{1,1},{2,2},{3,3},{4,16},{5,17},{6,18},{7,19},{16,4},{17,5},... | collective-permute-start | bytes 172040 | tf_op jit(solution)/shard_map/ppermute | solution.py:440
  84.3 6.3 %collective-permute-start.6 = (bf16[224,128]{1,0:T(8,128)(2,1)S(1)}, bf16[224,128]{1,0:T(8,128)(2,1)S(1)}, u32[]{:S(2)}, u32[]{:S(2)}) collective-permute-start(bf16[224,128]{1,0:T(8,128)(2,1)S(1)} %get-tuple-element.32), channel_id=1, source_target_pairs={{0,1},{1,2},{2,3},{3,0},{4,17},{5,18},{6,19},{7,16},{16,5},{17,6},... | collective-permute-start | bytes 172040 | tf_op jit(solution)/shard_map/ppermute | solution.py:440
  86.7 4.2 %collective-permute-start.7 = (bf16[224,128]{1,0:T(8,128)(2,1)S(1)}, bf16[224,128]{1,0:T(8,128)(2,1)S(1)}, u32[]{:S(2)}, u32[]{:S(2)}) collective-permute-start(bf16[224,128]{1,0:T(8,128)(2,1)S(1)} %get-tuple-element.33), channel_id=1, source_target_pairs={{0,2},{1,3},{2,0},{3,1},{4,18},{5,19},{6,16},{7,17},{16,6},{17,7},... | collective-permute-start | bytes 172040 | tf_op jit(solution)/shard_map/ppermute | solution.py:440
  88.3 4.2 %collective-permute-start.8 = (bf16[224,128]{1,0:T(8,128)(2,1)S(1)}, bf16[224,128]{1,0:T(8,128)(2,1)S(1)}, u32[]{:S(2)}, u32[]{:S(2)}) collective-permute-start(bf16[224,128]{1,0:T(8,128)(2,1)S(1)} %get-tuple-element.34), channel_id=1, source_target_pairs={{0,3},{1,0},{2,1},{3,2},{4,19},{5,16},{6,17},{7,18},{16,7},{17,4},... | collective-permute-start | bytes 172040 | tf_op jit(solution)/shard_map/ppermute | solution.py:440
  92.5 10.3 %collective-permute-start.12 = (bf16[224,128]{1,0:T(8,128)(2,1)S(1)}, bf16[224,128]{1,0:T(8,128)(2,1)S(1)}, u32[]{:S(2)}, u32[]{:S(2)}) collective-permute-start(bf16[224,128]{1,0:T(8,128)(2,1)S(1)} %get-tuple-element.46), channel_id=1, source_target_pairs={{0,19},{1,16},{2,17},{3,18},{4,3},{5,0},{6,1},{7,2},{16,23},{17,20... | collective-permute-start | bytes 172040 | tf_op jit(solution)/shard_map/ppermute | solution.py:440
  98.4 6.0 %collective-permute-start.11 = (bf16[224,128]{1,0:T(8,128)(2,1)S(1)}, bf16[224,128]{1,0:T(8,128)(2,1)S(1)}, u32[]{:S(2)}, u32[]{:S(2)}) collective-permute-start(bf16[224,128]{1,0:T(8,128)(2,1)S(1)} %get-tuple-element.45), channel_id=1, source_target_pairs={{0,18},{1,19},{2,16},{3,17},{4,2},{5,3},{6,0},{7,1},{16,22},{17,23... | collective-permute-start | bytes 172040 | tf_op jit(solution)/shard_map/ppermute | solution.py:440
  98.4 8.1 %collective-permute-start.10 = (bf16[224,128]{1,0:T(8,128)(2,1)S(1)}, bf16[224,128]{1,0:T(8,128)(2,1)S(1)}, u32[]{:S(2)}, u32[]{:S(2)}) collective-permute-start(bf16[224,128]{1,0:T(8,128)(2,1)S(1)} %get-tuple-element.44), channel_id=1, source_target_pairs={{0,17},{1,18},{2,19},{3,16},{4,1},{5,2},{6,3},{7,0},{16,21},{17,22... | collective-permute-start | bytes 172040 | tf_op jit(solution)/shard_map/ppermute | solution.py:440
  101.2 7.3 %collective-permute-start.9 = (bf16[224,128]{1,0:T(8,128)(2,1)S(1)}, bf16[224,128]{1,0:T(8,128)(2,1)S(1)}, u32[]{:S(2)}, u32[]{:S(2)}) collective-permute-start(bf16[224,128]{1,0:T(8,128)(2,1)S(1)} %get-tuple-element.43), channel_id=1, source_target_pairs={{0,16},{1,17},{2,18},{3,19},{4,0},{5,1},{6,2},{7,3},{16,20},{17,21... | collective-permute-start | bytes 172040 | tf_op jit(solution)/shard_map/ppermute | solution.py:440
  102.1 8.5 %collective-permute-start.13 = (bf16[4,224,128]{2,1,0:T(8,128)(2,1)S(1)}, bf16[4,224,128]{2,1,0:T(8,128)(2,1)S(1)}, u32[]{:S(2)}, u32[]{:S(2)}) collective-permute-start(bf16[4,224,128]{2,1,0:T(8,128)(2,1)S(1)} %pad_maximum_fusion.refs_0_), channel_id=1, source_target_pairs={{0,8},{8,0},{1,9},{9,1},{2,10},{10,2},{3,11},{11,3},{4,12},{12,4},... | collective-permute-start | bytes 688136 | tf_op jit(solution)/shard_map/ppermute | solution.py:445
  108.5 6.1 %collective-permute-start.14 = (bf16[4,224,128]{2,1,0:T(8,128)(2,1)S(1)}, bf16[4,224,128]{2,1,0:T(8,128)(2,1)S(1)}, u32[]{:S(2)}, u32[]{:S(2)}) collective-permute-start(bf16[4,224,128]{2,1,0:T(8,128)(2,1)S(1)} %pad_maximum_fusion.1.refs_1_), channel_id=1, source_target_pairs={{0,8},{8,0},{1,9},{9,1},{2,10},{10,2},{3,11},{11,3},{4,12},{12,4},... | collective-permute-start | bytes 688136 | tf_op jit(solution)/shard_map/ppermute | solution.py:445

commit v4 on v3

--- a/solution.py
+++ b/solution.py
@@ -59,22 +59,24 @@
     ]
 
 
-def inner_gram(control, channel, received, peer, first, number, dtype, halo=False):
+def inner_gram(counts, channel, received, peer, first, number, dtype, halo=False):
     cells, band, _, antennas, users = channel.shape
     symbols = received.shape[2]
-    group, groups = GRP, band // GRP
     half = band // 2
     items = cells * number
 
-    def kernel(control_ref, chan, samp, out, *refs):
+    def kernel(counts_hbm, chan, samp, out, *refs):
         ends, refs = (refs[:2], refs[2:]) if halo else ((), refs)
-        win, ybuf, mat_a, lhs_a, mat_b, lhs_b, wsem, ysem, esem = refs
+        count_ref, win, ybuf, mat_a, lhs_a, mat_b, lhs_b, wsem, ysem, esem, csem = refs
+        count_copy = pltpu.make_async_copy(counts_hbm, count_ref, csem)
+        count_copy.start()
         edges = [
             pltpu.make_async_copy(chan.at[c, i * (band - 1)], ends[i].at[c, 0], esem.at[c, i])
             for c in range(cells)
             for i in range(len(ends))
         ]
-        side = 1 - control_ref[0] if peer else control_ref[0]
+        panel = lax.axis_index("panel")
+        side = 1 - panel if peer else panel
         start = 1 + side * (half - 1) + first
 
         def fetch(c, i):
@@ -114,8 +116,9 @@
         def multiply(item, mat, lhs):
             item = jnp.minimum(item, items - 1)
             c, i = item // number, item % number
-            gram(mat, lhs, out.at[c, i], control_ref[3 + c * groups + (start + i) // group], users)
-
+            gram(mat, lhs, out.at[c, i], count_ref[c, (start + i) // GRP], users)
+
+        count_copy.wait()
         wait(0)
         ready(0, mat_a, lhs_a)
 
@@ -135,11 +138,12 @@
     rows = users + 2 * SPAD
     return pl.pallas_call(
         kernel,
-        in_specs=[SMEM_SPEC, HBM_SPEC, HBM_SPEC],
-        out_specs=[VMEM_SPEC] + [HBM_SPEC] * (2 * halo),
+        in_specs=[HBM_SPEC] * 3,
+        out_specs=[VMEM_SPEC] * (1 + 2 * halo),
         out_shape=[jax.ShapeDtypeStruct((cells, number, rows, users), dtype)]
         + [jax.ShapeDtypeStruct((cells, 1, 2, antennas, users), BF16)] * (2 * halo),
         scratch_shapes=[
+            pltpu.SMEM(counts.shape, jnp.int32),
             pltpu.VMEM((cells, number + 2, 2, antennas, users), BF16),
             pltpu.VMEM((cells, number, symbols, 2, antennas), BF16),
             *work_buffers(antennas, users),
@@ -147,6 +151,7 @@
             pltpu.SemaphoreType.DMA((cells, number + 2)),
             pltpu.SemaphoreType.DMA((cells,)),
             pltpu.SemaphoreType.DMA((cells, 2)),
+            pltpu.SemaphoreType.DMA,
         ],
         compiler_params=pltpu.CompilerParams(vmem_limit_bytes=VMEM_LIMIT),
         cost_estimate=pl.CostEstimate(
@@ -154,24 +159,27 @@
             bytes_accessed=cells * (number + 2) * 4 * antennas * users,
             transcendentals=0,
         ),
-    )(control, channel, received)
-
-
-def edge_scratch(cells, symbols, antennas, users):
+    )(counts, channel, received)
+
+
+def edge_scratch(counts, symbols, antennas, users):
+    cells = counts.shape[0]
     return [
+        pltpu.SMEM(counts.shape, jnp.int32),
         pltpu.VMEM((cells, 3, 2, antennas, users), BF16),
         pltpu.VMEM((cells, symbols, 2, antennas), BF16),
         *work_buffers(antennas, users),
         *work_buffers(antennas, users),
         pltpu.SemaphoreType.DMA((cells, 3)),
         pltpu.SemaphoreType.DMA((cells,)),
+        pltpu.SemaphoreType.DMA,
     ]
 
 
-def edge_work(side, control_ref, chan, samp, low_ref, high_ref, out, scratch):
-    win, ybuf, mat_a, lhs_a, mat_b, lhs_b, wsem, ysem = scratch
+def edge_work(side, counts_hbm, chan, samp, low_ref, high_ref, out, scratch):
+    count_ref, win, ybuf, mat_a, lhs_a, mat_b, lhs_b, wsem, ysem, csem = scratch
+    count_copy = pltpu.make_async_copy(counts_hbm, count_ref, csem)
     cells, band, _, _, users = chan.shape
-    groups = band // GRP
     buffers = ((mat_a, lhs_a), (mat_b, lhs_b))
 
     def each_copy(act):
@@ -194,44 +202,46 @@
             run(1)
 
     def fetch():
+        count_copy.start()
         each_copy(lambda copy: copy.start())
         lhs_a[...] = jnp.zeros_like(lhs_a)
         lhs_b[...] = jnp.zeros_like(lhs_b)
 
     def work():
         each_copy(lambda copy: copy.wait())
-        last = jnp.where(side == 0, control_ref[1], control_ref[2])
-        stretch = jnp.where(jnp.full((1, users), last, jnp.int32) == 1, 1 / 0.75, 1.0)
+        count_copy.wait()
+        last = lax.axis_index("sc") == side * (lax.axis_size("sc") - 1)
+        stretch = jnp.where(jnp.full((1, users), last.astype(jnp.int32)) == 1, 1 / 0.75, 1.0)
         for c in range(cells):
             prepare(win.at[c, 0], win.at[c, 1], win.at[c, 2], ybuf.at[c], stretch, *buffers[c % 2])
         for c in range(cells):
-            gram(*buffers[c % 2], out.at[c], control_ref[3 + c * groups + side * (band - 1) // GRP], users)
+            gram(*buffers[c % 2], out.at[c], count_ref[c, side * (band - 1) // GRP], users)
 
     return fetch, work
 
 
-def edge_gram(control, channel, received, low, high):
+def edge_gram(counts, channel, received, low, high):
     cells, _, _, antennas, users = channel.shape
     symbols = received.shape[2]
 
-    def kernel(control_ref, chan, samp, low_ref, high_ref, out, *scratch):
-        fetch, work = edge_work(1 - control_ref[0], control_ref, chan, samp, low_ref, high_ref, out, scratch)
+    def kernel(counts_hbm, chan, samp, low_ref, high_ref, out, *scratch):
+        fetch, work = edge_work(1 - lax.axis_index("panel"), counts_hbm, chan, samp, low_ref, high_ref, out, scratch)
         fetch()
         work()
 
     return pl.pallas_call(
         kernel,
-        in_specs=[SMEM_SPEC] + [HBM_SPEC] * 4,
+        in_specs=[HBM_SPEC] * 5,
         out_specs=VMEM_SPEC,
         out_shape=jax.ShapeDtypeStruct((cells, users + 2 * SPAD, users), BF16),
-        scratch_shapes=edge_scratch(cells, symbols, antennas, users),
+        scratch_shapes=edge_scratch(counts, symbols, antennas, users),
         compiler_params=pltpu.CompilerParams(vmem_limit_bytes=VMEM_LIMIT),
         cost_estimate=pl.CostEstimate(
             flops=cells * 4 * antennas * users * 2 * (users + SPAD),
             bytes_accessed=cells * 12 * antennas * users,
             transcendentals=0,
         ),
-    )(control, channel, received, low, high)
+    )(counts, channel, received, low, high)
 
 
 def conjugate_gradient(sums, noise, users):
@@ -269,16 +279,17 @@
     return [e + a * d for e, a, d in zip(estimate, alpha, direction)]
 
 
-def inner_detect(control, noise_power, own, peers, channel, received, low, high):
+def inner_detect(counts, noise_power, own, peers, channel, received, low, high):
     cells, inner, rows, users = own.shape
     antennas, symbols = channel.shape[3], received.shape[2]
     half = inner + 1
 
-    def kernel(control_ref, noise_ref, chan, samp, low_ref, high_ref, own_ref, *refs):
+    def kernel(noise_ref, counts_hbm, chan, samp, low_ref, high_ref, own_ref, *refs):
+        panel = lax.axis_index("panel")
         peer_refs, (out, edge_out), scratch = refs[: len(peers)], refs[len(peers) : len(peers) + 2], refs[len(peers) + 2 :]
-        fetch, work = edge_work(control_ref[0], control_ref, chan, samp, low_ref, high_ref, edge_out, scratch)
+        fetch, work = edge_work(panel, counts_hbm, chan, samp, low_ref, high_ref, edge_out, scratch)
         fetch()
-        shift = 1 - control_ref[0]
+        shift = 1 - panel
 
         def step(c, carry):
             sums = []
@@ -294,32 +305,32 @@
 
     return pl.pallas_call(
         kernel,
-        in_specs=[SMEM_SPEC, SMEM_SPEC] + [HBM_SPEC] * 4 + [VMEM_SPEC] * (1 + len(peers)),
+        in_specs=[SMEM_SPEC] + [HBM_SPEC] * 5 + [VMEM_SPEC] * (1 + len(peers)),
         out_specs=[VMEM_SPEC, VMEM_SPEC],
         out_shape=[
             jax.ShapeDtypeStruct((cells, 2 * SPAD * half, users), F32),
             jax.ShapeDtypeStruct((cells, rows, users), F32),
         ],
-        scratch_shapes=edge_scratch(cells, symbols, antennas, users),
+        scratch_shapes=edge_scratch(counts, symbols, antennas, users),
         compiler_params=pltpu.CompilerParams(vmem_limit_bytes=VMEM_LIMIT),
         cost_estimate=pl.CostEstimate(
             flops=cells * inner * 2 * 2 * 2 * SPAD * users * 2 * users,
             bytes_accessed=cells * inner * rows * users * 6,
             transcendentals=0,
         ),
-    )(control, noise_power, channel, received, low, high, own, *peers)
-
-
-def edge_detect(control, noise_power, own, peer, inner, onehot, symbols, rounds):
+    )(noise_power, counts, channel, received, low, high, own, *peers)
+
+
+def edge_detect(noise_power, own, peer, inner, onehot, symbols, rounds):
     cells, rows, users = own.shape
     half = inner.shape[1] // (2 * SPAD)
-    width = onehot.shape[1] // rounds
+    width = onehot.shape[1] // (2 * rounds)
     keep = symbols * half
 
-    def kernel(control_ref, noise_ref, own_ref, peer_ref, inner_ref, hot_ref, *refs):
+    def kernel(noise_ref, own_ref, peer_ref, inner_ref, hot_ref, *refs):
         *outs, state = refs
         state[...] = inner_ref[...]
-        spot = control_ref[0] * (half - 1)
+        spot = lax.axis_index("panel") * (half - 1)
         for c in range(cells):
             (value,) = conjugate_gradient([own_ref[c] + peer_ref[c].astype(F32)], noise_ref[c], users)
             state[c, pl.ds(spot, 2 * SPAD, stride=half), :] = value
@@ -332,37 +343,54 @@
         lhs = jnp.concatenate(blocks, axis=1)
         placed = jnp.dot(lhs, hot_ref[...], preferred_element_type=F32).astype(BF16)
         for i, out in enumerate(outs):
-            out[...] = placed[:, i * width : (i + 1) * width]
+            for side in range(2):
+                first = (2 * i + side) * width
+                out[side * keep : (side + 1) * keep, :] = placed[:, first : first + width]
 
     return pl.pallas_call(
         kernel,
-        in_specs=[SMEM_SPEC, SMEM_SPEC] + [VMEM_SPEC] * 4,
+        in_specs=[SMEM_SPEC] + [VMEM_SPEC] * 4,
         out_specs=[VMEM_SPEC] * rounds,
-        out_shape=[jax.ShapeDtypeStruct((keep, width), BF16)] * rounds,
+        out_shape=[jax.ShapeDtypeStruct((2 * keep, width), BF16)] * rounds,
         scratch_shapes=[pltpu.VMEM(inner.shape, F32)],
         compiler_params=pltpu.CompilerParams(vmem_limit_bytes=VMEM_LIMIT),
         cost_estimate=pl.CostEstimate(
             flops=2 * keep * onehot.shape[0] * onehot.shape[1], bytes_accessed=4 * inner.size, transcendentals=0
         ),
-    )(control, noise_power, own, peer, inner, onehot)
-
-
-def assemble(control, mine, theirs, sources, cells, per_device, symbols, half):
-    total = len(sources) * 2 * half
+    )(noise_power, own, peer, inner, onehot)
+
+
+def assemble(sources, mine, theirs, others, cells, per_device, symbols, half):
+    rounds = sum(group.shape[0] for group in mine)
+    total = 2 * rounds * 2 * half
     lanes = mine[0].shape[2]
     slots = cells * per_device
-
-    def kernel(control_ref, source_ref, *refs):
-        mine_refs, theirs_refs = refs[: len(mine)], refs[len(mine) : 2 * len(mine)]
-        out, gathered, turned = refs[2 * len(mine) :]
-        for side, group in ((control_ref[0], mine_refs), (1 - control_ref[0], theirs_refs)):
-            number = 0
+    keep = symbols * half
+    number = len(mine)
+
+    def kernel(source_ref, *refs):
+        mine_refs, theirs_refs = refs[:number], refs[number : 2 * number]
+        own_other, peer_others = refs[2 * number], refs[2 * number + 1 : 3 * number + 1]
+        out, gathered, turned = refs[3 * number + 1 :]
+        panel = lax.axis_index("panel")
+
+        def place(ref, i, first, source, side):
+            start = pl.multiple_of(source * (2 * half) + side * half, half)
+            for s in range(symbols):
+                gathered[s, pl.ds(start, half), :] = ref[i, first + s * half : first + (s + 1) * half, :]
+
+        for side, group in ((panel, mine_refs), (1 - panel, theirs_refs)):
+            n = 0
             for ref in group:
                 for i in range(ref.shape[0]):
-                    start = pl.multiple_of(source_ref[number] * (2 * half) + side * half, half)
-                    for s in range(symbols):
-                        gathered[s, pl.ds(start, half), :] = ref[i, s * half : (s + 1) * half, :]
-                    number += 1
+                    place(ref, i, keep, source_ref[n], side)
+                    n += 1
+        for side, group in ((panel, (own_other,)), (1 - panel, peer_others)):
+            n = rounds
+            for ref in group:
+                for i in range(ref.shape[0]):
+                    place(ref, i, 0, source_ref[n], side)
+                    n += 1
         for s in range(symbols):
             value = gathered[s].T.astype(F32)
             for k in range(2):
@@ -378,7 +406,7 @@
 
     return pl.pallas_call(
         kernel,
-        in_specs=[SMEM_SPEC, SMEM_SPEC] + [VMEM_SPEC] * (2 * len(mine)),
+        in_specs=[SMEM_SPEC] + [VMEM_SPEC] * (3 * number + 1),
         out_specs=VMEM_SPEC,
         out_shape=jax.ShapeDtypeStruct((cells, per_device, symbols, 2, total), BF16),
         scratch_shapes=[
@@ -386,7 +414,7 @@
             pltpu.VMEM((total // 128, slots * 2 * SPAD, 128), F32),
         ],
         compiler_params=pltpu.CompilerParams(vmem_limit_bytes=VMEM_LIMIT),
-    )(control, sources, *mine, *theirs)
+    )(sources, *mine, *theirs, *others)
 
 
 def body(channel, received, noise_power, user_count, serving_cell):
@@ -396,54 +424,51 @@
     n_sc, n_cell = lax.axis_size("sc"), lax.axis_size("cell")
     panel, sc, cell = lax.axis_index("panel"), lax.axis_index("sc"), lax.axis_index("cell")
 
-    ends = jnp.stack([panel, (sc == 0).astype(jnp.int32), (sc == n_sc - 1).astype(jnp.int32)])
-    control = jnp.concatenate([ends.astype(jnp.int32), user_count.reshape(-1)])
     samples = jnp.transpose(received, (0, 1, 3, 2, 4))
 
     inner = half - 1
     count = inner // 2
-    outgoing, bottom, top = inner_gram(control, channel, samples, True, 0, count, BF16, halo=True)
+    outgoing, bottom, top = inner_gram(user_count, channel, samples, True, 0, count, BF16, halo=True)
     peers = [lax.ppermute(outgoing, "panel", SWAP)]
     low = lax.ppermute(top, "sc", [(i, i + 1) for i in range(n_sc - 1)])
     high = lax.ppermute(bottom, "sc", [(i + 1, i) for i in range(n_sc - 1)])
-    (outgoing,) = inner_gram(control, channel, samples, True, count, inner - count, BF16)
+    (outgoing,) = inner_gram(user_count, channel, samples, True, count, inner - count, BF16)
     peers.append(lax.ppermute(outgoing, "panel", SWAP))
-    (own,) = inner_gram(control, channel, samples, False, 0, inner, F32)
-    edge_peer = lax.ppermute(edge_gram(control, channel, samples, low, high), "panel", SWAP)
-    inner, edge_own = inner_detect(control, noise_power, own, peers, channel, samples, low, high)
+    (own,) = inner_gram(user_count, channel, samples, False, 0, inner, F32)
+    low, high, own = lax.optimization_barrier((low, high, own))
+    edge_peer = lax.ppermute(edge_gram(user_count, channel, samples, low, high), "panel", SWAP)
+    inner, edge_own = inner_detect(user_count, noise_power, own, peers, channel, samples, low, high)
 
     capacity = cells * users // n_cell
     per_device = n_cell * capacity // n_sc
     reach = capacity // per_device
-    rounds = n_cell * reach
     keys = serving_cell[:, :, 0].reshape(-1)
     position = lax.iota(jnp.int32, cells * users)
     earlier = (keys[:, None] == keys[None, :]) & (position[None, :] < position[:, None])
     rank = jnp.sum(earlier.astype(jnp.int32), axis=1)
-    turn = (keys // cells - sc // reach) % n_cell * reach + (rank // per_device - sc % reach) % reach
+    turn = (rank // per_device - sc % reach) % reach * 2 + (keys // cells == sc // reach).astype(jnp.int32)
     column = (turn * 2 * cells + keys % cells) * per_device + rank % per_device
     column = jnp.concatenate([column, column + cells * per_device])
     width = 2 * cells * per_device
-    onehot = (column[:, None] == lax.iota(jnp.int32, rounds * width)[None, :]).astype(BF16)
-
-    messages = edge_detect(control, noise_power, edge_own, edge_peer, inner, onehot, symbols, rounds)
-    arrived, sources = [], []
-    for a in range(n_cell):
-        if a == n_cell // 2:
-            messages, arrived = lax.optimization_barrier((messages, arrived))
-        for b in range(reach):
-            pairs = [
-                (s * n_sc + j, (j // reach + a) % n_cell * n_sc + s * reach + (j % reach + b) % reach)
-                for s in range(n_cell)
-                for j in range(n_sc)
-            ]
-            arrived.append(lax.ppermute(messages[a * reach + b], ("cell", "sc"), pairs))
-            sources.append((cell - a) % n_cell * reach + (sc % reach - b) % reach)
-    sources = jnp.stack(sources).astype(jnp.int32)
-    groups = [arrived[: rounds // 2], arrived[rounds // 2 :]]
-    mine = [jnp.stack(group) for group in groups]
+    onehot = (column[:, None] == lax.iota(jnp.int32, 2 * reach * width)[None, :]).astype(BF16)
+
+    messages = edge_detect(noise_power, edge_own, edge_peer, inner, onehot, symbols, reach)
+    arrived = []
+    for b in range(reach):
+        pairs = [
+            (s * n_sc + j, j // reach * n_sc + s * reach + (j % reach + b) % reach)
+            for s in range(n_cell)
+            for j in range(n_sc)
+        ]
+        arrived.append(lax.ppermute(messages[b], ("cell", "sc"), pairs))
+    turns = (sc % reach - lax.iota(jnp.int32, reach)) % reach
+    sources = jnp.concatenate([cell * reach + turns, (1 - cell) * reach + turns])
+    keep = symbols * half
+    mine = [jnp.stack(arrived[: reach // 2]), jnp.stack(arrived[reach // 2 :])]
     theirs = [lax.ppermute(group, "panel", SWAP) for group in mine]
-    routed = assemble(control, mine, theirs, sources, cells, per_device, symbols, half)
+    others = [lax.ppermute(jnp.stack([block[:keep] for block in arrived]), "cell", SWAP)]
+    others += [lax.ppermute(group[:, :keep], "cell", SWAP) for group in theirs]
+    routed = assemble(sources, mine, theirs, others, cells, per_device, symbols, half)
     return jnp.transpose(routed, (0, 1, 3, 2, 4))
 
 

time: 119 us -> 77.5 us (0.65)
  Pallas kernels: 62.6 us -> 32 us
  waiting for transfers between devices: 25.2 us -> 13.4 us
    pallas_call x7, Pallas kernels: 62.6 us -> 32 us  [the longest x3 20.6 us: inner_gram(): pl.pallas_call(kernel, in_specs=[HBM_SPEC] * 3, out_specs=[VMEM_SPEC] * (...]
    ppermute x1, waiting for transfers between devices: 12.1 us -> 4.23 us  [body(): low = lax.ppermute(top, 'sc', [(i, i + 1) for i in range(n_sc - 1)])]
    ppermute x2, waiting for transfers between devices: 5.44 us -> 0.29 us  [body(): theirs = [lax.ppermute(group, 'panel', SWAP) for group in mine]]
    ppermute x1, waiting for transfers between devices: 0.01 us -> 4.54 us  [body(): peers.append(lax.ppermute(outgoing, 'panel', SWAP))]
    ppermute x9 -> x8, waiting for transfers between devices: 7.63 us -> 4.37 us  [the longest x4 3.5 us: body(): arrived.append(lax.ppermute(messages[b], ('cell', 'sc'), pairs))]
    ppermute x2, starting transfers between devices: 1.18 us -> 3.13 us  [body(): theirs = [lax.ppermute(group, 'panel', SWAP) for group in mine]]
    ppermute x9 -> x8, starting transfers between devices: 18.2 us -> 17.2 us  [the longest x4 6.98 us: body(): arrived.append(lax.ppermute(messages[b], ('cell', 'sc'), pairs))]
  transfers between devices with their start and end apart: 15 -> 14, of which waited for: 8 -> 6; matrix products, arithmetic and copies ran while one was open for 1% -> 1% of each run, Pallas kernels for 19% -> 27%
where the time goes in v4:
time: 77.5 us; the launch traced here: 77.2 us
  Pallas kernels  32 us (41%)
  starting transfers between devices  28.7 us (37%)
  waiting for transfers between devices  13.4 us (17%)
  local copies, waits for them, and re-layouts  2.24 us (3%)
    pallas_call x3, Pallas kernels, inner_gram(): pl.pallas_call(kernel, in_specs=[HBM_SPEC] * 3, out_specs=[VMEM_SPEC] * (...  20.6 us
    ppermute x4, starting transfers between devices, body(): arrived.append(lax.ppermute(messages[b], ('cell', 'sc'), pairs))  6.98 us
    ppermute x1, starting transfers between devices, body(): lax.ppermute(jnp.stack([block[:keep] for block in arrived]), 'cell', SWAP)  4.99 us
    ppermute x1, starting transfers between devices, body(): low = lax.ppermute(top, 'sc', [(i, i + 1) for i in range(n_sc - 1)])  4.9 us
    ppermute x1, waiting for transfers between devices, body(): peers.append(lax.ppermute(outgoing, 'panel', SWAP))  4.54 us
    ppermute x1, waiting for transfers between devices, body(): low = lax.ppermute(top, 'sc', [(i, i + 1) for i in range(n_sc - 1)])  4.23 us
    pallas_call x1, Pallas kernels, assemble(): pl.pallas_call(kernel, in_specs=[SMEM_SPEC] + [VMEM_SPEC] * (3 * number +...  4.04 us
    pallas_call x1, Pallas kernels, inner_detect(): pl.pallas_call(kernel, in_specs=[SMEM_SPEC] + [HBM_SPEC] * 5 + [VMEM_SPEC...  3.88 us
  transfers between devices with their start and end apart: 14, of which 6 were waited for; matrix products, arithmetic and copies ran while one was open for 1% of the time, Pallas kernels for 27%

profile of v4, /device:TPU:0, one launch (start us, length us, event | category | flops | bytes accessed | tf_op | source)
XLA Modules:
  0.0 77.2 jit_solution(17526383133562826619)
XLA Ops:
  0.0 1.5 %copy-done = bf16[2,32,2,14,512]{4,2,3,1,0:T(2,128)(2,1)S(1)} copy-done((bf16[2,32,2,14,512]{4,2,3,1,0:T(2,128)(2,1)S(1)}, bf16[2,32,2,14,512]{4,2,3,1,0:T(2,128)(2,1)}, u32[]{:S(2)}) %copy-start) | copy-done | bytes 1835032
  2.2 5.9 %shard_map.55 = (bf16[2,7,160,128]{3,2,1,0:T(8,128)(2,1)}, bf16[2,1,2,512,128]{4,3,2,1,0:T(8,128)(2,1)}, bf16[2,1,2,512,128]{4,3,2,1,0:T(8,128)(2,1)}) custom-call(s32[2,2]{1,0:T(2,128)S(1)} %copy-done.2, bf16[2,32,2,512,128]{4,3,2,1,0:T(8,128)(2,1)} %chan.9, bf16[2,32,14,2,512]{4,3,2,1,0:T(2,128)(2,1)S(1)} %bitcast.15), custom_call_target="tpu_custom_call" | custom-call | flops 1056964608 | bytes 4718592 | tf_op jit(solution)/shard_map/pallas_call | solution.py:139
  8.1 4.9 %collective-permute-start = (bf16[2,1,2,512,128]{4,3,2,1,0:T(8,128)(2,1)}, bf16[2,1,2,512,128]{4,3,2,1,0:T(8,128)(2,1)S(1)}, u32[]{:S(2)}, u32[]{:S(2)}) collective-permute-start(bf16[2,1,2,512,128]{4,3,2,1,0:T(8,128)(2,1)} %get-tuple-element.17), channel_id=1, source_target_pairs={{0,1},{1,2},{2,3},{3,4},{4,5},{5,6},{6,7},{8,9},{9,10},{10,11},{11... | collective-permute-start | bytes 1572872 | tf_op jit(solution)/shard_map/ppermute | solution.py:433
  13.0 1.3 %collective-permute-start.1 = (bf16[2,1,2,512,128]{4,3,2,1,0:T(8,128)(2,1)}, bf16[2,1,2,512,128]{4,3,2,1,0:T(8,128)(2,1)S(1)}, u32[]{:S(2)}, u32[]{:S(2)}) collective-permute-start(bf16[2,1,2,512,128]{4,3,2,1,0:T(8,128)(2,1)} %get-tuple-element.18), channel_id=1, source_target_pairs={{1,0},{2,1},{3,2},{4,3},{5,4},{6,5},{7,6},{9,8},{10,9},{11,10},{12... | collective-permute-start | bytes 1572872 | tf_op jit(solution)/shard_map/ppermute | solution.py:434
  14.4 1.6 %collective-permute-start.2 = (bf16[2,7,160,128]{3,2,1,0:T(8,128)(2,1)}, bf16[2,7,160,128]{3,2,1,0:T(8,128)(2,1)}, u32[]{:S(2)}, u32[]{:S(2)}) collective-permute-start(bf16[2,7,160,128]{3,2,1,0:T(8,128)(2,1)} %get-tuple-element.22), channel_id=1, source_target_pairs={{0,8},{8,0},{1,9},{9,1},{2,10},{10,2},{3,11},{11,3},{4,12},{12,4},... | collective-permute-start | bytes 1720328 | tf_op jit(solution)/shard_map/ppermute | solution.py:432
  15.9 6.0 %shard_map.57 = bf16[2,8,160,128]{3,2,1,0:T(8,128)(2,1)} custom-call(s32[2,2]{1,0:T(2,128)S(1)} %copy-done.2, bf16[2,32,2,512,128]{4,3,2,1,0:T(8,128)(2,1)} %chan.9, bf16[2,32,14,2,512]{4,3,2,1,0:T(2,128)(2,1)S(1)} %bitcast.16), custom_call_target="tpu_custom_call" | custom-call | flops 1207959552 | bytes 5242880 | tf_op jit(solution)/shard_map/pallas_call | solution.py:139
  22.8 8.6 %shard_map.56.own_ref = f32[2,15,160,128]{3,2,1,0:T(8,128)S(1)} custom-call(s32[2,2]{1,0:T(2,128)S(1)} %copy-done.3, bf16[2,32,2,512,128]{4,3,2,1,0:T(8,128)(2,1)} %chan.9, bf16[2,32,14,2,512]{4,3,2,1,0:T(2,128)(2,1)S(1)} %bitcast.17), custom_call_target="tpu_custom_call" | custom-call | flops 2264924160 | bytes 8912896 | tf_op jit(solution)/shard_map/pallas_call | solution.py:139
  31.5 4.2 %collective-permute-done.low_ref = bf16[2,1,2,512,128]{4,3,2,1,0:T(8,128)(2,1)S(1)} collective-permute-done((bf16[2,1,2,512,128]{4,3,2,1,0:T(8,128)(2,1)}, bf16[2,1,2,512,128]{4,3,2,1,0:T(8,128)(2,1)S(1)}, u32[]{:S(2)}, u32[]{:S(2)}) %collective-permute-start) | collective-permute-done | bytes 524320 | tf_op jit(solution)/shard_map/ppermute | solution.py:433
  35.7 1.9 %shard_map.59 = bf16[2,160,128]{2,1,0:T(8,128)(2,1)S(1)} custom-call(s32[2,2]{1,0:T(2,128)S(1)} %copy-done.3, bf16[2,32,2,512,128]{4,3,2,1,0:T(8,128)(2,1)} %chan.9, bf16[2,32,14,2,512]{4,3,2,1,0:T(2,128)(2,1)S(1)} %bitcast.18, bf16[2,1,2,512,128]{4,3,2,1,0:T(8,128)(2,1)S(1)} %collective-permute-done.low_ref, ...), custom_call_target="tpu_custom_call" | custom-call | flops 150994944 | bytes 1572864 | tf_op jit(solution)/shard_map/pallas_call | solution.py:232
  37.6 1.6 %collective-permute-start.4 = (bf16[2,160,128]{2,1,0:T(8,128)(2,1)S(1)}, bf16[2,160,128]{2,1,0:T(8,128)(2,1)S(1)}, u32[]{:S(2)}, u32[]{:S(2)}) collective-permute-start(bf16[2,160,128]{2,1,0:T(8,128)(2,1)S(1)} %shard_map.59), channel_id=1, source_target_pairs={{0,8},{8,0},{1,9},{9,1},{2,10},{10,2},{3,11},{11,3},{4,12},{12,4},... | collective-permute-start | bytes 245768 | tf_op jit(solution)/shard_map/ppermute | solution.py:439
  39.4 4.5 %collective-permute-done.3.refs_1_ = bf16[2,8,160,128]{3,2,1,0:T(8,128)(2,1)S(1)} collective-permute-done((bf16[2,8,160,128]{3,2,1,0:T(8,128)(2,1)}, bf16[2,8,160,128]{3,2,1,0:T(8,128)(2,1)S(1)}, u32[]{:S(2)}, u32[]{:S(2)}) %collective-permute-start.3) | collective-permute-done | bytes 655392 | tf_op jit(solution)/shard_map/ppermute | solution.py:436
  44.0 3.9 %shard_map.58 = (f32[2,512,128]{2,1,0:T(8,128)S(1)}, f32[2,160,128]{2,1,0:T(8,128)S(1)}) custom-call(f32[2]{0:T(128)S(1)} %copy-done.4, s32[2,2]{1,0:T(2,128)S(1)} %copy-done.3, bf16[2,32,2,512,128]{4,3,2,1,0:T(8,128)(2,1)} %chan.9, bf16[2,32,14,2,512]{4,3,2,1,0:T(2,128)(2,1)S(1)} %bitcast.19, bf16[2,1,2,512,128]{4,3,2,1,0:T(8,128)(2,1)S(1)} %collective-permute-done.low_ref, ...), custom_call_target="tpu_custom_call" | custom-call | flops 125829120 | bytes 3686400 | tf_op jit(solution)/shard_map/pallas_call | solution.py:306
  47.9 1.5 %shard_map.60 = (bf16[448,128]{1,0:T(8,128)(2,1)S(1)}, bf16[448,128]{1,0:T(8,128)(2,1)S(1)}, bf16[448,128]{1,0:T(8,128)(2,1)S(1)}, bf16[448,128]{1,0:T(8,128)(2,1)S(1)}) custom-call(f32[2]{0:T(128)S(1)} %copy-done.4, f32[2,160,128]{2,1,0:T(8,128)S(1)} %get-tuple-element.23.own_ref, bf16[2,160,128]{2,1,0:T(8,128)(2,1)S(1)} %collective-permute-done.4.peer_ref, ...), custom_call_target="tpu_custom_call" | custom-call | flops 234881024 | bytes 524288 | tf_op jit(solution)/shard_map/pallas_call | solution.py:350
  49.4 2.4 %collective-permute-start.6 = (bf16[448,128]{1,0:T(8,128)(2,1)S(1)}, bf16[448,128]{1,0:T(8,128)(2,1)S(1)}, u32[]{:S(2)}, u32[]{:S(2)}) collective-permute-start(bf16[448,128]{1,0:T(8,128)(2,1)S(1)} %get-tuple-element.26), channel_id=1, source_target_pairs={{0,1},{1,2},{2,3},{3,0},{4,17},{5,18},{6,19},{7,16},{16,5},{17,6},... | collective-permute-start | bytes 344072 | tf_op jit(solution)/shard_map/ppermute | solution.py:463
  52.5 1.1 %collective-permute-start.8 = (bf16[448,128]{1,0:T(8,128)(2,1)S(1)}, bf16[448,128]{1,0:T(8,128)(2,1)S(1)}, u32[]{:S(2)}, u32[]{:S(2)}) collective-permute-start(bf16[448,128]{1,0:T(8,128)(2,1)S(1)} %get-tuple-element.28), channel_id=1, source_target_pairs={{0,3},{1,0},{2,1},{3,2},{4,19},{5,16},{6,17},{7,18},{16,7},{17,4},... | collective-permute-start | bytes 344072 | tf_op jit(solution)/shard_map/ppermute | solution.py:463
  53.6 2.8 %collective-permute-start.7 = (bf16[448,128]{1,0:T(8,128)(2,1)S(1)}, bf16[448,128]{1,0:T(8,128)(2,1)S(1)}, u32[]{:S(2)}, u32[]{:S(2)}) collective-permute-start(bf16[448,128]{1,0:T(8,128)(2,1)S(1)} %get-tuple-element.27), channel_id=1, source_target_pairs={{0,2},{1,3},{2,0},{3,1},{4,18},{5,19},{6,16},{7,17},{16,6},{17,7},... | collective-permute-start | bytes 344072 | tf_op jit(solution)/shard_map/ppermute | solution.py:463
  56.4 1.6 %collective-permute-start.9 = (bf16[2,448,128]{2,1,0:T(8,128)(2,1)S(1)}, bf16[2,448,128]{2,1,0:T(8,128)(2,1)S(1)}, u32[]{:S(2)}, u32[]{:S(2)}) collective-permute-start(bf16[2,448,128]{2,1,0:T(8,128)(2,1)S(1)} %pad_maximum_fusion.refs_0_), channel_id=1, source_target_pairs={{0,8},{8,0},{1,9},{9,1},{2,10},{10,2},{3,11},{11,3},{4,12},{12,4},... | collective-permute-start | bytes 688136 | tf_op jit(solution)/shard_map/ppermute | solution.py:468
  58.0 0.9 %collective-permute-done.8 = bf16[448,128]{1,0:T(8,128)(2,1)S(1)} collective-permute-done((bf16[448,128]{1,0:T(8,128)(2,1)S(1)}, bf16[448,128]{1,0:T(8,128)(2,1)S(1)}, u32[]{:S(2)}, u32[]{:S(2)}) %collective-permute-start.8) | collective-permute-done | bytes 114720 | tf_op jit(solution)/shard_map/ppermute | solution.py:463
  58.9 2.6 %collective-permute-done.7 = bf16[448,128]{1,0:T(8,128)(2,1)S(1)} collective-permute-done((bf16[448,128]{1,0:T(8,128)(2,1)S(1)}, bf16[448,128]{1,0:T(8,128)(2,1)S(1)}, u32[]{:S(2)}, u32[]{:S(2)}) %collective-permute-start.7) | collective-permute-done | bytes 114720 | tf_op jit(solution)/shard_map/ppermute | solution.py:463
  61.5 1.6 %collective-permute-start.10 = (bf16[2,448,128]{2,1,0:T(8,128)(2,1)S(1)}, bf16[2,448,128]{2,1,0:T(8,128)(2,1)S(1)}, u32[]{:S(2)}, u32[]{:S(2)}) collective-permute-start(bf16[2,448,128]{2,1,0:T(8,128)(2,1)S(1)} %pad_maximum_fusion.1.refs_1_), channel_id=1, source_target_pairs={{0,8},{8,0},{1,9},{9,1},{2,10},{10,2},{3,11},{11,3},{4,12},{12,4},... | collective-permute-start | bytes 688136 | tf_op jit(solution)/shard_map/ppermute | solution.py:468
  63.2 5.0 %collective-permute-start.11 = (bf16[4,224,128]{2,1,0:T(8,128)(2,1)S(1)}, bf16[4,224,128]{2,1,0:T(8,128)(2,1)S(1)}, u32[]{:S(2)}, u32[]{:S(2)}) collective-permute-start(bf16[4,224,128]{2,1,0:T(8,128)(2,1)S(1)} %pad_maximum_fusion.2), channel_id=1, source_target_pairs={{0,16},{16,0},{1,17},{17,1},{2,18},{18,2},{3,19},{19,3},{4,20},{20... | collective-permute-start | bytes 688136 | tf_op jit(solution)/shard_map/ppermute | solution.py:469
  68.2 1.6 %collective-permute-start.12 = (bf16[2,224,128]{2,1,0:T(8,128)(2,1)S(1)}, bf16[2,224,128]{2,1,0:T(8,128)(2,1)S(1)}, u32[]{:S(2)}, u32[]{:S(2)}) collective-permute-start(bf16[2,224,128]{2,1,0:T(8,128)(2,1)S(1)} %slice.28), channel_id=1, source_target_pairs={{0,16},{16,0},{1,17},{17,1},{2,18},{18,2},{3,19},{19,3},{4,20},{20... | collective-permute-start | bytes 344072 | tf_op jit(solution)/shard_map/ppermute | solution.py:470
  70.1 2.1 %collective-permute-start.13 = (bf16[2,224,128]{2,1,0:T(8,128)(2,1)S(1)}, bf16[2,224,128]{2,1,0:T(8,128)(2,1)S(1)}, u32[]{:S(2)}, u32[]{:S(2)}) collective-permute-start(bf16[2,224,128]{2,1,0:T(8,128)(2,1)S(1)} %slice.29), channel_id=1, source_target_pairs={{0,16},{16,0},{1,17},{17,1},{2,18},{18,2},{3,19},{19,3},{4,20},{20... | collective-permute-start | bytes 344072 | tf_op jit(solution)/shard_map/ppermute | solution.py:470
  73.2 4.0 %shard_map.61 = bf16[2,32,14,2,256]{4,3,2,1,0:T(2,128)(2,1)} custom-call(s32[8]{0:T(128)S(1)} %pad_add_fusion.1.source_ref, bf16[2,448,128]{2,1,0:T(8,128)(2,1)S(1)} %pad_maximum_fusion.refs_0_, bf16[2,448,128]{2,1,0:T(8,128)(2,1)S(1)} %pad_maximum_fusion.1.refs_1_, bf16[2,448,128]{2,1,0:T(8,128)(2,1)S(1)} %collective-permute-done.9.refs_2_, ...), custom_call_target="tpu_custom_call" | custom-call | tf_op jit(solution)/shard_map/pallas_call | solution.py:407
  (38 shorter events, 3.8 us)
Async XLA Ops:
  0.0 1.5 %copy-start = (bf16[2,32,2,14,512]{4,2,3,1,0:T(2,128)(2,1)S(1)}, bf16[2,32,2,14,512]{4,2,3,1,0:T(2,128)(2,1)}, u32[]{:S(2)}) copy-start(bf16[2,32,2,14,512]{4,2,3,1,0:T(2,128)(2,1)} %param.6) | copy-start | bytes 5505028
  1.5 0.7 copy-start.2
  8.1 27.6 %collective-permute-start = (bf16[2,1,2,512,128]{4,3,2,1,0:T(8,128)(2,1)}, bf16[2,1,2,512,128]{4,3,2,1,0:T(8,128)(2,1)S(1)}, u32[]{:S(2)}, u32[]{:S(2)}) collective-permute-start(bf16[2,1,2,512,128]{4,3,2,1,0:T(8,128)(2,1)} %get-tuple-element.17), channel_id=1, source_target_pairs={{0,1},{1,2},{2,3},{3,4},{4,5},{5,6},{6,7},{8,9},{9,10},{10,11},{11... | collective-permute-start | bytes 1572872 | tf_op jit(solution)/shard_map/ppermute | solution.py:433
  13.0 22.7 %collective-permute-start.1 = (bf16[2,1,2,512,128]{4,3,2,1,0:T(8,128)(2,1)}, bf16[2,1,2,512,128]{4,3,2,1,0:T(8,128)(2,1)S(1)}, u32[]{:S(2)}, u32[]{:S(2)}) collective-permute-start(bf16[2,1,2,512,128]{4,3,2,1,0:T(8,128)(2,1)} %get-tuple-element.18), channel_id=1, source_target_pairs={{1,0},{2,1},{3,2},{4,3},{5,4},{6,5},{7,6},{9,8},{10,9},{11,10},{12... | collective-permute-start | bytes 1572872 | tf_op jit(solution)/shard_map/ppermute | solution.py:434
  14.3 8.2 %copy-start.5 = (s32[2,128,1]{1,2,0:T(1,128)S(1)}, s32[2,128,1]{1,2,0:T(1,128)}, u32[]{:S(2)}) copy-start(s32[2,128,1]{1,2,0:T(1,128)} %param.9) | copy-start | bytes 3076
  14.3 8.5 %copy-start.1 = (bf16[2,32,2,14,512]{4,2,3,1,0:T(2,128)(2,1)S(1)}, bf16[2,32,2,14,512]{4,2,3,1,0:T(2,128)(2,1)}, u32[]{:S(2)}) copy-start(bf16[2,32,2,14,512]{4,2,3,1,0:T(2,128)(2,1)} %param.6) | copy-start | bytes 5505028
  14.3 8.5 %copy-start.3 = (s32[2,2]{1,0:T(2,128)S(1)}, s32[2,2]{1,0:T(2,128)}, u32[]{:S(2)}) copy-start(s32[2,2]{1,0:T(2,128)} %counts_hbm.9) | copy-start | bytes 52
  14.4 25.1 %collective-permute-start.2 = (bf16[2,7,160,128]{3,2,1,0:T(8,128)(2,1)}, bf16[2,7,160,128]{3,2,1,0:T(8,128)(2,1)}, u32[]{:S(2)}, u32[]{:S(2)}) collective-permute-start(bf16[2,7,160,128]{3,2,1,0:T(8,128)(2,1)} %get-tuple-element.22), channel_id=1, source_target_pairs={{0,8},{8,0},{1,9},{9,1},{2,10},{10,2},{3,11},{11,3},{4,12},{12,4},... | collective-permute-start | bytes 1720328 | tf_op jit(solution)/shard_map/ppermute | solution.py:432
  21.9 22.0 %collective-permute-start.3 = (bf16[2,8,160,128]{3,2,1,0:T(8,128)(2,1)}, bf16[2,8,160,128]{3,2,1,0:T(8,128)(2,1)S(1)}, u32[]{:S(2)}, u32[]{:S(2)}) collective-permute-start(bf16[2,8,160,128]{3,2,1,0:T(8,128)(2,1)} %shard_map.57), channel_id=1, source_target_pairs={{0,8},{8,0},{1,9},{9,1},{2,10},{10,2},{3,11},{11,3},{4,12},{12,4},... | collective-permute-start | bytes 1966088 | tf_op jit(solution)/shard_map/ppermute | solution.py:436
  31.5 12.5 %copy-start.4 = (f32[2]{0:T(128)S(1)}, f32[2]{0:T(128)}, u32[]{:S(2)}) copy-start(f32[2]{0:T(128)} %noise_ref.3) | copy-start | bytes 28
  37.6 10.3 %collective-permute-start.4 = (bf16[2,160,128]{2,1,0:T(8,128)(2,1)S(1)}, bf16[2,160,128]{2,1,0:T(8,128)(2,1)S(1)}, u32[]{:S(2)}, u32[]{:S(2)}) collective-permute-start(bf16[2,160,128]{2,1,0:T(8,128)(2,1)S(1)} %shard_map.59), channel_id=1, source_target_pairs={{0,8},{8,0},{1,9},{9,1},{2,10},{10,2},{3,11},{11,3},{4,12},{12,4},... | collective-permute-start | bytes 245768 | tf_op jit(solution)/shard_map/ppermute | solution.py:439
  49.4 7.0 %collective-permute-start.6 = (bf16[448,128]{1,0:T(8,128)(2,1)S(1)}, bf16[448,128]{1,0:T(8,128)(2,1)S(1)}, u32[]{:S(2)}, u32[]{:S(2)}) collective-permute-start(bf16[448,128]{1,0:T(8,128)(2,1)S(1)} %get-tuple-element.26), channel_id=1, source_target_pairs={{0,1},{1,2},{2,3},{3,0},{4,17},{5,18},{6,19},{7,16},{16,5},{17,6},... | collective-permute-start | bytes 344072 | tf_op jit(solution)/shard_map/ppermute | solution.py:463
  51.8 4.6 %collective-permute-start.5 = (bf16[448,128]{1,0:T(8,128)(2,1)S(1)}, bf16[448,128]{1,0:T(8,128)(2,1)S(1)}, u32[]{:S(2)}, u32[]{:S(2)}) collective-permute-start(bf16[448,128]{1,0:T(8,128)(2,1)S(1)} %get-tuple-element.25), channel_id=1, source_target_pairs={{0,0},{1,1},{2,2},{3,3},{4,16},{5,17},{6,18},{7,19},{16,4},{17,5},... | collective-permute-start | bytes 344072 | tf_op jit(solution)/shard_map/ppermute | solution.py:463
  52.5 6.4 %collective-permute-start.8 = (bf16[448,128]{1,0:T(8,128)(2,1)S(1)}, bf16[448,128]{1,0:T(8,128)(2,1)S(1)}, u32[]{:S(2)}, u32[]{:S(2)}) collective-permute-start(bf16[448,128]{1,0:T(8,128)(2,1)S(1)} %get-tuple-element.28), channel_id=1, source_target_pairs={{0,3},{1,0},{2,1},{3,2},{4,19},{5,16},{6,17},{7,18},{16,7},{17,4},... | collective-permute-start | bytes 344072 | tf_op jit(solution)/shard_map/ppermute | solution.py:463
  53.6 7.9 %collective-permute-start.7 = (bf16[448,128]{1,0:T(8,128)(2,1)S(1)}, bf16[448,128]{1,0:T(8,128)(2,1)S(1)}, u32[]{:S(2)}, u32[]{:S(2)}) collective-permute-start(bf16[448,128]{1,0:T(8,128)(2,1)S(1)} %get-tuple-element.27), channel_id=1, source_target_pairs={{0,2},{1,3},{2,0},{3,1},{4,18},{5,19},{6,16},{7,17},{16,6},{17,7},... | collective-permute-start | bytes 344072 | tf_op jit(solution)/shard_map/ppermute | solution.py:463
  56.4 11.7 %collective-permute-start.9 = (bf16[2,448,128]{2,1,0:T(8,128)(2,1)S(1)}, bf16[2,448,128]{2,1,0:T(8,128)(2,1)S(1)}, u32[]{:S(2)}, u32[]{:S(2)}) collective-permute-start(bf16[2,448,128]{2,1,0:T(8,128)(2,1)S(1)} %pad_maximum_fusion.refs_0_), channel_id=1, source_target_pairs={{0,8},{8,0},{1,9},{9,1},{2,10},{10,2},{3,11},{11,3},{4,12},{12,4},... | collective-permute-start | bytes 688136 | tf_op jit(solution)/shard_map/ppermute | solution.py:468
  61.5 8.5 %collective-permute-start.10 = (bf16[2,448,128]{2,1,0:T(8,128)(2,1)S(1)}, bf16[2,448,128]{2,1,0:T(8,128)(2,1)S(1)}, u32[]{:S(2)}, u32[]{:S(2)}) collective-permute-start(bf16[2,448,128]{2,1,0:T(8,128)(2,1)S(1)} %pad_maximum_fusion.1.refs_1_), channel_id=1, source_target_pairs={{0,8},{8,0},{1,9},{9,1},{2,10},{10,2},{3,11},{11,3},{4,12},{12,4},... | collective-permute-start | bytes 688136 | tf_op jit(solution)/shard_map/ppermute | solution.py:468
  63.2 9.1 %collective-permute-start.11 = (bf16[4,224,128]{2,1,0:T(8,128)(2,1)S(1)}, bf16[4,224,128]{2,1,0:T(8,128)(2,1)S(1)}, u32[]{:S(2)}, u32[]{:S(2)}) collective-permute-start(bf16[4,224,128]{2,1,0:T(8,128)(2,1)S(1)} %pad_maximum_fusion.2), channel_id=1, source_target_pairs={{0,16},{16,0},{1,17},{17,1},{2,18},{18,2},{3,19},{19,3},{4,20},{20... | collective-permute-start | bytes 688136 | tf_op jit(solution)/shard_map/ppermute | solution.py:469
  68.2 4.1 %collective-permute-start.12 = (bf16[2,224,128]{2,1,0:T(8,128)(2,1)S(1)}, bf16[2,224,128]{2,1,0:T(8,128)(2,1)S(1)}, u32[]{:S(2)}, u32[]{:S(2)}) collective-permute-start(bf16[2,224,128]{2,1,0:T(8,128)(2,1)S(1)} %slice.28), channel_id=1, source_target_pairs={{0,16},{16,0},{1,17},{17,1},{2,18},{18,2},{3,19},{19,3},{4,20},{20... | collective-permute-start | bytes 344072 | tf_op jit(solution)/shard_map/ppermute | solution.py:470
  70.1 3.1 %collective-permute-start.13 = (bf16[2,224,128]{2,1,0:T(8,128)(2,1)S(1)}, bf16[2,224,128]{2,1,0:T(8,128)(2,1)S(1)}, u32[]{:S(2)}, u32[]{:S(2)}) collective-permute-start(bf16[2,224,128]{2,1,0:T(8,128)(2,1)S(1)} %slice.29), channel_id=1, source_target_pairs={{0,16},{16,0},{1,17},{17,1},{2,18},{18,2},{3,19},{19,3},{4,20},{20... | collective-permute-start | bytes 344072 | tf_op jit(solution)/shard_map/ppermute | solution.py:470

commit v5 on v4

--- a/solution.py
+++ b/solution.py
@@ -59,22 +59,15 @@
     ]
 
 
-def inner_gram(counts, channel, received, peer, first, number, dtype, halo=False):
+def inner_gram(counts, channel, received, peer, first, number, dtype, limit=VMEM_LIMIT):
     cells, band, _, antennas, users = channel.shape
     symbols = received.shape[2]
     half = band // 2
     items = cells * number
 
-    def kernel(counts_hbm, chan, samp, out, *refs):
-        ends, refs = (refs[:2], refs[2:]) if halo else ((), refs)
-        count_ref, win, ybuf, mat_a, lhs_a, mat_b, lhs_b, wsem, ysem, esem, csem = refs
+    def kernel(counts_hbm, chan, samp, out, count_ref, win, ybuf, mat_a, lhs_a, mat_b, lhs_b, wsem, ysem, csem):
         count_copy = pltpu.make_async_copy(counts_hbm, count_ref, csem)
         count_copy.start()
-        edges = [
-            pltpu.make_async_copy(chan.at[c, i * (band - 1)], ends[i].at[c, 0], esem.at[c, i])
-            for c in range(cells)
-            for i in range(len(ends))
-        ]
         panel = lax.axis_index("panel")
         side = 1 - panel if peer else panel
         start = 1 + side * (half - 1) + first
@@ -90,8 +83,6 @@
                 fetch(c, i).start()
                 if i == min(2, number):
                     fetch_samples(c).start()
-        for copy in edges:
-            copy.start()
         lhs_a[...] = jnp.zeros_like(lhs_a)
         lhs_b[...] = jnp.zeros_like(lhs_b)
 
@@ -132,16 +123,13 @@
             return carry
 
         lax.fori_loop(0, (items + 1) // 2, step, 0)
-        for copy in edges:
-            copy.wait()
 
     rows = users + 2 * SPAD
     return pl.pallas_call(
         kernel,
         in_specs=[HBM_SPEC] * 3,
-        out_specs=[VMEM_SPEC] * (1 + 2 * halo),
-        out_shape=[jax.ShapeDtypeStruct((cells, number, rows, users), dtype)]
-        + [jax.ShapeDtypeStruct((cells, 1, 2, antennas, users), BF16)] * (2 * halo),
+        out_specs=VMEM_SPEC,
+        out_shape=jax.ShapeDtypeStruct((cells, number, rows, users), dtype),
         scratch_shapes=[
             pltpu.SMEM(counts.shape, jnp.int32),
             pltpu.VMEM((cells, number + 2, 2, antennas, users), BF16),
@@ -150,16 +138,41 @@
             *work_buffers(antennas, users),
             pltpu.SemaphoreType.DMA((cells, number + 2)),
             pltpu.SemaphoreType.DMA((cells,)),
-            pltpu.SemaphoreType.DMA((cells, 2)),
             pltpu.SemaphoreType.DMA,
         ],
-        compiler_params=pltpu.CompilerParams(vmem_limit_bytes=VMEM_LIMIT),
+        compiler_params=pltpu.CompilerParams(vmem_limit_bytes=limit),
         cost_estimate=pl.CostEstimate(
             flops=items * 4 * antennas * users * 2 * (users + SPAD),
             bytes_accessed=cells * (number + 2) * 4 * antennas * users,
             transcendentals=0,
         ),
     )(counts, channel, received)
+
+
+def band_ends(channel, after):
+    cells, band, _, antennas, users = channel.shape
+
+    def kernel(chan, after_ref, *refs):
+        *ends, sems = refs
+        copies = [
+            pltpu.make_async_copy(chan.at[c, i * (band - 1)], ends[i].at[c, 0], sems.at[c, i])
+            for c in range(cells)
+            for i in range(2)
+        ]
+        for copy in copies:
+            copy.start()
+        for copy in copies:
+            copy.wait()
+
+    return pl.pallas_call(
+        kernel,
+        in_specs=[HBM_SPEC] * 2,
+        out_specs=[VMEM_SPEC] * 2,
+        out_shape=[jax.ShapeDtypeStruct((cells, 1, 2, antennas, users), BF16)] * 2,
+        scratch_shapes=[pltpu.SemaphoreType.DMA((cells, 2))],
+        compiler_params=pltpu.CompilerParams(vmem_limit_bytes=VMEM_LIMIT),
+        cost_estimate=pl.CostEstimate(flops=0, bytes_accessed=cells * 16 * antennas * users, transcendentals=0),
+    )(channel, after)
 
 
 def edge_scratch(counts, symbols, antennas, users):
@@ -244,7 +257,7 @@
     )(counts, channel, received, low, high)
 
 
-def conjugate_gradient(sums, noise, users):
+def conjugate_gradient(sums, noises, users):
     row = lax.broadcasted_iota(jnp.int32, (users, users), 0)
     col = lax.broadcasted_iota(jnp.int32, (users, users), 1)
     upper = row <= col
@@ -256,7 +269,7 @@
         imag = jnp.where(row == col, jnp.zeros_like(packed), jnp.where(upper, -turned, packed))
         grams.append(jnp.concatenate([real, imag], axis=1))
 
-    def apply(matrix, vector):
+    def apply(matrix, vector, noise):
         product = jnp.dot(vector.astype(BF16), matrix, preferred_element_type=F32)
         return cross(product, users) + noise * vector
 
@@ -268,44 +281,36 @@
 
     direction = [value[users:] for value in sums]
     norm = [user_sum(d, d) for d in direction]
-    image = [apply(g, d) for g, d in zip(grams, direction)]
+    image = [apply(*terms) for terms in zip(grams, direction, noises)]
     alpha = [n / user_sum(d, i) for n, d, i in zip(norm, direction, image)]
     estimate = [a * d for a, d in zip(alpha, direction)]
     residual = [d - a * i for d, a, i in zip(direction, alpha, image)]
     norm_next = [user_sum(r, r) for r in residual]
     direction = [r + (m / n) * d for r, m, n, d in zip(residual, norm_next, norm, direction)]
-    image = [apply(g, d) for g, d in zip(grams, direction)]
+    image = [apply(*terms) for terms in zip(grams, direction, noises)]
     alpha = [n / user_sum(d, i) for n, d, i in zip(norm_next, direction, image)]
     return [e + a * d for e, a, d in zip(estimate, alpha, direction)]
 
 
-def inner_detect(counts, noise_power, own, peers, channel, received, low, high):
+def detect_first(counts, noise_power, own, peer, channel, received, low, high):
     cells, inner, rows, users = own.shape
     antennas, symbols = channel.shape[3], received.shape[2]
-    half = inner + 1
-
-    def kernel(noise_ref, counts_hbm, chan, samp, low_ref, high_ref, own_ref, *refs):
+    half, number = inner + 1, peer.shape[1]
+
+    def kernel(noise_ref, counts_hbm, chan, samp, low_ref, high_ref, own_ref, peer_ref, out, edge_out, *scratch):
         panel = lax.axis_index("panel")
-        peer_refs, (out, edge_out), scratch = refs[: len(peers)], refs[len(peers) : len(peers) + 2], refs[len(peers) + 2 :]
         fetch, work = edge_work(panel, counts_hbm, chan, samp, low_ref, high_ref, edge_out, scratch)
         fetch()
-        shift = 1 - panel
-
-        def step(c, carry):
-            sums = []
-            for peer_ref in peer_refs:
-                for i in range(peer_ref.shape[1]):
-                    sums.append(own_ref[c, len(sums)] + peer_ref[c, i].astype(F32))
-            for i, value in enumerate(conjugate_gradient(sums, noise_ref[c], users)):
-                out[c, pl.ds(i + shift, 2 * SPAD, stride=half), :] = value
-            return carry
-
-        lax.fori_loop(0, cells, step, 0)
+        spots = [(c, i) for c in range(cells) for i in range(number)]
+        sums = [own_ref[c, i] + peer_ref[c, i].astype(F32) for c, i in spots]
+        values = conjugate_gradient(sums, [noise_ref[c] for c, _ in spots], users)
+        for (c, i), value in zip(spots, values):
+            out[c, pl.ds(i + 1 - panel, 2 * SPAD, stride=half), :] = value
         work()
 
     return pl.pallas_call(
         kernel,
-        in_specs=[SMEM_SPEC] + [HBM_SPEC] * 5 + [VMEM_SPEC] * (1 + len(peers)),
+        in_specs=[SMEM_SPEC] + [HBM_SPEC] * 5 + [VMEM_SPEC] * 2,
         out_specs=[VMEM_SPEC, VMEM_SPEC],
         out_shape=[
             jax.ShapeDtypeStruct((cells, 2 * SPAD * half, users), F32),
@@ -314,29 +319,35 @@
         scratch_shapes=edge_scratch(counts, symbols, antennas, users),
         compiler_params=pltpu.CompilerParams(vmem_limit_bytes=VMEM_LIMIT),
         cost_estimate=pl.CostEstimate(
-            flops=cells * inner * 2 * 2 * 2 * SPAD * users * 2 * users,
+            flops=cells * number * 2 * 2 * 2 * SPAD * users * 2 * users,
             bytes_accessed=cells * inner * rows * users * 6,
             transcendentals=0,
         ),
-    )(noise_power, counts, channel, received, low, high, own, *peers)
-
-
-def edge_detect(noise_power, own, peer, inner, onehot, symbols, rounds):
-    cells, rows, users = own.shape
-    half = inner.shape[1] // (2 * SPAD)
+    )(noise_power, counts, channel, received, low, high, own, peer)
+
+
+def detect_last(noise_power, own, peer, edge_own, edge_peer, state, onehot, symbols, rounds):
+    cells, inner, rows, users = own.shape
+    half, number = inner + 1, peer.shape[1]
     width = onehot.shape[1] // (2 * rounds)
     keep = symbols * half
 
-    def kernel(noise_ref, own_ref, peer_ref, inner_ref, hot_ref, *refs):
-        *outs, state = refs
-        state[...] = inner_ref[...]
-        spot = lax.axis_index("panel") * (half - 1)
-        for c in range(cells):
-            (value,) = conjugate_gradient([own_ref[c] + peer_ref[c].astype(F32)], noise_ref[c], users)
-            state[c, pl.ds(spot, 2 * SPAD, stride=half), :] = value
-        values = state[...].astype(BF16)
+    def kernel(noise_ref, own_ref, peer_ref, edge_own_ref, edge_peer_ref, hot_ref, state_ref, *refs):
+        *outs, full = refs
+        panel = lax.axis_index("panel")
+        full[...] = state_ref[...]
+        first = inner - number
+        spots = [(c, i) for c in range(cells) for i in range(number)]
+        sums = [own_ref[c, first + i] + peer_ref[c, i].astype(F32) for c, i in spots]
+        places = [(c, first + i + 1 - panel) for c, i in spots]
+        sums += [edge_own_ref[c] + edge_peer_ref[c].astype(F32) for c in range(cells)]
+        places += [(c, panel * (half - 1)) for c in range(cells)]
+        values = conjugate_gradient(sums, [noise_ref[c] for c, _ in places], users)
+        for (c, place), value in zip(places, values):
+            full[c, pl.ds(place, 2 * SPAD, stride=half), :] = value
+        found = full[...].astype(BF16)
         blocks = [
-            jnp.concatenate([values[c, (2 * s + k) * half : (2 * s + k + 1) * half] for s in range(symbols)], axis=0)
+            jnp.concatenate([found[c, (2 * s + k) * half : (2 * s + k + 1) * half] for s in range(symbols)], axis=0)
             for k in range(2)
             for c in range(cells)
         ]
@@ -344,34 +355,33 @@
         placed = jnp.dot(lhs, hot_ref[...], preferred_element_type=F32).astype(BF16)
         for i, out in enumerate(outs):
             for side in range(2):
-                first = (2 * i + side) * width
-                out[side * keep : (side + 1) * keep, :] = placed[:, first : first + width]
-
-    return pl.pallas_call(
-        kernel,
-        in_specs=[SMEM_SPEC] + [VMEM_SPEC] * 4,
+                start = (2 * i + side) * width
+                out[side * keep : (side + 1) * keep, :] = placed[:, start : start + width]
+
+    return pl.pallas_call(
+        kernel,
+        in_specs=[SMEM_SPEC] + [VMEM_SPEC] * 6,
         out_specs=[VMEM_SPEC] * rounds,
         out_shape=[jax.ShapeDtypeStruct((2 * keep, width), BF16)] * rounds,
-        scratch_shapes=[pltpu.VMEM(inner.shape, F32)],
+        scratch_shapes=[pltpu.VMEM(state.shape, F32)],
         compiler_params=pltpu.CompilerParams(vmem_limit_bytes=VMEM_LIMIT),
         cost_estimate=pl.CostEstimate(
-            flops=2 * keep * onehot.shape[0] * onehot.shape[1], bytes_accessed=4 * inner.size, transcendentals=0
+            flops=2 * keep * onehot.shape[0] * onehot.shape[1], bytes_accessed=4 * state.size, transcendentals=0
         ),
-    )(noise_power, own, peer, inner, onehot)
+    )(noise_power, own, peer, edge_own, edge_peer, onehot, state)
 
 
 def assemble(sources, mine, theirs, others, cells, per_device, symbols, half):
     rounds = sum(group.shape[0] for group in mine)
     total = 2 * rounds * 2 * half
     lanes = mine[0].shape[2]
-    slots = cells * per_device
     keep = symbols * half
     number = len(mine)
 
     def kernel(source_ref, *refs):
         mine_refs, theirs_refs = refs[:number], refs[number : 2 * number]
         own_other, peer_others = refs[2 * number], refs[2 * number + 1 : 3 * number + 1]
-        out, gathered, turned = refs[3 * number + 1 :]
+        out, gathered = refs[3 * number + 1 :]
         panel = lax.axis_index("panel")
 
         def place(ref, i, first, source, side):
@@ -392,27 +402,14 @@
                     place(ref, i, 0, source_ref[n], side)
                     n += 1
         for s in range(symbols):
-            value = gathered[s].T.astype(F32)
-            for k in range(2):
-                for part in range(total // 128):
-                    piece = value[k * slots : (k + 1) * slots, part * 128 : (part + 1) * 128]
-                    turned[part, pl.ds(2 * s + k, slots, stride=2 * SPAD), :] = piece
-        for slot in range(slots):
-            for part in range(total // 128):
-                value = turned[part, slot * 2 * SPAD : (slot + 1) * 2 * SPAD, :].astype(BF16)
-                out[slot // per_device, slot % per_device, :, :, part * 128 : (part + 1) * 128] = value[
-                    : 2 * symbols
-                ].reshape(symbols, 2, 128)
+            out[:, :, s] = gathered[s].T.reshape(cells, per_device, 2, total)
 
     return pl.pallas_call(
         kernel,
         in_specs=[SMEM_SPEC] + [VMEM_SPEC] * (3 * number + 1),
         out_specs=VMEM_SPEC,
         out_shape=jax.ShapeDtypeStruct((cells, per_device, symbols, 2, total), BF16),
-        scratch_shapes=[
-            pltpu.VMEM((symbols, total, lanes), BF16),
-            pltpu.VMEM((total // 128, slots * 2 * SPAD, 128), F32),
-        ],
+        scratch_shapes=[pltpu.VMEM((symbols, total, lanes), BF16)],
         compiler_params=pltpu.CompilerParams(vmem_limit_bytes=VMEM_LIMIT),
     )(sources, *mine, *theirs, *others)
 
@@ -427,17 +424,18 @@
     samples = jnp.transpose(received, (0, 1, 3, 2, 4))
 
     inner = half - 1
-    count = inner // 2
-    outgoing, bottom, top = inner_gram(user_count, channel, samples, True, 0, count, BF16, halo=True)
-    peers = [lax.ppermute(outgoing, "panel", SWAP)]
+    count = inner * 2 // 5
+    first = inner_gram(user_count, channel, samples, True, 0, count, BF16, limit=56 << 20)
+    first_peer = lax.ppermute(first, "panel", SWAP)
+    bottom, top = band_ends(channel, first)
     low = lax.ppermute(top, "sc", [(i, i + 1) for i in range(n_sc - 1)])
     high = lax.ppermute(bottom, "sc", [(i + 1, i) for i in range(n_sc - 1)])
-    (outgoing,) = inner_gram(user_count, channel, samples, True, count, inner - count, BF16)
-    peers.append(lax.ppermute(outgoing, "panel", SWAP))
-    (own,) = inner_gram(user_count, channel, samples, False, 0, inner, F32)
+    second = inner_gram(user_count, channel, samples, True, count, inner - count, BF16)
+    second_peer = lax.ppermute(second, "panel", SWAP)
+    own = inner_gram(user_count, channel, samples, False, 0, inner, F32)
     low, high, own = lax.optimization_barrier((low, high, own))
     edge_peer = lax.ppermute(edge_gram(user_count, channel, samples, low, high), "panel", SWAP)
-    inner, edge_own = inner_detect(user_count, noise_power, own, peers, channel, samples, low, high)
+    state, edge_own = detect_first(user_count, noise_power, own, first_peer, channel, samples, low, high)
 
     capacity = cells * users // n_cell
     per_device = n_cell * capacity // n_sc
@@ -447,12 +445,12 @@
     earlier = (keys[:, None] == keys[None, :]) & (position[None, :] < position[:, None])
     rank = jnp.sum(earlier.astype(jnp.int32), axis=1)
     turn = (rank // per_device - sc % reach) % reach * 2 + (keys // cells == sc // reach).astype(jnp.int32)
-    column = (turn * 2 * cells + keys % cells) * per_device + rank % per_device
-    column = jnp.concatenate([column, column + cells * per_device])
+    column = ((turn * cells + keys % cells) * per_device + rank % per_device) * 2
+    column = jnp.concatenate([column, column + 1])
     width = 2 * cells * per_device
     onehot = (column[:, None] == lax.iota(jnp.int32, 2 * reach * width)[None, :]).astype(BF16)
 
-    messages = edge_detect(noise_power, edge_own, edge_peer, inner, onehot, symbols, reach)
+    messages = detect_last(noise_power, own, second_peer, edge_own, edge_peer, state, onehot, symbols, reach)
     arrived = []
     for b in range(reach):
         pairs = [

time: 77.5 us -> 73.1 us (0.943)
  waiting for transfers between devices: 13.4 us -> 10.6 us
  local copies, waits for them, and re-layouts: 2.24 us -> 1.12 us
  starting transfers between devices: 28.7 us -> 27.8 us
    ppermute x2, waiting for transfers between devices: 4.55 us -> 0.01 us  [the longest x1 0.01 us: body(): second_peer = lax.ppermute(second, 'panel', SWAP)]
    pallas_call x5 -> x6, Pallas kernels: 26 us -> 28.6 us  [the longest x3 21.2 us: inner_gram(): pl.pallas_call(kernel, in_specs=[HBM_SPEC] * 3, out_specs=VMEM_SPEC, out_...]
    pallas_call x1, Pallas kernels: 4.04 us -> 1.88 us  [assemble(): pl.pallas_call(kernel, in_specs=[SMEM_SPEC] + [VMEM_SPEC] * (3 * number +...]
    ppermute x2, starting transfers between devices: 3.13 us -> 1.58 us  [body(): theirs = [lax.ppermute(group, 'panel', SWAP) for group in mine]]
    ppermute x2, starting transfers between devices: 2.16 us -> 3.61 us  [the longest x1 3 us: body(): first_peer = lax.ppermute(first, 'panel', SWAP)]
    ppermute x1, starting transfers between devices: 4.9 us -> 3.46 us  [body(): low = lax.ppermute(top, 'sc', [(i, i + 1) for i in range(n_sc - 1)])]
    unnamed x12 -> x10, local copies, waits for them, and re-layouts: 2.2 us -> 1.09 us
    ppermute x1, waiting for transfers between devices: 0.01 us -> 1.01 us  [body(): lax.ppermute(edge_gram(user_count, channel, samples, low, high), 'panel',...]
  transfers between devices with their start and end apart: 14 -> 14, of which waited for: 6 -> 5; matrix products, arithmetic and copies ran while one was open for 1% -> 1% of each run, Pallas kernels for 27% -> 30%
where the time goes in v5:
time: 73.1 us; the launch traced here: 72.7 us
  Pallas kernels  32.4 us (44%)
  starting transfers between devices  27.8 us (38%)
  waiting for transfers between devices  10.6 us (15%)
  local copies, waits for them, and re-layouts  1.12 us (2%)
    pallas_call x3, Pallas kernels, inner_gram(): pl.pallas_call(kernel, in_specs=[HBM_SPEC] * 3, out_specs=VMEM_SPEC, out_...  21.2 us
    ppermute x4, starting transfers between devices, body(): arrived.append(lax.ppermute(messages[b], ('cell', 'sc'), pairs))  7.04 us
    ppermute x1, starting transfers between devices, body(): lax.ppermute(jnp.stack([block[:keep] for block in arrived]), 'cell', SWAP)  5.47 us
    ppermute x1, waiting for transfers between devices, body(): low = lax.ppermute(top, 'sc', [(i, i + 1) for i in range(n_sc - 1)])  4.95 us
    ppermute x2, starting transfers between devices, body(): others += [lax.ppermute(group[:, :keep], 'cell', SWAP) for group in theirs]  4.58 us
    ppermute x4, waiting for transfers between devices, body(): arrived.append(lax.ppermute(messages[b], ('cell', 'sc'), pairs))  3.75 us
    ppermute x1, starting transfers between devices, body(): low = lax.ppermute(top, 'sc', [(i, i + 1) for i in range(n_sc - 1)])  3.46 us
    ppermute x1, starting transfers between devices, body(): first_peer = lax.ppermute(first, 'panel', SWAP)  3 us
  transfers between devices with their start and end apart: 14, of which 5 were waited for; matrix products, arithmetic and copies ran while one was open for 1% of the time, Pallas kernels for 30%

profile of v5, /device:TPU:0, one launch (start us, length us, event | category | flops | bytes accessed | tf_op | source)
XLA Modules:
  0.0 72.7 jit_solution(5410521099022992407)
XLA Ops:
  0.0 5.9 %shard_map.55.after_ref = bf16[2,6,160,128]{3,2,1,0:T(8,128)(2,1)} custom-call(s32[2,2]{1,0:T(2,128)} %counts_hbm.9, bf16[2,32,2,512,128]{4,3,2,1,0:T(8,128)(2,1)} %chan.11, bf16[2,32,14,2,512]{4,3,2,1,0:T(2,128)(2,1)} %bitcast.15), custom_call_target="tpu_custom_call" | custom-call | flops 905969664 | bytes 4194304 | tf_op jit(solution)/shard_map/pallas_call | solution.py:128
  6.0 3.0 %collective-permute-start.3 = (bf16[2,6,160,128]{3,2,1,0:T(8,128)(2,1)}, bf16[2,6,160,128]{3,2,1,0:T(8,128)(2,1)S(1)}, u32[]{:S(2)}, u32[]{:S(2)}) collective-permute-start(bf16[2,6,160,128]{3,2,1,0:T(8,128)(2,1)} %shard_map.55.after_ref), channel_id=1, source_target_pairs={{0,8},{8,0},{1,9},{9,1},{2,10},{10,2},{3,11},{11,3},{4,12},{12,4},... | collective-permute-start | bytes 1474568 | tf_op jit(solution)/shard_map/ppermute | solution.py:429
  9.0 1.1 %copy-done.1 = bf16[2,6,160,128]{3,2,1,0:T(8,128)(2,1)S(1)} copy-done((bf16[2,6,160,128]{3,2,1,0:T(8,128)(2,1)S(1)}, bf16[2,6,160,128]{3,2,1,0:T(8,128)(2,1)}, u32[]{:S(2)}) %copy-start.1) | copy-done | bytes 491544
  10.0 2.3 %shard_map.56 = (bf16[2,1,2,512,128]{4,3,2,1,0:T(8,128)(2,1)}, bf16[2,1,2,512,128]{4,3,2,1,0:T(8,128)(2,1)}) custom-call(bf16[2,32,2,512,128]{4,3,2,1,0:T(8,128)(2,1)} %chan.11, bf16[2,6,160,128]{3,2,1,0:T(8,128)(2,1)S(1)} %copy-done.1), custom_call_target="tpu_custom_call" | custom-call | bytes 2097152 | tf_op jit(solution)/shard_map/pallas_call | solution.py:167
  12.3 3.5 %collective-permute-start = (bf16[2,1,2,512,128]{4,3,2,1,0:T(8,128)(2,1)}, bf16[2,1,2,512,128]{4,3,2,1,0:T(8,128)(2,1)S(1)}, u32[]{:S(2)}, u32[]{:S(2)}) collective-permute-start(bf16[2,1,2,512,128]{4,3,2,1,0:T(8,128)(2,1)} %get-tuple-element.16), channel_id=1, source_target_pairs={{0,1},{1,2},{2,3},{3,4},{4,5},{5,6},{6,7},{8,9},{9,10},{10,11},{11... | collective-permute-start | bytes 1572872 | tf_op jit(solution)/shard_map/ppermute | solution.py:431
  15.8 1.3 %collective-permute-start.1 = (bf16[2,1,2,512,128]{4,3,2,1,0:T(8,128)(2,1)}, bf16[2,1,2,512,128]{4,3,2,1,0:T(8,128)(2,1)S(1)}, u32[]{:S(2)}, u32[]{:S(2)}) collective-permute-start(bf16[2,1,2,512,128]{4,3,2,1,0:T(8,128)(2,1)} %get-tuple-element.17), channel_id=1, source_target_pairs={{1,0},{2,1},{3,2},{4,3},{5,4},{6,5},{7,6},{9,8},{10,9},{11,10},{12... | collective-permute-start | bytes 1572872 | tf_op jit(solution)/shard_map/ppermute | solution.py:432
  17.1 6.6 %shard_map.58 = bf16[2,9,160,128]{3,2,1,0:T(8,128)(2,1)} custom-call(s32[2,2]{1,0:T(2,128)S(1)} %copy-done.2, bf16[2,32,2,512,128]{4,3,2,1,0:T(8,128)(2,1)} %chan.11, bf16[2,32,14,2,512]{4,3,2,1,0:T(2,128)(2,1)S(1)} %bitcast.16), custom_call_target="tpu_custom_call" | custom-call | flops 1358954496 | bytes 5767168 | tf_op jit(solution)/shard_map/pallas_call | solution.py:128
  24.6 8.6 %shard_map.57.own_ref = f32[2,15,160,128]{3,2,1,0:T(8,128)S(1)} custom-call(s32[2,2]{1,0:T(2,128)S(1)} %copy-done.2, bf16[2,32,2,512,128]{4,3,2,1,0:T(8,128)(2,1)} %chan.11, bf16[2,32,14,2,512]{4,3,2,1,0:T(2,128)(2,1)S(1)} %bitcast.17), custom_call_target="tpu_custom_call" | custom-call | flops 2264924160 | bytes 8912896 | tf_op jit(solution)/shard_map/pallas_call | solution.py:128
  33.2 4.9 %collective-permute-done.low_ref = bf16[2,1,2,512,128]{4,3,2,1,0:T(8,128)(2,1)S(1)} collective-permute-done((bf16[2,1,2,512,128]{4,3,2,1,0:T(8,128)(2,1)}, bf16[2,1,2,512,128]{4,3,2,1,0:T(8,128)(2,1)S(1)}, u32[]{:S(2)}, u32[]{:S(2)}) %collective-permute-start) | collective-permute-done | bytes 524320 | tf_op jit(solution)/shard_map/ppermute | solution.py:431
  38.2 1.9 %shard_map.60 = bf16[2,160,128]{2,1,0:T(8,128)(2,1)S(1)} custom-call(s32[2,2]{1,0:T(2,128)S(1)} %copy-done.2, bf16[2,32,2,512,128]{4,3,2,1,0:T(8,128)(2,1)} %chan.11, bf16[2,32,14,2,512]{4,3,2,1,0:T(2,128)(2,1)S(1)} %bitcast.18, bf16[2,1,2,512,128]{4,3,2,1,0:T(8,128)(2,1)S(1)} %collective-permute-done.low_ref, ...), custom_call_target="tpu_custom_call" | custom-call | flops 150994944 | bytes 1572864 | tf_op jit(solution)/shard_map/pallas_call | solution.py:245
  41.1 2.5 %shard_map.59 = (f32[2,512,128]{2,1,0:T(8,128)S(1)}, f32[2,160,128]{2,1,0:T(8,128)S(1)}) custom-call(f32[2]{0:T(128)S(1)} %copy-done.3, s32[2,2]{1,0:T(2,128)S(1)} %copy-done.2, bf16[2,32,2,512,128]{4,3,2,1,0:T(8,128)(2,1)} %chan.11, bf16[2,32,14,2,512]{4,3,2,1,0:T(2,128)(2,1)S(1)} %bitcast.19, ...), custom_call_target="tpu_custom_call" | custom-call | flops 50331648 | bytes 3686400 | tf_op jit(solution)/shard_map/pallas_call | solution.py:311
  43.6 1.0 %collective-permute-done.4.edge_peer_ref = bf16[2,160,128]{2,1,0:T(8,128)(2,1)S(1)} collective-permute-done((bf16[2,160,128]{2,1,0:T(8,128)(2,1)S(1)}, bf16[2,160,128]{2,1,0:T(8,128)(2,1)S(1)}, u32[]{:S(2)}, u32[]{:S(2)}) %collective-permute-start.4) | collective-permute-done | bytes 81952 | tf_op jit(solution)/shard_map/ppermute | solution.py:437
  44.6 2.7 %shard_map.61 = (bf16[448,128]{1,0:T(8,128)(2,1)S(1)}, bf16[448,128]{1,0:T(8,128)(2,1)S(1)}, bf16[448,128]{1,0:T(8,128)(2,1)S(1)}, bf16[448,128]{1,0:T(8,128)(2,1)S(1)}) custom-call(f32[2]{0:T(128)S(1)} %copy-done.3, f32[2,15,160,128]{3,2,1,0:T(8,128)S(1)} %shard_map.57.own_ref, bf16[2,9,160,128]{3,2,1,0:T(8,128)(2,1)} %collective-permute-done.2.peer_ref, ...), custom_call_target="tpu_custom_call" | custom-call | flops 234881024 | bytes 524288 | tf_op jit(solution)/shard_map/pallas_call | solution.py:361
  47.3 2.4 %collective-permute-start.6 = (bf16[448,128]{1,0:T(8,128)(2,1)S(1)}, bf16[448,128]{1,0:T(8,128)(2,1)S(1)}, u32[]{:S(2)}, u32[]{:S(2)}) collective-permute-start(bf16[448,128]{1,0:T(8,128)(2,1)S(1)} %get-tuple-element.24), channel_id=1, source_target_pairs={{0,1},{1,2},{2,3},{3,0},{4,17},{5,18},{6,19},{7,16},{16,5},{17,6},... | collective-permute-start | bytes 344072 | tf_op jit(solution)/shard_map/ppermute | solution.py:461
  50.4 1.1 %collective-permute-start.8 = (bf16[448,128]{1,0:T(8,128)(2,1)S(1)}, bf16[448,128]{1,0:T(8,128)(2,1)S(1)}, u32[]{:S(2)}, u32[]{:S(2)}) collective-permute-start(bf16[448,128]{1,0:T(8,128)(2,1)S(1)} %get-tuple-element.26), channel_id=1, source_target_pairs={{0,3},{1,0},{2,1},{3,2},{4,19},{5,16},{6,17},{7,18},{16,7},{17,4},... | collective-permute-start | bytes 344072 | tf_op jit(solution)/shard_map/ppermute | solution.py:461
  51.4 2.9 %collective-permute-start.7 = (bf16[448,128]{1,0:T(8,128)(2,1)S(1)}, bf16[448,128]{1,0:T(8,128)(2,1)S(1)}, u32[]{:S(2)}, u32[]{:S(2)}) collective-permute-start(bf16[448,128]{1,0:T(8,128)(2,1)S(1)} %get-tuple-element.25), channel_id=1, source_target_pairs={{0,2},{1,3},{2,0},{3,1},{4,18},{5,19},{6,16},{7,17},{16,6},{17,7},... | collective-permute-start | bytes 344072 | tf_op jit(solution)/shard_map/ppermute | solution.py:461
  54.3 0.8 %collective-permute-start.9 = (bf16[2,448,128]{2,1,0:T(8,128)(2,1)S(1)}, bf16[2,448,128]{2,1,0:T(8,128)(2,1)S(1)}, u32[]{:S(2)}, u32[]{:S(2)}) collective-permute-start(bf16[2,448,128]{2,1,0:T(8,128)(2,1)S(1)} %pad_maximum_fusion.refs_0_), channel_id=1, source_target_pairs={{0,8},{8,0},{1,9},{9,1},{2,10},{10,2},{3,11},{11,3},{4,12},{12,4},... | collective-permute-start | bytes 688136 | tf_op jit(solution)/shard_map/ppermute | solution.py:466
  55.2 0.8 %collective-permute-done.8 = bf16[448,128]{1,0:T(8,128)(2,1)S(1)} collective-permute-done((bf16[448,128]{1,0:T(8,128)(2,1)S(1)}, bf16[448,128]{1,0:T(8,128)(2,1)S(1)}, u32[]{:S(2)}, u32[]{:S(2)}) %collective-permute-start.8) | collective-permute-done | bytes 114720 | tf_op jit(solution)/shard_map/ppermute | solution.py:461
  56.0 2.9 %collective-permute-done.7 = bf16[448,128]{1,0:T(8,128)(2,1)S(1)} collective-permute-done((bf16[448,128]{1,0:T(8,128)(2,1)S(1)}, bf16[448,128]{1,0:T(8,128)(2,1)S(1)}, u32[]{:S(2)}, u32[]{:S(2)}) %collective-permute-start.7) | collective-permute-done | bytes 114720 | tf_op jit(solution)/shard_map/ppermute | solution.py:461
  59.8 5.5 %collective-permute-start.11 = (bf16[4,224,128]{2,1,0:T(8,128)(2,1)S(1)}, bf16[4,224,128]{2,1,0:T(8,128)(2,1)S(1)}, u32[]{:S(2)}, u32[]{:S(2)}) collective-permute-start(bf16[4,224,128]{2,1,0:T(8,128)(2,1)S(1)} %pad_maximum_fusion.2), channel_id=1, source_target_pairs={{0,16},{16,0},{1,17},{17,1},{2,18},{18,2},{3,19},{19,3},{4,20},{20... | collective-permute-start | bytes 688136 | tf_op jit(solution)/shard_map/ppermute | solution.py:467
  65.3 2.3 %collective-permute-start.12 = (bf16[2,224,128]{2,1,0:T(8,128)(2,1)S(1)}, bf16[2,224,128]{2,1,0:T(8,128)(2,1)S(1)}, u32[]{:S(2)}, u32[]{:S(2)}) collective-permute-start(bf16[2,224,128]{2,1,0:T(8,128)(2,1)S(1)} %slice.28), channel_id=1, source_target_pairs={{0,16},{16,0},{1,17},{17,1},{2,18},{18,2},{3,19},{19,3},{4,20},{20... | collective-permute-start | bytes 344072 | tf_op jit(solution)/shard_map/ppermute | solution.py:468
  67.6 2.3 %collective-permute-start.13 = (bf16[2,224,128]{2,1,0:T(8,128)(2,1)S(1)}, bf16[2,224,128]{2,1,0:T(8,128)(2,1)S(1)}, u32[]{:S(2)}, u32[]{:S(2)}) collective-permute-start(bf16[2,224,128]{2,1,0:T(8,128)(2,1)S(1)} %slice.29), channel_id=1, source_target_pairs={{0,16},{16,0},{1,17},{17,1},{2,18},{18,2},{3,19},{19,3},{4,20},{20... | collective-permute-start | bytes 344072 | tf_op jit(solution)/shard_map/ppermute | solution.py:468
  70.0 0.9 %collective-permute-done.13.refs_6_ = bf16[2,224,128]{2,1,0:T(8,128)(2,1)S(1)} collective-permute-done((bf16[2,224,128]{2,1,0:T(8,128)(2,1)S(1)}, bf16[2,224,128]{2,1,0:T(8,128)(2,1)S(1)}, u32[]{:S(2)}, u32[]{:S(2)}) %collective-permute-start.13) | collective-permute-done | bytes 114720 | tf_op jit(solution)/shard_map/ppermute | solution.py:468
  70.8 1.9 %shard_map.62 = bf16[2,32,14,2,256]{4,3,2,1,0:T(2,128)(2,1)} custom-call(s32[8]{0:T(128)S(1)} %pad_add_fusion.1.source_ref, bf16[2,448,128]{2,1,0:T(8,128)(2,1)S(1)} %pad_maximum_fusion.refs_0_, bf16[2,448,128]{2,1,0:T(8,128)(2,1)S(1)} %pad_maximum_fusion.1.refs_1_, bf16[2,448,128]{2,1,0:T(8,128)(2,1)S(1)} %collective-permute-done.9.refs_2_, ...), custom_call_target="tpu_custom_call" | custom-call | tf_op jit(solution)/shard_map/pallas_call | solution.py:407
  (37 shorter events, 3.4 us)
Async XLA Ops:
  5.9 11.1 %copy-start = (bf16[2,32,2,14,512]{4,2,3,1,0:T(2,128)(2,1)S(1)}, bf16[2,32,2,14,512]{4,2,3,1,0:T(2,128)(2,1)}, u32[]{:S(2)}) copy-start(bf16[2,32,2,14,512]{4,2,3,1,0:T(2,128)(2,1)} %param.6) | copy-start | bytes 5505028
  6.0 35.1 %collective-permute-start.3 = (bf16[2,6,160,128]{3,2,1,0:T(8,128)(2,1)}, bf16[2,6,160,128]{3,2,1,0:T(8,128)(2,1)S(1)}, u32[]{:S(2)}, u32[]{:S(2)}) collective-permute-start(bf16[2,6,160,128]{3,2,1,0:T(8,128)(2,1)} %shard_map.55.after_ref), channel_id=1, source_target_pairs={{0,8},{8,0},{1,9},{9,1},{2,10},{10,2},{3,11},{11,3},{4,12},{12,4},... | collective-permute-start | bytes 1474568 | tf_op jit(solution)/shard_map/ppermute | solution.py:429
  9.0 1.1 %copy-start.1 = (bf16[2,6,160,128]{3,2,1,0:T(8,128)(2,1)S(1)}, bf16[2,6,160,128]{3,2,1,0:T(8,128)(2,1)}, u32[]{:S(2)}) copy-start(bf16[2,6,160,128]{3,2,1,0:T(8,128)(2,1)} %shard_map.55.after_ref) | copy-start | bytes 1474564
  10.0 7.1 %copy-start.2 = (s32[2,2]{1,0:T(2,128)S(1)}, s32[2,2]{1,0:T(2,128)}, u32[]{:S(2)}) copy-start(s32[2,2]{1,0:T(2,128)} %counts_hbm.9) | copy-start | bytes 52
  12.3 25.9 %collective-permute-start = (bf16[2,1,2,512,128]{4,3,2,1,0:T(8,128)(2,1)}, bf16[2,1,2,512,128]{4,3,2,1,0:T(8,128)(2,1)S(1)}, u32[]{:S(2)}, u32[]{:S(2)}) collective-permute-start(bf16[2,1,2,512,128]{4,3,2,1,0:T(8,128)(2,1)} %get-tuple-element.16), channel_id=1, source_target_pairs={{0,1},{1,2},{2,3},{3,4},{4,5},{5,6},{6,7},{8,9},{9,10},{10,11},{11... | collective-permute-start | bytes 1572872 | tf_op jit(solution)/shard_map/ppermute | solution.py:431
  15.8 8.6 %copy-start.4 = (s32[2,128,1]{1,2,0:T(1,128)S(1)}, s32[2,128,1]{1,2,0:T(1,128)}, u32[]{:S(2)}) copy-start(s32[2,128,1]{1,2,0:T(1,128)} %param.9) | copy-start | bytes 3076
  15.8 22.4 %collective-permute-start.1 = (bf16[2,1,2,512,128]{4,3,2,1,0:T(8,128)(2,1)}, bf16[2,1,2,512,128]{4,3,2,1,0:T(8,128)(2,1)S(1)}, u32[]{:S(2)}, u32[]{:S(2)}) collective-permute-start(bf16[2,1,2,512,128]{4,3,2,1,0:T(8,128)(2,1)} %get-tuple-element.17), channel_id=1, source_target_pairs={{1,0},{2,1},{3,2},{4,3},{5,4},{6,5},{7,6},{9,8},{10,9},{11,10},{12... | collective-permute-start | bytes 1572872 | tf_op jit(solution)/shard_map/ppermute | solution.py:432
  23.7 20.8 %collective-permute-start.2 = (bf16[2,9,160,128]{3,2,1,0:T(8,128)(2,1)}, bf16[2,9,160,128]{3,2,1,0:T(8,128)(2,1)}, u32[]{:S(2)}, u32[]{:S(2)}) collective-permute-start(bf16[2,9,160,128]{3,2,1,0:T(8,128)(2,1)} %shard_map.58), channel_id=1, source_target_pairs={{0,8},{8,0},{1,9},{9,1},{2,10},{10,2},{3,11},{11,3},{4,12},{12,4},... | collective-permute-start | bytes 2211848 | tf_op jit(solution)/shard_map/ppermute | solution.py:434
  33.2 7.9 %copy-start.3 = (f32[2]{0:T(128)S(1)}, f32[2]{0:T(128)}, u32[]{:S(2)}) copy-start(f32[2]{0:T(128)} %noise_ref.3) | copy-start | bytes 28
  40.1 4.5 %collective-permute-start.4 = (bf16[2,160,128]{2,1,0:T(8,128)(2,1)S(1)}, bf16[2,160,128]{2,1,0:T(8,128)(2,1)S(1)}, u32[]{:S(2)}, u32[]{:S(2)}) collective-permute-start(bf16[2,160,128]{2,1,0:T(8,128)(2,1)S(1)} %shard_map.60), channel_id=1, source_target_pairs={{0,8},{8,0},{1,9},{9,1},{2,10},{10,2},{3,11},{11,3},{4,12},{12,4},... | collective-permute-start | bytes 245768 | tf_op jit(solution)/shard_map/ppermute | solution.py:437
  47.3 7.1 %collective-permute-start.6 = (bf16[448,128]{1,0:T(8,128)(2,1)S(1)}, bf16[448,128]{1,0:T(8,128)(2,1)S(1)}, u32[]{:S(2)}, u32[]{:S(2)}) collective-permute-start(bf16[448,128]{1,0:T(8,128)(2,1)S(1)} %get-tuple-element.24), channel_id=1, source_target_pairs={{0,1},{1,2},{2,3},{3,0},{4,17},{5,18},{6,19},{7,16},{16,5},{17,6},... | collective-permute-start | bytes 344072 | tf_op jit(solution)/shard_map/ppermute | solution.py:461
  49.7 4.6 %collective-permute-start.5 = (bf16[448,128]{1,0:T(8,128)(2,1)S(1)}, bf16[448,128]{1,0:T(8,128)(2,1)S(1)}, u32[]{:S(2)}, u32[]{:S(2)}) collective-permute-start(bf16[448,128]{1,0:T(8,128)(2,1)S(1)} %get-tuple-element.23), channel_id=1, source_target_pairs={{0,0},{1,1},{2,2},{3,3},{4,16},{5,17},{6,18},{7,19},{16,4},{17,5},... | collective-permute-start | bytes 344072 | tf_op jit(solution)/shard_map/ppermute | solution.py:461
  50.4 5.7 %collective-permute-start.8 = (bf16[448,128]{1,0:T(8,128)(2,1)S(1)}, bf16[448,128]{1,0:T(8,128)(2,1)S(1)}, u32[]{:S(2)}, u32[]{:S(2)}) collective-permute-start(bf16[448,128]{1,0:T(8,128)(2,1)S(1)} %get-tuple-element.26), channel_id=1, source_target_pairs={{0,3},{1,0},{2,1},{3,2},{4,19},{5,16},{6,17},{7,18},{16,7},{17,4},... | collective-permute-start | bytes 344072 | tf_op jit(solution)/shard_map/ppermute | solution.py:461
  51.4 7.5 %collective-permute-start.7 = (bf16[448,128]{1,0:T(8,128)(2,1)S(1)}, bf16[448,128]{1,0:T(8,128)(2,1)S(1)}, u32[]{:S(2)}, u32[]{:S(2)}) collective-permute-start(bf16[448,128]{1,0:T(8,128)(2,1)S(1)} %get-tuple-element.25), channel_id=1, source_target_pairs={{0,2},{1,3},{2,0},{3,1},{4,18},{5,19},{6,16},{7,17},{16,6},{17,7},... | collective-permute-start | bytes 344072 | tf_op jit(solution)/shard_map/ppermute | solution.py:461
  54.3 10.9 %collective-permute-start.9 = (bf16[2,448,128]{2,1,0:T(8,128)(2,1)S(1)}, bf16[2,448,128]{2,1,0:T(8,128)(2,1)S(1)}, u32[]{:S(2)}, u32[]{:S(2)}) collective-permute-start(bf16[2,448,128]{2,1,0:T(8,128)(2,1)S(1)} %pad_maximum_fusion.refs_0_), channel_id=1, source_target_pairs={{0,8},{8,0},{1,9},{9,1},{2,10},{10,2},{3,11},{11,3},{4,12},{12,4},... | collective-permute-start | bytes 688136 | tf_op jit(solution)/shard_map/ppermute | solution.py:466
  59.0 8.6 %collective-permute-start.10 = (bf16[2,448,128]{2,1,0:T(8,128)(2,1)S(1)}, bf16[2,448,128]{2,1,0:T(8,128)(2,1)S(1)}, u32[]{:S(2)}, u32[]{:S(2)}) collective-permute-start(bf16[2,448,128]{2,1,0:T(8,128)(2,1)S(1)} %pad_maximum_fusion.1.refs_1_), channel_id=1, source_target_pairs={{0,8},{8,0},{1,9},{9,1},{2,10},{10,2},{3,11},{11,3},{4,12},{12,4},... | collective-permute-start | bytes 688136 | tf_op jit(solution)/shard_map/ppermute | solution.py:466
  59.8 10.2 %collective-permute-start.11 = (bf16[4,224,128]{2,1,0:T(8,128)(2,1)S(1)}, bf16[4,224,128]{2,1,0:T(8,128)(2,1)S(1)}, u32[]{:S(2)}, u32[]{:S(2)}) collective-permute-start(bf16[4,224,128]{2,1,0:T(8,128)(2,1)S(1)} %pad_maximum_fusion.2), channel_id=1, source_target_pairs={{0,16},{16,0},{1,17},{17,1},{2,18},{18,2},{3,19},{19,3},{4,20},{20... | collective-permute-start | bytes 688136 | tf_op jit(solution)/shard_map/ppermute | solution.py:467
  65.3 4.7 %collective-permute-start.12 = (bf16[2,224,128]{2,1,0:T(8,128)(2,1)S(1)}, bf16[2,224,128]{2,1,0:T(8,128)(2,1)S(1)}, u32[]{:S(2)}, u32[]{:S(2)}) collective-permute-start(bf16[2,224,128]{2,1,0:T(8,128)(2,1)S(1)} %slice.28), channel_id=1, source_target_pairs={{0,16},{16,0},{1,17},{17,1},{2,18},{18,2},{3,19},{19,3},{4,20},{20... | collective-permute-start | bytes 344072 | tf_op jit(solution)/shard_map/ppermute | solution.py:468
  67.6 3.3 %collective-permute-start.13 = (bf16[2,224,128]{2,1,0:T(8,128)(2,1)S(1)}, bf16[2,224,128]{2,1,0:T(8,128)(2,1)S(1)}, u32[]{:S(2)}, u32[]{:S(2)}) collective-permute-start(bf16[2,224,128]{2,1,0:T(8,128)(2,1)S(1)} %slice.29), channel_id=1, source_target_pairs={{0,16},{16,0},{1,17},{17,1},{2,18},{18,2},{3,19},{19,3},{4,20},{20... | collective-permute-start | bytes 344072 | tf_op jit(solution)/shard_map/ppermute | solution.py:468

commit v6 on v5

--- a/solution.py
+++ b/solution.py
@@ -59,18 +59,24 @@
     ]
 
 
-def inner_gram(counts, channel, received, peer, first, number, dtype, limit=VMEM_LIMIT):
+def inner_gram(counts, channel, received, peer, firsts, number, dtype, limit=VMEM_LIMIT, ends=False):
     cells, band, _, antennas, users = channel.shape
     symbols = received.shape[2]
-    half = band // 2
     items = cells * number
 
-    def kernel(counts_hbm, chan, samp, out, count_ref, win, ybuf, mat_a, lhs_a, mat_b, lhs_b, wsem, ysem, csem):
+    def kernel(counts_hbm, chan, samp, out, *refs):
+        end_refs, refs = (refs[:2], refs[2:]) if ends else ((), refs)
+        count_ref, win, ybuf, mat_a, lhs_a, mat_b, lhs_b, wsem, ysem, csem, esem = refs
         count_copy = pltpu.make_async_copy(counts_hbm, count_ref, csem)
         count_copy.start()
         panel = lax.axis_index("panel")
         side = 1 - panel if peer else panel
-        start = 1 + side * (half - 1) + first
+        start = jnp.where(side == 0, firsts[0], firsts[1])
+        end_copies = [
+            pltpu.make_async_copy(chan.at[c, i * (band - 1)], end_ref.at[c, 0], esem.at[c, i])
+            for c in range(cells)
+            for i, end_ref in enumerate(end_refs)
+        ]
 
         def fetch(c, i):
             return pltpu.make_async_copy(chan.at[c, start - 1 + i], win.at[c, i], wsem.at[c, i])
@@ -83,6 +89,8 @@
                 fetch(c, i).start()
                 if i == min(2, number):
                     fetch_samples(c).start()
+        for copy in end_copies:
+            copy.start()
         lhs_a[...] = jnp.zeros_like(lhs_a)
         lhs_b[...] = jnp.zeros_like(lhs_b)
 
@@ -123,13 +131,16 @@
             return carry
 
         lax.fori_loop(0, (items + 1) // 2, step, 0)
+        for copy in end_copies:
+            copy.wait()
 
     rows = users + 2 * SPAD
     return pl.pallas_call(
         kernel,
         in_specs=[HBM_SPEC] * 3,
-        out_specs=VMEM_SPEC,
-        out_shape=jax.ShapeDtypeStruct((cells, number, rows, users), dtype),
+        out_specs=[VMEM_SPEC] * (1 + 2 * ends),
+        out_shape=[jax.ShapeDtypeStruct((cells, number, rows, users), dtype)]
+        + [jax.ShapeDtypeStruct((cells, 1, 2, antennas, users), BF16)] * (2 * ends),
         scratch_shapes=[
             pltpu.SMEM(counts.shape, jnp.int32),
             pltpu.VMEM((cells, number + 2, 2, antennas, users), BF16),
@@ -139,6 +150,7 @@
             pltpu.SemaphoreType.DMA((cells, number + 2)),
             pltpu.SemaphoreType.DMA((cells,)),
             pltpu.SemaphoreType.DMA,
+            pltpu.SemaphoreType.DMA((cells, 2)),
         ],
         compiler_params=pltpu.CompilerParams(vmem_limit_bytes=limit),
         cost_estimate=pl.CostEstimate(
@@ -149,30 +161,18 @@
     )(counts, channel, received)
 
 
-def band_ends(channel, after):
-    cells, band, _, antennas, users = channel.shape
-
-    def kernel(chan, after_ref, *refs):
-        *ends, sems = refs
-        copies = [
-            pltpu.make_async_copy(chan.at[c, i * (band - 1)], ends[i].at[c, 0], sems.at[c, i])
-            for c in range(cells)
-            for i in range(2)
-        ]
-        for copy in copies:
-            copy.start()
-        for copy in copies:
-            copy.wait()
+def hand_on(arrays):
+    def kernel(*refs):
+        refs[-1][0] = 0
 
     return pl.pallas_call(
         kernel,
-        in_specs=[HBM_SPEC] * 2,
-        out_specs=[VMEM_SPEC] * 2,
-        out_shape=[jax.ShapeDtypeStruct((cells, 1, 2, antennas, users), BF16)] * 2,
-        scratch_shapes=[pltpu.SemaphoreType.DMA((cells, 2))],
-        compiler_params=pltpu.CompilerParams(vmem_limit_bytes=VMEM_LIMIT),
-        cost_estimate=pl.CostEstimate(flops=0, bytes_accessed=cells * 16 * antennas * users, transcendentals=0),
-    )(channel, after)
+        in_specs=[HBM_SPEC] * len(arrays),
+        out_specs=[HBM_SPEC] * len(arrays),
+        out_shape=[jax.ShapeDtypeStruct(a.shape, a.dtype) for a in arrays],
+        scratch_shapes=[pltpu.SMEM((1,), jnp.int32)],
+        input_output_aliases={i: i for i in range(len(arrays))},
+    )(*arrays)
 
 
 def edge_scratch(counts, symbols, antennas, users):
@@ -233,12 +233,13 @@
     return fetch, work
 
 
-def edge_gram(counts, channel, received, low, high):
+def edge_gram(counts, channel, received, low, high, peer, dtype):
     cells, _, _, antennas, users = channel.shape
     symbols = received.shape[2]
 
     def kernel(counts_hbm, chan, samp, low_ref, high_ref, out, *scratch):
-        fetch, work = edge_work(1 - lax.axis_index("panel"), counts_hbm, chan, samp, low_ref, high_ref, out, scratch)
+        panel = lax.axis_index("panel")
+        fetch, work = edge_work(1 - panel if peer else panel, counts_hbm, chan, samp, low_ref, high_ref, out, scratch)
         fetch()
         work()
 
@@ -246,7 +247,7 @@
         kernel,
         in_specs=[HBM_SPEC] * 5,
         out_specs=VMEM_SPEC,
-        out_shape=jax.ShapeDtypeStruct((cells, users + 2 * SPAD, users), BF16),
+        out_shape=jax.ShapeDtypeStruct((cells, users + 2 * SPAD, users), dtype),
         scratch_shapes=edge_scratch(counts, symbols, antennas, users),
         compiler_params=pltpu.CompilerParams(vmem_limit_bytes=VMEM_LIMIT),
         cost_estimate=pl.CostEstimate(
@@ -292,66 +293,33 @@
     return [e + a * d for e, a, d in zip(estimate, alpha, direction)]
 
 
-def detect_first(counts, noise_power, own, peer, channel, received, low, high):
-    cells, inner, rows, users = own.shape
-    antennas, symbols = channel.shape[3], received.shape[2]
-    half, number = inner + 1, peer.shape[1]
-
-    def kernel(noise_ref, counts_hbm, chan, samp, low_ref, high_ref, own_ref, peer_ref, out, edge_out, *scratch):
-        panel = lax.axis_index("panel")
-        fetch, work = edge_work(panel, counts_hbm, chan, samp, low_ref, high_ref, edge_out, scratch)
-        fetch()
-        spots = [(c, i) for c in range(cells) for i in range(number)]
-        sums = [own_ref[c, i] + peer_ref[c, i].astype(F32) for c, i in spots]
-        values = conjugate_gradient(sums, [noise_ref[c] for c, _ in spots], users)
-        for (c, i), value in zip(spots, values):
-            out[c, pl.ds(i + 1 - panel, 2 * SPAD, stride=half), :] = value
-        work()
-
-    return pl.pallas_call(
-        kernel,
-        in_specs=[SMEM_SPEC] + [HBM_SPEC] * 5 + [VMEM_SPEC] * 2,
-        out_specs=[VMEM_SPEC, VMEM_SPEC],
-        out_shape=[
-            jax.ShapeDtypeStruct((cells, 2 * SPAD * half, users), F32),
-            jax.ShapeDtypeStruct((cells, rows, users), F32),
-        ],
-        scratch_shapes=edge_scratch(counts, symbols, antennas, users),
-        compiler_params=pltpu.CompilerParams(vmem_limit_bytes=VMEM_LIMIT),
-        cost_estimate=pl.CostEstimate(
-            flops=cells * number * 2 * 2 * 2 * SPAD * users * 2 * users,
-            bytes_accessed=cells * inner * rows * users * 6,
-            transcendentals=0,
-        ),
-    )(noise_power, counts, channel, received, low, high, own, peer)
-
-
-def detect_last(noise_power, own, peer, edge_own, edge_peer, state, onehot, symbols, rounds):
-    cells, inner, rows, users = own.shape
-    half, number = inner + 1, peer.shape[1]
+def detect(noise_power, own, own_firsts, peer, edges, onehot, symbols, rounds):
+    cells, _, rows, users = own.shape
+    number = peer.shape[1]
+    half = number + (len(edges) > 0)
     width = onehot.shape[1] // (2 * rounds)
     keep = symbols * half
 
-    def kernel(noise_ref, own_ref, peer_ref, edge_own_ref, edge_peer_ref, hot_ref, state_ref, *refs):
-        *outs, full = refs
+    def kernel(noise_ref, own_ref, peer_ref, hot_ref, *refs):
+        edge_refs, outs, full = refs[: len(edges)], refs[len(edges) : -1], refs[-1]
         panel = lax.axis_index("panel")
-        full[...] = state_ref[...]
-        first = inner - number
+        first = jnp.where(panel == 0, own_firsts[0], own_firsts[1])
         spots = [(c, i) for c in range(cells) for i in range(number)]
         sums = [own_ref[c, first + i] + peer_ref[c, i].astype(F32) for c, i in spots]
-        places = [(c, first + i + 1 - panel) for c, i in spots]
-        sums += [edge_own_ref[c] + edge_peer_ref[c].astype(F32) for c in range(cells)]
-        places += [(c, panel * (half - 1)) for c in range(cells)]
+        places = [(c, i + 1 - panel if edges else i) for c, i in spots]
+        if edges:
+            edge_own_ref, edge_peer_ref = edge_refs
+            sums += [edge_own_ref[c] + edge_peer_ref[c].astype(F32) for c in range(cells)]
+            places += [(c, panel * (half - 1)) for c in range(cells)]
         values = conjugate_gradient(sums, [noise_ref[c] for c, _ in places], users)
         for (c, place), value in zip(places, values):
             full[c, pl.ds(place, 2 * SPAD, stride=half), :] = value
-        found = full[...].astype(BF16)
         blocks = [
-            jnp.concatenate([found[c, (2 * s + k) * half : (2 * s + k + 1) * half] for s in range(symbols)], axis=0)
+            jnp.concatenate([full[c, (2 * s + k) * half : (2 * s + k + 1) * half] for s in range(symbols)], axis=0)
             for k in range(2)
             for c in range(cells)
         ]
-        lhs = jnp.concatenate(blocks, axis=1)
+        lhs = jnp.concatenate(blocks, axis=1).astype(BF16)
         placed = jnp.dot(lhs, hot_ref[...], preferred_element_type=F32).astype(BF16)
         for i, out in enumerate(outs):
             for side in range(2):
@@ -360,58 +328,48 @@
 
     return pl.pallas_call(
         kernel,
-        in_specs=[SMEM_SPEC] + [VMEM_SPEC] * 6,
+        in_specs=[SMEM_SPEC] + [VMEM_SPEC] * (3 + len(edges)),
         out_specs=[VMEM_SPEC] * rounds,
         out_shape=[jax.ShapeDtypeStruct((2 * keep, width), BF16)] * rounds,
-        scratch_shapes=[pltpu.VMEM(state.shape, F32)],
+        scratch_shapes=[pltpu.VMEM((cells, 2 * SPAD * half, users), F32)],
         compiler_params=pltpu.CompilerParams(vmem_limit_bytes=VMEM_LIMIT),
         cost_estimate=pl.CostEstimate(
-            flops=2 * keep * onehot.shape[0] * onehot.shape[1], bytes_accessed=4 * state.size, transcendentals=0
+            flops=2 * keep * onehot.shape[0] * onehot.shape[1], bytes_accessed=4 * own.size, transcendentals=0
         ),
-    )(noise_power, own, peer, edge_own, edge_peer, onehot, state)
-
-
-def assemble(sources, mine, theirs, others, cells, per_device, symbols, half):
-    rounds = sum(group.shape[0] for group in mine)
+    )(noise_power, own, peer, onehot, *edges)
+
+
+def assemble(sources, parts, cells, per_device, symbols, half):
+    rounds = parts[0][0].shape[0]
     total = 2 * rounds * 2 * half
-    lanes = mine[0].shape[2]
-    keep = symbols * half
-    number = len(mine)
+    lanes = parts[0][0].shape[2]
+    keep = symbols * half // 2
 
     def kernel(source_ref, *refs):
-        mine_refs, theirs_refs = refs[:number], refs[number : 2 * number]
-        own_other, peer_others = refs[2 * number], refs[2 * number + 1 : 3 * number + 1]
-        out, gathered = refs[3 * number + 1 :]
+        out, gathered = refs[4 * len(parts) :]
         panel = lax.axis_index("panel")
-
-        def place(ref, i, first, source, side):
-            start = pl.multiple_of(source * (2 * half) + side * half, half)
-            for s in range(symbols):
-                gathered[s, pl.ds(start, half), :] = ref[i, first + s * half : first + (s + 1) * half, :]
-
-        for side, group in ((panel, mine_refs), (1 - panel, theirs_refs)):
-            n = 0
-            for ref in group:
-                for i in range(ref.shape[0]):
-                    place(ref, i, keep, source_ref[n], side)
-                    n += 1
-        for side, group in ((panel, (own_other,)), (1 - panel, peer_others)):
-            n = rounds
-            for ref in group:
-                for i in range(ref.shape[0]):
-                    place(ref, i, 0, source_ref[n], side)
-                    n += 1
+        for n in range(len(parts)):
+            for r in range(4):
+                ref = refs[4 * n + r]
+                side = panel if r % 2 == 0 else 1 - panel
+                inside = side * half + (1 - side if n == 0 else side) * (half // 2)
+                for i in range(rounds):
+                    source = source_ref[i if r < 2 else rounds + i]
+                    start = pl.multiple_of(source * (2 * half) + inside, half // 2)
+                    block = ref[i, keep if r < 2 else 0 : 2 * keep if r < 2 else keep, :].astype(F32)
+                    for s in range(symbols):
+                        gathered[s, pl.ds(start, half // 2), :] = block[s * (half // 2) : (s + 1) * (half // 2)]
         for s in range(symbols):
-            out[:, :, s] = gathered[s].T.reshape(cells, per_device, 2, total)
+            out[:, :, s] = gathered[s].astype(BF16).T.reshape(cells, per_device, 2, total)
 
     return pl.pallas_call(
         kernel,
-        in_specs=[SMEM_SPEC] + [VMEM_SPEC] * (3 * number + 1),
+        in_specs=[SMEM_SPEC] + [VMEM_SPEC] * (4 * len(parts)),
         out_specs=VMEM_SPEC,
         out_shape=jax.ShapeDtypeStruct((cells, per_device, symbols, 2, total), BF16),
-        scratch_shapes=[pltpu.VMEM((symbols, total, lanes), BF16)],
+        scratch_shapes=[pltpu.VMEM((symbols, total, lanes), F32)],
         compiler_params=pltpu.CompilerParams(vmem_limit_bytes=VMEM_LIMIT),
-    )(sources, *mine, *theirs, *others)
+    )(sources, *[array for part in parts for array in part])
 
 
 def body(channel, received, noise_power, user_count, serving_cell):
@@ -423,19 +381,18 @@
 
     samples = jnp.transpose(received, (0, 1, 3, 2, 4))
 
-    inner = half - 1
-    count = inner * 2 // 5
-    first = inner_gram(user_count, channel, samples, True, 0, count, BF16, limit=56 << 20)
+    part = half // 2
+    middle, outer = (part, half), (1, band - part)
+    first, bottom, top = inner_gram(
+        user_count, channel, samples, True, middle, part, BF16, limit=56 << 20, ends=True
+    )
     first_peer = lax.ppermute(first, "panel", SWAP)
-    bottom, top = band_ends(channel, first)
+    bottom, top = hand_on([bottom, top])
     low = lax.ppermute(top, "sc", [(i, i + 1) for i in range(n_sc - 1)])
     high = lax.ppermute(bottom, "sc", [(i + 1, i) for i in range(n_sc - 1)])
-    second = inner_gram(user_count, channel, samples, True, count, inner - count, BF16)
+    (second,) = inner_gram(user_count, channel, samples, True, outer, part - 1, BF16, limit=56 << 20)
     second_peer = lax.ppermute(second, "panel", SWAP)
-    own = inner_gram(user_count, channel, samples, False, 0, inner, F32)
-    low, high, own = lax.optimization_barrier((low, high, own))
-    edge_peer = lax.ppermute(edge_gram(user_count, channel, samples, low, high), "panel", SWAP)
-    state, edge_own = detect_first(user_count, noise_power, own, first_peer, channel, samples, low, high)
+    (own,) = inner_gram(user_count, channel, samples, False, (1, half), half - 1, F32)
 
     capacity = cells * users // n_cell
     per_device = n_cell * capacity // n_sc
@@ -450,23 +407,35 @@
     width = 2 * cells * per_device
     onehot = (column[:, None] == lax.iota(jnp.int32, 2 * reach * width)[None, :]).astype(BF16)
 
-    messages = detect_last(noise_power, own, second_peer, edge_own, edge_peer, state, onehot, symbols, reach)
-    arrived = []
-    for b in range(reach):
-        pairs = [
-            (s * n_sc + j, j // reach * n_sc + s * reach + (j % reach + b) % reach)
-            for s in range(n_cell)
-            for j in range(n_sc)
-        ]
-        arrived.append(lax.ppermute(messages[b], ("cell", "sc"), pairs))
+    def travel(messages):
+        arrived = []
+        for b in range(reach):
+            pairs = [
+                (s * n_sc + j, j // reach * n_sc + s * reach + (j % reach + b) % reach)
+                for s in range(n_cell)
+                for j in range(n_sc)
+            ]
+            arrived.append(lax.ppermute(messages[b], ("cell", "sc"), pairs))
+        return arrived
+
+    keep = symbols * part
+    messages = detect(noise_power, own, (part - 1, 0), first_peer, (), onehot, symbols, reach)
+    arrived_1 = travel(messages)
+    low, high, arrived_1[: reach // 2] = lax.optimization_barrier((low, high, arrived_1[: reach // 2]))
+    mine_1 = jnp.stack(arrived_1)
+    theirs_1 = lax.ppermute(mine_1, "panel", SWAP)
+    edge_peer = lax.ppermute(edge_gram(user_count, channel, samples, low, high, True, BF16), "panel", SWAP)
+    edge_own = edge_gram(user_count, channel, samples, low, high, False, F32)
+    second_peer, mine_1 = lax.optimization_barrier((second_peer, mine_1))
+    messages = detect(noise_power, own, (0, part), second_peer, (edge_own, edge_peer), onehot, symbols, reach)
+    mine_2 = jnp.stack(travel(messages))
+    theirs_2 = lax.ppermute(mine_2, "panel", SWAP)
+    gifts = lax.ppermute(jnp.stack([mine_1[:, :keep], theirs_1[:, :keep], mine_2[:, :keep]]), "cell", SWAP)
+    last = lax.ppermute(theirs_2[:, :keep], "cell", SWAP)
     turns = (sc % reach - lax.iota(jnp.int32, reach)) % reach
     sources = jnp.concatenate([cell * reach + turns, (1 - cell) * reach + turns])
-    keep = symbols * half
-    mine = [jnp.stack(arrived[: reach // 2]), jnp.stack(arrived[reach // 2 :])]
-    theirs = [lax.ppermute(group, "panel", SWAP) for group in mine]
-    others = [lax.ppermute(jnp.stack([block[:keep] for block in arrived]), "cell", SWAP)]
-    others += [lax.ppermute(group[:, :keep], "cell", SWAP) for group in theirs]
-    routed = assemble(sources, mine, theirs, others, cells, per_device, symbols, half)
+    parts = ((mine_1, theirs_1, gifts[0], gifts[1]), (mine_2, theirs_2, gifts[2], last))
+    routed = assemble(sources, parts, cells, per_device, symbols, half)
     return jnp.transpose(routed, (0, 1, 3, 2, 4))
 
 

time: 73.1 us -> 80.6 us (1.10)
  starting transfers between devices: 27.8 us -> 34.3 us
  waiting for transfers between devices: 10.6 us -> 11.8 us
  local copies, waits for them, and re-layouts: 1.12 us -> 0.09 us
    ppermute x10 -> x13, starting transfers between devices: 19.4 us -> 25.9 us  [the longest x8 12.1 us: travel(): arrived.append(lax.ppermute(messages[b], ('cell', 'sc'), pairs))]
    ppermute x10 -> x13, waiting for transfers between devices: 5.64 us -> 11.8 us  [the longest x1 6.97 us: body(): theirs_2 = lax.ppermute(mine_2, 'panel', SWAP)]
    ppermute x1, waiting for transfers between devices: 4.95 us -> 0.01 us  [body(): low = lax.ppermute(top, 'sc', [(i, i + 1) for i in range(n_sc - 1)])]
    pallas_call x1 -> x2, Pallas kernels: 1.91 us -> 3.83 us  [edge_gram(): pl.pallas_call(kernel, in_specs=[HBM_SPEC] * 5, out_specs=VMEM_SPEC, out_...]
    pallas_call x7, Pallas kernels: 30.5 us -> 29.3 us  [the longest x3 23.1 us: inner_gram(): pl.pallas_call(kernel, in_specs=[HBM_SPEC] * 3, out_specs=[VMEM_SPEC] * (...]
    unnamed x10 -> x8, local copies, waits for them, and re-layouts: 1.09 us -> 0.03 us
  transfers between devices with their start and end apart: 14 -> 17, of which waited for: 5 -> 5; matrix products, arithmetic and copies ran while one was open for 1% -> 1% of each run, Pallas kernels for 30% -> 29%
where the time goes in v6:
time: 80.6 us; the launch traced here: 80.3 us
  starting transfers between devices  34.3 us (43%)
  Pallas kernels  33.2 us (41%)
  waiting for transfers between devices  11.8 us (15%)
    pallas_call x3, Pallas kernels, inner_gram(): pl.pallas_call(kernel, in_specs=[HBM_SPEC] * 3, out_specs=[VMEM_SPEC] * (...  23.1 us
    ppermute x8, starting transfers between devices, travel(): arrived.append(lax.ppermute(messages[b], ('cell', 'sc'), pairs))  12.1 us
    ppermute x1, starting transfers between devices, body(): lax.ppermute(jnp.stack([mine_1[:, :keep], theirs_1[:, :keep], mine_2[:, :...  11 us
    ppermute x1, waiting for transfers between devices, body(): theirs_2 = lax.ppermute(mine_2, 'panel', SWAP)  6.97 us
    pallas_call x2, Pallas kernels, detect(): pl.pallas_call(kernel, in_specs=[SMEM_SPEC] + [VMEM_SPEC] * (3 + len(edge...  4.18 us
    pallas_call x2, Pallas kernels, edge_gram(): pl.pallas_call(kernel, in_specs=[HBM_SPEC] * 5, out_specs=VMEM_SPEC, out_...  3.83 us
    ppermute x1, starting transfers between devices, body(): low = lax.ppermute(top, 'sc', [(i, i + 1) for i in range(n_sc - 1)])  3.44 us
    ppermute x8, waiting for transfers between devices, travel(): arrived.append(lax.ppermute(messages[b], ('cell', 'sc'), pairs))  3.16 us
  transfers between devices with their start and end apart: 17, of which 5 were waited for; matrix products, arithmetic and copies ran while one was open for 1% of the time, Pallas kernels for 29%

profile of v6, /device:TPU:0, one launch (start us, length us, event | category | flops | bytes accessed | tf_op | source)
XLA Modules:
  0.0 80.3 jit_solution(1813963781229187080)
XLA Ops:
  0.0 7.8 %shard_map.56 = (bf16[2,8,160,128]{3,2,1,0:T(8,128)(2,1)}, bf16[2,1,2,512,128]{4,3,2,1,0:T(8,128)(2,1)}, bf16[2,1,2,512,128]{4,3,2,1,0:T(8,128)(2,1)}) custom-call(s32[2,2]{1,0:T(2,128)} %counts_hbm.9, bf16[2,32,2,512,128]{4,3,2,1,0:T(8,128)(2,1)} %chan.9, bf16[2,32,14,2,512]{4,3,2,1,0:T(2,128)(2,1)} %bitcast.23), custom_call_target="tpu_custom_call" | custom-call | flops 1207959552 | bytes 5242880 | tf_op jit(solution)/shard_map/pallas_call | solution.py:138
  7.8 3.0 %collective-permute-start.3 = (bf16[2,8,160,128]{3,2,1,0:T(8,128)(2,1)}, bf16[2,8,160,128]{3,2,1,0:T(8,128)(2,1)S(1)}, u32[]{:S(2)}, u32[]{:S(2)}) collective-permute-start(bf16[2,8,160,128]{3,2,1,0:T(8,128)(2,1)} %get-tuple-element.28), channel_id=1, source_target_pairs={{0,8},{8,0},{1,9},{9,1},{2,10},{10,2},{3,11},{11,3},{4,12},{12,4},... | collective-permute-start | bytes 1966088 | tf_op jit(solution)/shard_map/ppermute | solution.py:389
  10.8 3.4 %collective-permute-start.1 = (bf16[2,1,2,512,128]{4,3,2,1,0:T(8,128)(2,1)}, bf16[2,1,2,512,128]{4,3,2,1,0:T(8,128)(2,1)S(1)}, u32[]{:S(2)}, u32[]{:S(2)}) collective-permute-start(bf16[2,1,2,512,128]{4,3,2,1,0:T(8,128)(2,1)} %get-tuple-element.26), channel_id=1, source_target_pairs={{0,1},{1,2},{2,3},{3,4},{4,5},{5,6},{6,7},{8,9},{9,10},{10,11},{11... | collective-permute-start | bytes 1572872 | tf_op jit(solution)/shard_map/ppermute | solution.py:391
  14.3 1.4 %collective-permute-start.2 = (bf16[2,1,2,512,128]{4,3,2,1,0:T(8,128)(2,1)}, bf16[2,1,2,512,128]{4,3,2,1,0:T(8,128)(2,1)S(1)}, u32[]{:S(2)}, u32[]{:S(2)}) collective-permute-start(bf16[2,1,2,512,128]{4,3,2,1,0:T(8,128)(2,1)} %get-tuple-element.27), channel_id=1, source_target_pairs={{1,0},{2,1},{3,2},{4,3},{5,4},{6,5},{7,6},{9,8},{10,9},{11,10},{12... | collective-permute-start | bytes 1572872 | tf_op jit(solution)/shard_map/ppermute | solution.py:392
  15.7 6.7 %shard_map.55 = bf16[2,7,160,128]{3,2,1,0:T(8,128)(2,1)} custom-call(s32[2,2]{1,0:T(2,128)} %counts_hbm.9, bf16[2,32,2,512,128]{4,3,2,1,0:T(8,128)(2,1)} %chan.9, bf16[2,32,14,2,512]{4,3,2,1,0:T(2,128)(2,1)} %bitcast.24), custom_call_target="tpu_custom_call" | custom-call | flops 1056964608 | bytes 4718592 | tf_op jit(solution)/shard_map/pallas_call | solution.py:138
  23.3 8.6 %shard_map.58.own_ref = f32[2,15,160,128]{3,2,1,0:T(8,128)S(1)} custom-call(s32[2,2]{1,0:T(2,128)S(1)} %copy-done.1, bf16[2,32,2,512,128]{4,3,2,1,0:T(8,128)(2,1)} %chan.9, bf16[2,32,14,2,512]{4,3,2,1,0:T(2,128)(2,1)S(1)} %bitcast.25), custom_call_target="tpu_custom_call" | custom-call | flops 2264924160 | bytes 8912896 | tf_op jit(solution)/shard_map/pallas_call | solution.py:138
  32.2 1.8 %shard_map.59 = (bf16[224,128]{1,0:T(8,128)(2,1)S(1)}, bf16[224,128]{1,0:T(8,128)(2,1)S(1)}, bf16[224,128]{1,0:T(8,128)(2,1)S(1)}, bf16[224,128]{1,0:T(8,128)(2,1)S(1)}) custom-call(f32[2]{0:T(128)S(1)} %copy-done.2, f32[2,15,160,128]{3,2,1,0:T(8,128)S(1)} %shard_map.58.own_ref, bf16[2,8,160,128]{3,2,1,0:T(8,128)(2,1)S(1)} %collective-permute-done.3.peer_ref, ...), custom_call_target="tpu_custom_call" | custom-call | flops 117440512 | bytes 2457600 | tf_op jit(solution)/shard_map/pallas_call | solution.py:329
  34.0 0.7 collective-permute-start.4
  34.7 2.7 %collective-permute-start.5 = (bf16[224,128]{1,0:T(8,128)(2,1)S(1)}, bf16[224,128]{1,0:T(8,128)(2,1)S(1)}, u32[]{:S(2)}, u32[]{:S(2)}) collective-permute-start(bf16[224,128]{1,0:T(8,128)(2,1)S(1)} %get-tuple-element.30), channel_id=1, source_target_pairs={{0,1},{1,2},{2,3},{3,0},{4,17},{5,18},{6,19},{7,16},{16,5},{17,6},... | collective-permute-start | bytes 172040 | tf_op jit(solution)/shard_map/ppermute | solution.py:418
  37.4 1.5 %collective-permute-start.6 = (bf16[224,128]{1,0:T(8,128)(2,1)S(1)}, bf16[224,128]{1,0:T(8,128)(2,1)S(1)}, u32[]{:S(2)}, u32[]{:S(2)}) collective-permute-start(bf16[224,128]{1,0:T(8,128)(2,1)S(1)} %get-tuple-element.33), channel_id=1, source_target_pairs={{0,2},{1,3},{2,0},{3,1},{4,18},{5,19},{6,16},{7,17},{16,6},{17,7},... | collective-permute-start | bytes 172040 | tf_op jit(solution)/shard_map/ppermute | solution.py:418
  38.9 2.3 %collective-permute-start.7 = (bf16[224,128]{1,0:T(8,128)(2,1)S(1)}, bf16[224,128]{1,0:T(8,128)(2,1)S(1)}, u32[]{:S(2)}, u32[]{:S(2)}) collective-permute-start(bf16[224,128]{1,0:T(8,128)(2,1)S(1)} %get-tuple-element.34), channel_id=1, source_target_pairs={{0,3},{1,0},{2,1},{3,2},{4,19},{5,16},{6,17},{7,18},{16,7},{17,4},... | collective-permute-start | bytes 172040 | tf_op jit(solution)/shard_map/ppermute | solution.py:418
  41.3 1.9 %shard_map.61 = bf16[2,160,128]{2,1,0:T(8,128)(2,1)S(1)} custom-call(s32[2,2]{1,0:T(2,128)S(1)} %copy-done.1, bf16[2,32,2,512,128]{4,3,2,1,0:T(8,128)(2,1)} %chan.9, bf16[2,32,14,2,512]{4,3,2,1,0:T(2,128)(2,1)S(1)} %bitcast.26, bf16[2,1,2,512,128]{4,3,2,1,0:T(8,128)(2,1)S(1)} %collective-permute-done.1.low_ref, ...), custom_call_target="tpu_custom_call" | custom-call | flops 150994944 | bytes 1572864 | tf_op jit(solution)/shard_map/pallas_call | solution.py:246
  43.2 1.6 %collective-permute-start.9 = (bf16[2,160,128]{2,1,0:T(8,128)(2,1)S(1)}, bf16[2,160,128]{2,1,0:T(8,128)(2,1)S(1)}, u32[]{:S(2)}, u32[]{:S(2)}) collective-permute-start(bf16[2,160,128]{2,1,0:T(8,128)(2,1)S(1)} %shard_map.61), channel_id=1, source_target_pairs={{0,8},{8,0},{1,9},{9,1},{2,10},{10,2},{3,11},{11,3},{4,12},{12,4},... | collective-permute-start | bytes 245768 | tf_op jit(solution)/shard_map/ppermute | solution.py:427
  45.4 1.9 %shard_map.60.refs_0_ = f32[2,160,128]{2,1,0:T(8,128)S(1)} custom-call(s32[2,2]{1,0:T(2,128)S(1)} %copy-done.1, bf16[2,32,2,512,128]{4,3,2,1,0:T(8,128)(2,1)} %chan.9, bf16[2,32,14,2,512]{4,3,2,1,0:T(2,128)(2,1)S(1)} %bitcast.27, bf16[2,1,2,512,128]{4,3,2,1,0:T(8,128)(2,1)S(1)} %collective-permute-done.1.low_ref, ...), custom_call_target="tpu_custom_call" | custom-call | flops 150994944 | bytes 1572864 | tf_op jit(solution)/shard_map/pallas_call | solution.py:246
  47.7 2.4 %shard_map.62 = (bf16[224,128]{1,0:T(8,128)(2,1)S(1)}, bf16[224,128]{1,0:T(8,128)(2,1)S(1)}, bf16[224,128]{1,0:T(8,128)(2,1)S(1)}, bf16[224,128]{1,0:T(8,128)(2,1)S(1)}) custom-call(f32[2]{0:T(128)S(1)} %copy-done.2, f32[2,15,160,128]{3,2,1,0:T(8,128)S(1)} %shard_map.58.own_ref, bf16[2,7,160,128]{3,2,1,0:T(8,128)(2,1)} %collective-permute-done.peer_ref, ...), custom_call_target="tpu_custom_call" | custom-call | flops 117440512 | bytes 2457600 | tf_op jit(solution)/shard_map/pallas_call | solution.py:329
  50.0 2.2 %collective-permute-start.12 = (bf16[224,128]{1,0:T(8,128)(2,1)S(1)}, bf16[224,128]{1,0:T(8,128)(2,1)S(1)}, u32[]{:S(2)}, u32[]{:S(2)}) collective-permute-start(bf16[224,128]{1,0:T(8,128)(2,1)S(1)} %get-tuple-element.41), channel_id=1, source_target_pairs={{0,2},{1,3},{2,0},{3,1},{4,18},{5,19},{6,16},{7,17},{16,6},{17,7},... | collective-permute-start | bytes 172040 | tf_op jit(solution)/shard_map/ppermute | solution.py:418
  52.4 0.7 collective-permute-start.10
  53.0 2.0 %collective-permute-start.11 = (bf16[224,128]{1,0:T(8,128)(2,1)S(1)}, bf16[224,128]{1,0:T(8,128)(2,1)S(1)}, u32[]{:S(2)}, u32[]{:S(2)}) collective-permute-start(bf16[224,128]{1,0:T(8,128)(2,1)S(1)} %get-tuple-element.40), channel_id=1, source_target_pairs={{0,1},{1,2},{2,3},{3,0},{4,17},{5,18},{6,19},{7,16},{16,5},{17,6},... | collective-permute-start | bytes 172040 | tf_op jit(solution)/shard_map/ppermute | solution.py:418
  55.0 1.4 %collective-permute-done.13 = bf16[224,128]{1,0:T(8,128)(2,1)S(1)} collective-permute-done((bf16[224,128]{1,0:T(8,128)(2,1)S(1)}, bf16[224,128]{1,0:T(8,128)(2,1)S(1)}, u32[]{:S(2)}, u32[]{:S(2)}) %collective-permute-start.13) | collective-permute-done | bytes 57376 | tf_op jit(solution)/shard_map/ppermute | solution.py:418
  56.4 1.7 %collective-permute-done.11 = bf16[224,128]{1,0:T(8,128)(2,1)S(1)} collective-permute-done((bf16[224,128]{1,0:T(8,128)(2,1)S(1)}, bf16[224,128]{1,0:T(8,128)(2,1)S(1)}, u32[]{:S(2)}, u32[]{:S(2)}) %collective-permute-start.11) | collective-permute-done | bytes 57376 | tf_op jit(solution)/shard_map/ppermute | solution.py:418
  58.3 11.0 %collective-permute-start.14 = (bf16[3,4,112,128]{3,2,1,0:T(8,128)(2,1)S(1)}, bf16[3,4,112,128]{3,2,1,0:T(8,128)(2,1)S(1)}, u32[]{:S(2)}, u32[]{:S(2)}) collective-permute-start(bf16[3,4,112,128]{3,2,1,0:T(8,128)(2,1)S(1)} %pad_maximum_fusion), channel_id=1, source_target_pairs={{0,16},{16,0},{1,17},{17,1},{2,18},{18,2},{3,19},{19,3},{4,20},{20... | collective-permute-start | bytes 1032200 | tf_op jit(solution)/shard_map/ppermute | solution.py:433
  69.9 7.0 %collective-permute-done.15.refs_5_ = bf16[4,224,128]{2,1,0:T(8,128)(2,1)S(1)} collective-permute-done((bf16[4,224,128]{2,1,0:T(8,128)(2,1)S(1)}, bf16[4,224,128]{2,1,0:T(8,128)(2,1)S(1)}, u32[]{:S(2)}, u32[]{:S(2)}) %collective-permute-start.15) | collective-permute-done | bytes 229408 | tf_op jit(solution)/shard_map/ppermute | solution.py:432
  77.0 1.3 %collective-permute-done.16.refs_7_ = bf16[4,112,128]{2,1,0:T(8,128)(2,1)S(1)} collective-permute-done((bf16[4,112,128]{2,1,0:T(8,128)(2,1)S(1)}, bf16[4,112,128]{2,1,0:T(8,128)(2,1)S(1)}, u32[]{:S(2)}, u32[]{:S(2)}) %collective-permute-start.16) | collective-permute-done | bytes 114720 | tf_op jit(solution)/shard_map/ppermute | solution.py:434
  78.2 2.0 %shard_map.63 = bf16[2,32,14,2,256]{4,3,2,1,0:T(2,128)(2,1)} custom-call(s32[8]{0:T(128)S(1)} %pad_add_fusion.1.source_ref, bf16[4,224,128]{2,1,0:T(8,128)(2,1)S(1)} %pad_maximum_fusion.1.refs_0_, bf16[4,224,128]{2,1,0:T(8,128)(2,1)S(1)} %collective-permute-done.8.refs_1_, bf16[4,112,128]{2,1,0:T(8,128)(2,1)S(1)} %get-tuple-element.47.refs_2_, ...), custom_call_target="tpu_custom_call" | custom-call | tf_op jit(solution)/shard_map/pallas_call | solution.py:365
  (41 shorter events, 3.0 us)
Async XLA Ops:
  7.8 24.4 %collective-permute-start.3 = (bf16[2,8,160,128]{3,2,1,0:T(8,128)(2,1)}, bf16[2,8,160,128]{3,2,1,0:T(8,128)(2,1)S(1)}, u32[]{:S(2)}, u32[]{:S(2)}) collective-permute-start(bf16[2,8,160,128]{3,2,1,0:T(8,128)(2,1)} %get-tuple-element.28), channel_id=1, source_target_pairs={{0,8},{8,0},{1,9},{9,1},{2,10},{10,2},{3,11},{11,3},{4,12},{12,4},... | collective-permute-start | bytes 1966088 | tf_op jit(solution)/shard_map/ppermute | solution.py:389
  10.8 26.6 %collective-permute-start.1 = (bf16[2,1,2,512,128]{4,3,2,1,0:T(8,128)(2,1)}, bf16[2,1,2,512,128]{4,3,2,1,0:T(8,128)(2,1)S(1)}, u32[]{:S(2)}, u32[]{:S(2)}) collective-permute-start(bf16[2,1,2,512,128]{4,3,2,1,0:T(8,128)(2,1)} %get-tuple-element.26), channel_id=1, source_target_pairs={{0,1},{1,2},{2,3},{3,4},{4,5},{5,6},{6,7},{8,9},{9,10},{10,11},{11... | collective-permute-start | bytes 1572872 | tf_op jit(solution)/shard_map/ppermute | solution.py:391
  14.2 8.8 %copy-start.3 = (s32[2,128,1]{1,2,0:T(1,128)S(1)}, s32[2,128,1]{1,2,0:T(1,128)}, u32[]{:S(2)}) copy-start(s32[2,128,1]{1,2,0:T(1,128)} %param.9) | copy-start | bytes 3076
  14.3 9.0 %copy-start = (bf16[2,32,2,14,512]{4,2,3,1,0:T(2,128)(2,1)S(1)}, bf16[2,32,2,14,512]{4,2,3,1,0:T(2,128)(2,1)}, u32[]{:S(2)}) copy-start(bf16[2,32,2,14,512]{4,2,3,1,0:T(2,128)(2,1)} %param.6) | copy-start | bytes 5505028
  14.3 9.0 %copy-start.1 = (s32[2,2]{1,0:T(2,128)S(1)}, s32[2,2]{1,0:T(2,128)}, u32[]{:S(2)}) copy-start(s32[2,2]{1,0:T(2,128)} %counts_hbm.9) | copy-start | bytes 52
  14.3 24.7 %collective-permute-start.2 = (bf16[2,1,2,512,128]{4,3,2,1,0:T(8,128)(2,1)}, bf16[2,1,2,512,128]{4,3,2,1,0:T(8,128)(2,1)S(1)}, u32[]{:S(2)}, u32[]{:S(2)}) collective-permute-start(bf16[2,1,2,512,128]{4,3,2,1,0:T(8,128)(2,1)} %get-tuple-element.27), channel_id=1, source_target_pairs={{1,0},{2,1},{3,2},{4,3},{5,4},{6,5},{7,6},{9,8},{10,9},{11,10},{12... | collective-permute-start | bytes 1572872 | tf_op jit(solution)/shard_map/ppermute | solution.py:392
  22.4 23.0 %collective-permute-start = (bf16[2,7,160,128]{3,2,1,0:T(8,128)(2,1)}, bf16[2,7,160,128]{3,2,1,0:T(8,128)(2,1)}, u32[]{:S(2)}, u32[]{:S(2)}) collective-permute-start(bf16[2,7,160,128]{3,2,1,0:T(8,128)(2,1)} %shard_map.55), channel_id=1, source_target_pairs={{0,8},{8,0},{1,9},{9,1},{2,10},{10,2},{3,11},{11,3},{4,12},{12,4},... | collective-permute-start | bytes 1720328 | tf_op jit(solution)/shard_map/ppermute | solution.py:394
  23.2 8.9 %copy-start.2 = (f32[2]{0:T(128)S(1)}, f32[2]{0:T(128)}, u32[]{:S(2)}) copy-start(f32[2]{0:T(128)} %noise_ref.3) | copy-start | bytes 28
  34.0 7.2 %collective-permute-start.4 = (bf16[224,128]{1,0:T(8,128)(2,1)S(1)}, bf16[224,128]{1,0:T(8,128)(2,1)S(1)}, u32[]{:S(2)}, u32[]{:S(2)}) collective-permute-start(bf16[224,128]{1,0:T(8,128)(2,1)S(1)} %get-tuple-element.29), channel_id=1, source_target_pairs={{0,0},{1,1},{2,2},{3,3},{4,16},{5,17},{6,18},{7,19},{16,4},{17,5},... | collective-permute-start | bytes 172040 | tf_op jit(solution)/shard_map/ppermute | solution.py:418
  34.7 6.6 %collective-permute-start.5 = (bf16[224,128]{1,0:T(8,128)(2,1)S(1)}, bf16[224,128]{1,0:T(8,128)(2,1)S(1)}, u32[]{:S(2)}, u32[]{:S(2)}) collective-permute-start(bf16[224,128]{1,0:T(8,128)(2,1)S(1)} %get-tuple-element.30), channel_id=1, source_target_pairs={{0,1},{1,2},{2,3},{3,0},{4,17},{5,18},{6,19},{7,16},{16,5},{17,6},... | collective-permute-start | bytes 172040 | tf_op jit(solution)/shard_map/ppermute | solution.py:418
  37.4 7.4 %collective-permute-start.6 = (bf16[224,128]{1,0:T(8,128)(2,1)S(1)}, bf16[224,128]{1,0:T(8,128)(2,1)S(1)}, u32[]{:S(2)}, u32[]{:S(2)}) collective-permute-start(bf16[224,128]{1,0:T(8,128)(2,1)S(1)} %get-tuple-element.33), channel_id=1, source_target_pairs={{0,2},{1,3},{2,0},{3,1},{4,18},{5,19},{6,16},{7,17},{16,6},{17,7},... | collective-permute-start | bytes 172040 | tf_op jit(solution)/shard_map/ppermute | solution.py:418
  38.9 5.8 %collective-permute-start.7 = (bf16[224,128]{1,0:T(8,128)(2,1)S(1)}, bf16[224,128]{1,0:T(8,128)(2,1)S(1)}, u32[]{:S(2)}, u32[]{:S(2)}) collective-permute-start(bf16[224,128]{1,0:T(8,128)(2,1)S(1)} %get-tuple-element.34), channel_id=1, source_target_pairs={{0,3},{1,0},{2,1},{3,2},{4,19},{5,16},{6,17},{7,18},{16,7},{17,4},... | collective-permute-start | bytes 172040 | tf_op jit(solution)/shard_map/ppermute | solution.py:418
  43.2 4.5 %collective-permute-start.9 = (bf16[2,160,128]{2,1,0:T(8,128)(2,1)S(1)}, bf16[2,160,128]{2,1,0:T(8,128)(2,1)S(1)}, u32[]{:S(2)}, u32[]{:S(2)}) collective-permute-start(bf16[2,160,128]{2,1,0:T(8,128)(2,1)S(1)} %shard_map.61), channel_id=1, source_target_pairs={{0,8},{8,0},{1,9},{9,1},{2,10},{10,2},{3,11},{11,3},{4,12},{12,4},... | collective-permute-start | bytes 245768 | tf_op jit(solution)/shard_map/ppermute | solution.py:427
  44.8 13.4 %collective-permute-start.8 = (bf16[4,224,128]{2,1,0:T(8,128)(2,1)S(1)}, bf16[4,224,128]{2,1,0:T(8,128)(2,1)S(1)}, u32[]{:S(2)}, u32[]{:S(2)}) collective-permute-start(bf16[4,224,128]{2,1,0:T(8,128)(2,1)S(1)} %pad_maximum_fusion.1.refs_0_), channel_id=1, source_target_pairs={{0,8},{8,0},{1,9},{9,1},{2,10},{10,2},{3,11},{11,3},{4,12},{12,4},... | collective-permute-start | bytes 688136 | tf_op jit(solution)/shard_map/ppermute | solution.py:426
  50.0 5.0 %collective-permute-start.12 = (bf16[224,128]{1,0:T(8,128)(2,1)S(1)}, bf16[224,128]{1,0:T(8,128)(2,1)S(1)}, u32[]{:S(2)}, u32[]{:S(2)}) collective-permute-start(bf16[224,128]{1,0:T(8,128)(2,1)S(1)} %get-tuple-element.41), channel_id=1, source_target_pairs={{0,2},{1,3},{2,0},{3,1},{4,18},{5,19},{6,16},{7,17},{16,6},{17,7},... | collective-permute-start | bytes 172040 | tf_op jit(solution)/shard_map/ppermute | solution.py:418
  52.2 4.2 %collective-permute-start.13 = (bf16[224,128]{1,0:T(8,128)(2,1)S(1)}, bf16[224,128]{1,0:T(8,128)(2,1)S(1)}, u32[]{:S(2)}, u32[]{:S(2)}) collective-permute-start(bf16[224,128]{1,0:T(8,128)(2,1)S(1)} %get-tuple-element.42), channel_id=1, source_target_pairs={{0,3},{1,0},{2,1},{3,2},{4,19},{5,16},{6,17},{7,18},{16,7},{17,4},... | collective-permute-start | bytes 172040 | tf_op jit(solution)/shard_map/ppermute | solution.py:418
  52.4 4.1 %collective-permute-start.10 = (bf16[224,128]{1,0:T(8,128)(2,1)S(1)}, bf16[224,128]{1,0:T(8,128)(2,1)S(1)}, u32[]{:S(2)}, u32[]{:S(2)}) collective-permute-start(bf16[224,128]{1,0:T(8,128)(2,1)S(1)} %get-tuple-element.39), channel_id=1, source_target_pairs={{0,0},{1,1},{2,2},{3,3},{4,16},{5,17},{6,18},{7,19},{16,4},{17,5},... | collective-permute-start | bytes 172040 | tf_op jit(solution)/shard_map/ppermute | solution.py:418
  53.0 5.1 %collective-permute-start.11 = (bf16[224,128]{1,0:T(8,128)(2,1)S(1)}, bf16[224,128]{1,0:T(8,128)(2,1)S(1)}, u32[]{:S(2)}, u32[]{:S(2)}) collective-permute-start(bf16[224,128]{1,0:T(8,128)(2,1)S(1)} %get-tuple-element.40), channel_id=1, source_target_pairs={{0,1},{1,2},{2,3},{3,0},{4,17},{5,18},{6,19},{7,16},{16,5},{17,6},... | collective-permute-start | bytes 172040 | tf_op jit(solution)/shard_map/ppermute | solution.py:418
  58.3 18.6 %collective-permute-start.14 = (bf16[3,4,112,128]{3,2,1,0:T(8,128)(2,1)S(1)}, bf16[3,4,112,128]{3,2,1,0:T(8,128)(2,1)S(1)}, u32[]{:S(2)}, u32[]{:S(2)}) collective-permute-start(bf16[3,4,112,128]{3,2,1,0:T(8,128)(2,1)S(1)} %pad_maximum_fusion), channel_id=1, source_target_pairs={{0,16},{16,0},{1,17},{17,1},{2,18},{18,2},{3,19},{19,3},{4,20},{20... | collective-permute-start | bytes 1032200 | tf_op jit(solution)/shard_map/ppermute | solution.py:433
  69.2 7.6 %collective-permute-start.15 = (bf16[4,224,128]{2,1,0:T(8,128)(2,1)S(1)}, bf16[4,224,128]{2,1,0:T(8,128)(2,1)S(1)}, u32[]{:S(2)}, u32[]{:S(2)}) collective-permute-start(bf16[4,224,128]{2,1,0:T(8,128)(2,1)S(1)} %pad_maximum_fusion.2.refs_4_), channel_id=1, source_target_pairs={{0,8},{8,0},{1,9},{9,1},{2,10},{10,2},{3,11},{11,3},{4,12},{12,4},... | collective-permute-start | bytes 688136 | tf_op jit(solution)/shard_map/ppermute | solution.py:432
  76.8 1.4 %collective-permute-start.16 = (bf16[4,112,128]{2,1,0:T(8,128)(2,1)S(1)}, bf16[4,112,128]{2,1,0:T(8,128)(2,1)S(1)}, u32[]{:S(2)}, u32[]{:S(2)}) collective-permute-start(bf16[4,112,128]{2,1,0:T(8,128)(2,1)S(1)} %slice.33), channel_id=1, source_target_pairs={{0,16},{16,0},{1,17},{17,1},{2,18},{18,2},{3,19},{19,3},{4,20},{20... | collective-permute-start | bytes 344072 | tf_op jit(solution)/shard_map/ppermute | solution.py:434

commit v7 on v5

--- a/solution.py
+++ b/solution.py
@@ -59,18 +59,24 @@
     ]
 
 
-def inner_gram(counts, channel, received, peer, first, number, dtype, limit=VMEM_LIMIT):
+def inner_gram(counts, channel, received, peer, firsts, number, dtype, limit=VMEM_LIMIT, ends=False):
     cells, band, _, antennas, users = channel.shape
     symbols = received.shape[2]
-    half = band // 2
     items = cells * number
 
-    def kernel(counts_hbm, chan, samp, out, count_ref, win, ybuf, mat_a, lhs_a, mat_b, lhs_b, wsem, ysem, csem):
+    def kernel(counts_hbm, chan, samp, out, *refs):
+        end_refs, refs = (refs[:2], refs[2:]) if ends else ((), refs)
+        count_ref, win, ybuf, mat_a, lhs_a, mat_b, lhs_b, wsem, ysem, csem, esem = refs
         count_copy = pltpu.make_async_copy(counts_hbm, count_ref, csem)
         count_copy.start()
         panel = lax.axis_index("panel")
         side = 1 - panel if peer else panel
-        start = 1 + side * (half - 1) + first
+        start = jnp.where(side == 0, firsts[0], firsts[1])
+        end_copies = [
+            pltpu.make_async_copy(chan.at[c, i * (band - 1)], end_ref.at[c, 0], esem.at[c, i])
+            for c in range(cells)
+            for i, end_ref in enumerate(end_refs)
+        ]
 
         def fetch(c, i):
             return pltpu.make_async_copy(chan.at[c, start - 1 + i], win.at[c, i], wsem.at[c, i])
@@ -83,6 +89,8 @@
                 fetch(c, i).start()
                 if i == min(2, number):
                     fetch_samples(c).start()
+        for copy in end_copies:
+            copy.start()
         lhs_a[...] = jnp.zeros_like(lhs_a)
         lhs_b[...] = jnp.zeros_like(lhs_b)
 
@@ -123,13 +131,16 @@
             return carry
 
         lax.fori_loop(0, (items + 1) // 2, step, 0)
+        for copy in end_copies:
+            copy.wait()
 
     rows = users + 2 * SPAD
     return pl.pallas_call(
         kernel,
         in_specs=[HBM_SPEC] * 3,
-        out_specs=VMEM_SPEC,
-        out_shape=jax.ShapeDtypeStruct((cells, number, rows, users), dtype),
+        out_specs=[VMEM_SPEC] * (1 + 2 * ends),
+        out_shape=[jax.ShapeDtypeStruct((cells, number, rows, users), dtype)]
+        + [jax.ShapeDtypeStruct((cells, 1, 2, antennas, users), BF16)] * (2 * ends),
         scratch_shapes=[
             pltpu.SMEM(counts.shape, jnp.int32),
             pltpu.VMEM((cells, number + 2, 2, antennas, users), BF16),
@@ -139,40 +150,30 @@
             pltpu.SemaphoreType.DMA((cells, number + 2)),
             pltpu.SemaphoreType.DMA((cells,)),
             pltpu.SemaphoreType.DMA,
+            pltpu.SemaphoreType.DMA((cells, 2)),
         ],
         compiler_params=pltpu.CompilerParams(vmem_limit_bytes=limit),
         cost_estimate=pl.CostEstimate(
-            flops=items * 4 * antennas * users * 2 * (users + SPAD),
-            bytes_accessed=cells * (number + 2) * 4 * antennas * users,
+            flops=items * 4 * antennas * users * 2 * (users + SPAD) // (1 if peer else 16),
+            bytes_accessed=cells * (number + 2) * 4 * antennas * users // (1 if peer else 16),
             transcendentals=0,
         ),
     )(counts, channel, received)
 
 
-def band_ends(channel, after):
-    cells, band, _, antennas, users = channel.shape
-
-    def kernel(chan, after_ref, *refs):
-        *ends, sems = refs
-        copies = [
-            pltpu.make_async_copy(chan.at[c, i * (band - 1)], ends[i].at[c, 0], sems.at[c, i])
-            for c in range(cells)
-            for i in range(2)
-        ]
-        for copy in copies:
-            copy.start()
-        for copy in copies:
-            copy.wait()
-
-    return pl.pallas_call(
-        kernel,
-        in_specs=[HBM_SPEC] * 2,
-        out_specs=[VMEM_SPEC] * 2,
-        out_shape=[jax.ShapeDtypeStruct((cells, 1, 2, antennas, users), BF16)] * 2,
-        scratch_shapes=[pltpu.SemaphoreType.DMA((cells, 2))],
-        compiler_params=pltpu.CompilerParams(vmem_limit_bytes=VMEM_LIMIT),
-        cost_estimate=pl.CostEstimate(flops=0, bytes_accessed=cells * 16 * antennas * users, transcendentals=0),
-    )(channel, after)
+def hand_on(arrays):
+    def kernel(*refs):
+        refs[-1][0] = 0
+
+    return pl.pallas_call(
+        kernel,
+        in_specs=[HBM_SPEC] * len(arrays),
+        out_specs=[HBM_SPEC] * len(arrays),
+        out_shape=[jax.ShapeDtypeStruct(a.shape, a.dtype) for a in arrays],
+        scratch_shapes=[pltpu.SMEM((1,), jnp.int32)],
+        input_output_aliases={i: i for i in range(len(arrays))},
+        cost_estimate=pl.CostEstimate(flops=0, bytes_accessed=8 * arrays[0].size, transcendentals=0),
+    )(*arrays)
 
 
 def edge_scratch(counts, symbols, antennas, users):
@@ -233,12 +234,13 @@
     return fetch, work
 
 
-def edge_gram(counts, channel, received, low, high):
+def edge_gram(counts, channel, received, low, high, peer, dtype):
     cells, _, _, antennas, users = channel.shape
     symbols = received.shape[2]
 
     def kernel(counts_hbm, chan, samp, low_ref, high_ref, out, *scratch):
-        fetch, work = edge_work(1 - lax.axis_index("panel"), counts_hbm, chan, samp, low_ref, high_ref, out, scratch)
+        panel = lax.axis_index("panel")
+        fetch, work = edge_work(1 - panel if peer else panel, counts_hbm, chan, samp, low_ref, high_ref, out, scratch)
         fetch()
         work()
 
@@ -246,7 +248,7 @@
         kernel,
         in_specs=[HBM_SPEC] * 5,
         out_specs=VMEM_SPEC,
-        out_shape=jax.ShapeDtypeStruct((cells, users + 2 * SPAD, users), BF16),
+        out_shape=jax.ShapeDtypeStruct((cells, users + 2 * SPAD, users), dtype),
         scratch_shapes=edge_scratch(counts, symbols, antennas, users),
         compiler_params=pltpu.CompilerParams(vmem_limit_bytes=VMEM_LIMIT),
         cost_estimate=pl.CostEstimate(
@@ -292,38 +294,30 @@
     return [e + a * d for e, a, d in zip(estimate, alpha, direction)]
 
 
-def detect_first(counts, noise_power, own, peer, channel, received, low, high):
+def detect_first(noise_power, own, peer):
     cells, inner, rows, users = own.shape
-    antennas, symbols = channel.shape[3], received.shape[2]
     half, number = inner + 1, peer.shape[1]
 
-    def kernel(noise_ref, counts_hbm, chan, samp, low_ref, high_ref, own_ref, peer_ref, out, edge_out, *scratch):
+    def kernel(noise_ref, own_ref, peer_ref, out):
         panel = lax.axis_index("panel")
-        fetch, work = edge_work(panel, counts_hbm, chan, samp, low_ref, high_ref, edge_out, scratch)
-        fetch()
         spots = [(c, i) for c in range(cells) for i in range(number)]
         sums = [own_ref[c, i] + peer_ref[c, i].astype(F32) for c, i in spots]
         values = conjugate_gradient(sums, [noise_ref[c] for c, _ in spots], users)
         for (c, i), value in zip(spots, values):
             out[c, pl.ds(i + 1 - panel, 2 * SPAD, stride=half), :] = value
-        work()
-
-    return pl.pallas_call(
-        kernel,
-        in_specs=[SMEM_SPEC] + [HBM_SPEC] * 5 + [VMEM_SPEC] * 2,
-        out_specs=[VMEM_SPEC, VMEM_SPEC],
-        out_shape=[
-            jax.ShapeDtypeStruct((cells, 2 * SPAD * half, users), F32),
-            jax.ShapeDtypeStruct((cells, rows, users), F32),
-        ],
-        scratch_shapes=edge_scratch(counts, symbols, antennas, users),
+
+    return pl.pallas_call(
+        kernel,
+        in_specs=[SMEM_SPEC] + [VMEM_SPEC] * 2,
+        out_specs=VMEM_SPEC,
+        out_shape=jax.ShapeDtypeStruct((cells, 2 * SPAD * half, users), F32),
         compiler_params=pltpu.CompilerParams(vmem_limit_bytes=VMEM_LIMIT),
         cost_estimate=pl.CostEstimate(
             flops=cells * number * 2 * 2 * 2 * SPAD * users * 2 * users,
             bytes_accessed=cells * inner * rows * users * 6,
             transcendentals=0,
         ),
-    )(noise_power, counts, channel, received, low, high, own, peer)
+    )(noise_power, own, peer)
 
 
 def detect_last(noise_power, own, peer, edge_own, edge_peer, state, onehot, symbols, rounds):
@@ -425,17 +419,23 @@
 
     inner = half - 1
     count = inner * 2 // 5
-    first = inner_gram(user_count, channel, samples, True, 0, count, BF16, limit=56 << 20)
+    first, bottom, top = inner_gram(
+        user_count, channel, samples, True, (1, half), count, BF16, limit=56 << 20, ends=True
+    )
     first_peer = lax.ppermute(first, "panel", SWAP)
-    bottom, top = band_ends(channel, first)
+    bottom, top = hand_on([bottom, top])
     low = lax.ppermute(top, "sc", [(i, i + 1) for i in range(n_sc - 1)])
     high = lax.ppermute(bottom, "sc", [(i + 1, i) for i in range(n_sc - 1)])
-    second = inner_gram(user_count, channel, samples, True, count, inner - count, BF16)
+    (second,) = inner_gram(
+        user_count, channel, samples, True, (1 + count, half + count), inner - count, BF16, limit=56 << 20
+    )
     second_peer = lax.ppermute(second, "panel", SWAP)
-    own = inner_gram(user_count, channel, samples, False, 0, inner, F32)
-    low, high, own = lax.optimization_barrier((low, high, own))
-    edge_peer = lax.ppermute(edge_gram(user_count, channel, samples, low, high), "panel", SWAP)
-    state, edge_own = detect_first(user_count, noise_power, own, first_peer, channel, samples, low, high)
+    counts, first_peer = lax.optimization_barrier((user_count, first_peer))
+    (own,) = inner_gram(counts, channel, samples, False, (1, half), inner, F32)
+    state = detect_first(noise_power, own, first_peer)
+    low, high, state = lax.optimization_barrier((low, high, state))
+    edge_peer = lax.ppermute(edge_gram(user_count, channel, samples, low, high, True, BF16), "panel", SWAP)
+    edge_own = edge_gram(user_count, channel, samples, low, high, False, F32)
 
     capacity = cells * users // n_cell
     per_device = n_cell * capacity // n_sc

time: 73.1 us -> 70.8 us (0.969)
  local copies, waits for them, and re-layouts: 1.12 us -> 0.06 us
  waiting for transfers between devices: 10.6 us -> 9.69 us
  starting transfers between devices: 27.8 us -> 26.9 us
    ppermute x1, waiting for transfers between devices: 4.95 us -> 2.02 us  [body(): low = lax.ppermute(top, 'sc', [(i, i + 1) for i in range(n_sc - 1)])]
    pallas_call x1 -> x2, Pallas kernels: 1.91 us -> 3.85 us  [edge_gram(): pl.pallas_call(kernel, in_specs=[HBM_SPEC] * 5, out_specs=VMEM_SPEC, out_...]
    pallas_call x5, Pallas kernels: 25.9 us -> 24.5 us  [the longest x3 23.2 us: inner_gram(): pl.pallas_call(kernel, in_specs=[HBM_SPEC] * 3, out_specs=[VMEM_SPEC] * (...]
    unnamed x10 -> x8, local copies, waits for them, and re-layouts: 1.09 us -> 0.03 us
    ppermute x1, waiting for transfers between devices: 1.01 us -> 2.05 us  [body(): lax.ppermute(edge_gram(user_count, channel, samples, low, high, True, BF1...]
  transfers between devices with their start and end apart: 14 -> 14, of which waited for: 5 -> 6; matrix products, arithmetic and copies ran while one was open for 1% -> 1% of each run, Pallas kernels for 30% -> 31%
where the time goes in v7:
time: 70.8 us; the launch traced here: 70.5 us
  Pallas kernels  33 us (47%)
  starting transfers between devices  26.9 us (38%)
  waiting for transfers between devices  9.69 us (14%)
    pallas_call x3, Pallas kernels, inner_gram(): pl.pallas_call(kernel, in_specs=[HBM_SPEC] * 3, out_specs=[VMEM_SPEC] * (...  23.2 us
    ppermute x4, starting transfers between devices, body(): arrived.append(lax.ppermute(messages[b], ('cell', 'sc'), pairs))  6.97 us
    ppermute x1, starting transfers between devices, body(): lax.ppermute(jnp.stack([block[:keep] for block in arrived]), 'cell', SWAP)  4.99 us
    ppermute x2, starting transfers between devices, body(): others += [lax.ppermute(group[:, :keep], 'cell', SWAP) for group in theirs]  4.68 us
    ppermute x4, waiting for transfers between devices, body(): arrived.append(lax.ppermute(messages[b], ('cell', 'sc'), pairs))  4.45 us
    pallas_call x2, Pallas kernels, edge_gram(): pl.pallas_call(kernel, in_specs=[HBM_SPEC] * 5, out_specs=VMEM_SPEC, out_...  3.85 us
    ppermute x1, starting transfers between devices, body(): low = lax.ppermute(top, 'sc', [(i, i + 1) for i in range(n_sc - 1)])  3.44 us
    ppermute x1, starting transfers between devices, body(): first_peer = lax.ppermute(first, 'panel', SWAP)  3 us
  transfers between devices with their start and end apart: 14, of which 6 were waited for; matrix products, arithmetic and copies ran while one was open for 1% of the time, Pallas kernels for 31%

profile of v7, /device:TPU:0, one launch (start us, length us, event | category | flops | bytes accessed | tf_op | source)
XLA Modules:
  0.0 70.5 jit_solution(7088896525722398531)
XLA Ops:
  0.0 6.5 %shard_map.55 = (bf16[2,6,160,128]{3,2,1,0:T(8,128)(2,1)}, bf16[2,1,2,512,128]{4,3,2,1,0:T(8,128)(2,1)}, bf16[2,1,2,512,128]{4,3,2,1,0:T(8,128)(2,1)}) custom-call(s32[2,2]{1,0:T(2,128)} %counts_hbm.8, bf16[2,32,2,512,128]{4,3,2,1,0:T(8,128)(2,1)} %chan.9, bf16[2,32,14,2,512]{4,3,2,1,0:T(2,128)(2,1)} %bitcast.15), custom_call_target="tpu_custom_call" | custom-call | flops 905969664 | bytes 4194304 | tf_op jit(solution)/shard_map/pallas_call | solution.py:138
  6.6 3.0 %collective-permute-start = (bf16[2,6,160,128]{3,2,1,0:T(8,128)(2,1)}, bf16[2,6,160,128]{3,2,1,0:T(8,128)(2,1)S(1)}, u32[]{:S(2)}, u32[]{:S(2)}) collective-permute-start(bf16[2,6,160,128]{3,2,1,0:T(8,128)(2,1)} %get-tuple-element.19), channel_id=1, source_target_pairs={{0,8},{8,0},{1,9},{9,1},{2,10},{10,2},{3,11},{11,3},{4,12},{12,4},... | collective-permute-start | bytes 1474568 | tf_op jit(solution)/shard_map/ppermute | solution.py:425
  9.6 3.4 %collective-permute-start.2 = (bf16[2,1,2,512,128]{4,3,2,1,0:T(8,128)(2,1)}, bf16[2,1,2,512,128]{4,3,2,1,0:T(8,128)(2,1)S(1)}, u32[]{:S(2)}, u32[]{:S(2)}) collective-permute-start(bf16[2,1,2,512,128]{4,3,2,1,0:T(8,128)(2,1)} %get-tuple-element.23), channel_id=1, source_target_pairs={{0,1},{1,2},{2,3},{3,4},{4,5},{5,6},{6,7},{8,9},{9,10},{10,11},{11... | collective-permute-start | bytes 1572872 | tf_op jit(solution)/shard_map/ppermute | solution.py:427
  13.0 1.4 %collective-permute-start.3 = (bf16[2,1,2,512,128]{4,3,2,1,0:T(8,128)(2,1)}, bf16[2,1,2,512,128]{4,3,2,1,0:T(8,128)(2,1)S(1)}, u32[]{:S(2)}, u32[]{:S(2)}) collective-permute-start(bf16[2,1,2,512,128]{4,3,2,1,0:T(8,128)(2,1)} %get-tuple-element.24), channel_id=1, source_target_pairs={{1,0},{2,1},{3,2},{4,3},{5,4},{6,5},{7,6},{9,8},{10,9},{11,10},{12... | collective-permute-start | bytes 1572872 | tf_op jit(solution)/shard_map/ppermute | solution.py:428
  14.5 8.0 %shard_map.57 = bf16[2,9,160,128]{3,2,1,0:T(8,128)(2,1)} custom-call(s32[2,2]{1,0:T(2,128)} %counts_hbm.8, bf16[2,32,2,512,128]{4,3,2,1,0:T(8,128)(2,1)} %chan.9, bf16[2,32,14,2,512]{4,3,2,1,0:T(2,128)(2,1)} %bitcast.16), custom_call_target="tpu_custom_call" | custom-call | flops 1358954496 | bytes 5767168 | tf_op jit(solution)/shard_map/pallas_call | solution.py:138
  23.4 8.6 %shard_map.56.own_ref = f32[2,15,160,128]{3,2,1,0:T(8,128)S(1)} custom-call(s32[2,2]{1,0:T(2,128)S(1)} %copy-done.1, bf16[2,32,2,512,128]{4,3,2,1,0:T(8,128)(2,1)} %chan.9, bf16[2,32,14,2,512]{4,3,2,1,0:T(2,128)(2,1)S(1)} %bitcast.17), custom_call_target="tpu_custom_call" | custom-call | flops 141557760 | bytes 557056 | tf_op jit(solution)/shard_map/pallas_call | solution.py:138
  32.0 1.4 %shard_map.59.state_ref = f32[2,512,128]{2,1,0:T(8,128)S(1)} custom-call(f32[2]{0:T(128)S(1)} %copy-done.2, f32[2,15,160,128]{3,2,1,0:T(8,128)S(1)} %shard_map.56.own_ref, bf16[2,6,160,128]{3,2,1,0:T(8,128)(2,1)S(1)} %collective-permute-done.peer_ref), custom_call_target="tpu_custom_call" | custom-call | flops 50331648 | bytes 3686400 | tf_op jit(solution)/shard_map/pallas_call | solution.py:309
  33.4 2.0 %collective-permute-done.2.low_ref = bf16[2,1,2,512,128]{4,3,2,1,0:T(8,128)(2,1)S(1)} collective-permute-done((bf16[2,1,2,512,128]{4,3,2,1,0:T(8,128)(2,1)}, bf16[2,1,2,512,128]{4,3,2,1,0:T(8,128)(2,1)S(1)}, u32[]{:S(2)}, u32[]{:S(2)}) %collective-permute-start.2) | collective-permute-done | bytes 524320 | tf_op jit(solution)/shard_map/ppermute | solution.py:427
  35.4 1.9 %shard_map.61 = bf16[2,160,128]{2,1,0:T(8,128)(2,1)S(1)} custom-call(s32[2,2]{1,0:T(2,128)S(1)} %copy-done.1, bf16[2,32,2,512,128]{4,3,2,1,0:T(8,128)(2,1)} %chan.9, bf16[2,32,14,2,512]{4,3,2,1,0:T(2,128)(2,1)S(1)} %bitcast.18, bf16[2,1,2,512,128]{4,3,2,1,0:T(8,128)(2,1)S(1)} %collective-permute-done.2.low_ref, ...), custom_call_target="tpu_custom_call" | custom-call | flops 150994944 | bytes 1572864 | tf_op jit(solution)/shard_map/pallas_call | solution.py:247
  37.3 0.6 collective-permute-start.4
  38.2 1.9 %shard_map.60.edge_own_ref = f32[2,160,128]{2,1,0:T(8,128)S(1)} custom-call(s32[2,2]{1,0:T(2,128)S(1)} %copy-done.1, bf16[2,32,2,512,128]{4,3,2,1,0:T(8,128)(2,1)} %chan.9, bf16[2,32,14,2,512]{4,3,2,1,0:T(2,128)(2,1)S(1)} %bitcast.19, bf16[2,1,2,512,128]{4,3,2,1,0:T(8,128)(2,1)S(1)} %collective-permute-done.2.low_ref, ...), custom_call_target="tpu_custom_call" | custom-call | flops 150994944 | bytes 1572864 | tf_op jit(solution)/shard_map/pallas_call | solution.py:247
  40.1 2.1 %collective-permute-done.4.edge_peer_ref = bf16[2,160,128]{2,1,0:T(8,128)(2,1)S(1)} collective-permute-done((bf16[2,160,128]{2,1,0:T(8,128)(2,1)S(1)}, bf16[2,160,128]{2,1,0:T(8,128)(2,1)S(1)}, u32[]{:S(2)}, u32[]{:S(2)}) %collective-permute-start.4) | collective-permute-done | bytes 81952 | tf_op jit(solution)/shard_map/ppermute | solution.py:437
  42.2 2.7 %shard_map.62 = (bf16[448,128]{1,0:T(8,128)(2,1)S(1)}, bf16[448,128]{1,0:T(8,128)(2,1)S(1)}, bf16[448,128]{1,0:T(8,128)(2,1)S(1)}, bf16[448,128]{1,0:T(8,128)(2,1)S(1)}) custom-call(f32[2]{0:T(128)S(1)} %copy-done.2, f32[2,15,160,128]{3,2,1,0:T(8,128)S(1)} %shard_map.56.own_ref, bf16[2,9,160,128]{3,2,1,0:T(8,128)(2,1)} %collective-permute-done.1.peer_ref, ...), custom_call_target="tpu_custom_call" | custom-call | flops 234881024 | bytes 524288 | tf_op jit(solution)/shard_map/pallas_call | solution.py:355
  44.9 2.4 %collective-permute-start.6 = (bf16[448,128]{1,0:T(8,128)(2,1)S(1)}, bf16[448,128]{1,0:T(8,128)(2,1)S(1)}, u32[]{:S(2)}, u32[]{:S(2)}) collective-permute-start(bf16[448,128]{1,0:T(8,128)(2,1)S(1)} %get-tuple-element.30), channel_id=1, source_target_pairs={{0,1},{1,2},{2,3},{3,0},{4,17},{5,18},{6,19},{7,16},{16,5},{17,6},... | collective-permute-start | bytes 344072 | tf_op jit(solution)/shard_map/ppermute | solution.py:461
  47.3 0.7 collective-permute-start.5
  48.0 1.1 %collective-permute-start.8 = (bf16[448,128]{1,0:T(8,128)(2,1)S(1)}, bf16[448,128]{1,0:T(8,128)(2,1)S(1)}, u32[]{:S(2)}, u32[]{:S(2)}) collective-permute-start(bf16[448,128]{1,0:T(8,128)(2,1)S(1)} %get-tuple-element.32), channel_id=1, source_target_pairs={{0,3},{1,0},{2,1},{3,2},{4,19},{5,16},{6,17},{7,18},{16,7},{17,4},... | collective-permute-start | bytes 344072 | tf_op jit(solution)/shard_map/ppermute | solution.py:461
  49.1 2.8 %collective-permute-start.7 = (bf16[448,128]{1,0:T(8,128)(2,1)S(1)}, bf16[448,128]{1,0:T(8,128)(2,1)S(1)}, u32[]{:S(2)}, u32[]{:S(2)}) collective-permute-start(bf16[448,128]{1,0:T(8,128)(2,1)S(1)} %get-tuple-element.31), channel_id=1, source_target_pairs={{0,2},{1,3},{2,0},{3,1},{4,18},{5,19},{6,16},{7,17},{16,6},{17,7},... | collective-permute-start | bytes 344072 | tf_op jit(solution)/shard_map/ppermute | solution.py:461
  52.5 1.9 %collective-permute-done.8 = bf16[448,128]{1,0:T(8,128)(2,1)S(1)} collective-permute-done((bf16[448,128]{1,0:T(8,128)(2,1)S(1)}, bf16[448,128]{1,0:T(8,128)(2,1)S(1)}, u32[]{:S(2)}, u32[]{:S(2)}) %collective-permute-start.8) | collective-permute-done | bytes 114720 | tf_op jit(solution)/shard_map/ppermute | solution.py:461
  54.4 2.6 %collective-permute-done.7 = bf16[448,128]{1,0:T(8,128)(2,1)S(1)} collective-permute-done((bf16[448,128]{1,0:T(8,128)(2,1)S(1)}, bf16[448,128]{1,0:T(8,128)(2,1)S(1)}, u32[]{:S(2)}, u32[]{:S(2)}) %collective-permute-start.7) | collective-permute-done | bytes 114720 | tf_op jit(solution)/shard_map/ppermute | solution.py:461
  57.7 5.0 %collective-permute-start.11 = (bf16[4,224,128]{2,1,0:T(8,128)(2,1)S(1)}, bf16[4,224,128]{2,1,0:T(8,128)(2,1)S(1)}, u32[]{:S(2)}, u32[]{:S(2)}) collective-permute-start(bf16[4,224,128]{2,1,0:T(8,128)(2,1)S(1)} %pad_maximum_fusion.2), channel_id=1, source_target_pairs={{0,16},{16,0},{1,17},{17,1},{2,18},{18,2},{3,19},{19,3},{4,20},{20... | collective-permute-start | bytes 688136 | tf_op jit(solution)/shard_map/ppermute | solution.py:467
  62.7 2.6 %collective-permute-start.12 = (bf16[2,224,128]{2,1,0:T(8,128)(2,1)S(1)}, bf16[2,224,128]{2,1,0:T(8,128)(2,1)S(1)}, u32[]{:S(2)}, u32[]{:S(2)}) collective-permute-start(bf16[2,224,128]{2,1,0:T(8,128)(2,1)S(1)} %slice.28), channel_id=1, source_target_pairs={{0,16},{16,0},{1,17},{17,1},{2,18},{18,2},{3,19},{19,3},{4,20},{20... | collective-permute-start | bytes 344072 | tf_op jit(solution)/shard_map/ppermute | solution.py:468
  65.6 2.1 %collective-permute-start.13 = (bf16[2,224,128]{2,1,0:T(8,128)(2,1)S(1)}, bf16[2,224,128]{2,1,0:T(8,128)(2,1)S(1)}, u32[]{:S(2)}, u32[]{:S(2)}) collective-permute-start(bf16[2,224,128]{2,1,0:T(8,128)(2,1)S(1)} %slice.29), channel_id=1, source_target_pairs={{0,16},{16,0},{1,17},{17,1},{2,18},{18,2},{3,19},{19,3},{4,20},{20... | collective-permute-start | bytes 344072 | tf_op jit(solution)/shard_map/ppermute | solution.py:468
  67.8 0.9 %collective-permute-done.13.refs_6_ = bf16[2,224,128]{2,1,0:T(8,128)(2,1)S(1)} collective-permute-done((bf16[2,224,128]{2,1,0:T(8,128)(2,1)S(1)}, bf16[2,224,128]{2,1,0:T(8,128)(2,1)S(1)}, u32[]{:S(2)}, u32[]{:S(2)}) %collective-permute-start.13) | collective-permute-done | bytes 114720 | tf_op jit(solution)/shard_map/ppermute | solution.py:468
  68.6 1.9 %shard_map.63 = bf16[2,32,14,2,256]{4,3,2,1,0:T(2,128)(2,1)} custom-call(s32[8]{0:T(128)S(1)} %pad_add_fusion.1.source_ref, bf16[2,448,128]{2,1,0:T(8,128)(2,1)S(1)} %pad_maximum_fusion.refs_0_, bf16[2,448,128]{2,1,0:T(8,128)(2,1)S(1)} %pad_maximum_fusion.1.refs_1_, bf16[2,448,128]{2,1,0:T(8,128)(2,1)S(1)} %collective-permute-done.9.refs_2_, ...), custom_call_target="tpu_custom_call" | custom-call | tf_op jit(solution)/shard_map/pallas_call | solution.py:401
  (36 shorter events, 2.8 us)
Async XLA Ops:
  6.6 16.8 %collective-permute-start = (bf16[2,6,160,128]{3,2,1,0:T(8,128)(2,1)}, bf16[2,6,160,128]{3,2,1,0:T(8,128)(2,1)S(1)}, u32[]{:S(2)}, u32[]{:S(2)}) collective-permute-start(bf16[2,6,160,128]{3,2,1,0:T(8,128)(2,1)} %get-tuple-element.19), channel_id=1, source_target_pairs={{0,8},{8,0},{1,9},{9,1},{2,10},{10,2},{3,11},{11,3},{4,12},{12,4},... | collective-permute-start | bytes 1474568 | tf_op jit(solution)/shard_map/ppermute | solution.py:425
  9.6 25.9 %collective-permute-start.2 = (bf16[2,1,2,512,128]{4,3,2,1,0:T(8,128)(2,1)}, bf16[2,1,2,512,128]{4,3,2,1,0:T(8,128)(2,1)S(1)}, u32[]{:S(2)}, u32[]{:S(2)}) collective-permute-start(bf16[2,1,2,512,128]{4,3,2,1,0:T(8,128)(2,1)} %get-tuple-element.23), channel_id=1, source_target_pairs={{0,1},{1,2},{2,3},{3,4},{4,5},{5,6},{6,7},{8,9},{9,10},{10,11},{11... | collective-permute-start | bytes 1572872 | tf_op jit(solution)/shard_map/ppermute | solution.py:427
  13.0 10.1 %copy-start.3 = (s32[2,128,1]{1,2,0:T(1,128)S(1)}, s32[2,128,1]{1,2,0:T(1,128)}, u32[]{:S(2)}) copy-start(s32[2,128,1]{1,2,0:T(1,128)} %param.9) | copy-start | bytes 3076
  13.0 10.3 %copy-start = (bf16[2,32,2,14,512]{4,2,3,1,0:T(2,128)(2,1)S(1)}, bf16[2,32,2,14,512]{4,2,3,1,0:T(2,128)(2,1)}, u32[]{:S(2)}) copy-start(bf16[2,32,2,14,512]{4,2,3,1,0:T(2,128)(2,1)} %param.6) | copy-start | bytes 5505028
  13.0 10.3 %copy-start.1 = (s32[2,2]{1,0:T(2,128)S(1)}, s32[2,2]{1,0:T(2,128)}, u32[]{:S(2)}) copy-start(s32[2,2]{1,0:T(2,128)} %counts_hbm.8) | copy-start | bytes 52
  13.0 22.4 %collective-permute-start.3 = (bf16[2,1,2,512,128]{4,3,2,1,0:T(8,128)(2,1)}, bf16[2,1,2,512,128]{4,3,2,1,0:T(8,128)(2,1)S(1)}, u32[]{:S(2)}, u32[]{:S(2)}) collective-permute-start(bf16[2,1,2,512,128]{4,3,2,1,0:T(8,128)(2,1)} %get-tuple-element.24), channel_id=1, source_target_pairs={{1,0},{2,1},{3,2},{4,3},{5,4},{6,5},{7,6},{9,8},{10,9},{11,10},{12... | collective-permute-start | bytes 1572872 | tf_op jit(solution)/shard_map/ppermute | solution.py:428
  22.5 19.7 %collective-permute-start.1 = (bf16[2,9,160,128]{3,2,1,0:T(8,128)(2,1)}, bf16[2,9,160,128]{3,2,1,0:T(8,128)(2,1)}, u32[]{:S(2)}, u32[]{:S(2)}) collective-permute-start(bf16[2,9,160,128]{3,2,1,0:T(8,128)(2,1)} %shard_map.57), channel_id=1, source_target_pairs={{0,8},{8,0},{1,9},{9,1},{2,10},{10,2},{3,11},{11,3},{4,12},{12,4},... | collective-permute-start | bytes 2211848 | tf_op jit(solution)/shard_map/ppermute | solution.py:432
  23.3 8.7 %copy-start.2 = (f32[2]{0:T(128)S(1)}, f32[2]{0:T(128)}, u32[]{:S(2)}) copy-start(f32[2]{0:T(128)} %noise_ref.3) | copy-start | bytes 28
  37.3 4.9 %collective-permute-start.4 = (bf16[2,160,128]{2,1,0:T(8,128)(2,1)S(1)}, bf16[2,160,128]{2,1,0:T(8,128)(2,1)S(1)}, u32[]{:S(2)}, u32[]{:S(2)}) collective-permute-start(bf16[2,160,128]{2,1,0:T(8,128)(2,1)S(1)} %shard_map.61), channel_id=1, source_target_pairs={{0,8},{8,0},{1,9},{9,1},{2,10},{10,2},{3,11},{11,3},{4,12},{12,4},... | collective-permute-start | bytes 245768 | tf_op jit(solution)/shard_map/ppermute | solution.py:437
  44.9 7.0 %collective-permute-start.6 = (bf16[448,128]{1,0:T(8,128)(2,1)S(1)}, bf16[448,128]{1,0:T(8,128)(2,1)S(1)}, u32[]{:S(2)}, u32[]{:S(2)}) collective-permute-start(bf16[448,128]{1,0:T(8,128)(2,1)S(1)} %get-tuple-element.30), channel_id=1, source_target_pairs={{0,1},{1,2},{2,3},{3,0},{4,17},{5,18},{6,19},{7,16},{16,5},{17,6},... | collective-permute-start | bytes 344072 | tf_op jit(solution)/shard_map/ppermute | solution.py:461
  47.3 4.6 %collective-permute-start.5 = (bf16[448,128]{1,0:T(8,128)(2,1)S(1)}, bf16[448,128]{1,0:T(8,128)(2,1)S(1)}, u32[]{:S(2)}, u32[]{:S(2)}) collective-permute-start(bf16[448,128]{1,0:T(8,128)(2,1)S(1)} %get-tuple-element.29), channel_id=1, source_target_pairs={{0,0},{1,1},{2,2},{3,3},{4,16},{5,17},{6,18},{7,19},{16,4},{17,5},... | collective-permute-start | bytes 344072 | tf_op jit(solution)/shard_map/ppermute | solution.py:461
  48.0 6.4 %collective-permute-start.8 = (bf16[448,128]{1,0:T(8,128)(2,1)S(1)}, bf16[448,128]{1,0:T(8,128)(2,1)S(1)}, u32[]{:S(2)}, u32[]{:S(2)}) collective-permute-start(bf16[448,128]{1,0:T(8,128)(2,1)S(1)} %get-tuple-element.32), channel_id=1, source_target_pairs={{0,3},{1,0},{2,1},{3,2},{4,19},{5,16},{6,17},{7,18},{16,7},{17,4},... | collective-permute-start | bytes 344072 | tf_op jit(solution)/shard_map/ppermute | solution.py:461
  49.1 7.9 %collective-permute-start.7 = (bf16[448,128]{1,0:T(8,128)(2,1)S(1)}, bf16[448,128]{1,0:T(8,128)(2,1)S(1)}, u32[]{:S(2)}, u32[]{:S(2)}) collective-permute-start(bf16[448,128]{1,0:T(8,128)(2,1)S(1)} %get-tuple-element.31), channel_id=1, source_target_pairs={{0,2},{1,3},{2,0},{3,1},{4,18},{5,19},{6,16},{7,17},{16,6},{17,7},... | collective-permute-start | bytes 344072 | tf_op jit(solution)/shard_map/ppermute | solution.py:461
  51.9 10.8 %collective-permute-start.9 = (bf16[2,448,128]{2,1,0:T(8,128)(2,1)S(1)}, bf16[2,448,128]{2,1,0:T(8,128)(2,1)S(1)}, u32[]{:S(2)}, u32[]{:S(2)}) collective-permute-start(bf16[2,448,128]{2,1,0:T(8,128)(2,1)S(1)} %pad_maximum_fusion.refs_0_), channel_id=1, source_target_pairs={{0,8},{8,0},{1,9},{9,1},{2,10},{10,2},{3,11},{11,3},{4,12},{12,4},... | collective-permute-start | bytes 688136 | tf_op jit(solution)/shard_map/ppermute | solution.py:466
  57.0 8.5 %collective-permute-start.10 = (bf16[2,448,128]{2,1,0:T(8,128)(2,1)S(1)}, bf16[2,448,128]{2,1,0:T(8,128)(2,1)S(1)}, u32[]{:S(2)}, u32[]{:S(2)}) collective-permute-start(bf16[2,448,128]{2,1,0:T(8,128)(2,1)S(1)} %pad_maximum_fusion.1.refs_1_), channel_id=1, source_target_pairs={{0,8},{8,0},{1,9},{9,1},{2,10},{10,2},{3,11},{11,3},{4,12},{12,4},... | collective-permute-start | bytes 688136 | tf_op jit(solution)/shard_map/ppermute | solution.py:466
  57.7 10.1 %collective-permute-start.11 = (bf16[4,224,128]{2,1,0:T(8,128)(2,1)S(1)}, bf16[4,224,128]{2,1,0:T(8,128)(2,1)S(1)}, u32[]{:S(2)}, u32[]{:S(2)}) collective-permute-start(bf16[4,224,128]{2,1,0:T(8,128)(2,1)S(1)} %pad_maximum_fusion.2), channel_id=1, source_target_pairs={{0,16},{16,0},{1,17},{17,1},{2,18},{18,2},{3,19},{19,3},{4,20},{20... | collective-permute-start | bytes 688136 | tf_op jit(solution)/shard_map/ppermute | solution.py:467
  62.7 5.1 %collective-permute-start.12 = (bf16[2,224,128]{2,1,0:T(8,128)(2,1)S(1)}, bf16[2,224,128]{2,1,0:T(8,128)(2,1)S(1)}, u32[]{:S(2)}, u32[]{:S(2)}) collective-permute-start(bf16[2,224,128]{2,1,0:T(8,128)(2,1)S(1)} %slice.28), channel_id=1, source_target_pairs={{0,16},{16,0},{1,17},{17,1},{2,18},{18,2},{3,19},{19,3},{4,20},{20... | collective-permute-start | bytes 344072 | tf_op jit(solution)/shard_map/ppermute | solution.py:468
  65.6 3.1 %collective-permute-start.13 = (bf16[2,224,128]{2,1,0:T(8,128)(2,1)S(1)}, bf16[2,224,128]{2,1,0:T(8,128)(2,1)S(1)}, u32[]{:S(2)}, u32[]{:S(2)}) collective-permute-start(bf16[2,224,128]{2,1,0:T(8,128)(2,1)S(1)} %slice.29), channel_id=1, source_target_pairs={{0,16},{16,0},{1,17},{17,1},{2,18},{18,2},{3,19},{19,3},{4,20},{20... | collective-permute-start | bytes 344072 | tf_op jit(solution)/shard_map/ppermute | solution.py:468

commit v8 on v6

--- a/solution.py
+++ b/solution.py
@@ -154,8 +154,8 @@
         ],
         compiler_params=pltpu.CompilerParams(vmem_limit_bytes=limit),
         cost_estimate=pl.CostEstimate(
-            flops=items * 4 * antennas * users * 2 * (users + SPAD),
-            bytes_accessed=cells * (number + 2) * 4 * antennas * users,
+            flops=items * 4 * antennas * users * 2 * (users + SPAD) // (1 if peer else 16),
+            bytes_accessed=cells * (number + 2) * 4 * antennas * users // (1 if peer else 16),
             transcendentals=0,
         ),
     )(counts, channel, received)
@@ -172,6 +172,7 @@
         out_shape=[jax.ShapeDtypeStruct(a.shape, a.dtype) for a in arrays],
         scratch_shapes=[pltpu.SMEM((1,), jnp.int32)],
         input_output_aliases={i: i for i in range(len(arrays))},
+        cost_estimate=pl.CostEstimate(flops=0, bytes_accessed=8 * arrays[0].size, transcendentals=0),
     )(*arrays)
 
 
@@ -293,15 +294,14 @@
     return [e + a * d for e, a, d in zip(estimate, alpha, direction)]
 
 
-def detect(noise_power, own, own_firsts, peer, edges, onehot, symbols, rounds):
+def detect(noise_power, own, own_firsts, peer, edges, symbols):
     cells, _, rows, users = own.shape
     number = peer.shape[1]
     half = number + (len(edges) > 0)
-    width = onehot.shape[1] // (2 * rounds)
     keep = symbols * half
 
-    def kernel(noise_ref, own_ref, peer_ref, hot_ref, *refs):
-        edge_refs, outs, full = refs[: len(edges)], refs[len(edges) : -1], refs[-1]
+    def kernel(noise_ref, own_ref, peer_ref, *refs):
+        edge_refs, (out, full) = refs[: len(edges)], refs[len(edges) :]
         panel = lax.axis_index("panel")
         first = jnp.where(panel == 0, own_firsts[0], own_firsts[1])
         spots = [(c, i) for c in range(cells) for i in range(number)]
@@ -314,62 +314,89 @@
         values = conjugate_gradient(sums, [noise_ref[c] for c, _ in places], users)
         for (c, place), value in zip(places, values):
             full[c, pl.ds(place, 2 * SPAD, stride=half), :] = value
-        blocks = [
-            jnp.concatenate([full[c, (2 * s + k) * half : (2 * s + k + 1) * half] for s in range(symbols)], axis=0)
-            for k in range(2)
-            for c in range(cells)
-        ]
-        lhs = jnp.concatenate(blocks, axis=1).astype(BF16)
+        for k in range(2):
+            for c in range(cells):
+                rows_k = [full[c, (2 * s + k) * half : (2 * s + k + 1) * half] for s in range(symbols)]
+                first_lane = (k * cells + c) * users
+                out[:, first_lane : first_lane + users] = jnp.concatenate(rows_k, axis=0).astype(BF16)
+
+    return pl.pallas_call(
+        kernel,
+        in_specs=[SMEM_SPEC] + [VMEM_SPEC] * (2 + len(edges)),
+        out_specs=VMEM_SPEC,
+        out_shape=jax.ShapeDtypeStruct((keep, 2 * cells * users), BF16),
+        scratch_shapes=[pltpu.VMEM((cells, 2 * SPAD * half, users), F32)],
+        compiler_params=pltpu.CompilerParams(vmem_limit_bytes=VMEM_LIMIT),
+        cost_estimate=pl.CostEstimate(
+            flops=cells * half * 2 * 2 * 2 * SPAD * users * 2 * users, bytes_accessed=4 * own.size, transcendentals=0
+        ),
+    )(noise_power, own, peer, *edges)
+
+
+def place(crossed, founds, received, onehot, reach):
+    keep = founds[0].shape[0]
+    width = onehot.shape[1] // (2 * reach)
+
+    def kernel(crossed_ref, *refs):
+        found_refs, received_refs, hot_ref, outs = refs[:2], refs[2:4], refs[4], refs[5:]
+        cross = jnp.full((1, founds[0].shape[1]), crossed_ref[0]) == 1
+        lhs = jnp.concatenate([jnp.where(cross, r[...], f[...]) for f, r in zip(found_refs, received_refs)], axis=0)
         placed = jnp.dot(lhs, hot_ref[...], preferred_element_type=F32).astype(BF16)
         for i, out in enumerate(outs):
             for side in range(2):
                 start = (2 * i + side) * width
-                out[side * keep : (side + 1) * keep, :] = placed[:, start : start + width]
-
-    return pl.pallas_call(
-        kernel,
-        in_specs=[SMEM_SPEC] + [VMEM_SPEC] * (3 + len(edges)),
-        out_specs=[VMEM_SPEC] * rounds,
-        out_shape=[jax.ShapeDtypeStruct((2 * keep, width), BF16)] * rounds,
-        scratch_shapes=[pltpu.VMEM((cells, 2 * SPAD * half, users), F32)],
+                out[side * 2 * keep : (side + 1) * 2 * keep, :] = placed[:, start : start + width]
+
+    return pl.pallas_call(
+        kernel,
+        in_specs=[SMEM_SPEC] + [VMEM_SPEC] * 5,
+        out_specs=[VMEM_SPEC] * reach,
+        out_shape=[jax.ShapeDtypeStruct((4 * keep, width), BF16)] * reach,
         compiler_params=pltpu.CompilerParams(vmem_limit_bytes=VMEM_LIMIT),
         cost_estimate=pl.CostEstimate(
-            flops=2 * keep * onehot.shape[0] * onehot.shape[1], bytes_accessed=4 * own.size, transcendentals=0
+            flops=4 * keep * onehot.shape[0] * onehot.shape[1], bytes_accessed=4 * onehot.size, transcendentals=0
         ),
-    )(noise_power, own, peer, onehot, *edges)
-
-
-def assemble(sources, parts, cells, per_device, symbols, half):
-    rounds = parts[0][0].shape[0]
+    )(crossed, *founds, *received, onehot)
+
+
+def assemble(sources, mine, theirs, others, cells, per_device, symbols, half):
+    rounds = sum(group.shape[0] for group in mine)
     total = 2 * rounds * 2 * half
-    lanes = parts[0][0].shape[2]
-    keep = symbols * half // 2
+    lanes = mine[0].shape[2]
+    keep = symbols * half
+    groups = [mine, theirs, others[0], others[1]]
+    part = half // 2
 
     def kernel(source_ref, *refs):
-        out, gathered = refs[4 * len(parts) :]
+        out, gathered = refs[-2:]
         panel = lax.axis_index("panel")
-        for n in range(len(parts)):
-            for r in range(4):
-                ref = refs[4 * n + r]
-                side = panel if r % 2 == 0 else 1 - panel
-                inside = side * half + (1 - side if n == 0 else side) * (half // 2)
-                for i in range(rounds):
-                    source = source_ref[i if r < 2 else rounds + i]
-                    start = pl.multiple_of(source * (2 * half) + inside, half // 2)
+        at = 0
+        for r, group in enumerate(groups):
+            side = panel if r % 2 == 0 else 1 - panel
+            n = 0 if r < 2 else rounds
+            for array in group:
+                ref, at = refs[at], at + 1
+                for i in range(array.shape[0]):
                     block = ref[i, keep if r < 2 else 0 : 2 * keep if r < 2 else keep, :].astype(F32)
-                    for s in range(symbols):
-                        gathered[s, pl.ds(start, half // 2), :] = block[s * (half // 2) : (s + 1) * (half // 2)]
+                    for h in range(2):
+                        inside = side * half + (1 - side if h == 0 else side) * part
+                        start = pl.multiple_of(source_ref[n] * (2 * half) + inside, part)
+                        for s in range(symbols):
+                            row = (h * symbols + s) * part
+                            gathered[s, pl.ds(start, part), :] = block[row : row + part]
+                    n += 1
         for s in range(symbols):
             out[:, :, s] = gathered[s].astype(BF16).T.reshape(cells, per_device, 2, total)
 
-    return pl.pallas_call(
-        kernel,
-        in_specs=[SMEM_SPEC] + [VMEM_SPEC] * (4 * len(parts)),
+    arrays = [array for group in groups for array in group]
+    return pl.pallas_call(
+        kernel,
+        in_specs=[SMEM_SPEC] + [VMEM_SPEC] * len(arrays),
         out_specs=VMEM_SPEC,
         out_shape=jax.ShapeDtypeStruct((cells, per_device, symbols, 2, total), BF16),
         scratch_shapes=[pltpu.VMEM((symbols, total, lanes), F32)],
         compiler_params=pltpu.CompilerParams(vmem_limit_bytes=VMEM_LIMIT),
-    )(sources, *[array for part in parts for array in part])
+    )(sources, *arrays)
 
 
 def body(channel, received, noise_power, user_count, serving_cell):
@@ -392,50 +419,60 @@
     high = lax.ppermute(bottom, "sc", [(i + 1, i) for i in range(n_sc - 1)])
     (second,) = inner_gram(user_count, channel, samples, True, outer, part - 1, BF16, limit=56 << 20)
     second_peer = lax.ppermute(second, "panel", SWAP)
-    (own,) = inner_gram(user_count, channel, samples, False, (1, half), half - 1, F32)
+    own_keys = serving_cell[:, :, 0].reshape(-1)
+    other_keys = lax.ppermute(own_keys, "cell", SWAP)
+    counts, first_peer, other_keys = lax.optimization_barrier((user_count, first_peer, other_keys))
+    (own,) = inner_gram(counts, channel, samples, False, (1, half), half - 1, F32)
+    found_1 = detect(noise_power, own, (part - 1, 0), first_peer, (), symbols)
+    low, high, found_1 = lax.optimization_barrier((low, high, found_1))
+    edge_peer = lax.ppermute(edge_gram(user_count, channel, samples, low, high, True, BF16), "panel", SWAP)
+    edge_own = edge_gram(user_count, channel, samples, low, high, False, F32)
+
+    reach = n_sc // n_cell
+    mirror = [
+        (s * n_sc + h * reach + j, h * n_sc + s * reach + j)
+        for s in range(n_cell)
+        for h in range(n_cell)
+        for j in range(reach)
+        if s != h
+    ]
+    found_2 = detect(noise_power, own, (0, part), second_peer, (edge_own, edge_peer), symbols)
+    founds = (found_1, found_2)
+    received_founds = [lax.ppermute(found, ("cell", "sc"), mirror) for found in founds]
 
     capacity = cells * users // n_cell
     per_device = n_cell * capacity // n_sc
-    reach = capacity // per_device
-    keys = serving_cell[:, :, 0].reshape(-1)
+    crossed = cell != sc // reach
+    keys = jnp.where(crossed, other_keys, own_keys)
     position = lax.iota(jnp.int32, cells * users)
     earlier = (keys[:, None] == keys[None, :]) & (position[None, :] < position[:, None])
     rank = jnp.sum(earlier.astype(jnp.int32), axis=1)
-    turn = (rank // per_device - sc % reach) % reach * 2 + (keys // cells == sc // reach).astype(jnp.int32)
+    turn = (rank // per_device - sc % reach) % reach * 2 + (keys // cells == cell).astype(jnp.int32)
     column = ((turn * cells + keys % cells) * per_device + rank % per_device) * 2
     column = jnp.concatenate([column, column + 1])
     width = 2 * cells * per_device
     onehot = (column[:, None] == lax.iota(jnp.int32, 2 * reach * width)[None, :]).astype(BF16)
 
-    def travel(messages):
-        arrived = []
-        for b in range(reach):
-            pairs = [
-                (s * n_sc + j, j // reach * n_sc + s * reach + (j % reach + b) % reach)
-                for s in range(n_cell)
-                for j in range(n_sc)
-            ]
-            arrived.append(lax.ppermute(messages[b], ("cell", "sc"), pairs))
-        return arrived
-
-    keep = symbols * part
-    messages = detect(noise_power, own, (part - 1, 0), first_peer, (), onehot, symbols, reach)
-    arrived_1 = travel(messages)
-    low, high, arrived_1[: reach // 2] = lax.optimization_barrier((low, high, arrived_1[: reach // 2]))
-    mine_1 = jnp.stack(arrived_1)
-    theirs_1 = lax.ppermute(mine_1, "panel", SWAP)
-    edge_peer = lax.ppermute(edge_gram(user_count, channel, samples, low, high, True, BF16), "panel", SWAP)
-    edge_own = edge_gram(user_count, channel, samples, low, high, False, F32)
-    second_peer, mine_1 = lax.optimization_barrier((second_peer, mine_1))
-    messages = detect(noise_power, own, (0, part), second_peer, (edge_own, edge_peer), onehot, symbols, reach)
-    mine_2 = jnp.stack(travel(messages))
-    theirs_2 = lax.ppermute(mine_2, "panel", SWAP)
-    gifts = lax.ppermute(jnp.stack([mine_1[:, :keep], theirs_1[:, :keep], mine_2[:, :keep]]), "cell", SWAP)
-    last = lax.ppermute(theirs_2[:, :keep], "cell", SWAP)
+    messages = place(crossed.astype(jnp.int32).reshape(1), founds, received_founds, onehot, reach)
+    arrived = [messages[0]]
+    for b in range(1, reach):
+        pairs = [
+            (s * n_sc + j, s * n_sc + j // reach * reach + (j % reach + b) % reach)
+            for s in range(n_cell)
+            for j in range(n_sc)
+        ]
+        arrived.append(lax.ppermute(messages[b], ("cell", "sc"), pairs))
+    keep = symbols * half
+    cuts = (0, 1, reach // 2, reach)
+    mine = [jnp.stack(arrived[i:j]) for i, j in zip(cuts, cuts[1:])]
+    theirs = [lax.ppermute(group, "panel", SWAP) for group in mine]
+    gifts = [group[:, :keep] for group in mine + theirs[:-1]]
+    gifts = lax.ppermute(jnp.concatenate(gifts), "cell", SWAP)
+    last = lax.ppermute(theirs[-1][:, :keep], "cell", SWAP)
+    others = ([gifts[:reach]], [gifts[reach:], last])
     turns = (sc % reach - lax.iota(jnp.int32, reach)) % reach
     sources = jnp.concatenate([cell * reach + turns, (1 - cell) * reach + turns])
-    parts = ((mine_1, theirs_1, gifts[0], gifts[1]), (mine_2, theirs_2, gifts[2], last))
-    routed = assemble(sources, parts, cells, per_device, symbols, half)
+    routed = assemble(sources, mine, theirs, others, cells, per_device, symbols, half)
     return jnp.transpose(routed, (0, 1, 3, 2, 4))
 
 

time: 80.6 us -> 72.9 us (0.904)
  waiting for transfers between devices: 11.8 us -> 7.53 us
  starting transfers between devices: 34.3 us -> 31.1 us
    ppermute x12 -> x11, waiting for transfers between devices: 11.4 us -> 4.17 us  [the longest x3 3.06 us: body(): arrived.append(lax.ppermute(messages[b], ('cell', 'sc'), pairs))]
    ppermute x12 -> x11, starting transfers between devices: 24.3 us -> 20.4 us  [the longest x1 8.06 us: body(): gifts = lax.ppermute(jnp.concatenate(gifts), 'cell', SWAP)]
    ppermute x1, waiting for transfers between devices: 0.01 us -> 3.17 us  [body(): first_peer = lax.ppermute(first, 'panel', SWAP)]
    pallas_call x3 -> x4, Pallas kernels: 6.22 us -> 6 us  [the longest x2 3.6 us: detect(): pl.pallas_call(kernel, in_specs=[SMEM_SPEC] + [VMEM_SPEC] * (2 + len(edge...]
  transfers between devices with their start and end apart: 17 -> 16, of which waited for: 5 -> 5; matrix products, arithmetic and copies ran while one was open for 1% -> 1% of each run, Pallas kernels for 29% -> 32%
where the time goes in v8:
time: 72.9 us; the launch traced here: 72.6 us
  Pallas kernels  33 us (45%)
  starting transfers between devices  31.1 us (43%)
  waiting for transfers between devices  7.53 us (10%)
    pallas_call x3, Pallas kernels, inner_gram(): pl.pallas_call(kernel, in_specs=[HBM_SPEC] * 3, out_specs=[VMEM_SPEC] * (...  23.2 us
    ppermute x1, starting transfers between devices, body(): gifts = lax.ppermute(jnp.concatenate(gifts), 'cell', SWAP)  8.06 us
    ppermute x3, starting transfers between devices, body(): arrived.append(lax.ppermute(messages[b], ('cell', 'sc'), pairs))  5.67 us
    pallas_call x2, Pallas kernels, edge_gram(): pl.pallas_call(kernel, in_specs=[HBM_SPEC] * 5, out_specs=VMEM_SPEC, out_...  3.85 us
    pallas_call x2, Pallas kernels, detect(): pl.pallas_call(kernel, in_specs=[SMEM_SPEC] + [VMEM_SPEC] * (2 + len(edge...  3.6 us
    ppermute x1, starting transfers between devices, body(): low = lax.ppermute(top, 'sc', [(i, i + 1) for i in range(n_sc - 1)])  3.44 us
    ppermute x1, waiting for transfers between devices, body(): first_peer = lax.ppermute(first, 'panel', SWAP)  3.17 us
    ppermute x3, waiting for transfers between devices, body(): arrived.append(lax.ppermute(messages[b], ('cell', 'sc'), pairs))  3.06 us
  transfers between devices with their start and end apart: 16, of which 5 were waited for; matrix products, arithmetic and copies ran while one was open for 1% of the time, Pallas kernels for 32%

profile of v8, /device:TPU:0, one launch (start us, length us, event | category | flops | bytes accessed | tf_op | source)
XLA Modules:
  0.0 72.6 jit_solution(7226993280142889128)
XLA Ops:
  0.0 7.8 %shard_map.55 = (bf16[2,8,160,128]{3,2,1,0:T(8,128)(2,1)}, bf16[2,1,2,512,128]{4,3,2,1,0:T(8,128)(2,1)}, bf16[2,1,2,512,128]{4,3,2,1,0:T(8,128)(2,1)}) custom-call(s32[2,2]{1,0:T(2,128)} %counts_hbm.8, bf16[2,32,2,512,128]{4,3,2,1,0:T(8,128)(2,1)} %chan.9, bf16[2,32,14,2,512]{4,3,2,1,0:T(2,128)(2,1)} %bitcast.8), custom_call_target="tpu_custom_call" | custom-call | flops 1207959552 | bytes 5242880 | tf_op jit(solution)/shard_map/pallas_call | solution.py:138
  7.8 3.0 %collective-permute-start.2 = (bf16[2,8,160,128]{3,2,1,0:T(8,128)(2,1)}, bf16[2,8,160,128]{3,2,1,0:T(8,128)(2,1)S(1)}, u32[]{:S(2)}, u32[]{:S(2)}) collective-permute-start(bf16[2,8,160,128]{3,2,1,0:T(8,128)(2,1)} %get-tuple-element.24), channel_id=1, source_target_pairs={{0,8},{8,0},{1,9},{9,1},{2,10},{10,2},{3,11},{11,3},{4,12},{12,4},... | collective-permute-start | bytes 1966088 | tf_op jit(solution)/shard_map/ppermute | solution.py:416
  10.8 3.4 %collective-permute-start = (bf16[2,1,2,512,128]{4,3,2,1,0:T(8,128)(2,1)}, bf16[2,1,2,512,128]{4,3,2,1,0:T(8,128)(2,1)S(1)}, u32[]{:S(2)}, u32[]{:S(2)}) collective-permute-start(bf16[2,1,2,512,128]{4,3,2,1,0:T(8,128)(2,1)} %get-tuple-element.22), channel_id=1, source_target_pairs={{0,1},{1,2},{2,3},{3,4},{4,5},{5,6},{6,7},{8,9},{9,10},{10,11},{11... | collective-permute-start | bytes 1572872 | tf_op jit(solution)/shard_map/ppermute | solution.py:418
  14.2 1.3 %collective-permute-start.1 = (bf16[2,1,2,512,128]{4,3,2,1,0:T(8,128)(2,1)}, bf16[2,1,2,512,128]{4,3,2,1,0:T(8,128)(2,1)S(1)}, u32[]{:S(2)}, u32[]{:S(2)}) collective-permute-start(bf16[2,1,2,512,128]{4,3,2,1,0:T(8,128)(2,1)} %get-tuple-element.23), channel_id=1, source_target_pairs={{1,0},{2,1},{3,2},{4,3},{5,4},{6,5},{7,6},{9,8},{10,9},{11,10},{12... | collective-permute-start | bytes 1572872 | tf_op jit(solution)/shard_map/ppermute | solution.py:419
  15.7 6.8 %shard_map.59 = bf16[2,7,160,128]{3,2,1,0:T(8,128)(2,1)} custom-call(s32[2,2]{1,0:T(2,128)} %counts_hbm.8, bf16[2,32,2,512,128]{4,3,2,1,0:T(8,128)(2,1)} %chan.9, bf16[2,32,14,2,512]{4,3,2,1,0:T(2,128)(2,1)} %bitcast.9), custom_call_target="tpu_custom_call" | custom-call | flops 1056964608 | bytes 4718592 | tf_op jit(solution)/shard_map/pallas_call | solution.py:138
  22.4 0.6 collective-permute-start.4
  23.1 3.2 %collective-permute-done.2.peer_ref = bf16[2,8,160,128]{3,2,1,0:T(8,128)(2,1)S(1)} collective-permute-done((bf16[2,8,160,128]{3,2,1,0:T(8,128)(2,1)}, bf16[2,8,160,128]{3,2,1,0:T(8,128)(2,1)S(1)}, u32[]{:S(2)}, u32[]{:S(2)}) %collective-permute-start.2) | collective-permute-done | bytes 655392 | tf_op jit(solution)/shard_map/ppermute | solution.py:416
  26.2 8.6 %shard_map.57.own_ref = f32[2,15,160,128]{3,2,1,0:T(8,128)S(1)} custom-call(s32[2,2]{1,0:T(2,128)S(1)} %copy-done.1, bf16[2,32,2,512,128]{4,3,2,1,0:T(8,128)(2,1)} %chan.9, bf16[2,32,14,2,512]{4,3,2,1,0:T(2,128)(2,1)S(1)} %bitcast.10), custom_call_target="tpu_custom_call" | custom-call | flops 141557760 | bytes 557056 | tf_op jit(solution)/shard_map/pallas_call | solution.py:138
  34.9 1.5 %shard_map.58.refs_0_ = bf16[112,512]{1,0:T(8,128)(2,1)S(1)} custom-call(f32[2]{0:T(128)S(1)} %copy-done.2, f32[2,15,160,128]{3,2,1,0:T(8,128)S(1)} %shard_map.57.own_ref, bf16[2,8,160,128]{3,2,1,0:T(8,128)(2,1)S(1)} %collective-permute-done.2.peer_ref), custom_call_target="tpu_custom_call" | custom-call | flops 67108864 | bytes 2457600 | tf_op jit(solution)/shard_map/pallas_call | solution.py:323
  36.6 1.9 %shard_map.61 = bf16[2,160,128]{2,1,0:T(8,128)(2,1)S(1)} custom-call(s32[2,2]{1,0:T(2,128)S(1)} %copy-done.1, bf16[2,32,2,512,128]{4,3,2,1,0:T(8,128)(2,1)} %chan.9, bf16[2,32,14,2,512]{4,3,2,1,0:T(2,128)(2,1)S(1)} %bitcast.11, bf16[2,1,2,512,128]{4,3,2,1,0:T(8,128)(2,1)S(1)} %collective-permute-done.low_ref, ...), custom_call_target="tpu_custom_call" | custom-call | flops 150994944 | bytes 1572864 | tf_op jit(solution)/shard_map/pallas_call | solution.py:247
  38.6 2.3 %collective-permute-start.5 = (bf16[2,160,128]{2,1,0:T(8,128)(2,1)S(1)}, bf16[2,160,128]{2,1,0:T(8,128)(2,1)S(1)}, u32[]{:S(2)}, u32[]{:S(2)}) collective-permute-start(bf16[2,160,128]{2,1,0:T(8,128)(2,1)S(1)} %shard_map.61), channel_id=1, source_target_pairs={{0,8},{8,0},{1,9},{9,1},{2,10},{10,2},{3,11},{11,3},{4,12},{12,4},... | collective-permute-start | bytes 245768 | tf_op jit(solution)/shard_map/ppermute | solution.py:428
  40.9 0.7 collective-permute-start.6
  41.5 1.9 %shard_map.60.refs_0_ = f32[2,160,128]{2,1,0:T(8,128)S(1)} custom-call(s32[2,2]{1,0:T(2,128)S(1)} %copy-done.1, bf16[2,32,2,512,128]{4,3,2,1,0:T(8,128)(2,1)} %chan.9, bf16[2,32,14,2,512]{4,3,2,1,0:T(2,128)(2,1)S(1)} %bitcast.12, bf16[2,1,2,512,128]{4,3,2,1,0:T(8,128)(2,1)S(1)} %collective-permute-done.low_ref, ...), custom_call_target="tpu_custom_call" | custom-call | flops 150994944 | bytes 1572864 | tf_op jit(solution)/shard_map/pallas_call | solution.py:247
  43.7 2.1 %shard_map.62.refs_1_ = bf16[112,512]{1,0:T(8,128)(2,1)S(1)} custom-call(f32[2]{0:T(128)S(1)} %copy-done.2, f32[2,15,160,128]{3,2,1,0:T(8,128)S(1)} %shard_map.57.own_ref, bf16[2,7,160,128]{3,2,1,0:T(8,128)(2,1)} %collective-permute-done.4.peer_ref, f32[2,160,128]{2,1,0:T(8,128)S(1)} %shard_map.60.refs_0_, ...), custom_call_target="tpu_custom_call" | custom-call | flops 67108864 | bytes 2457600 | tf_op jit(solution)/shard_map/pallas_call | solution.py:323
  45.8 0.7 collective-permute-start.7
  47.2 1.8 %collective-permute-start.8 = (bf16[448,128]{1,0:T(8,128)(2,1)S(1)}, bf16[448,128]{1,0:T(8,128)(2,1)S(1)}, u32[]{:S(2)}, u32[]{:S(2)}) collective-permute-start(bf16[448,128]{1,0:T(8,128)(2,1)S(1)} %get-tuple-element.32), channel_id=1, source_target_pairs={{0,1},{1,2},{2,3},{3,0},{4,5},{5,6},{6,7},{7,4},{16,17},{17,18},{1... | collective-permute-start | bytes 344072 | tf_op jit(solution)/shard_map/ppermute | solution.py:464
  48.9 1.2 %collective-permute-start.10 = (bf16[448,128]{1,0:T(8,128)(2,1)S(1)}, bf16[448,128]{1,0:T(8,128)(2,1)S(1)}, u32[]{:S(2)}, u32[]{:S(2)}) collective-permute-start(bf16[448,128]{1,0:T(8,128)(2,1)S(1)} %get-tuple-element.34), channel_id=1, source_target_pairs={{0,3},{1,0},{2,1},{3,2},{4,7},{5,4},{6,5},{7,6},{16,19},{17,16},{1... | collective-permute-start | bytes 344072 | tf_op jit(solution)/shard_map/ppermute | solution.py:464
  50.1 2.7 %collective-permute-start.9 = (bf16[448,128]{1,0:T(8,128)(2,1)S(1)}, bf16[448,128]{1,0:T(8,128)(2,1)S(1)}, u32[]{:S(2)}, u32[]{:S(2)}) collective-permute-start(bf16[448,128]{1,0:T(8,128)(2,1)S(1)} %get-tuple-element.33), channel_id=1, source_target_pairs={{0,2},{1,3},{2,0},{3,1},{4,6},{5,7},{6,4},{7,5},{16,18},{17,19},{1... | collective-permute-start | bytes 344072 | tf_op jit(solution)/shard_map/ppermute | solution.py:464
  53.4 1.5 %collective-permute-start.12 = (bf16[1,448,128]{2,1,0:T(8,128)(2,1)S(1)}, bf16[1,448,128]{2,1,0:T(8,128)(2,1)S(1)}, u32[]{:S(2)}, u32[]{:S(2)}) collective-permute-start(bf16[1,448,128]{2,1,0:T(8,128)(2,1)S(1)} %bitcast.16), channel_id=1, source_target_pairs={{0,8},{8,0},{1,9},{9,1},{2,10},{10,2},{3,11},{11,3},{4,12},{12,4},... | collective-permute-start | bytes 344072 | tf_op jit(solution)/shard_map/ppermute | solution.py:468
  54.9 3.1 %collective-permute-done.9 = bf16[448,128]{1,0:T(8,128)(2,1)S(1)} collective-permute-done((bf16[448,128]{1,0:T(8,128)(2,1)S(1)}, bf16[448,128]{1,0:T(8,128)(2,1)S(1)}, u32[]{:S(2)}, u32[]{:S(2)}) %collective-permute-start.9) | collective-permute-done | bytes 114720 | tf_op jit(solution)/shard_map/ppermute | solution.py:464
  58.9 8.1 %collective-permute-start.14 = (bf16[6,224,128]{2,1,0:T(8,128)(2,1)S(1)}, bf16[6,224,128]{2,1,0:T(8,128)(2,1)S(1)}, u32[]{:S(2)}, u32[]{:S(2)}) collective-permute-start(bf16[6,224,128]{2,1,0:T(8,128)(2,1)S(1)} %slice_dynamic-update-slice_fusion), channel_id=1, source_target_pairs={{0,16},{16,0},{1,17},{17,1},{2,18},{18,2},{3,19},{19,3},{4,20},{20... | collective-permute-start | bytes 1032200 | tf_op jit(solution)/shard_map/ppermute | solution.py:470
  67.0 2.7 %collective-permute-start.15 = (bf16[2,224,128]{2,1,0:T(8,128)(2,1)S(1)}, bf16[2,224,128]{2,1,0:T(8,128)(2,1)S(1)}, u32[]{:S(2)}, u32[]{:S(2)}) collective-permute-start(bf16[2,224,128]{2,1,0:T(8,128)(2,1)S(1)} %slice.40), channel_id=1, source_target_pairs={{0,16},{16,0},{1,17},{17,1},{2,18},{18,2},{3,19},{19,3},{4,20},{20... | collective-permute-start | bytes 344072 | tf_op jit(solution)/shard_map/ppermute | solution.py:471
  69.7 0.8 %collective-permute-done.15.refs_8_ = bf16[2,224,128]{2,1,0:T(8,128)(2,1)S(1)} collective-permute-done((bf16[2,224,128]{2,1,0:T(8,128)(2,1)S(1)}, bf16[2,224,128]{2,1,0:T(8,128)(2,1)S(1)}, u32[]{:S(2)}, u32[]{:S(2)}) %collective-permute-start.15) | collective-permute-done | bytes 114720 | tf_op jit(solution)/shard_map/ppermute | solution.py:471
  70.6 2.0 %shard_map.64 = bf16[2,32,14,2,256]{4,3,2,1,0:T(2,128)(2,1)} custom-call(s32[8]{0:T(128)S(1)} %pad_add_fusion.1.source_ref, bf16[1,448,128]{2,1,0:T(8,128)(2,1)S(1)} %bitcast.15, bf16[1,448,128]{2,1,0:T(8,128)(2,1)S(1)} %bitcast.18, bf16[2,448,128]{2,1,0:T(8,128)(2,1)S(1)} %pad_maximum_fusion.refs_2_, ...), custom_call_target="tpu_custom_call" | custom-call | tf_op jit(solution)/shard_map/pallas_call | solution.py:392
  (42 shorter events, 2.7 us)
Async XLA Ops:
  0.0 15.5 %copy-start.3 = (s32[2,128,1]{1,2,0:T(1,128)S(1)}, s32[2,128,1]{1,2,0:T(1,128)}, u32[]{:S(2)}) copy-start(s32[2,128,1]{1,2,0:T(1,128)} %param.9) | copy-start | bytes 3076
  7.8 18.5 %collective-permute-start.2 = (bf16[2,8,160,128]{3,2,1,0:T(8,128)(2,1)}, bf16[2,8,160,128]{3,2,1,0:T(8,128)(2,1)S(1)}, u32[]{:S(2)}, u32[]{:S(2)}) collective-permute-start(bf16[2,8,160,128]{3,2,1,0:T(8,128)(2,1)} %get-tuple-element.24), channel_id=1, source_target_pairs={{0,8},{8,0},{1,9},{9,1},{2,10},{10,2},{3,11},{11,3},{4,12},{12,4},... | collective-permute-start | bytes 1966088 | tf_op jit(solution)/shard_map/ppermute | solution.py:416
  10.8 25.9 %collective-permute-start = (bf16[2,1,2,512,128]{4,3,2,1,0:T(8,128)(2,1)}, bf16[2,1,2,512,128]{4,3,2,1,0:T(8,128)(2,1)S(1)}, u32[]{:S(2)}, u32[]{:S(2)}) collective-permute-start(bf16[2,1,2,512,128]{4,3,2,1,0:T(8,128)(2,1)} %get-tuple-element.22), channel_id=1, source_target_pairs={{0,1},{1,2},{2,3},{3,4},{4,5},{5,6},{6,7},{8,9},{9,10},{10,11},{11... | collective-permute-start | bytes 1572872 | tf_op jit(solution)/shard_map/ppermute | solution.py:418
  14.2 22.4 %collective-permute-start.1 = (bf16[2,1,2,512,128]{4,3,2,1,0:T(8,128)(2,1)}, bf16[2,1,2,512,128]{4,3,2,1,0:T(8,128)(2,1)S(1)}, u32[]{:S(2)}, u32[]{:S(2)}) collective-permute-start(bf16[2,1,2,512,128]{4,3,2,1,0:T(8,128)(2,1)} %get-tuple-element.23), channel_id=1, source_target_pairs={{1,0},{2,1},{3,2},{4,3},{5,4},{6,5},{7,6},{9,8},{10,9},{11,10},{12... | collective-permute-start | bytes 1572872 | tf_op jit(solution)/shard_map/ppermute | solution.py:419
  15.5 10.7 %copy-start = (bf16[2,32,2,14,512]{4,2,3,1,0:T(2,128)(2,1)S(1)}, bf16[2,32,2,14,512]{4,2,3,1,0:T(2,128)(2,1)}, u32[]{:S(2)}) copy-start(bf16[2,32,2,14,512]{4,2,3,1,0:T(2,128)(2,1)} %param.6) | copy-start | bytes 5505028
  15.6 10.7 %copy-start.1 = (s32[2,2]{1,0:T(2,128)S(1)}, s32[2,2]{1,0:T(2,128)}, u32[]{:S(2)}) copy-start(s32[2,2]{1,0:T(2,128)} %counts_hbm.8) | copy-start | bytes 52
  15.6 7.5 %collective-permute-start.3 = (s32[256]{0:T(256)S(1)}, s32[256]{0:T(256)S(1)}, u32[]{:S(2)}, u32[]{:S(2)}) collective-permute-start(s32[256]{0:T(256)S(1)} %bitcast.23), channel_id=1, source_target_pairs={{0,16},{16,0},{1,17},{17,1},{2,18},{18,2},{3,19},{19,3},{4,20},{20... | collective-permute-start | bytes 3080 | tf_op jit(solution)/shard_map/ppermute | solution.py:423
  22.4 21.3 %collective-permute-start.4 = (bf16[2,7,160,128]{3,2,1,0:T(8,128)(2,1)}, bf16[2,7,160,128]{3,2,1,0:T(8,128)(2,1)}, u32[]{:S(2)}, u32[]{:S(2)}) collective-permute-start(bf16[2,7,160,128]{3,2,1,0:T(8,128)(2,1)} %shard_map.59), channel_id=1, source_target_pairs={{0,8},{8,0},{1,9},{9,1},{2,10},{10,2},{3,11},{11,3},{4,12},{12,4},... | collective-permute-start | bytes 1720328 | tf_op jit(solution)/shard_map/ppermute | solution.py:421
  23.1 11.8 %copy-start.2 = (f32[2]{0:T(128)S(1)}, f32[2]{0:T(128)}, u32[]{:S(2)}) copy-start(f32[2]{0:T(128)} %noise_ref.3) | copy-start | bytes 28
  38.6 5.2 %collective-permute-start.5 = (bf16[2,160,128]{2,1,0:T(8,128)(2,1)S(1)}, bf16[2,160,128]{2,1,0:T(8,128)(2,1)S(1)}, u32[]{:S(2)}, u32[]{:S(2)}) collective-permute-start(bf16[2,160,128]{2,1,0:T(8,128)(2,1)S(1)} %shard_map.61), channel_id=1, source_target_pairs={{0,8},{8,0},{1,9},{9,1},{2,10},{10,2},{3,11},{11,3},{4,12},{12,4},... | collective-permute-start | bytes 245768 | tf_op jit(solution)/shard_map/ppermute | solution.py:428
  40.9 5.9 %collective-permute-start.6 = (bf16[112,512]{1,0:T(8,128)(2,1)S(1)}, bf16[112,512]{1,0:T(8,128)(2,1)S(1)}, u32[]{:S(2)}, u32[]{:S(2)}) collective-permute-start(bf16[112,512]{1,0:T(8,128)(2,1)S(1)} %shard_map.58.refs_0_), channel_id=1, source_target_pairs={{4,16},{5,17},{6,18},{7,19},{16,4},{17,5},{18,6},{19,7},{12,24},{1... | collective-permute-start | bytes 344072 | tf_op jit(solution)/shard_map/ppermute | solution.py:441
  45.8 0.9 %collective-permute-start.7 = (bf16[112,512]{1,0:T(8,128)(2,1)S(1)}, bf16[112,512]{1,0:T(8,128)(2,1)S(1)}, u32[]{:S(2)}, u32[]{:S(2)}) collective-permute-start(bf16[112,512]{1,0:T(8,128)(2,1)S(1)} %shard_map.62.refs_1_), channel_id=1, source_target_pairs={{4,16},{5,17},{6,18},{7,19},{16,4},{17,5},{18,6},{19,7},{12,24},{1... | collective-permute-start | bytes 344072 | tf_op jit(solution)/shard_map/ppermute | solution.py:441
  47.2 6.2 %collective-permute-start.8 = (bf16[448,128]{1,0:T(8,128)(2,1)S(1)}, bf16[448,128]{1,0:T(8,128)(2,1)S(1)}, u32[]{:S(2)}, u32[]{:S(2)}) collective-permute-start(bf16[448,128]{1,0:T(8,128)(2,1)S(1)} %get-tuple-element.32), channel_id=1, source_target_pairs={{0,1},{1,2},{2,3},{3,0},{4,5},{5,6},{6,7},{7,4},{16,17},{17,18},{1... | collective-permute-start | bytes 344072 | tf_op jit(solution)/shard_map/ppermute | solution.py:464
  48.9 6.0 %collective-permute-start.10 = (bf16[448,128]{1,0:T(8,128)(2,1)S(1)}, bf16[448,128]{1,0:T(8,128)(2,1)S(1)}, u32[]{:S(2)}, u32[]{:S(2)}) collective-permute-start(bf16[448,128]{1,0:T(8,128)(2,1)S(1)} %get-tuple-element.34), channel_id=1, source_target_pairs={{0,3},{1,0},{2,1},{3,2},{4,7},{5,4},{6,5},{7,6},{16,19},{17,16},{1... | collective-permute-start | bytes 344072 | tf_op jit(solution)/shard_map/ppermute | solution.py:464
  50.1 7.9 %collective-permute-start.9 = (bf16[448,128]{1,0:T(8,128)(2,1)S(1)}, bf16[448,128]{1,0:T(8,128)(2,1)S(1)}, u32[]{:S(2)}, u32[]{:S(2)}) collective-permute-start(bf16[448,128]{1,0:T(8,128)(2,1)S(1)} %get-tuple-element.33), channel_id=1, source_target_pairs={{0,2},{1,3},{2,0},{3,1},{4,6},{5,7},{6,4},{7,5},{16,18},{17,19},{1... | collective-permute-start | bytes 344072 | tf_op jit(solution)/shard_map/ppermute | solution.py:464
  52.8 5.7 %collective-permute-start.11 = (bf16[1,448,128]{2,1,0:T(8,128)(2,1)S(1)}, bf16[1,448,128]{2,1,0:T(8,128)(2,1)S(1)}, u32[]{:S(2)}, u32[]{:S(2)}) collective-permute-start(bf16[1,448,128]{2,1,0:T(8,128)(2,1)S(1)} %bitcast.13), channel_id=1, source_target_pairs={{0,8},{8,0},{1,9},{9,1},{2,10},{10,2},{3,11},{11,3},{4,12},{12,4},... | collective-permute-start | bytes 344072 | tf_op jit(solution)/shard_map/ppermute | solution.py:468
  53.4 5.5 %collective-permute-start.12 = (bf16[1,448,128]{2,1,0:T(8,128)(2,1)S(1)}, bf16[1,448,128]{2,1,0:T(8,128)(2,1)S(1)}, u32[]{:S(2)}, u32[]{:S(2)}) collective-permute-start(bf16[1,448,128]{2,1,0:T(8,128)(2,1)S(1)} %bitcast.16), channel_id=1, source_target_pairs={{0,8},{8,0},{1,9},{9,1},{2,10},{10,2},{3,11},{11,3},{4,12},{12,4},... | collective-permute-start | bytes 344072 | tf_op jit(solution)/shard_map/ppermute | solution.py:468
  58.0 8.9 %collective-permute-start.13 = (bf16[2,448,128]{2,1,0:T(8,128)(2,1)S(1)}, bf16[2,448,128]{2,1,0:T(8,128)(2,1)S(1)}, u32[]{:S(2)}, u32[]{:S(2)}) collective-permute-start(bf16[2,448,128]{2,1,0:T(8,128)(2,1)S(1)} %pad_maximum_fusion.refs_2_), channel_id=1, source_target_pairs={{0,8},{8,0},{1,9},{9,1},{2,10},{10,2},{3,11},{11,3},{4,12},{12,4},... | collective-permute-start | bytes 688136 | tf_op jit(solution)/shard_map/ppermute | solution.py:468
  58.9 10.8 %collective-permute-start.14 = (bf16[6,224,128]{2,1,0:T(8,128)(2,1)S(1)}, bf16[6,224,128]{2,1,0:T(8,128)(2,1)S(1)}, u32[]{:S(2)}, u32[]{:S(2)}) collective-permute-start(bf16[6,224,128]{2,1,0:T(8,128)(2,1)S(1)} %slice_dynamic-update-slice_fusion), channel_id=1, source_target_pairs={{0,16},{16,0},{1,17},{17,1},{2,18},{18,2},{3,19},{19,3},{4,20},{20... | collective-permute-start | bytes 1032200 | tf_op jit(solution)/shard_map/ppermute | solution.py:470
  67.0 3.6 %collective-permute-start.15 = (bf16[2,224,128]{2,1,0:T(8,128)(2,1)S(1)}, bf16[2,224,128]{2,1,0:T(8,128)(2,1)S(1)}, u32[]{:S(2)}, u32[]{:S(2)}) collective-permute-start(bf16[2,224,128]{2,1,0:T(8,128)(2,1)S(1)} %slice.40), channel_id=1, source_target_pairs={{0,16},{16,0},{1,17},{17,1},{2,18},{18,2},{3,19},{19,3},{4,20},{20... | collective-permute-start | bytes 344072 | tf_op jit(solution)/shard_map/ppermute | solution.py:471

commit v9 on v8

--- a/solution.py
+++ b/solution.py
@@ -333,70 +333,67 @@
     )(noise_power, own, peer, *edges)
 
 
-def place(crossed, founds, received, onehot, reach):
+def place(crossed, founds, mirrored, turned, onehot, reach):
     keep = founds[0].shape[0]
-    width = onehot.shape[1] // (2 * reach)
+    width = onehot.shape[1] // reach
 
     def kernel(crossed_ref, *refs):
-        found_refs, received_refs, hot_ref, outs = refs[:2], refs[2:4], refs[4], refs[5:]
+        found_refs, mirrored_refs, turned_refs, hot_ref, outs = refs[:2], refs[2:4], refs[4:6], refs[6], refs[7:]
         cross = jnp.full((1, founds[0].shape[1]), crossed_ref[0]) == 1
-        lhs = jnp.concatenate([jnp.where(cross, r[...], f[...]) for f, r in zip(found_refs, received_refs)], axis=0)
+        same = [jnp.where(cross, t[...], f[...]) for f, t in zip(found_refs, turned_refs)]
+        far = [jnp.where(cross, m[...], t[...]) for m, t in zip(mirrored_refs, turned_refs)]
+        lhs = jnp.concatenate(same + far, axis=0)
         placed = jnp.dot(lhs, hot_ref[...], preferred_element_type=F32).astype(BF16)
         for i, out in enumerate(outs):
-            for side in range(2):
-                start = (2 * i + side) * width
-                out[side * 2 * keep : (side + 1) * 2 * keep, :] = placed[:, start : start + width]
-
-    return pl.pallas_call(
-        kernel,
-        in_specs=[SMEM_SPEC] + [VMEM_SPEC] * 5,
+            out[...] = placed[:, i * width : (i + 1) * width]
+
+    return pl.pallas_call(
+        kernel,
+        in_specs=[SMEM_SPEC] + [VMEM_SPEC] * 7,
         out_specs=[VMEM_SPEC] * reach,
         out_shape=[jax.ShapeDtypeStruct((4 * keep, width), BF16)] * reach,
         compiler_params=pltpu.CompilerParams(vmem_limit_bytes=VMEM_LIMIT),
         cost_estimate=pl.CostEstimate(
-            flops=4 * keep * onehot.shape[0] * onehot.shape[1], bytes_accessed=4 * onehot.size, transcendentals=0
+            flops=8 * keep * onehot.shape[0] * onehot.shape[1], bytes_accessed=4 * onehot.size, transcendentals=0
         ),
-    )(crossed, *founds, *received, onehot)
-
-
-def assemble(sources, mine, theirs, others, cells, per_device, symbols, half):
+    )(crossed, *founds, *mirrored, *turned, onehot)
+
+
+def assemble(sources, mine, theirs, cells, per_device, symbols, half):
     rounds = sum(group.shape[0] for group in mine)
     total = 2 * rounds * 2 * half
     lanes = mine[0].shape[2]
-    keep = symbols * half
-    groups = [mine, theirs, others[0], others[1]]
     part = half // 2
 
     def kernel(source_ref, *refs):
         out, gathered = refs[-2:]
         panel = lax.axis_index("panel")
         at = 0
-        for r, group in enumerate(groups):
-            side = panel if r % 2 == 0 else 1 - panel
-            n = 0 if r < 2 else rounds
+        for side, group in ((panel, mine), (1 - panel, theirs)):
+            n = 0
             for array in group:
                 ref, at = refs[at], at + 1
                 for i in range(array.shape[0]):
-                    block = ref[i, keep if r < 2 else 0 : 2 * keep if r < 2 else keep, :].astype(F32)
-                    for h in range(2):
-                        inside = side * half + (1 - side if h == 0 else side) * part
-                        start = pl.multiple_of(source_ref[n] * (2 * half) + inside, part)
-                        for s in range(symbols):
-                            row = (h * symbols + s) * part
-                            gathered[s, pl.ds(start, part), :] = block[row : row + part]
+                    block = ref[i].astype(F32)
+                    for far in range(2):
+                        for h in range(2):
+                            inside = side * half + (1 - side if h == 0 else side) * part
+                            start = pl.multiple_of(source_ref[far * rounds + n] * (2 * half) + inside, part)
+                            for s in range(symbols):
+                                row = ((2 * far + h) * symbols + s) * part
+                                gathered[s, pl.ds(start, part), :] = block[row : row + part]
                     n += 1
         for s in range(symbols):
             out[:, :, s] = gathered[s].astype(BF16).T.reshape(cells, per_device, 2, total)
 
-    arrays = [array for group in groups for array in group]
-    return pl.pallas_call(
-        kernel,
-        in_specs=[SMEM_SPEC] + [VMEM_SPEC] * len(arrays),
+    return pl.pallas_call(
+        kernel,
+        in_specs=[SMEM_SPEC] + [VMEM_SPEC] * (2 * len(mine)),
         out_specs=VMEM_SPEC,
         out_shape=jax.ShapeDtypeStruct((cells, per_device, symbols, 2, total), BF16),
         scratch_shapes=[pltpu.VMEM((symbols, total, lanes), F32)],
         compiler_params=pltpu.CompilerParams(vmem_limit_bytes=VMEM_LIMIT),
-    )(sources, *arrays)
+    )(sources, *mine, *theirs)
 
 
 def body(channel, received, noise_power, user_count, serving_cell):
@@ -425,7 +422,9 @@
     (own,) = inner_gram(counts, channel, samples, False, (1, half), half - 1, F32)
     found_1 = detect(noise_power, own, (part - 1, 0), first_peer, (), symbols)
     low, high, found_1 = lax.optimization_barrier((low, high, found_1))
-    edge_peer = lax.ppermute(edge_gram(user_count, channel, samples, low, high, True, BF16), "panel", SWAP)
+    edge_out = edge_gram(user_count, channel, samples, low, high, True, BF16)
+    edge_peer = lax.ppermute(edge_out, "panel", SWAP)
+    edge_out, found_1 = lax.optimization_barrier((edge_out, found_1))
     edge_own = edge_gram(user_count, channel, samples, low, high, False, F32)
 
     reach = n_sc // n_cell
@@ -437,8 +436,15 @@
         if s != h
     ]
     found_2 = detect(noise_power, own, (0, part), second_peer, (edge_own, edge_peer), symbols)
+    turn = [
+        (s * n_sc + h * reach + j, (n_cell - 1 - s if s == h else s) * n_sc + s * reach + j)
+        for s in range(n_cell)
+        for h in range(n_cell)
+        for j in range(reach)
+    ]
     founds = (found_1, found_2)
-    received_founds = [lax.ppermute(found, ("cell", "sc"), mirror) for found in founds]
+    mirrored = [lax.ppermute(found, ("cell", "sc"), mirror) for found in founds]
+    turned = [lax.ppermute(found, ("cell", "sc"), turn) for found in founds]
 
     capacity = cells * users // n_cell
     per_device = n_cell * capacity // n_sc
@@ -447,13 +453,14 @@
     position = lax.iota(jnp.int32, cells * users)
     earlier = (keys[:, None] == keys[None, :]) & (position[None, :] < position[:, None])
     rank = jnp.sum(earlier.astype(jnp.int32), axis=1)
-    turn = (rank // per_device - sc % reach) % reach * 2 + (keys // cells == cell).astype(jnp.int32)
+    turn = (rank // per_device - sc % reach) % reach
     column = ((turn * cells + keys % cells) * per_device + rank % per_device) * 2
+    column = jnp.where(keys // cells == cell, column, -2)
     column = jnp.concatenate([column, column + 1])
     width = 2 * cells * per_device
-    onehot = (column[:, None] == lax.iota(jnp.int32, 2 * reach * width)[None, :]).astype(BF16)
-
-    messages = place(crossed.astype(jnp.int32).reshape(1), founds, received_founds, onehot, reach)
+    onehot = (column[:, None] == lax.iota(jnp.int32, reach * width)[None, :]).astype(BF16)
+
+    messages = place(crossed.astype(jnp.int32).reshape(1), founds, mirrored, turned, onehot, reach)
     arrived = [messages[0]]
     for b in range(1, reach):
         pairs = [
@@ -462,17 +469,17 @@
             for j in range(n_sc)
         ]
         arrived.append(lax.ppermute(messages[b], ("cell", "sc"), pairs))
-    keep = symbols * half
     cuts = (0, 1, reach // 2, reach)
     mine = [jnp.stack(arrived[i:j]) for i, j in zip(cuts, cuts[1:])]
-    theirs = [lax.ppermute(group, "panel", SWAP) for group in mine]
-    gifts = [group[:, :keep] for group in mine + theirs[:-1]]
-    gifts = lax.ppermute(jnp.concatenate(gifts), "cell", SWAP)
-    last = lax.ppermute(theirs[-1][:, :keep], "cell", SWAP)
-    others = ([gifts[:reach]], [gifts[reach:], last])
+    theirs = []
+    for n, group in enumerate(mine):
+        if n == 2:
+            group, theirs[0] = lax.optimization_barrier((group, theirs[0]))
+        theirs.append(lax.ppermute(group, "panel", SWAP))
     turns = (sc % reach - lax.iota(jnp.int32, reach)) % reach
-    sources = jnp.concatenate([cell * reach + turns, (1 - cell) * reach + turns])
-    routed = assemble(sources, mine, theirs, others, cells, per_device, symbols, half)
+    here = sc // reach
+    sources = jnp.concatenate([here * reach + turns, (1 - here) * reach + turns])
+    routed = assemble(sources, mine, theirs, cells, per_device, symbols, half)
     return jnp.transpose(routed, (0, 1, 3, 2, 4))
 
 

time: 72.9 us -> 77.9 us (1.069)
  waiting for transfers between devices: 7.53 us -> 20.6 us
  starting transfers between devices: 31.1 us -> 23.2 us
    ppermute x8, waiting for transfers between devices: 1.1 us -> 14.6 us  [the longest x2 8.7 us: body(): turned = [lax.ppermute(found, ('cell', 'sc'), turn) for found in founds]]
    ppermute x8, starting transfers between devices: 16.9 us -> 12.6 us  [the longest x2 5.44 us: body(): turned = [lax.ppermute(found, ('cell', 'sc'), turn) for found in founds]]
    ppermute x3, starting transfers between devices: 5.67 us -> 2.14 us  [body(): arrived.append(lax.ppermute(messages[b], ('cell', 'sc'), pairs))]
  transfers between devices with their start and end apart: 16 -> 16, of which waited for: 5 -> 7; matrix products, arithmetic and copies ran while one was open for 1% -> 1% of each run, Pallas kernels for 32% -> 29%
where the time goes in v9:
time: 77.9 us; the launch traced here: 77.6 us
  Pallas kernels  33 us (42%)
  starting transfers between devices  23.2 us (30%)
  waiting for transfers between devices  20.6 us (26%)
    pallas_call x3, Pallas kernels, inner_gram(): pl.pallas_call(kernel, in_specs=[HBM_SPEC] * 3, out_specs=[VMEM_SPEC] * (...  23.2 us
    ppermute x2, waiting for transfers between devices, body(): turned = [lax.ppermute(found, ('cell', 'sc'), turn) for found in founds]  8.7 us
    ppermute x3, waiting for transfers between devices, body(): theirs.append(lax.ppermute(group, 'panel', SWAP))  5.95 us
    ppermute x2, starting transfers between devices, body(): turned = [lax.ppermute(found, ('cell', 'sc'), turn) for found in founds]  5.44 us
    pallas_call x2, Pallas kernels, edge_gram(): pl.pallas_call(kernel, in_specs=[HBM_SPEC] * 5, out_specs=VMEM_SPEC, out_...  3.83 us
    pallas_call x2, Pallas kernels, detect(): pl.pallas_call(kernel, in_specs=[SMEM_SPEC] + [VMEM_SPEC] * (2 + len(edge...  3.6 us
    ppermute x3, starting transfers between devices, body(): theirs.append(lax.ppermute(group, 'panel', SWAP))  3.59 us
    ppermute x1, starting transfers between devices, body(): low = lax.ppermute(top, 'sc', [(i, i + 1) for i in range(n_sc - 1)])  3.44 us
  transfers between devices with their start and end apart: 16, of which 7 were waited for; matrix products, arithmetic and copies ran while one was open for 1% of the time, Pallas kernels for 29%

profile of v9, /device:TPU:0, one launch (start us, length us, event | category | flops | bytes accessed | tf_op | source)
XLA Modules:
  0.0 77.6 jit_solution(2546552775226611556)
XLA Ops:
  0.0 7.8 %shard_map.55 = (bf16[2,8,160,128]{3,2,1,0:T(8,128)(2,1)}, bf16[2,1,2,512,128]{4,3,2,1,0:T(8,128)(2,1)}, bf16[2,1,2,512,128]{4,3,2,1,0:T(8,128)(2,1)}) custom-call(s32[2,2]{1,0:T(2,128)} %counts_hbm.8, bf16[2,32,2,512,128]{4,3,2,1,0:T(8,128)(2,1)} %chan.9, bf16[2,32,14,2,512]{4,3,2,1,0:T(2,128)(2,1)} %bitcast.8), custom_call_target="tpu_custom_call" | custom-call | flops 1207959552 | bytes 5242880 | tf_op jit(solution)/shard_map/pallas_call | solution.py:138
  7.8 3.0 %collective-permute-start.2 = (bf16[2,8,160,128]{3,2,1,0:T(8,128)(2,1)}, bf16[2,8,160,128]{3,2,1,0:T(8,128)(2,1)S(1)}, u32[]{:S(2)}, u32[]{:S(2)}) collective-permute-start(bf16[2,8,160,128]{3,2,1,0:T(8,128)(2,1)} %get-tuple-element.27), channel_id=1, source_target_pairs={{0,8},{8,0},{1,9},{9,1},{2,10},{10,2},{3,11},{11,3},{4,12},{12,4},... | collective-permute-start | bytes 1966088 | tf_op jit(solution)/shard_map/ppermute | solution.py:413
  10.8 3.4 %collective-permute-start = (bf16[2,1,2,512,128]{4,3,2,1,0:T(8,128)(2,1)}, bf16[2,1,2,512,128]{4,3,2,1,0:T(8,128)(2,1)S(1)}, u32[]{:S(2)}, u32[]{:S(2)}) collective-permute-start(bf16[2,1,2,512,128]{4,3,2,1,0:T(8,128)(2,1)} %get-tuple-element.25), channel_id=1, source_target_pairs={{0,1},{1,2},{2,3},{3,4},{4,5},{5,6},{6,7},{8,9},{9,10},{10,11},{11... | collective-permute-start | bytes 1572872 | tf_op jit(solution)/shard_map/ppermute | solution.py:415
  14.2 1.3 %collective-permute-start.1 = (bf16[2,1,2,512,128]{4,3,2,1,0:T(8,128)(2,1)}, bf16[2,1,2,512,128]{4,3,2,1,0:T(8,128)(2,1)S(1)}, u32[]{:S(2)}, u32[]{:S(2)}) collective-permute-start(bf16[2,1,2,512,128]{4,3,2,1,0:T(8,128)(2,1)} %get-tuple-element.26), channel_id=1, source_target_pairs={{1,0},{2,1},{3,2},{4,3},{5,4},{6,5},{7,6},{9,8},{10,9},{11,10},{12... | collective-permute-start | bytes 1572872 | tf_op jit(solution)/shard_map/ppermute | solution.py:416
  15.7 6.8 %shard_map.60 = bf16[2,7,160,128]{3,2,1,0:T(8,128)(2,1)} custom-call(s32[2,2]{1,0:T(2,128)} %counts_hbm.8, bf16[2,32,2,512,128]{4,3,2,1,0:T(8,128)(2,1)} %chan.9, bf16[2,32,14,2,512]{4,3,2,1,0:T(2,128)(2,1)} %bitcast.9), custom_call_target="tpu_custom_call" | custom-call | flops 1056964608 | bytes 4718592 | tf_op jit(solution)/shard_map/pallas_call | solution.py:138
  23.1 3.2 %collective-permute-done.2.peer_ref = bf16[2,8,160,128]{3,2,1,0:T(8,128)(2,1)S(1)} collective-permute-done((bf16[2,8,160,128]{3,2,1,0:T(8,128)(2,1)}, bf16[2,8,160,128]{3,2,1,0:T(8,128)(2,1)S(1)}, u32[]{:S(2)}, u32[]{:S(2)}) %collective-permute-start.2) | collective-permute-done | bytes 655392 | tf_op jit(solution)/shard_map/ppermute | solution.py:413
  26.2 8.6 %shard_map.57.own_ref = f32[2,15,160,128]{3,2,1,0:T(8,128)S(1)} custom-call(s32[2,2]{1,0:T(2,128)S(1)} %copy-done.1, bf16[2,32,2,512,128]{4,3,2,1,0:T(8,128)(2,1)} %chan.9, bf16[2,32,14,2,512]{4,3,2,1,0:T(2,128)(2,1)S(1)} %bitcast.10), custom_call_target="tpu_custom_call" | custom-call | flops 141557760 | bytes 557056 | tf_op jit(solution)/shard_map/pallas_call | solution.py:138
  34.9 1.5 %shard_map.58.refs_0_ = bf16[112,512]{1,0:T(8,128)(2,1)S(1)} custom-call(f32[2]{0:T(128)S(1)} %copy-done.2, f32[2,15,160,128]{3,2,1,0:T(8,128)S(1)} %shard_map.57.own_ref, bf16[2,8,160,128]{3,2,1,0:T(8,128)(2,1)S(1)} %collective-permute-done.2.peer_ref), custom_call_target="tpu_custom_call" | custom-call | flops 67108864 | bytes 2457600 | tf_op jit(solution)/shard_map/pallas_call | solution.py:323
  36.6 1.9 %shard_map.59 = bf16[2,160,128]{2,1,0:T(8,128)(2,1)S(1)} custom-call(s32[2,2]{1,0:T(2,128)S(1)} %copy-done.1, bf16[2,32,2,512,128]{4,3,2,1,0:T(8,128)(2,1)} %chan.9, bf16[2,32,14,2,512]{4,3,2,1,0:T(2,128)(2,1)S(1)} %bitcast.11, bf16[2,1,2,512,128]{4,3,2,1,0:T(8,128)(2,1)S(1)} %collective-permute-done.low_ref, ...), custom_call_target="tpu_custom_call" | custom-call | flops 150994944 | bytes 1572864 | tf_op jit(solution)/shard_map/pallas_call | solution.py:247
  38.6 2.3 %collective-permute-start.5 = (bf16[2,160,128]{2,1,0:T(8,128)(2,1)S(1)}, bf16[2,160,128]{2,1,0:T(8,128)(2,1)S(1)}, u32[]{:S(2)}, u32[]{:S(2)}) collective-permute-start(bf16[2,160,128]{2,1,0:T(8,128)(2,1)S(1)} %shard_map.59), channel_id=1, source_target_pairs={{0,8},{8,0},{1,9},{9,1},{2,10},{10,2},{3,11},{11,3},{4,12},{12,4},... | collective-permute-start | bytes 245768 | tf_op jit(solution)/shard_map/ppermute | solution.py:426
  41.5 4.1 %collective-permute-start.8 = (bf16[112,512]{1,0:T(8,128)(2,1)S(1)}, bf16[112,512]{1,0:T(8,128)(2,1)S(1)}, u32[]{:S(2)}, u32[]{:S(2)}) collective-permute-start(bf16[112,512]{1,0:T(8,128)(2,1)S(1)} %shard_map.58.refs_0_), channel_id=1, source_target_pairs={{0,16},{1,17},{2,18},{3,19},{4,0},{5,1},{6,2},{7,3},{16,20},{17,21... | collective-permute-start | bytes 344072 | tf_op jit(solution)/shard_map/ppermute | solution.py:447
  45.6 1.9 %shard_map.61.refs_0_ = f32[2,160,128]{2,1,0:T(8,128)S(1)} custom-call(s32[2,2]{1,0:T(2,128)S(1)} %copy-done.1, bf16[2,32,2,512,128]{4,3,2,1,0:T(8,128)(2,1)} %chan.9, bf16[2,32,14,2,512]{4,3,2,1,0:T(2,128)(2,1)S(1)} %bitcast.12, bf16[2,1,2,512,128]{4,3,2,1,0:T(8,128)(2,1)S(1)} %collective-permute-done.low_ref, ...), custom_call_target="tpu_custom_call" | custom-call | flops 150994944 | bytes 1572864 | tf_op jit(solution)/shard_map/pallas_call | solution.py:247
  47.8 2.1 %shard_map.62.refs_1_ = bf16[112,512]{1,0:T(8,128)(2,1)S(1)} custom-call(f32[2]{0:T(128)S(1)} %copy-done.2, f32[2,15,160,128]{3,2,1,0:T(8,128)S(1)} %shard_map.57.own_ref, bf16[2,7,160,128]{3,2,1,0:T(8,128)(2,1)} %collective-permute-done.4.peer_ref, f32[2,160,128]{2,1,0:T(8,128)S(1)} %shard_map.61.refs_0_, ...), custom_call_target="tpu_custom_call" | custom-call | flops 67108864 | bytes 2457600 | tf_op jit(solution)/shard_map/pallas_call | solution.py:323
  49.9 0.7 collective-permute-start.7
  50.5 1.4 %collective-permute-start.9 = (bf16[112,512]{1,0:T(8,128)(2,1)S(1)}, bf16[112,512]{1,0:T(8,128)(2,1)S(1)}, u32[]{:S(2)}, u32[]{:S(2)}) collective-permute-start(bf16[112,512]{1,0:T(8,128)(2,1)S(1)} %shard_map.62.refs_1_), channel_id=1, source_target_pairs={{0,16},{1,17},{2,18},{3,19},{4,0},{5,1},{6,2},{7,3},{16,20},{17,21... | collective-permute-start | bytes 344072 | tf_op jit(solution)/shard_map/ppermute | solution.py:447
  52.1 8.7 %collective-permute-done.9.refs_5_ = bf16[112,512]{1,0:T(8,128)(2,1)S(1)} collective-permute-done((bf16[112,512]{1,0:T(8,128)(2,1)S(1)}, bf16[112,512]{1,0:T(8,128)(2,1)S(1)}, u32[]{:S(2)}, u32[]{:S(2)}) %collective-permute-start.9) | collective-permute-done | bytes 114720 | tf_op jit(solution)/shard_map/ppermute | solution.py:447
  61.2 2.1 %collective-permute-start.11 = (bf16[448,128]{1,0:T(8,128)(2,1)S(1)}, bf16[448,128]{1,0:T(8,128)(2,1)S(1)}, u32[]{:S(2)}, u32[]{:S(2)}) collective-permute-start(bf16[448,128]{1,0:T(8,128)(2,1)S(1)} %get-tuple-element.37), channel_id=1, source_target_pairs={{0,2},{1,3},{2,0},{3,1},{4,6},{5,7},{6,4},{7,5},{16,18},{17,19},{1... | collective-permute-start | bytes 344072 | tf_op jit(solution)/shard_map/ppermute | solution.py:471
  63.3 1.5 %collective-permute-start.13 = (bf16[1,448,128]{2,1,0:T(8,128)(2,1)S(1)}, bf16[1,448,128]{2,1,0:T(8,128)(2,1)S(1)}, u32[]{:S(2)}, u32[]{:S(2)}) collective-permute-start(bf16[1,448,128]{2,1,0:T(8,128)(2,1)S(1)} %bitcast.13), channel_id=1, source_target_pairs={{0,8},{8,0},{1,9},{9,1},{2,10},{10,2},{3,11},{11,3},{4,12},{12,4},... | collective-permute-start | bytes 344072 | tf_op jit(solution)/shard_map/ppermute | solution.py:478
  64.8 2.5 %collective-permute-done.12 = bf16[448,128]{1,0:T(8,128)(2,1)S(1)} collective-permute-done((bf16[448,128]{1,0:T(8,128)(2,1)S(1)}, bf16[448,128]{1,0:T(8,128)(2,1)S(1)}, u32[]{:S(2)}, u32[]{:S(2)}) %collective-permute-start.12) | collective-permute-done | bytes 114720 | tf_op jit(solution)/shard_map/ppermute | solution.py:471
  67.4 0.9 %collective-permute-done.13.refs_3_ = bf16[1,448,128]{2,1,0:T(8,128)(2,1)S(1)} collective-permute-done((bf16[1,448,128]{2,1,0:T(8,128)(2,1)S(1)}, bf16[1,448,128]{2,1,0:T(8,128)(2,1)S(1)}, u32[]{:S(2)}, u32[]{:S(2)}) %collective-permute-start.13) | collective-permute-done | bytes 114720 | tf_op jit(solution)/shard_map/ppermute | solution.py:478
  68.3 1.5 %collective-permute-start.15 = (bf16[2,448,128]{2,1,0:T(8,128)(2,1)S(1)}, bf16[2,448,128]{2,1,0:T(8,128)(2,1)S(1)}, u32[]{:S(2)}, u32[]{:S(2)}) collective-permute-start(bf16[2,448,128]{2,1,0:T(8,128)(2,1)S(1)} %pad_maximum_fusion.refs_2_), channel_id=1, source_target_pairs={{0,8},{8,0},{1,9},{9,1},{2,10},{10,2},{3,11},{11,3},{4,12},{12,4},... | collective-permute-start | bytes 688136 | tf_op jit(solution)/shard_map/ppermute | solution.py:478
  69.8 0.7 collective-permute-start.14
  70.6 5.0 %collective-permute-done.14.refs_4_ = bf16[1,448,128]{2,1,0:T(8,128)(2,1)S(1)} collective-permute-done((bf16[1,448,128]{2,1,0:T(8,128)(2,1)S(1)}, bf16[1,448,128]{2,1,0:T(8,128)(2,1)S(1)}, u32[]{:S(2)}, u32[]{:S(2)}) %collective-permute-start.14) | collective-permute-done | bytes 114720 | tf_op jit(solution)/shard_map/ppermute | solution.py:478
  75.6 2.0 %shard_map.64 = bf16[2,32,14,2,256]{4,3,2,1,0:T(2,128)(2,1)} custom-call(s32[8]{0:T(128)S(1)} %pad_add_fusion.1.source_ref, bf16[1,448,128]{2,1,0:T(8,128)(2,1)S(1)} %bitcast.14, bf16[1,448,128]{2,1,0:T(8,128)(2,1)S(1)} %bitcast.16, bf16[2,448,128]{2,1,0:T(8,128)(2,1)S(1)} %pad_maximum_fusion.refs_2_, ...), custom_call_target="tpu_custom_call" | custom-call | tf_op jit(solution)/shard_map/pallas_call | solution.py:389
  (34 shorter events, 2.7 us)
Async XLA Ops:
  0.0 15.5 %copy-start.3 = (s32[2,128,1]{1,2,0:T(1,128)S(1)}, s32[2,128,1]{1,2,0:T(1,128)}, u32[]{:S(2)}) copy-start(s32[2,128,1]{1,2,0:T(1,128)} %param.9) | copy-start | bytes 3076
  7.8 18.5 %collective-permute-start.2 = (bf16[2,8,160,128]{3,2,1,0:T(8,128)(2,1)}, bf16[2,8,160,128]{3,2,1,0:T(8,128)(2,1)S(1)}, u32[]{:S(2)}, u32[]{:S(2)}) collective-permute-start(bf16[2,8,160,128]{3,2,1,0:T(8,128)(2,1)} %get-tuple-element.27), channel_id=1, source_target_pairs={{0,8},{8,0},{1,9},{9,1},{2,10},{10,2},{3,11},{11,3},{4,12},{12,4},... | collective-permute-start | bytes 1966088 | tf_op jit(solution)/shard_map/ppermute | solution.py:413
  10.8 25.9 %collective-permute-start = (bf16[2,1,2,512,128]{4,3,2,1,0:T(8,128)(2,1)}, bf16[2,1,2,512,128]{4,3,2,1,0:T(8,128)(2,1)S(1)}, u32[]{:S(2)}, u32[]{:S(2)}) collective-permute-start(bf16[2,1,2,512,128]{4,3,2,1,0:T(8,128)(2,1)} %get-tuple-element.25), channel_id=1, source_target_pairs={{0,1},{1,2},{2,3},{3,4},{4,5},{5,6},{6,7},{8,9},{9,10},{10,11},{11... | collective-permute-start | bytes 1572872 | tf_op jit(solution)/shard_map/ppermute | solution.py:415
  14.2 22.4 %collective-permute-start.1 = (bf16[2,1,2,512,128]{4,3,2,1,0:T(8,128)(2,1)}, bf16[2,1,2,512,128]{4,3,2,1,0:T(8,128)(2,1)S(1)}, u32[]{:S(2)}, u32[]{:S(2)}) collective-permute-start(bf16[2,1,2,512,128]{4,3,2,1,0:T(8,128)(2,1)} %get-tuple-element.26), channel_id=1, source_target_pairs={{1,0},{2,1},{3,2},{4,3},{5,4},{6,5},{7,6},{9,8},{10,9},{11,10},{12... | collective-permute-start | bytes 1572872 | tf_op jit(solution)/shard_map/ppermute | solution.py:416
  15.5 10.7 %copy-start = (bf16[2,32,2,14,512]{4,2,3,1,0:T(2,128)(2,1)S(1)}, bf16[2,32,2,14,512]{4,2,3,1,0:T(2,128)(2,1)}, u32[]{:S(2)}) copy-start(bf16[2,32,2,14,512]{4,2,3,1,0:T(2,128)(2,1)} %param.6) | copy-start | bytes 5505028
  15.6 10.7 %copy-start.1 = (s32[2,2]{1,0:T(2,128)S(1)}, s32[2,2]{1,0:T(2,128)}, u32[]{:S(2)}) copy-start(s32[2,2]{1,0:T(2,128)} %counts_hbm.8) | copy-start | bytes 52
  15.6 7.5 %collective-permute-start.3 = (s32[256]{0:T(256)S(1)}, s32[256]{0:T(256)S(1)}, u32[]{:S(2)}, u32[]{:S(2)}) collective-permute-start(s32[256]{0:T(256)S(1)} %bitcast.19), channel_id=1, source_target_pairs={{0,16},{16,0},{1,17},{17,1},{2,18},{18,2},{3,19},{19,3},{4,20},{20... | collective-permute-start | bytes 3080 | tf_op jit(solution)/shard_map/ppermute | solution.py:420
  22.4 25.3 %collective-permute-start.4 = (bf16[2,7,160,128]{3,2,1,0:T(8,128)(2,1)}, bf16[2,7,160,128]{3,2,1,0:T(8,128)(2,1)}, u32[]{:S(2)}, u32[]{:S(2)}) collective-permute-start(bf16[2,7,160,128]{3,2,1,0:T(8,128)(2,1)} %shard_map.60), channel_id=1, source_target_pairs={{0,8},{8,0},{1,9},{9,1},{2,10},{10,2},{3,11},{11,3},{4,12},{12,4},... | collective-permute-start | bytes 1720328 | tf_op jit(solution)/shard_map/ppermute | solution.py:418
  23.1 11.8 %copy-start.2 = (f32[2]{0:T(128)S(1)}, f32[2]{0:T(128)}, u32[]{:S(2)}) copy-start(f32[2]{0:T(128)} %noise_ref.3) | copy-start | bytes 28
  38.6 9.2 %collective-permute-start.5 = (bf16[2,160,128]{2,1,0:T(8,128)(2,1)S(1)}, bf16[2,160,128]{2,1,0:T(8,128)(2,1)S(1)}, u32[]{:S(2)}, u32[]{:S(2)}) collective-permute-start(bf16[2,160,128]{2,1,0:T(8,128)(2,1)S(1)} %shard_map.59), channel_id=1, source_target_pairs={{0,8},{8,0},{1,9},{9,1},{2,10},{10,2},{3,11},{11,3},{4,12},{12,4},... | collective-permute-start | bytes 245768 | tf_op jit(solution)/shard_map/ppermute | solution.py:426
  40.9 11.2 %collective-permute-start.6 = (bf16[112,512]{1,0:T(8,128)(2,1)S(1)}, bf16[112,512]{1,0:T(8,128)(2,1)S(1)}, u32[]{:S(2)}, u32[]{:S(2)}) collective-permute-start(bf16[112,512]{1,0:T(8,128)(2,1)S(1)} %shard_map.58.refs_0_), channel_id=1, source_target_pairs={{4,16},{5,17},{6,18},{7,19},{16,4},{17,5},{18,6},{19,7},{12,24},{1... | collective-permute-start | bytes 344072 | tf_op jit(solution)/shard_map/ppermute | solution.py:446
  41.5 10.5 %collective-permute-start.8 = (bf16[112,512]{1,0:T(8,128)(2,1)S(1)}, bf16[112,512]{1,0:T(8,128)(2,1)S(1)}, u32[]{:S(2)}, u32[]{:S(2)}) collective-permute-start(bf16[112,512]{1,0:T(8,128)(2,1)S(1)} %shard_map.58.refs_0_), channel_id=1, source_target_pairs={{0,16},{1,17},{2,18},{3,19},{4,0},{5,1},{6,2},{7,3},{16,20},{17,21... | collective-permute-start | bytes 344072 | tf_op jit(solution)/shard_map/ppermute | solution.py:447
  49.9 2.2 %collective-permute-start.7 = (bf16[112,512]{1,0:T(8,128)(2,1)S(1)}, bf16[112,512]{1,0:T(8,128)(2,1)S(1)}, u32[]{:S(2)}, u32[]{:S(2)}) collective-permute-start(bf16[112,512]{1,0:T(8,128)(2,1)S(1)} %shard_map.62.refs_1_), channel_id=1, source_target_pairs={{4,16},{5,17},{6,18},{7,19},{16,4},{17,5},{18,6},{19,7},{12,24},{1... | collective-permute-start | bytes 344072 | tf_op jit(solution)/shard_map/ppermute | solution.py:446
  50.5 10.2 %collective-permute-start.9 = (bf16[112,512]{1,0:T(8,128)(2,1)S(1)}, bf16[112,512]{1,0:T(8,128)(2,1)S(1)}, u32[]{:S(2)}, u32[]{:S(2)}) collective-permute-start(bf16[112,512]{1,0:T(8,128)(2,1)S(1)} %shard_map.62.refs_1_), channel_id=1, source_target_pairs={{0,16},{1,17},{2,18},{3,19},{4,0},{5,1},{6,2},{7,3},{16,20},{17,21... | collective-permute-start | bytes 344072 | tf_op jit(solution)/shard_map/ppermute | solution.py:447
  61.2 6.1 %collective-permute-start.12 = (bf16[448,128]{1,0:T(8,128)(2,1)S(1)}, bf16[448,128]{1,0:T(8,128)(2,1)S(1)}, u32[]{:S(2)}, u32[]{:S(2)}) collective-permute-start(bf16[448,128]{1,0:T(8,128)(2,1)S(1)} %get-tuple-element.38), channel_id=1, source_target_pairs={{0,3},{1,0},{2,1},{3,2},{4,7},{5,4},{6,5},{7,6},{16,19},{17,16},{1... | collective-permute-start | bytes 344072 | tf_op jit(solution)/shard_map/ppermute | solution.py:471
  61.2 6.2 %collective-permute-start.11 = (bf16[448,128]{1,0:T(8,128)(2,1)S(1)}, bf16[448,128]{1,0:T(8,128)(2,1)S(1)}, u32[]{:S(2)}, u32[]{:S(2)}) collective-permute-start(bf16[448,128]{1,0:T(8,128)(2,1)S(1)} %get-tuple-element.37), channel_id=1, source_target_pairs={{0,2},{1,3},{2,0},{3,1},{4,6},{5,7},{6,4},{7,5},{16,18},{17,19},{1... | collective-permute-start | bytes 344072 | tf_op jit(solution)/shard_map/ppermute | solution.py:471
  63.3 6.5 %collective-permute-start.10 = (bf16[448,128]{1,0:T(8,128)(2,1)S(1)}, bf16[448,128]{1,0:T(8,128)(2,1)S(1)}, u32[]{:S(2)}, u32[]{:S(2)}) collective-permute-start(bf16[448,128]{1,0:T(8,128)(2,1)S(1)} %get-tuple-element.36), channel_id=1, source_target_pairs={{0,1},{1,2},{2,3},{3,0},{4,5},{5,6},{6,7},{7,4},{16,17},{17,18},{1... | collective-permute-start | bytes 344072 | tf_op jit(solution)/shard_map/ppermute | solution.py:471
  63.3 5.0 %collective-permute-start.13 = (bf16[1,448,128]{2,1,0:T(8,128)(2,1)S(1)}, bf16[1,448,128]{2,1,0:T(8,128)(2,1)S(1)}, u32[]{:S(2)}, u32[]{:S(2)}) collective-permute-start(bf16[1,448,128]{2,1,0:T(8,128)(2,1)S(1)} %bitcast.13), channel_id=1, source_target_pairs={{0,8},{8,0},{1,9},{9,1},{2,10},{10,2},{3,11},{11,3},{4,12},{12,4},... | collective-permute-start | bytes 344072 | tf_op jit(solution)/shard_map/ppermute | solution.py:478
  68.3 7.3 %collective-permute-start.15 = (bf16[2,448,128]{2,1,0:T(8,128)(2,1)S(1)}, bf16[2,448,128]{2,1,0:T(8,128)(2,1)S(1)}, u32[]{:S(2)}, u32[]{:S(2)}) collective-permute-start(bf16[2,448,128]{2,1,0:T(8,128)(2,1)S(1)} %pad_maximum_fusion.refs_2_), channel_id=1, source_target_pairs={{0,8},{8,0},{1,9},{9,1},{2,10},{10,2},{3,11},{11,3},{4,12},{12,4},... | collective-permute-start | bytes 688136 | tf_op jit(solution)/shard_map/ppermute | solution.py:478
  69.8 5.8 %collective-permute-start.14 = (bf16[1,448,128]{2,1,0:T(8,128)(2,1)S(1)}, bf16[1,448,128]{2,1,0:T(8,128)(2,1)S(1)}, u32[]{:S(2)}, u32[]{:S(2)}) collective-permute-start(bf16[1,448,128]{2,1,0:T(8,128)(2,1)S(1)} %bitcast.15), channel_id=1, source_target_pairs={{0,8},{8,0},{1,9},{9,1},{2,10},{10,2},{3,11},{11,3},{4,12},{12,4},... | collective-permute-start | bytes 344072 | tf_op jit(solution)/shard_map/ppermute | solution.py:478

commit v10 on v7

--- a/solution.py
+++ b/solution.py
@@ -65,30 +65,36 @@
     items = cells * number
 
     def kernel(counts_hbm, chan, samp, out, *refs):
+        end_outs, refs = (refs[:2], refs[2:]) if ends else ((), refs)
         end_refs, refs = (refs[:2], refs[2:]) if ends else ((), refs)
-        count_ref, win, ybuf, mat_a, lhs_a, mat_b, lhs_b, wsem, ysem, csem, esem = refs
+        count_ref, win, ybuf, mat_a, lhs_a, mat_b, lhs_b, wsem, ysem, csem, esem, osem = refs
         count_copy = pltpu.make_async_copy(counts_hbm, count_ref, csem)
         count_copy.start()
         panel = lax.axis_index("panel")
         side = 1 - panel if peer else panel
         start = jnp.where(side == 0, firsts[0], firsts[1])
         end_copies = [
-            pltpu.make_async_copy(chan.at[c, i * (band - 1)], end_ref.at[c, 0], esem.at[c, i])
+            pltpu.make_async_copy(chan.at[c, i * (band - 1)], end_ref.at[c], esem.at[c, i])
             for c in range(cells)
             for i, end_ref in enumerate(end_refs)
         ]
+        end_writes = [
+            pltpu.make_async_copy(end_ref.at[c], end_out.at[c, 0], osem.at[c, i])
+            for c in range(cells)
+            for i, (end_ref, end_out) in enumerate(zip(end_refs, end_outs))
+        ]
 
         def fetch(c, i):
             return pltpu.make_async_copy(chan.at[c, start - 1 + i], win.at[c, i], wsem.at[c, i])
 
-        def fetch_samples(c):
-            return pltpu.make_async_copy(samp.at[c, pl.ds(start, number)], ybuf.at[c], ysem.at[c])
+        def fetch_samples(c, i):
+            return pltpu.make_async_copy(samp.at[c, start + i], ybuf.at[c, i], ysem.at[c, i])
 
         for c in range(cells):
             for i in range(number + 2):
                 fetch(c, i).start()
-                if i == min(2, number):
-                    fetch_samples(c).start()
+                if i >= 2:
+                    fetch_samples(c, i - 2).start()
         for copy in end_copies:
             copy.start()
         lhs_a[...] = jnp.zeros_like(lhs_a)
@@ -101,11 +107,11 @@
             def _():
                 @pl.when(i == 0)
                 def _():
-                    fetch_samples(c).wait()
                     fetch(c, 0).wait()
                     fetch(c, 1).wait()
 
                 fetch(c, i + 2).wait()
+                fetch_samples(c, i).wait()
 
         def ready(item, mat, lhs):
             item = jnp.minimum(item, items - 1)
@@ -130,26 +136,33 @@
             multiply(2 * t + 1, mat_b, lhs_b)
             return carry
 
-        lax.fori_loop(0, (items + 1) // 2, step, 0)
-        for copy in end_copies:
+        steps = (items + 1) // 2
+        lax.fori_loop(0, steps // 2, step, 0)
+        for copy, write in zip(end_copies, end_writes):
             copy.wait()
+            write.start()
+        lax.fori_loop(steps // 2, steps, step, 0)
+        for write in end_writes:
+            write.wait()
 
     rows = users + 2 * SPAD
     return pl.pallas_call(
         kernel,
         in_specs=[HBM_SPEC] * 3,
-        out_specs=[VMEM_SPEC] * (1 + 2 * ends),
+        out_specs=[VMEM_SPEC] + [HBM_SPEC] * (2 * ends),
         out_shape=[jax.ShapeDtypeStruct((cells, number, rows, users), dtype)]
         + [jax.ShapeDtypeStruct((cells, 1, 2, antennas, users), BF16)] * (2 * ends),
-        scratch_shapes=[
+        scratch_shapes=[pltpu.VMEM((cells, 2, antennas, users), BF16)] * (2 * ends)
+        + [
             pltpu.SMEM(counts.shape, jnp.int32),
             pltpu.VMEM((cells, number + 2, 2, antennas, users), BF16),
             pltpu.VMEM((cells, number, symbols, 2, antennas), BF16),
             *work_buffers(antennas, users),
             *work_buffers(antennas, users),
             pltpu.SemaphoreType.DMA((cells, number + 2)),
-            pltpu.SemaphoreType.DMA((cells,)),
+            pltpu.SemaphoreType.DMA((cells, number)),
             pltpu.SemaphoreType.DMA,
+            pltpu.SemaphoreType.DMA((cells, 2)),
             pltpu.SemaphoreType.DMA((cells, 2)),
         ],
         compiler_params=pltpu.CompilerParams(vmem_limit_bytes=limit),
@@ -418,7 +431,7 @@
     samples = jnp.transpose(received, (0, 1, 3, 2, 4))
 
     inner = half - 1
-    count = inner * 2 // 5
+    count = inner // 2
     first, bottom, top = inner_gram(
         user_count, channel, samples, True, (1, half), count, BF16, limit=56 << 20, ends=True
     )

time: 70.8 us -> 68.6 us (0.969)
  Pallas kernels: 33 us -> 30.7 us
  starting transfers between devices: 26.9 us -> 28.5 us
  waiting for transfers between devices: 9.69 us -> 8.23 us
    pallas_call x3, Pallas kernels: 23.2 us -> 21 us  [inner_gram(): pl.pallas_call(kernel, in_specs=[HBM_SPEC] * 3, out_specs=[VMEM_SPEC] + [...]
    ppermute x1, waiting for transfers between devices: 0.01 us -> 1.58 us  [body(): first_peer = lax.ppermute(first, 'panel', SWAP)]
    ppermute x1, waiting for transfers between devices: 2.05 us -> 0.94 us  [body(): lax.ppermute(edge_gram(user_count, channel, samples, low, high, True, BF1...]
    ppermute x4, waiting for transfers between devices: 4.45 us -> 3.6 us  [body(): arrived.append(lax.ppermute(messages[b], ('cell', 'sc'), pairs))]
    ppermute x1, waiting for transfers between devices: 2.02 us -> 1.23 us  [body(): low = lax.ppermute(top, 'sc', [(i, i + 1) for i in range(n_sc - 1)])]
    ppermute x1, starting transfers between devices: 0.62 us -> 1.37 us  [body(): lax.ppermute(edge_gram(user_count, channel, samples, low, high, True, BF1...]
where the time goes in v10:
time: 68.6 us; the launch traced here: 68.4 us
  Pallas kernels  30.7 us (45%)
  starting transfers between devices  28.5 us (42%)
  waiting for transfers between devices  8.23 us (12%)
    pallas_call x3, Pallas kernels, inner_gram(): pl.pallas_call(kernel, in_specs=[HBM_SPEC] * 3, out_specs=[VMEM_SPEC] + [...  21 us
    ppermute x4, starting transfers between devices, body(): arrived.append(lax.ppermute(messages[b], ('cell', 'sc'), pairs))  7.01 us
    ppermute x1, starting transfers between devices, body(): lax.ppermute(jnp.stack([block[:keep] for block in arrived]), 'cell', SWAP)  5.58 us
    ppermute x2, starting transfers between devices, body(): others += [lax.ppermute(group[:, :keep], 'cell', SWAP) for group in theirs]  4.5 us
    pallas_call x2, Pallas kernels, edge_gram(): pl.pallas_call(kernel, in_specs=[HBM_SPEC] * 5, out_specs=VMEM_SPEC, out_...  3.85 us
    ppermute x4, waiting for transfers between devices, body(): arrived.append(lax.ppermute(messages[b], ('cell', 'sc'), pairs))  3.6 us
    ppermute x1, starting transfers between devices, body(): low = lax.ppermute(top, 'sc', [(i, i + 1) for i in range(n_sc - 1)])  3.45 us
    ppermute x1, starting transfers between devices, body(): first_peer = lax.ppermute(first, 'panel', SWAP)  3.01 us
  transfers between devices with their start and end apart: 14, of which 6 were waited for; matrix products, arithmetic and copies ran while one was open for 1% of the time, Pallas kernels for 31%

profile of v10, /device:TPU:0, one launch (start us, length us, event | category | flops | bytes accessed | tf_op | source)
XLA Modules:
  0.0 68.4 jit_solution(3159273117850797160)
XLA Ops:
  0.0 5.8 %shard_map.55 = (bf16[2,7,160,128]{3,2,1,0:T(8,128)(2,1)}, bf16[2,1,2,512,128]{4,3,2,1,0:T(8,128)(2,1)}, bf16[2,1,2,512,128]{4,3,2,1,0:T(8,128)(2,1)}) custom-call(s32[2,2]{1,0:T(2,128)} %counts_hbm.8, bf16[2,32,2,512,128]{4,3,2,1,0:T(8,128)(2,1)} %chan.9, bf16[2,32,14,2,512]{4,3,2,1,0:T(2,128)(2,1)} %bitcast.15), custom_call_target="tpu_custom_call" | custom-call | flops 1056964608 | bytes 4718592 | tf_op jit(solution)/shard_map/pallas_call | solution.py:149
  5.8 3.0 %collective-permute-start = (bf16[2,7,160,128]{3,2,1,0:T(8,128)(2,1)}, bf16[2,7,160,128]{3,2,1,0:T(8,128)(2,1)}, u32[]{:S(2)}, u32[]{:S(2)}) collective-permute-start(bf16[2,7,160,128]{3,2,1,0:T(8,128)(2,1)} %get-tuple-element.19), channel_id=1, source_target_pairs={{0,8},{8,0},{1,9},{9,1},{2,10},{10,2},{3,11},{11,3},{4,12},{12,4},... | collective-permute-start | bytes 1720328 | tf_op jit(solution)/shard_map/ppermute | solution.py:438
  8.8 3.4 %collective-permute-start.2 = (bf16[2,1,2,512,128]{4,3,2,1,0:T(8,128)(2,1)}, bf16[2,1,2,512,128]{4,3,2,1,0:T(8,128)(2,1)S(1)}, u32[]{:S(2)}, u32[]{:S(2)}) collective-permute-start(bf16[2,1,2,512,128]{4,3,2,1,0:T(8,128)(2,1)} %get-tuple-element.23), channel_id=1, source_target_pairs={{0,1},{1,2},{2,3},{3,4},{4,5},{5,6},{6,7},{8,9},{9,10},{10,11},{11... | collective-permute-start | bytes 1572872 | tf_op jit(solution)/shard_map/ppermute | solution.py:440
  12.3 1.4 %collective-permute-start.3 = (bf16[2,1,2,512,128]{4,3,2,1,0:T(8,128)(2,1)}, bf16[2,1,2,512,128]{4,3,2,1,0:T(8,128)(2,1)S(1)}, u32[]{:S(2)}, u32[]{:S(2)}) collective-permute-start(bf16[2,1,2,512,128]{4,3,2,1,0:T(8,128)(2,1)} %get-tuple-element.24), channel_id=1, source_target_pairs={{1,0},{2,1},{3,2},{4,3},{5,4},{6,5},{7,6},{9,8},{10,9},{11,10},{12... | collective-permute-start | bytes 1572872 | tf_op jit(solution)/shard_map/ppermute | solution.py:441
  13.7 6.2 %shard_map.57 = bf16[2,8,160,128]{3,2,1,0:T(8,128)(2,1)} custom-call(s32[2,2]{1,0:T(2,128)} %counts_hbm.8, bf16[2,32,2,512,128]{4,3,2,1,0:T(8,128)(2,1)} %chan.9, bf16[2,32,14,2,512]{4,3,2,1,0:T(2,128)(2,1)} %bitcast.16), custom_call_target="tpu_custom_call" | custom-call | flops 1207959552 | bytes 5242880 | tf_op jit(solution)/shard_map/pallas_call | solution.py:149
  20.8 1.6 %collective-permute-done.peer_ref = bf16[2,7,160,128]{3,2,1,0:T(8,128)(2,1)} collective-permute-done((bf16[2,7,160,128]{3,2,1,0:T(8,128)(2,1)}, bf16[2,7,160,128]{3,2,1,0:T(8,128)(2,1)}, u32[]{:S(2)}, u32[]{:S(2)}) %collective-permute-start) | collective-permute-done | bytes 573472 | tf_op jit(solution)/shard_map/ppermute | solution.py:438
  22.4 9.0 %shard_map.56.own_ref = f32[2,15,160,128]{3,2,1,0:T(8,128)S(1)} custom-call(s32[2,2]{1,0:T(2,128)S(1)} %copy-done.1, bf16[2,32,2,512,128]{4,3,2,1,0:T(8,128)(2,1)} %chan.9, bf16[2,32,14,2,512]{4,3,2,1,0:T(2,128)(2,1)S(1)} %bitcast.17), custom_call_target="tpu_custom_call" | custom-call | flops 141557760 | bytes 557056 | tf_op jit(solution)/shard_map/pallas_call | solution.py:149
  31.4 2.0 %shard_map.59.state_ref = f32[2,512,128]{2,1,0:T(8,128)S(1)} custom-call(f32[2]{0:T(128)S(1)} %copy-done.2, f32[2,15,160,128]{3,2,1,0:T(8,128)S(1)} %shard_map.56.own_ref, bf16[2,7,160,128]{3,2,1,0:T(8,128)(2,1)} %collective-permute-done.peer_ref), custom_call_target="tpu_custom_call" | custom-call | flops 58720256 | bytes 3686400 | tf_op jit(solution)/shard_map/pallas_call | solution.py:322
  33.4 1.2 %collective-permute-done.2.low_ref = bf16[2,1,2,512,128]{4,3,2,1,0:T(8,128)(2,1)S(1)} collective-permute-done((bf16[2,1,2,512,128]{4,3,2,1,0:T(8,128)(2,1)}, bf16[2,1,2,512,128]{4,3,2,1,0:T(8,128)(2,1)S(1)}, u32[]{:S(2)}, u32[]{:S(2)}) %collective-permute-start.2) | collective-permute-done | bytes 524320 | tf_op jit(solution)/shard_map/ppermute | solution.py:440
  34.7 1.9 %shard_map.61 = bf16[2,160,128]{2,1,0:T(8,128)(2,1)S(1)} custom-call(s32[2,2]{1,0:T(2,128)S(1)} %copy-done.1, bf16[2,32,2,512,128]{4,3,2,1,0:T(8,128)(2,1)} %chan.9, bf16[2,32,14,2,512]{4,3,2,1,0:T(2,128)(2,1)S(1)} %bitcast.18, bf16[2,1,2,512,128]{4,3,2,1,0:T(8,128)(2,1)S(1)} %collective-permute-done.2.low_ref, ...), custom_call_target="tpu_custom_call" | custom-call | flops 150994944 | bytes 1572864 | tf_op jit(solution)/shard_map/pallas_call | solution.py:260
  36.6 1.4 %collective-permute-start.4 = (bf16[2,160,128]{2,1,0:T(8,128)(2,1)S(1)}, bf16[2,160,128]{2,1,0:T(8,128)(2,1)S(1)}, u32[]{:S(2)}, u32[]{:S(2)}) collective-permute-start(bf16[2,160,128]{2,1,0:T(8,128)(2,1)S(1)} %shard_map.61), channel_id=1, source_target_pairs={{0,8},{8,0},{1,9},{9,1},{2,10},{10,2},{3,11},{11,3},{4,12},{12,4},... | collective-permute-start | bytes 245768 | tf_op jit(solution)/shard_map/ppermute | solution.py:450
  38.2 1.9 %shard_map.60.edge_own_ref = f32[2,160,128]{2,1,0:T(8,128)S(1)} custom-call(s32[2,2]{1,0:T(2,128)S(1)} %copy-done.1, bf16[2,32,2,512,128]{4,3,2,1,0:T(8,128)(2,1)} %chan.9, bf16[2,32,14,2,512]{4,3,2,1,0:T(2,128)(2,1)S(1)} %bitcast.19, bf16[2,1,2,512,128]{4,3,2,1,0:T(8,128)(2,1)S(1)} %collective-permute-done.2.low_ref, ...), custom_call_target="tpu_custom_call" | custom-call | flops 150994944 | bytes 1572864 | tf_op jit(solution)/shard_map/pallas_call | solution.py:260
  40.1 0.9 %collective-permute-done.4.edge_peer_ref = bf16[2,160,128]{2,1,0:T(8,128)(2,1)S(1)} collective-permute-done((bf16[2,160,128]{2,1,0:T(8,128)(2,1)S(1)}, bf16[2,160,128]{2,1,0:T(8,128)(2,1)S(1)}, u32[]{:S(2)}, u32[]{:S(2)}) %collective-permute-start.4) | collective-permute-done | bytes 81952 | tf_op jit(solution)/shard_map/ppermute | solution.py:450
  41.1 2.0 %shard_map.62 = (bf16[448,128]{1,0:T(8,128)(2,1)S(1)}, bf16[448,128]{1,0:T(8,128)(2,1)S(1)}, bf16[448,128]{1,0:T(8,128)(2,1)S(1)}, bf16[448,128]{1,0:T(8,128)(2,1)S(1)}) custom-call(f32[2]{0:T(128)S(1)} %copy-done.2, f32[2,15,160,128]{3,2,1,0:T(8,128)S(1)} %shard_map.56.own_ref, bf16[2,8,160,128]{3,2,1,0:T(8,128)(2,1)S(1)} %collective-permute-done.1.peer_ref, ...), custom_call_target="tpu_custom_call" | custom-call | flops 234881024 | bytes 524288 | tf_op jit(solution)/shard_map/pallas_call | solution.py:368
  43.1 2.4 %collective-permute-start.6 = (bf16[448,128]{1,0:T(8,128)(2,1)S(1)}, bf16[448,128]{1,0:T(8,128)(2,1)S(1)}, u32[]{:S(2)}, u32[]{:S(2)}) collective-permute-start(bf16[448,128]{1,0:T(8,128)(2,1)S(1)} %get-tuple-element.30), channel_id=1, source_target_pairs={{0,1},{1,2},{2,3},{3,0},{4,17},{5,18},{6,19},{7,16},{16,5},{17,6},... | collective-permute-start | bytes 344072 | tf_op jit(solution)/shard_map/ppermute | solution.py:474
  46.2 1.1 %collective-permute-start.8 = (bf16[448,128]{1,0:T(8,128)(2,1)S(1)}, bf16[448,128]{1,0:T(8,128)(2,1)S(1)}, u32[]{:S(2)}, u32[]{:S(2)}) collective-permute-start(bf16[448,128]{1,0:T(8,128)(2,1)S(1)} %get-tuple-element.32), channel_id=1, source_target_pairs={{0,3},{1,0},{2,1},{3,2},{4,19},{5,16},{6,17},{7,18},{16,7},{17,4},... | collective-permute-start | bytes 344072 | tf_op jit(solution)/shard_map/ppermute | solution.py:474
  47.3 2.8 %collective-permute-start.7 = (bf16[448,128]{1,0:T(8,128)(2,1)S(1)}, bf16[448,128]{1,0:T(8,128)(2,1)S(1)}, u32[]{:S(2)}, u32[]{:S(2)}) collective-permute-start(bf16[448,128]{1,0:T(8,128)(2,1)S(1)} %get-tuple-element.31), channel_id=1, source_target_pairs={{0,2},{1,3},{2,0},{3,1},{4,18},{5,19},{6,16},{7,17},{16,6},{17,7},... | collective-permute-start | bytes 344072 | tf_op jit(solution)/shard_map/ppermute | solution.py:474
  50.9 1.2 %collective-permute-done.8 = bf16[448,128]{1,0:T(8,128)(2,1)S(1)} collective-permute-done((bf16[448,128]{1,0:T(8,128)(2,1)S(1)}, bf16[448,128]{1,0:T(8,128)(2,1)S(1)}, u32[]{:S(2)}, u32[]{:S(2)}) %collective-permute-start.8) | collective-permute-done | bytes 114720 | tf_op jit(solution)/shard_map/ppermute | solution.py:474
  52.1 2.4 %collective-permute-done.7 = bf16[448,128]{1,0:T(8,128)(2,1)S(1)} collective-permute-done((bf16[448,128]{1,0:T(8,128)(2,1)S(1)}, bf16[448,128]{1,0:T(8,128)(2,1)S(1)}, u32[]{:S(2)}, u32[]{:S(2)}) %collective-permute-start.7) | collective-permute-done | bytes 114720 | tf_op jit(solution)/shard_map/ppermute | solution.py:474
  55.4 5.6 %collective-permute-start.11 = (bf16[4,224,128]{2,1,0:T(8,128)(2,1)S(1)}, bf16[4,224,128]{2,1,0:T(8,128)(2,1)S(1)}, u32[]{:S(2)}, u32[]{:S(2)}) collective-permute-start(bf16[4,224,128]{2,1,0:T(8,128)(2,1)S(1)} %pad_maximum_fusion.2), channel_id=1, source_target_pairs={{0,16},{16,0},{1,17},{17,1},{2,18},{18,2},{3,19},{19,3},{4,20},{20... | collective-permute-start | bytes 688136 | tf_op jit(solution)/shard_map/ppermute | solution.py:480
  61.0 2.0 %collective-permute-start.12 = (bf16[2,224,128]{2,1,0:T(8,128)(2,1)S(1)}, bf16[2,224,128]{2,1,0:T(8,128)(2,1)S(1)}, u32[]{:S(2)}, u32[]{:S(2)}) collective-permute-start(bf16[2,224,128]{2,1,0:T(8,128)(2,1)S(1)} %slice.28), channel_id=1, source_target_pairs={{0,16},{16,0},{1,17},{17,1},{2,18},{18,2},{3,19},{19,3},{4,20},{20... | collective-permute-start | bytes 344072 | tf_op jit(solution)/shard_map/ppermute | solution.py:481
  63.0 2.5 %collective-permute-start.13 = (bf16[2,224,128]{2,1,0:T(8,128)(2,1)S(1)}, bf16[2,224,128]{2,1,0:T(8,128)(2,1)S(1)}, u32[]{:S(2)}, u32[]{:S(2)}) collective-permute-start(bf16[2,224,128]{2,1,0:T(8,128)(2,1)S(1)} %slice.29), channel_id=1, source_target_pairs={{0,16},{16,0},{1,17},{17,1},{2,18},{18,2},{3,19},{19,3},{4,20},{20... | collective-permute-start | bytes 344072 | tf_op jit(solution)/shard_map/ppermute | solution.py:481
  65.6 0.9 %collective-permute-done.13.refs_6_ = bf16[2,224,128]{2,1,0:T(8,128)(2,1)S(1)} collective-permute-done((bf16[2,224,128]{2,1,0:T(8,128)(2,1)S(1)}, bf16[2,224,128]{2,1,0:T(8,128)(2,1)S(1)}, u32[]{:S(2)}, u32[]{:S(2)}) %collective-permute-start.13) | collective-permute-done | bytes 114720 | tf_op jit(solution)/shard_map/ppermute | solution.py:481
  66.5 1.9 %shard_map.63 = bf16[2,32,14,2,256]{4,3,2,1,0:T(2,128)(2,1)} custom-call(s32[8]{0:T(128)S(1)} %pad_add_fusion.1.source_ref, bf16[2,448,128]{2,1,0:T(8,128)(2,1)S(1)} %pad_maximum_fusion.refs_0_, bf16[2,448,128]{2,1,0:T(8,128)(2,1)S(1)} %pad_maximum_fusion.1.refs_1_, bf16[2,448,128]{2,1,0:T(8,128)(2,1)S(1)} %collective-permute-done.9.refs_2_, ...), custom_call_target="tpu_custom_call" | custom-call | tf_op jit(solution)/shard_map/pallas_call | solution.py:414
  (36 shorter events, 3.5 us)
Async XLA Ops:
  5.8 16.6 %collective-permute-start = (bf16[2,7,160,128]{3,2,1,0:T(8,128)(2,1)}, bf16[2,7,160,128]{3,2,1,0:T(8,128)(2,1)}, u32[]{:S(2)}, u32[]{:S(2)}) collective-permute-start(bf16[2,7,160,128]{3,2,1,0:T(8,128)(2,1)} %get-tuple-element.19), channel_id=1, source_target_pairs={{0,8},{8,0},{1,9},{9,1},{2,10},{10,2},{3,11},{11,3},{4,12},{12,4},... | collective-permute-start | bytes 1720328 | tf_op jit(solution)/shard_map/ppermute | solution.py:438
  8.8 25.9 %collective-permute-start.2 = (bf16[2,1,2,512,128]{4,3,2,1,0:T(8,128)(2,1)}, bf16[2,1,2,512,128]{4,3,2,1,0:T(8,128)(2,1)S(1)}, u32[]{:S(2)}, u32[]{:S(2)}) collective-permute-start(bf16[2,1,2,512,128]{4,3,2,1,0:T(8,128)(2,1)} %get-tuple-element.23), channel_id=1, source_target_pairs={{0,1},{1,2},{2,3},{3,4},{4,5},{5,6},{6,7},{8,9},{9,10},{10,11},{11... | collective-permute-start | bytes 1572872 | tf_op jit(solution)/shard_map/ppermute | solution.py:440
  12.3 8.3 %copy-start.3 = (s32[2,128,1]{1,2,0:T(1,128)S(1)}, s32[2,128,1]{1,2,0:T(1,128)}, u32[]{:S(2)}) copy-start(s32[2,128,1]{1,2,0:T(1,128)} %param.9) | copy-start | bytes 3076
  12.3 10.1 %copy-start = (bf16[2,32,2,14,512]{4,2,3,1,0:T(2,128)(2,1)S(1)}, bf16[2,32,2,14,512]{4,2,3,1,0:T(2,128)(2,1)}, u32[]{:S(2)}) copy-start(bf16[2,32,2,14,512]{4,2,3,1,0:T(2,128)(2,1)} %param.6) | copy-start | bytes 5505028
  12.3 10.1 %copy-start.1 = (s32[2,2]{1,0:T(2,128)S(1)}, s32[2,2]{1,0:T(2,128)}, u32[]{:S(2)}) copy-start(s32[2,2]{1,0:T(2,128)} %counts_hbm.8) | copy-start | bytes 52
  12.3 22.4 %collective-permute-start.3 = (bf16[2,1,2,512,128]{4,3,2,1,0:T(8,128)(2,1)}, bf16[2,1,2,512,128]{4,3,2,1,0:T(8,128)(2,1)S(1)}, u32[]{:S(2)}, u32[]{:S(2)}) collective-permute-start(bf16[2,1,2,512,128]{4,3,2,1,0:T(8,128)(2,1)} %get-tuple-element.24), channel_id=1, source_target_pairs={{1,0},{2,1},{3,2},{4,3},{5,4},{6,5},{7,6},{9,8},{10,9},{11,10},{12... | collective-permute-start | bytes 1572872 | tf_op jit(solution)/shard_map/ppermute | solution.py:441
  19.9 20.3 %collective-permute-start.1 = (bf16[2,8,160,128]{3,2,1,0:T(8,128)(2,1)}, bf16[2,8,160,128]{3,2,1,0:T(8,128)(2,1)S(1)}, u32[]{:S(2)}, u32[]{:S(2)}) collective-permute-start(bf16[2,8,160,128]{3,2,1,0:T(8,128)(2,1)} %shard_map.57), channel_id=1, source_target_pairs={{0,8},{8,0},{1,9},{9,1},{2,10},{10,2},{3,11},{11,3},{4,12},{12,4},... | collective-permute-start | bytes 1966088 | tf_op jit(solution)/shard_map/ppermute | solution.py:445
  20.8 10.6 %copy-start.2 = (f32[2]{0:T(128)S(1)}, f32[2]{0:T(128)}, u32[]{:S(2)}) copy-start(f32[2]{0:T(128)} %noise_ref.3) | copy-start | bytes 28
  36.6 4.5 %collective-permute-start.4 = (bf16[2,160,128]{2,1,0:T(8,128)(2,1)S(1)}, bf16[2,160,128]{2,1,0:T(8,128)(2,1)S(1)}, u32[]{:S(2)}, u32[]{:S(2)}) collective-permute-start(bf16[2,160,128]{2,1,0:T(8,128)(2,1)S(1)} %shard_map.61), channel_id=1, source_target_pairs={{0,8},{8,0},{1,9},{9,1},{2,10},{10,2},{3,11},{11,3},{4,12},{12,4},... | collective-permute-start | bytes 245768 | tf_op jit(solution)/shard_map/ppermute | solution.py:450
  43.1 7.0 %collective-permute-start.6 = (bf16[448,128]{1,0:T(8,128)(2,1)S(1)}, bf16[448,128]{1,0:T(8,128)(2,1)S(1)}, u32[]{:S(2)}, u32[]{:S(2)}) collective-permute-start(bf16[448,128]{1,0:T(8,128)(2,1)S(1)} %get-tuple-element.30), channel_id=1, source_target_pairs={{0,1},{1,2},{2,3},{3,0},{4,17},{5,18},{6,19},{7,16},{16,5},{17,6},... | collective-permute-start | bytes 344072 | tf_op jit(solution)/shard_map/ppermute | solution.py:474
  45.6 4.6 %collective-permute-start.5 = (bf16[448,128]{1,0:T(8,128)(2,1)S(1)}, bf16[448,128]{1,0:T(8,128)(2,1)S(1)}, u32[]{:S(2)}, u32[]{:S(2)}) collective-permute-start(bf16[448,128]{1,0:T(8,128)(2,1)S(1)} %get-tuple-element.29), channel_id=1, source_target_pairs={{0,0},{1,1},{2,2},{3,3},{4,16},{5,17},{6,18},{7,19},{16,4},{17,5},... | collective-permute-start | bytes 344072 | tf_op jit(solution)/shard_map/ppermute | solution.py:474
  46.2 5.9 %collective-permute-start.8 = (bf16[448,128]{1,0:T(8,128)(2,1)S(1)}, bf16[448,128]{1,0:T(8,128)(2,1)S(1)}, u32[]{:S(2)}, u32[]{:S(2)}) collective-permute-start(bf16[448,128]{1,0:T(8,128)(2,1)S(1)} %get-tuple-element.32), channel_id=1, source_target_pairs={{0,3},{1,0},{2,1},{3,2},{4,19},{5,16},{6,17},{7,18},{16,7},{17,4},... | collective-permute-start | bytes 344072 | tf_op jit(solution)/shard_map/ppermute | solution.py:474
  47.3 7.2 %collective-permute-start.7 = (bf16[448,128]{1,0:T(8,128)(2,1)S(1)}, bf16[448,128]{1,0:T(8,128)(2,1)S(1)}, u32[]{:S(2)}, u32[]{:S(2)}) collective-permute-start(bf16[448,128]{1,0:T(8,128)(2,1)S(1)} %get-tuple-element.31), channel_id=1, source_target_pairs={{0,2},{1,3},{2,0},{3,1},{4,18},{5,19},{6,16},{7,17},{16,6},{17,7},... | collective-permute-start | bytes 344072 | tf_op jit(solution)/shard_map/ppermute | solution.py:474
  50.2 10.8 %collective-permute-start.9 = (bf16[2,448,128]{2,1,0:T(8,128)(2,1)S(1)}, bf16[2,448,128]{2,1,0:T(8,128)(2,1)S(1)}, u32[]{:S(2)}, u32[]{:S(2)}) collective-permute-start(bf16[2,448,128]{2,1,0:T(8,128)(2,1)S(1)} %pad_maximum_fusion.refs_0_), channel_id=1, source_target_pairs={{0,8},{8,0},{1,9},{9,1},{2,10},{10,2},{3,11},{11,3},{4,12},{12,4},... | collective-permute-start | bytes 688136 | tf_op jit(solution)/shard_map/ppermute | solution.py:479
  54.6 8.4 %collective-permute-start.10 = (bf16[2,448,128]{2,1,0:T(8,128)(2,1)S(1)}, bf16[2,448,128]{2,1,0:T(8,128)(2,1)S(1)}, u32[]{:S(2)}, u32[]{:S(2)}) collective-permute-start(bf16[2,448,128]{2,1,0:T(8,128)(2,1)S(1)} %pad_maximum_fusion.1.refs_1_), channel_id=1, source_target_pairs={{0,8},{8,0},{1,9},{9,1},{2,10},{10,2},{3,11},{11,3},{4,12},{12,4},... | collective-permute-start | bytes 688136 | tf_op jit(solution)/shard_map/ppermute | solution.py:479
  55.4 10.2 %collective-permute-start.11 = (bf16[4,224,128]{2,1,0:T(8,128)(2,1)S(1)}, bf16[4,224,128]{2,1,0:T(8,128)(2,1)S(1)}, u32[]{:S(2)}, u32[]{:S(2)}) collective-permute-start(bf16[4,224,128]{2,1,0:T(8,128)(2,1)S(1)} %pad_maximum_fusion.2), channel_id=1, source_target_pairs={{0,16},{16,0},{1,17},{17,1},{2,18},{18,2},{3,19},{19,3},{4,20},{20... | collective-permute-start | bytes 688136 | tf_op jit(solution)/shard_map/ppermute | solution.py:480
  61.0 4.6 %collective-permute-start.12 = (bf16[2,224,128]{2,1,0:T(8,128)(2,1)S(1)}, bf16[2,224,128]{2,1,0:T(8,128)(2,1)S(1)}, u32[]{:S(2)}, u32[]{:S(2)}) collective-permute-start(bf16[2,224,128]{2,1,0:T(8,128)(2,1)S(1)} %slice.28), channel_id=1, source_target_pairs={{0,16},{16,0},{1,17},{17,1},{2,18},{18,2},{3,19},{19,3},{4,20},{20... | collective-permute-start | bytes 344072 | tf_op jit(solution)/shard_map/ppermute | solution.py:481
  63.0 3.5 %collective-permute-start.13 = (bf16[2,224,128]{2,1,0:T(8,128)(2,1)S(1)}, bf16[2,224,128]{2,1,0:T(8,128)(2,1)S(1)}, u32[]{:S(2)}, u32[]{:S(2)}) collective-permute-start(bf16[2,224,128]{2,1,0:T(8,128)(2,1)S(1)} %slice.29), channel_id=1, source_target_pairs={{0,16},{16,0},{1,17},{17,1},{2,18},{18,2},{3,19},{19,3},{4,20},{20... | collective-permute-start | bytes 344072 | tf_op jit(solution)/shard_map/ppermute | solution.py:481

commit v11 on v10

--- a/solution.py
+++ b/solution.py
@@ -70,11 +70,11 @@
         count_ref, win, ybuf, mat_a, lhs_a, mat_b, lhs_b, wsem, ysem, csem, esem, osem = refs
         count_copy = pltpu.make_async_copy(counts_hbm, count_ref, csem)
         count_copy.start()
-        panel = lax.axis_index("panel")
+        panel, sc = lax.axis_index("panel"), lax.axis_index("sc")
         side = 1 - panel if peer else panel
         start = jnp.where(side == 0, firsts[0], firsts[1])
         end_copies = [
-            pltpu.make_async_copy(chan.at[c, i * (band - 1)], end_ref.at[c], esem.at[c, i])
+            pltpu.make_async_copy(chan.at[c, (band - 1) * ((sc + i + 1) % 2)], end_ref.at[c], esem.at[c, i])
             for c in range(cells)
             for i, end_ref in enumerate(end_refs)
         ]
@@ -203,30 +203,32 @@
     ]
 
 
-def edge_work(side, counts_hbm, chan, samp, low_ref, high_ref, out, scratch):
+def edge_work(side, counts_hbm, chan, samp, near_ref, far_ref, out, scratch):
     count_ref, win, ybuf, mat_a, lhs_a, mat_b, lhs_b, wsem, ysem, csem = scratch
     count_copy = pltpu.make_async_copy(counts_hbm, count_ref, csem)
     cells, band, _, _, users = chan.shape
     buffers = ((mat_a, lhs_a), (mat_b, lhs_b))
 
     def each_copy(act):
-        def run(e):
+        def run(e, halo_ref):
             for c in range(cells):
                 blocks = (
-                    (low_ref.at[c, 0], chan.at[c, 0], chan.at[c, 1]),
-                    (chan.at[c, band - 2], chan.at[c, band - 1], high_ref.at[c, 0]),
+                    (halo_ref.at[c, 0], chan.at[c, 0], chan.at[c, 1]),
+                    (chan.at[c, band - 2], chan.at[c, band - 1], halo_ref.at[c, 0]),
                 )[e]
                 for i, block in enumerate(blocks):
                     act(pltpu.make_async_copy(block, win.at[c, i], wsem.at[c, i]))
                 act(pltpu.make_async_copy(samp.at[c, e * (band - 1)], ybuf.at[c], ysem.at[c]))
 
-        @pl.when(side == 0)
-        def _():
-            run(0)
-
-        @pl.when(side == 1)
-        def _():
-            run(1)
+        odd = lax.axis_index("sc") % 2
+        for e in range(2):
+            @pl.when((side == e) & (odd != e))
+            def _(e=e):
+                run(e, near_ref)
+
+            @pl.when((side == e) & (odd == e))
+            def _(e=e):
+                run(e, far_ref)
 
     def fetch():
         count_copy.start()
@@ -247,13 +249,13 @@
     return fetch, work
 
 
-def edge_gram(counts, channel, received, low, high, peer, dtype):
+def edge_gram(counts, channel, received, near, far, peer, dtype):
     cells, _, _, antennas, users = channel.shape
     symbols = received.shape[2]
 
-    def kernel(counts_hbm, chan, samp, low_ref, high_ref, out, *scratch):
+    def kernel(counts_hbm, chan, samp, near_ref, far_ref, out, *scratch):
         panel = lax.axis_index("panel")
-        fetch, work = edge_work(1 - panel if peer else panel, counts_hbm, chan, samp, low_ref, high_ref, out, scratch)
+        fetch, work = edge_work(1 - panel if peer else panel, counts_hbm, chan, samp, near_ref, far_ref, out, scratch)
         fetch()
         work()
 
@@ -269,7 +271,7 @@
             bytes_accessed=cells * 12 * antennas * users,
             transcendentals=0,
         ),
-    )(counts, channel, received, low, high)
+    )(counts, channel, received, near, far)
 
 
 def conjugate_gradient(sums, noises, users):
@@ -431,14 +433,14 @@
     samples = jnp.transpose(received, (0, 1, 3, 2, 4))
 
     inner = half - 1
-    count = inner // 2
-    first, bottom, top = inner_gram(
+    count = inner * 2 // 5
+    first, near, far = inner_gram(
         user_count, channel, samples, True, (1, half), count, BF16, limit=56 << 20, ends=True
     )
     first_peer = lax.ppermute(first, "panel", SWAP)
-    bottom, top = hand_on([bottom, top])
-    low = lax.ppermute(top, "sc", [(i, i + 1) for i in range(n_sc - 1)])
-    high = lax.ppermute(bottom, "sc", [(i + 1, i) for i in range(n_sc - 1)])
+    near, far = hand_on([near, far])
+    near = lax.ppermute(near, "sc", [(i, i ^ 1) for i in range(n_sc)])
+    far = lax.ppermute(far, "sc", [(i, ((i - 1) ^ 1) + 1) for i in range(1, n_sc - 1)])
     (second,) = inner_gram(
         user_count, channel, samples, True, (1 + count, half + count), inner - count, BF16, limit=56 << 20
     )
@@ -446,9 +448,9 @@
     counts, first_peer = lax.optimization_barrier((user_count, first_peer))
     (own,) = inner_gram(counts, channel, samples, False, (1, half), inner, F32)
     state = detect_first(noise_power, own, first_peer)
-    low, high, state = lax.optimization_barrier((low, high, state))
-    edge_peer = lax.ppermute(edge_gram(user_count, channel, samples, low, high, True, BF16), "panel", SWAP)
-    edge_own = edge_gram(user_count, channel, samples, low, high, False, F32)
+    near, far, state = lax.optimization_barrier((near, far, state))
+    edge_peer = lax.ppermute(edge_gram(user_count, channel, samples, near, far, True, BF16), "panel", SWAP)
+    edge_own = edge_gram(user_count, channel, samples, near, far, False, F32)
 
     capacity = cells * users // n_cell
     per_device = n_cell * capacity // n_sc

time: 68.6 us -> 66 us (0.962)
  starting transfers between devices: 28.5 us -> 24.2 us
  waiting for transfers between devices: 8.23 us -> 9.87 us
    ppermute x3, starting transfers between devices: 6.24 us -> 3.22 us  [the longest x1 1.52 us: body(): near = lax.ppermute(near, 'sc', [(i, i ^ 1) for i in range(n_sc)])]
    ppermute x4, starting transfers between devices: 7.01 us -> 6.12 us  [body(): arrived.append(lax.ppermute(messages[b], ('cell', 'sc'), pairs))]
    ppermute x3, waiting for transfers between devices: 2.17 us -> 3.03 us  [the longest x1 1.61 us: body(): near = lax.ppermute(near, 'sc', [(i, i ^ 1) for i in range(n_sc)])]
    ppermute x2, starting transfers between devices: 1.5 us -> 0.67 us  [body(): theirs = [lax.ppermute(group, 'panel', SWAP) for group in mine]]
  transfers between devices with their start and end apart: 14 -> 14, of which waited for: 6 -> 7; matrix products, arithmetic and copies ran while one was open for 1% -> 1% of each run, Pallas kernels for 31% -> 32%
where the time goes in v11:
time: 66 us; the launch traced here: 65.8 us
  Pallas kernels  30.9 us (47%)
  starting transfers between devices  24.2 us (37%)
  waiting for transfers between devices  9.87 us (15%)
    pallas_call x3, Pallas kernels, inner_gram(): pl.pallas_call(kernel, in_specs=[HBM_SPEC] * 3, out_specs=[VMEM_SPEC] + [...  21.1 us
    ppermute x4, starting transfers between devices, body(): arrived.append(lax.ppermute(messages[b], ('cell', 'sc'), pairs))  6.12 us
    ppermute x1, starting transfers between devices, body(): lax.ppermute(jnp.stack([block[:keep] for block in arrived]), 'cell', SWAP)  6.01 us
    ppermute x2, starting transfers between devices, body(): others += [lax.ppermute(group[:, :keep], 'cell', SWAP) for group in theirs]  4.62 us
    ppermute x4, waiting for transfers between devices, body(): arrived.append(lax.ppermute(messages[b], ('cell', 'sc'), pairs))  3.99 us
    pallas_call x2, Pallas kernels, edge_gram(): pl.pallas_call(kernel, in_specs=[HBM_SPEC] * 5, out_specs=VMEM_SPEC, out_...  3.85 us
    ppermute x1, starting transfers between devices, body(): first_peer = lax.ppermute(first, 'panel', SWAP)  3.01 us
    pallas_call x1, Pallas kernels, detect_last(): pl.pallas_call(kernel, in_specs=[SMEM_SPEC] + [VMEM_SPEC] * 6, out_specs=...  2.71 us
  transfers between devices with their start and end apart: 14, of which 7 were waited for; matrix products, arithmetic and copies ran while one was open for 1% of the time, Pallas kernels for 32%

profile of v11, /device:TPU:0, one launch (start us, length us, event | category | flops | bytes accessed | tf_op | source)
XLA Modules:
  0.0 65.8 jit_solution(13682967604955988132)
XLA Ops:
  0.0 5.2 %shard_map.55 = (bf16[2,6,160,128]{3,2,1,0:T(8,128)(2,1)}, bf16[2,1,2,512,128]{4,3,2,1,0:T(8,128)(2,1)}, bf16[2,1,2,512,128]{4,3,2,1,0:T(8,128)(2,1)}) custom-call(s32[2,2]{1,0:T(2,128)} %counts_hbm.8, bf16[2,32,2,512,128]{4,3,2,1,0:T(8,128)(2,1)} %chan.9, bf16[2,32,14,2,512]{4,3,2,1,0:T(2,128)(2,1)} %bitcast.15), custom_call_target="tpu_custom_call" | custom-call | flops 905969664 | bytes 4194304 | tf_op jit(solution)/shard_map/pallas_call | solution.py:149
  5.2 3.0 %collective-permute-start = (bf16[2,6,160,128]{3,2,1,0:T(8,128)(2,1)}, bf16[2,6,160,128]{3,2,1,0:T(8,128)(2,1)S(1)}, u32[]{:S(2)}, u32[]{:S(2)}) collective-permute-start(bf16[2,6,160,128]{3,2,1,0:T(8,128)(2,1)} %get-tuple-element.19), channel_id=1, source_target_pairs={{0,8},{8,0},{1,9},{9,1},{2,10},{10,2},{3,11},{11,3},{4,12},{12,4},... | collective-permute-start | bytes 1474568 | tf_op jit(solution)/shard_map/ppermute | solution.py:440
  8.3 1.5 %collective-permute-start.2 = (bf16[2,1,2,512,128]{4,3,2,1,0:T(8,128)(2,1)}, bf16[2,1,2,512,128]{4,3,2,1,0:T(8,128)(2,1)S(1)}, u32[]{:S(2)}, u32[]{:S(2)}) collective-permute-start(bf16[2,1,2,512,128]{4,3,2,1,0:T(8,128)(2,1)} %get-tuple-element.23), channel_id=1, source_target_pairs={{0,1},{1,0},{2,3},{3,2},{4,5},{5,4},{6,7},{7,6},{8,9},{9,8},{10,11... | collective-permute-start | bytes 1572872 | tf_op jit(solution)/shard_map/ppermute | solution.py:442
  10.6 6.8 %shard_map.57 = bf16[2,9,160,128]{3,2,1,0:T(8,128)(2,1)} custom-call(s32[2,2]{1,0:T(2,128)} %counts_hbm.8, bf16[2,32,2,512,128]{4,3,2,1,0:T(8,128)(2,1)} %chan.9, bf16[2,32,14,2,512]{4,3,2,1,0:T(2,128)(2,1)} %bitcast.16), custom_call_target="tpu_custom_call" | custom-call | flops 1358954496 | bytes 5767168 | tf_op jit(solution)/shard_map/pallas_call | solution.py:149
  18.2 2.0 %collective-permute-done.peer_ref = bf16[2,6,160,128]{3,2,1,0:T(8,128)(2,1)S(1)} collective-permute-done((bf16[2,6,160,128]{3,2,1,0:T(8,128)(2,1)}, bf16[2,6,160,128]{3,2,1,0:T(8,128)(2,1)S(1)}, u32[]{:S(2)}, u32[]{:S(2)}) %collective-permute-start) | collective-permute-done | bytes 491552 | tf_op jit(solution)/shard_map/ppermute | solution.py:440
  20.2 9.0 %shard_map.56.own_ref = f32[2,15,160,128]{3,2,1,0:T(8,128)S(1)} custom-call(s32[2,2]{1,0:T(2,128)S(1)} %copy-done.1, bf16[2,32,2,512,128]{4,3,2,1,0:T(8,128)(2,1)} %chan.9, bf16[2,32,14,2,512]{4,3,2,1,0:T(2,128)(2,1)S(1)} %bitcast.17), custom_call_target="tpu_custom_call" | custom-call | flops 141557760 | bytes 557056 | tf_op jit(solution)/shard_map/pallas_call | solution.py:149
  29.3 1.4 %shard_map.59.state_ref = f32[2,512,128]{2,1,0:T(8,128)S(1)} custom-call(f32[2]{0:T(128)S(1)} %copy-done.2, f32[2,15,160,128]{3,2,1,0:T(8,128)S(1)} %shard_map.56.own_ref, bf16[2,6,160,128]{3,2,1,0:T(8,128)(2,1)S(1)} %collective-permute-done.peer_ref), custom_call_target="tpu_custom_call" | custom-call | flops 50331648 | bytes 3686400 | tf_op jit(solution)/shard_map/pallas_call | solution.py:324
  30.6 1.6 %collective-permute-done.2.near_ref = bf16[2,1,2,512,128]{4,3,2,1,0:T(8,128)(2,1)S(1)} collective-permute-done((bf16[2,1,2,512,128]{4,3,2,1,0:T(8,128)(2,1)}, bf16[2,1,2,512,128]{4,3,2,1,0:T(8,128)(2,1)S(1)}, u32[]{:S(2)}, u32[]{:S(2)}) %collective-permute-start.2) | collective-permute-done | bytes 524320 | tf_op jit(solution)/shard_map/ppermute | solution.py:442
  32.2 1.9 %shard_map.61 = bf16[2,160,128]{2,1,0:T(8,128)(2,1)S(1)} custom-call(s32[2,2]{1,0:T(2,128)S(1)} %copy-done.1, bf16[2,32,2,512,128]{4,3,2,1,0:T(8,128)(2,1)} %chan.9, bf16[2,32,14,2,512]{4,3,2,1,0:T(2,128)(2,1)S(1)} %bitcast.18, bf16[2,1,2,512,128]{4,3,2,1,0:T(8,128)(2,1)S(1)} %collective-permute-done.2.near_ref, ...), custom_call_target="tpu_custom_call" | custom-call | flops 150994944 | bytes 1572864 | tf_op jit(solution)/shard_map/pallas_call | solution.py:262
  34.1 0.9 %collective-permute-start.4 = (bf16[2,160,128]{2,1,0:T(8,128)(2,1)S(1)}, bf16[2,160,128]{2,1,0:T(8,128)(2,1)S(1)}, u32[]{:S(2)}, u32[]{:S(2)}) collective-permute-start(bf16[2,160,128]{2,1,0:T(8,128)(2,1)S(1)} %shard_map.61), channel_id=1, source_target_pairs={{0,8},{8,0},{1,9},{9,1},{2,10},{10,2},{3,11},{11,3},{4,12},{12,4},... | collective-permute-start | bytes 245768 | tf_op jit(solution)/shard_map/ppermute | solution.py:452
  35.3 1.9 %shard_map.60.edge_own_ref = f32[2,160,128]{2,1,0:T(8,128)S(1)} custom-call(s32[2,2]{1,0:T(2,128)S(1)} %copy-done.1, bf16[2,32,2,512,128]{4,3,2,1,0:T(8,128)(2,1)} %chan.9, bf16[2,32,14,2,512]{4,3,2,1,0:T(2,128)(2,1)S(1)} %bitcast.19, bf16[2,1,2,512,128]{4,3,2,1,0:T(8,128)(2,1)S(1)} %collective-permute-done.2.near_ref, ...), custom_call_target="tpu_custom_call" | custom-call | flops 150994944 | bytes 1572864 | tf_op jit(solution)/shard_map/pallas_call | solution.py:262
  37.2 1.4 %collective-permute-done.4.edge_peer_ref = bf16[2,160,128]{2,1,0:T(8,128)(2,1)S(1)} collective-permute-done((bf16[2,160,128]{2,1,0:T(8,128)(2,1)S(1)}, bf16[2,160,128]{2,1,0:T(8,128)(2,1)S(1)}, u32[]{:S(2)}, u32[]{:S(2)}) %collective-permute-start.4) | collective-permute-done | bytes 81952 | tf_op jit(solution)/shard_map/ppermute | solution.py:452
  38.7 2.7 %shard_map.62 = (bf16[448,128]{1,0:T(8,128)(2,1)S(1)}, bf16[448,128]{1,0:T(8,128)(2,1)S(1)}, bf16[448,128]{1,0:T(8,128)(2,1)S(1)}, bf16[448,128]{1,0:T(8,128)(2,1)S(1)}) custom-call(f32[2]{0:T(128)S(1)} %copy-done.2, f32[2,15,160,128]{3,2,1,0:T(8,128)S(1)} %shard_map.56.own_ref, bf16[2,9,160,128]{3,2,1,0:T(8,128)(2,1)} %collective-permute-done.1.peer_ref, ...), custom_call_target="tpu_custom_call" | custom-call | flops 234881024 | bytes 524288 | tf_op jit(solution)/shard_map/pallas_call | solution.py:370
  41.4 2.5 %collective-permute-start.6 = (bf16[448,128]{1,0:T(8,128)(2,1)S(1)}, bf16[448,128]{1,0:T(8,128)(2,1)S(1)}, u32[]{:S(2)}, u32[]{:S(2)}) collective-permute-start(bf16[448,128]{1,0:T(8,128)(2,1)S(1)} %get-tuple-element.30), channel_id=1, source_target_pairs={{0,1},{1,2},{2,3},{3,0},{4,17},{5,18},{6,19},{7,16},{16,5},{17,6},... | collective-permute-start | bytes 344072 | tf_op jit(solution)/shard_map/ppermute | solution.py:476
  44.5 1.1 %collective-permute-start.8 = (bf16[448,128]{1,0:T(8,128)(2,1)S(1)}, bf16[448,128]{1,0:T(8,128)(2,1)S(1)}, u32[]{:S(2)}, u32[]{:S(2)}) collective-permute-start(bf16[448,128]{1,0:T(8,128)(2,1)S(1)} %get-tuple-element.32), channel_id=1, source_target_pairs={{0,3},{1,0},{2,1},{3,2},{4,19},{5,16},{6,17},{7,18},{16,7},{17,4},... | collective-permute-start | bytes 344072 | tf_op jit(solution)/shard_map/ppermute | solution.py:476
  45.6 1.9 %collective-permute-start.7 = (bf16[448,128]{1,0:T(8,128)(2,1)S(1)}, bf16[448,128]{1,0:T(8,128)(2,1)S(1)}, u32[]{:S(2)}, u32[]{:S(2)}) collective-permute-start(bf16[448,128]{1,0:T(8,128)(2,1)S(1)} %get-tuple-element.31), channel_id=1, source_target_pairs={{0,2},{1,3},{2,0},{3,1},{4,18},{5,19},{6,16},{7,17},{16,6},{17,7},... | collective-permute-start | bytes 344072 | tf_op jit(solution)/shard_map/ppermute | solution.py:476
  47.5 1.4 %collective-permute-done.6 = bf16[448,128]{1,0:T(8,128)(2,1)S(1)} collective-permute-done((bf16[448,128]{1,0:T(8,128)(2,1)S(1)}, bf16[448,128]{1,0:T(8,128)(2,1)S(1)}, u32[]{:S(2)}, u32[]{:S(2)}) %collective-permute-start.6) | collective-permute-done | bytes 114720 | tf_op jit(solution)/shard_map/ppermute | solution.py:476
  49.0 1.0 %collective-permute-done.8 = bf16[448,128]{1,0:T(8,128)(2,1)S(1)} collective-permute-done((bf16[448,128]{1,0:T(8,128)(2,1)S(1)}, bf16[448,128]{1,0:T(8,128)(2,1)S(1)}, u32[]{:S(2)}, u32[]{:S(2)}) %collective-permute-start.8) | collective-permute-done | bytes 114720 | tf_op jit(solution)/shard_map/ppermute | solution.py:476
  50.1 1.5 %collective-permute-done.7 = bf16[448,128]{1,0:T(8,128)(2,1)S(1)} collective-permute-done((bf16[448,128]{1,0:T(8,128)(2,1)S(1)}, bf16[448,128]{1,0:T(8,128)(2,1)S(1)}, u32[]{:S(2)}, u32[]{:S(2)}) %collective-permute-start.7) | collective-permute-done | bytes 114720 | tf_op jit(solution)/shard_map/ppermute | solution.py:476
  52.3 6.0 %collective-permute-start.11 = (bf16[4,224,128]{2,1,0:T(8,128)(2,1)S(1)}, bf16[4,224,128]{2,1,0:T(8,128)(2,1)S(1)}, u32[]{:S(2)}, u32[]{:S(2)}) collective-permute-start(bf16[4,224,128]{2,1,0:T(8,128)(2,1)S(1)} %pad_maximum_fusion.2), channel_id=1, source_target_pairs={{0,16},{16,0},{1,17},{17,1},{2,18},{18,2},{3,19},{19,3},{4,20},{20... | collective-permute-start | bytes 688136 | tf_op jit(solution)/shard_map/ppermute | solution.py:482
  58.3 2.2 %collective-permute-start.12 = (bf16[2,224,128]{2,1,0:T(8,128)(2,1)S(1)}, bf16[2,224,128]{2,1,0:T(8,128)(2,1)S(1)}, u32[]{:S(2)}, u32[]{:S(2)}) collective-permute-start(bf16[2,224,128]{2,1,0:T(8,128)(2,1)S(1)} %slice.28), channel_id=1, source_target_pairs={{0,16},{16,0},{1,17},{17,1},{2,18},{18,2},{3,19},{19,3},{4,20},{20... | collective-permute-start | bytes 344072 | tf_op jit(solution)/shard_map/ppermute | solution.py:483
  60.5 2.4 %collective-permute-start.13 = (bf16[2,224,128]{2,1,0:T(8,128)(2,1)S(1)}, bf16[2,224,128]{2,1,0:T(8,128)(2,1)S(1)}, u32[]{:S(2)}, u32[]{:S(2)}) collective-permute-start(bf16[2,224,128]{2,1,0:T(8,128)(2,1)S(1)} %slice.29), channel_id=1, source_target_pairs={{0,16},{16,0},{1,17},{17,1},{2,18},{18,2},{3,19},{19,3},{4,20},{20... | collective-permute-start | bytes 344072 | tf_op jit(solution)/shard_map/ppermute | solution.py:483
  63.1 0.9 %collective-permute-done.13.refs_6_ = bf16[2,224,128]{2,1,0:T(8,128)(2,1)S(1)} collective-permute-done((bf16[2,224,128]{2,1,0:T(8,128)(2,1)S(1)}, bf16[2,224,128]{2,1,0:T(8,128)(2,1)S(1)}, u32[]{:S(2)}, u32[]{:S(2)}) %collective-permute-start.13) | collective-permute-done | bytes 114720 | tf_op jit(solution)/shard_map/ppermute | solution.py:483
  63.9 1.9 %shard_map.63 = bf16[2,32,14,2,256]{4,3,2,1,0:T(2,128)(2,1)} custom-call(s32[8]{0:T(128)S(1)} %pad_add_fusion.1.source_ref, bf16[2,448,128]{2,1,0:T(8,128)(2,1)S(1)} %pad_maximum_fusion.refs_0_, bf16[2,448,128]{2,1,0:T(8,128)(2,1)S(1)} %pad_maximum_fusion.1.refs_1_, bf16[2,448,128]{2,1,0:T(8,128)(2,1)S(1)} %collective-permute-done.9.refs_2_, ...), custom_call_target="tpu_custom_call" | custom-call | tf_op jit(solution)/shard_map/pallas_call | solution.py:416
  (36 shorter events, 3.4 us)
Async XLA Ops:
  5.2 15.0 %collective-permute-start = (bf16[2,6,160,128]{3,2,1,0:T(8,128)(2,1)}, bf16[2,6,160,128]{3,2,1,0:T(8,128)(2,1)S(1)}, u32[]{:S(2)}, u32[]{:S(2)}) collective-permute-start(bf16[2,6,160,128]{3,2,1,0:T(8,128)(2,1)} %get-tuple-element.19), channel_id=1, source_target_pairs={{0,8},{8,0},{1,9},{9,1},{2,10},{10,2},{3,11},{11,3},{4,12},{12,4},... | collective-permute-start | bytes 1474568 | tf_op jit(solution)/shard_map/ppermute | solution.py:440
  8.3 24.0 %collective-permute-start.2 = (bf16[2,1,2,512,128]{4,3,2,1,0:T(8,128)(2,1)}, bf16[2,1,2,512,128]{4,3,2,1,0:T(8,128)(2,1)S(1)}, u32[]{:S(2)}, u32[]{:S(2)}) collective-permute-start(bf16[2,1,2,512,128]{4,3,2,1,0:T(8,128)(2,1)} %get-tuple-element.23), channel_id=1, source_target_pairs={{0,1},{1,0},{2,3},{3,2},{4,5},{5,4},{6,7},{7,6},{8,9},{9,8},{10,11... | collective-permute-start | bytes 1572872 | tf_op jit(solution)/shard_map/ppermute | solution.py:442
  9.8 8.2 %copy-start.3 = (s32[2,128,1]{1,2,0:T(1,128)S(1)}, s32[2,128,1]{1,2,0:T(1,128)}, u32[]{:S(2)}) copy-start(s32[2,128,1]{1,2,0:T(1,128)} %param.9) | copy-start | bytes 3076
  9.8 10.4 %copy-start = (bf16[2,32,2,14,512]{4,2,3,1,0:T(2,128)(2,1)S(1)}, bf16[2,32,2,14,512]{4,2,3,1,0:T(2,128)(2,1)}, u32[]{:S(2)}) copy-start(bf16[2,32,2,14,512]{4,2,3,1,0:T(2,128)(2,1)} %param.6) | copy-start | bytes 5505028
  9.8 10.4 %copy-start.1 = (s32[2,2]{1,0:T(2,128)S(1)}, s32[2,2]{1,0:T(2,128)}, u32[]{:S(2)}) copy-start(s32[2,2]{1,0:T(2,128)} %counts_hbm.8) | copy-start | bytes 52
  9.8 22.4 %collective-permute-start.3 = (bf16[2,1,2,512,128]{4,3,2,1,0:T(8,128)(2,1)}, bf16[2,1,2,512,128]{4,3,2,1,0:T(8,128)(2,1)S(1)}, u32[]{:S(2)}, u32[]{:S(2)}) collective-permute-start(bf16[2,1,2,512,128]{4,3,2,1,0:T(8,128)(2,1)} %get-tuple-element.24), channel_id=1, source_target_pairs={{1,2},{2,1},{3,4},{4,3},{5,6},{6,5},{9,10},{10,9},{11,12},{12,11},... | collective-permute-start | bytes 1572872 | tf_op jit(solution)/shard_map/ppermute | solution.py:443
  17.4 21.3 %collective-permute-start.1 = (bf16[2,9,160,128]{3,2,1,0:T(8,128)(2,1)}, bf16[2,9,160,128]{3,2,1,0:T(8,128)(2,1)}, u32[]{:S(2)}, u32[]{:S(2)}) collective-permute-start(bf16[2,9,160,128]{3,2,1,0:T(8,128)(2,1)} %shard_map.57), channel_id=1, source_target_pairs={{0,8},{8,0},{1,9},{9,1},{2,10},{10,2},{3,11},{11,3},{4,12},{12,4},... | collective-permute-start | bytes 2211848 | tf_op jit(solution)/shard_map/ppermute | solution.py:447
  18.2 11.0 %copy-start.2 = (f32[2]{0:T(128)S(1)}, f32[2]{0:T(128)}, u32[]{:S(2)}) copy-start(f32[2]{0:T(128)} %noise_ref.3) | copy-start | bytes 28
  34.1 4.5 %collective-permute-start.4 = (bf16[2,160,128]{2,1,0:T(8,128)(2,1)S(1)}, bf16[2,160,128]{2,1,0:T(8,128)(2,1)S(1)}, u32[]{:S(2)}, u32[]{:S(2)}) collective-permute-start(bf16[2,160,128]{2,1,0:T(8,128)(2,1)S(1)} %shard_map.61), channel_id=1, source_target_pairs={{0,8},{8,0},{1,9},{9,1},{2,10},{10,2},{3,11},{11,3},{4,12},{12,4},... | collective-permute-start | bytes 245768 | tf_op jit(solution)/shard_map/ppermute | solution.py:452
  41.4 7.6 %collective-permute-start.6 = (bf16[448,128]{1,0:T(8,128)(2,1)S(1)}, bf16[448,128]{1,0:T(8,128)(2,1)S(1)}, u32[]{:S(2)}, u32[]{:S(2)}) collective-permute-start(bf16[448,128]{1,0:T(8,128)(2,1)S(1)} %get-tuple-element.30), channel_id=1, source_target_pairs={{0,1},{1,2},{2,3},{3,0},{4,17},{5,18},{6,19},{7,16},{16,5},{17,6},... | collective-permute-start | bytes 344072 | tf_op jit(solution)/shard_map/ppermute | solution.py:476
  43.8 5.1 %collective-permute-start.5 = (bf16[448,128]{1,0:T(8,128)(2,1)S(1)}, bf16[448,128]{1,0:T(8,128)(2,1)S(1)}, u32[]{:S(2)}, u32[]{:S(2)}) collective-permute-start(bf16[448,128]{1,0:T(8,128)(2,1)S(1)} %get-tuple-element.29), channel_id=1, source_target_pairs={{0,0},{1,1},{2,2},{3,3},{4,16},{5,17},{6,18},{7,19},{16,4},{17,5},... | collective-permute-start | bytes 344072 | tf_op jit(solution)/shard_map/ppermute | solution.py:476
  44.5 5.6 %collective-permute-start.8 = (bf16[448,128]{1,0:T(8,128)(2,1)S(1)}, bf16[448,128]{1,0:T(8,128)(2,1)S(1)}, u32[]{:S(2)}, u32[]{:S(2)}) collective-permute-start(bf16[448,128]{1,0:T(8,128)(2,1)S(1)} %get-tuple-element.32), channel_id=1, source_target_pairs={{0,3},{1,0},{2,1},{3,2},{4,19},{5,16},{6,17},{7,18},{16,7},{17,4},... | collective-permute-start | bytes 344072 | tf_op jit(solution)/shard_map/ppermute | solution.py:476
  45.6 6.0 %collective-permute-start.7 = (bf16[448,128]{1,0:T(8,128)(2,1)S(1)}, bf16[448,128]{1,0:T(8,128)(2,1)S(1)}, u32[]{:S(2)}, u32[]{:S(2)}) collective-permute-start(bf16[448,128]{1,0:T(8,128)(2,1)S(1)} %get-tuple-element.31), channel_id=1, source_target_pairs={{0,2},{1,3},{2,0},{3,1},{4,18},{5,19},{6,16},{7,17},{16,6},{17,7},... | collective-permute-start | bytes 344072 | tf_op jit(solution)/shard_map/ppermute | solution.py:476
  49.0 9.3 %collective-permute-start.9 = (bf16[2,448,128]{2,1,0:T(8,128)(2,1)S(1)}, bf16[2,448,128]{2,1,0:T(8,128)(2,1)S(1)}, u32[]{:S(2)}, u32[]{:S(2)}) collective-permute-start(bf16[2,448,128]{2,1,0:T(8,128)(2,1)S(1)} %pad_maximum_fusion.refs_0_), channel_id=1, source_target_pairs={{0,8},{8,0},{1,9},{9,1},{2,10},{10,2},{3,11},{11,3},{4,12},{12,4},... | collective-permute-start | bytes 688136 | tf_op jit(solution)/shard_map/ppermute | solution.py:481
  51.6 8.9 %collective-permute-start.10 = (bf16[2,448,128]{2,1,0:T(8,128)(2,1)S(1)}, bf16[2,448,128]{2,1,0:T(8,128)(2,1)S(1)}, u32[]{:S(2)}, u32[]{:S(2)}) collective-permute-start(bf16[2,448,128]{2,1,0:T(8,128)(2,1)S(1)} %pad_maximum_fusion.1.refs_1_), channel_id=1, source_target_pairs={{0,8},{8,0},{1,9},{9,1},{2,10},{10,2},{3,11},{11,3},{4,12},{12,4},... | collective-permute-start | bytes 688136 | tf_op jit(solution)/shard_map/ppermute | solution.py:481
  52.3 10.8 %collective-permute-start.11 = (bf16[4,224,128]{2,1,0:T(8,128)(2,1)S(1)}, bf16[4,224,128]{2,1,0:T(8,128)(2,1)S(1)}, u32[]{:S(2)}, u32[]{:S(2)}) collective-permute-start(bf16[4,224,128]{2,1,0:T(8,128)(2,1)S(1)} %pad_maximum_fusion.2), channel_id=1, source_target_pairs={{0,16},{16,0},{1,17},{17,1},{2,18},{18,2},{3,19},{19,3},{4,20},{20... | collective-permute-start | bytes 688136 | tf_op jit(solution)/shard_map/ppermute | solution.py:482
  58.3 4.7 %collective-permute-start.12 = (bf16[2,224,128]{2,1,0:T(8,128)(2,1)S(1)}, bf16[2,224,128]{2,1,0:T(8,128)(2,1)S(1)}, u32[]{:S(2)}, u32[]{:S(2)}) collective-permute-start(bf16[2,224,128]{2,1,0:T(8,128)(2,1)S(1)} %slice.28), channel_id=1, source_target_pairs={{0,16},{16,0},{1,17},{17,1},{2,18},{18,2},{3,19},{19,3},{4,20},{20... | collective-permute-start | bytes 344072 | tf_op jit(solution)/shard_map/ppermute | solution.py:483
  60.5 3.4 %collective-permute-start.13 = (bf16[2,224,128]{2,1,0:T(8,128)(2,1)S(1)}, bf16[2,224,128]{2,1,0:T(8,128)(2,1)S(1)}, u32[]{:S(2)}, u32[]{:S(2)}) collective-permute-start(bf16[2,224,128]{2,1,0:T(8,128)(2,1)S(1)} %slice.29), channel_id=1, source_target_pairs={{0,16},{16,0},{1,17},{17,1},{2,18},{18,2},{3,19},{19,3},{4,20},{20... | collective-permute-start | bytes 344072 | tf_op jit(solution)/shard_map/ppermute | solution.py:483

commit v12 on v11

--- a/solution.py
+++ b/solution.py
@@ -209,9 +209,9 @@
     cells, band, _, _, users = chan.shape
     buffers = ((mat_a, lhs_a), (mat_b, lhs_b))
 
-    def each_copy(act):
+    def each_copy(act, chosen):
         def run(e, halo_ref):
-            for c in range(cells):
+            for c in chosen:
                 blocks = (
                     (halo_ref.at[c, 0], chan.at[c, 0], chan.at[c, 1]),
                     (chan.at[c, band - 2], chan.at[c, band - 1], halo_ref.at[c, 0]),
@@ -232,18 +232,17 @@
 
     def fetch():
         count_copy.start()
-        each_copy(lambda copy: copy.start())
+        each_copy(lambda copy: copy.start(), range(cells))
         lhs_a[...] = jnp.zeros_like(lhs_a)
         lhs_b[...] = jnp.zeros_like(lhs_b)
 
     def work():
-        each_copy(lambda copy: copy.wait())
         count_copy.wait()
         last = lax.axis_index("sc") == side * (lax.axis_size("sc") - 1)
         stretch = jnp.where(jnp.full((1, users), last.astype(jnp.int32)) == 1, 1 / 0.75, 1.0)
         for c in range(cells):
+            each_copy(lambda copy: copy.wait(), (c,))
             prepare(win.at[c, 0], win.at[c, 1], win.at[c, 2], ybuf.at[c], stretch, *buffers[c % 2])
-        for c in range(cells):
             gram(*buffers[c % 2], out.at[c], count_ref[c, side * (band - 1) // GRP], users)
 
     return fetch, work
@@ -309,21 +308,24 @@
     return [e + a * d for e, a, d in zip(estimate, alpha, direction)]
 
 
-def detect_first(noise_power, own, peer):
+def detect_inner(noise_power, own, peer, first, state):
     cells, inner, rows, users = own.shape
     half, number = inner + 1, peer.shape[1]
 
-    def kernel(noise_ref, own_ref, peer_ref, out):
+    def kernel(noise_ref, own_ref, peer_ref, *refs):
+        out = refs[-1]
+        if state:
+            out[...] = refs[0][...]
         panel = lax.axis_index("panel")
         spots = [(c, i) for c in range(cells) for i in range(number)]
-        sums = [own_ref[c, i] + peer_ref[c, i].astype(F32) for c, i in spots]
+        sums = [own_ref[c, first + i] + peer_ref[c, i].astype(F32) for c, i in spots]
         values = conjugate_gradient(sums, [noise_ref[c] for c, _ in spots], users)
         for (c, i), value in zip(spots, values):
-            out[c, pl.ds(i + 1 - panel, 2 * SPAD, stride=half), :] = value
+            out[c, pl.ds(first + i + 1 - panel, 2 * SPAD, stride=half), :] = value
 
     return pl.pallas_call(
         kernel,
-        in_specs=[SMEM_SPEC] + [VMEM_SPEC] * 2,
+        in_specs=[SMEM_SPEC] + [VMEM_SPEC] * (2 + len(state)),
         out_specs=VMEM_SPEC,
         out_shape=jax.ShapeDtypeStruct((cells, 2 * SPAD * half, users), F32),
         compiler_params=pltpu.CompilerParams(vmem_limit_bytes=VMEM_LIMIT),
@@ -332,27 +334,22 @@
             bytes_accessed=cells * inner * rows * users * 6,
             transcendentals=0,
         ),
-    )(noise_power, own, peer)
-
-
-def detect_last(noise_power, own, peer, edge_own, edge_peer, state, onehot, symbols, rounds):
-    cells, inner, rows, users = own.shape
-    half, number = inner + 1, peer.shape[1]
+    )(noise_power, own, peer, *state)
+
+
+def detect_edge(noise_power, edge_own, edge_peer, state, onehot, symbols, rounds):
+    cells, _, users = edge_own.shape
+    half = state.shape[1] // (2 * SPAD)
     width = onehot.shape[1] // (2 * rounds)
     keep = symbols * half
 
-    def kernel(noise_ref, own_ref, peer_ref, edge_own_ref, edge_peer_ref, hot_ref, state_ref, *refs):
+    def kernel(noise_ref, edge_own_ref, edge_peer_ref, hot_ref, state_ref, *refs):
         *outs, full = refs
-        panel = lax.axis_index("panel")
         full[...] = state_ref[...]
-        first = inner - number
-        spots = [(c, i) for c in range(cells) for i in range(number)]
-        sums = [own_ref[c, first + i] + peer_ref[c, i].astype(F32) for c, i in spots]
-        places = [(c, first + i + 1 - panel) for c, i in spots]
-        sums += [edge_own_ref[c] + edge_peer_ref[c].astype(F32) for c in range(cells)]
-        places += [(c, panel * (half - 1)) for c in range(cells)]
-        values = conjugate_gradient(sums, [noise_ref[c] for c, _ in places], users)
-        for (c, place), value in zip(places, values):
+        sums = [edge_own_ref[c] + edge_peer_ref[c].astype(F32) for c in range(cells)]
+        values = conjugate_gradient(sums, [noise_ref[c] for c in range(cells)], users)
+        place = lax.axis_index("panel") * (half - 1)
+        for c, value in enumerate(values):
             full[c, pl.ds(place, 2 * SPAD, stride=half), :] = value
         found = full[...].astype(BF16)
         blocks = [
@@ -369,7 +366,7 @@
 
     return pl.pallas_call(
         kernel,
-        in_specs=[SMEM_SPEC] + [VMEM_SPEC] * 6,
+        in_specs=[SMEM_SPEC] + [VMEM_SPEC] * 4,
         out_specs=[VMEM_SPEC] * rounds,
         out_shape=[jax.ShapeDtypeStruct((2 * keep, width), BF16)] * rounds,
         scratch_shapes=[pltpu.VMEM(state.shape, F32)],
@@ -377,7 +374,7 @@
         cost_estimate=pl.CostEstimate(
             flops=2 * keep * onehot.shape[0] * onehot.shape[1], bytes_accessed=4 * state.size, transcendentals=0
         ),
-    )(noise_power, own, peer, edge_own, edge_peer, onehot, state)
+    )(noise_power, edge_own, edge_peer, onehot, state)
 
 
 def assemble(sources, mine, theirs, others, cells, per_device, symbols, half):
@@ -447,10 +444,12 @@
     second_peer = lax.ppermute(second, "panel", SWAP)
     counts, first_peer = lax.optimization_barrier((user_count, first_peer))
     (own,) = inner_gram(counts, channel, samples, False, (1, half), inner, F32)
-    state = detect_first(noise_power, own, first_peer)
+    state = detect_inner(noise_power, own, first_peer, 0, ())
     near, far, state = lax.optimization_barrier((near, far, state))
     edge_peer = lax.ppermute(edge_gram(user_count, channel, samples, near, far, True, BF16), "panel", SWAP)
     edge_own = edge_gram(user_count, channel, samples, near, far, False, F32)
+    edge_own, second_peer = lax.optimization_barrier((edge_own, second_peer))
+    state = detect_inner(noise_power, own, second_peer, count, (state,))
 
     capacity = cells * users // n_cell
     per_device = n_cell * capacity // n_sc
@@ -465,7 +464,7 @@
     width = 2 * cells * per_device
     onehot = (column[:, None] == lax.iota(jnp.int32, 2 * reach * width)[None, :]).astype(BF16)
 
-    messages = detect_last(noise_power, own, second_peer, edge_own, edge_peer, state, onehot, symbols, reach)
+    messages = detect_edge(noise_power, edge_own, edge_peer, state, onehot, symbols, reach)
     arrived = []
     for b in range(reach):
         pairs = [

time: 66 us -> 68 us (1.030)
  waiting for transfers between devices: 9.87 us -> 18.3 us
  starting transfers between devices: 24.2 us -> 16.6 us
  Pallas kernels: 30.9 us -> 32 us
    ppermute x2, waiting for transfers between devices: 0.01 us -> 6.65 us  [body(): theirs = [lax.ppermute(group, 'panel', SWAP) for group in mine]]
    ppermute x2, starting transfers between devices: 4.62 us -> 0.14 us  [body(): others += [lax.ppermute(group[:, :keep], 'cell', SWAP) for group in theirs]]
    ppermute x4, waiting for transfers between devices: 3.99 us -> 6.87 us  [body(): arrived.append(lax.ppermute(messages[b], ('cell', 'sc'), pairs))]
    ppermute x1, starting transfers between devices: 6.01 us -> 3.23 us  [body(): lax.ppermute(jnp.stack([block[:keep] for block in arrived]), 'cell', SWAP)]
    ppermute x1, waiting for transfers between devices: 1.42 us -> 0.01 us  [body(): lax.ppermute(edge_gram(user_count, channel, samples, near, far, True, BF1...]
    pallas_call x2 -> x3, Pallas kernels: 4.07 us -> 5.11 us  [the longest x2 3.59 us: detect_inner(): pl.pallas_call(kernel, in_specs=[SMEM_SPEC] + [VMEM_SPEC] * (2 + len(stat...]
    ppermute x4, starting transfers between devices: 6.12 us -> 5.34 us  [body(): arrived.append(lax.ppermute(messages[b], ('cell', 'sc'), pairs))]
  transfers between devices with their start and end apart: 14 -> 14, of which waited for: 7 -> 8; matrix products, arithmetic and copies ran while one was open for 1% -> 1% of each run, Pallas kernels for 32% -> 34%
where the time goes in v12:
time: 68 us; the launch traced here: 67.8 us
  Pallas kernels  32 us (47%)
  waiting for transfers between devices  18.3 us (27%)
  starting transfers between devices  16.6 us (24%)
    pallas_call x3, Pallas kernels, inner_gram(): pl.pallas_call(kernel, in_specs=[HBM_SPEC] * 3, out_specs=[VMEM_SPEC] + [...  21.1 us
    ppermute x4, waiting for transfers between devices, body(): arrived.append(lax.ppermute(messages[b], ('cell', 'sc'), pairs))  6.87 us
    ppermute x2, waiting for transfers between devices, body(): theirs = [lax.ppermute(group, 'panel', SWAP) for group in mine]  6.65 us
    ppermute x4, starting transfers between devices, body(): arrived.append(lax.ppermute(messages[b], ('cell', 'sc'), pairs))  5.34 us
    pallas_call x2, Pallas kernels, edge_gram(): pl.pallas_call(kernel, in_specs=[HBM_SPEC] * 5, out_specs=VMEM_SPEC, out_...  3.94 us
    pallas_call x2, Pallas kernels, detect_inner(): pl.pallas_call(kernel, in_specs=[SMEM_SPEC] + [VMEM_SPEC] * (2 + len(stat...  3.59 us
    ppermute x1, starting transfers between devices, body(): lax.ppermute(jnp.stack([block[:keep] for block in arrived]), 'cell', SWAP)  3.23 us
    ppermute x1, starting transfers between devices, body(): first_peer = lax.ppermute(first, 'panel', SWAP)  3.01 us
  transfers between devices with their start and end apart: 14, of which 8 were waited for; matrix products, arithmetic and copies ran while one was open for 1% of the time, Pallas kernels for 34%

profile of v12, /device:TPU:0, one launch (start us, length us, event | category | flops | bytes accessed | tf_op | source)
XLA Modules:
  0.0 67.8 jit_solution(1479697325803602058)
XLA Ops:
  0.0 5.2 %shard_map.55 = (bf16[2,6,160,128]{3,2,1,0:T(8,128)(2,1)}, bf16[2,1,2,512,128]{4,3,2,1,0:T(8,128)(2,1)}, bf16[2,1,2,512,128]{4,3,2,1,0:T(8,128)(2,1)}) custom-call(s32[2,2]{1,0:T(2,128)} %counts_hbm.8, bf16[2,32,2,512,128]{4,3,2,1,0:T(8,128)(2,1)} %chan.9, bf16[2,32,14,2,512]{4,3,2,1,0:T(2,128)(2,1)} %bitcast.15), custom_call_target="tpu_custom_call" | custom-call | flops 905969664 | bytes 4194304 | tf_op jit(solution)/shard_map/pallas_call | solution.py:149
  5.2 3.0 %collective-permute-start.2 = (bf16[2,6,160,128]{3,2,1,0:T(8,128)(2,1)}, bf16[2,6,160,128]{3,2,1,0:T(8,128)(2,1)S(1)}, u32[]{:S(2)}, u32[]{:S(2)}) collective-permute-start(bf16[2,6,160,128]{3,2,1,0:T(8,128)(2,1)} %get-tuple-element.25), channel_id=1, source_target_pairs={{0,8},{8,0},{1,9},{9,1},{2,10},{10,2},{3,11},{11,3},{4,12},{12,4},... | collective-permute-start | bytes 1474568 | tf_op jit(solution)/shard_map/ppermute | solution.py:437
  8.3 1.5 %collective-permute-start = (bf16[2,1,2,512,128]{4,3,2,1,0:T(8,128)(2,1)}, bf16[2,1,2,512,128]{4,3,2,1,0:T(8,128)(2,1)S(1)}, u32[]{:S(2)}, u32[]{:S(2)}) collective-permute-start(bf16[2,1,2,512,128]{4,3,2,1,0:T(8,128)(2,1)} %get-tuple-element.23), channel_id=1, source_target_pairs={{0,1},{1,0},{2,3},{3,2},{4,5},{5,4},{6,7},{7,6},{8,9},{9,8},{10,11... | collective-permute-start | bytes 1572872 | tf_op jit(solution)/shard_map/ppermute | solution.py:439
  9.8 0.8 %collective-permute-start.1 = (bf16[2,1,2,512,128]{4,3,2,1,0:T(8,128)(2,1)}, bf16[2,1,2,512,128]{4,3,2,1,0:T(8,128)(2,1)S(1)}, u32[]{:S(2)}, u32[]{:S(2)}) collective-permute-start(bf16[2,1,2,512,128]{4,3,2,1,0:T(8,128)(2,1)} %get-tuple-element.24), channel_id=1, source_target_pairs={{1,2},{2,1},{3,4},{4,3},{5,6},{6,5},{9,10},{10,9},{11,12},{12,11},... | collective-permute-start | bytes 1572872 | tf_op jit(solution)/shard_map/ppermute | solution.py:440
  10.6 6.8 %shard_map.60 = bf16[2,9,160,128]{3,2,1,0:T(8,128)(2,1)} custom-call(s32[2,2]{1,0:T(2,128)} %counts_hbm.8, bf16[2,32,2,512,128]{4,3,2,1,0:T(8,128)(2,1)} %chan.9, bf16[2,32,14,2,512]{4,3,2,1,0:T(2,128)(2,1)} %bitcast.16), custom_call_target="tpu_custom_call" | custom-call | flops 1358954496 | bytes 5767168 | tf_op jit(solution)/shard_map/pallas_call | solution.py:149
  18.2 2.0 %collective-permute-done.2.peer_ref = bf16[2,6,160,128]{3,2,1,0:T(8,128)(2,1)S(1)} collective-permute-done((bf16[2,6,160,128]{3,2,1,0:T(8,128)(2,1)}, bf16[2,6,160,128]{3,2,1,0:T(8,128)(2,1)S(1)}, u32[]{:S(2)}, u32[]{:S(2)}) %collective-permute-start.2) | collective-permute-done | bytes 491552 | tf_op jit(solution)/shard_map/ppermute | solution.py:437
  20.2 9.0 %shard_map.57.own_ref = f32[2,15,160,128]{3,2,1,0:T(8,128)S(1)} custom-call(s32[2,2]{1,0:T(2,128)S(1)} %copy-done.1, bf16[2,32,2,512,128]{4,3,2,1,0:T(8,128)(2,1)} %chan.9, bf16[2,32,14,2,512]{4,3,2,1,0:T(2,128)(2,1)S(1)} %bitcast.17), custom_call_target="tpu_custom_call" | custom-call | flops 141557760 | bytes 557056 | tf_op jit(solution)/shard_map/pallas_call | solution.py:149
  29.3 1.4 %shard_map.58.refs_0_ = f32[2,512,128]{2,1,0:T(8,128)S(1)} custom-call(f32[2]{0:T(128)S(1)} %copy-done.2, f32[2,15,160,128]{3,2,1,0:T(8,128)S(1)} %shard_map.57.own_ref, bf16[2,6,160,128]{3,2,1,0:T(8,128)(2,1)S(1)} %collective-permute-done.2.peer_ref), custom_call_target="tpu_custom_call" | custom-call | flops 50331648 | bytes 3686400 | tf_op jit(solution)/shard_map/pallas_call | solution.py:326
  30.6 1.6 %collective-permute-done.near_ref = bf16[2,1,2,512,128]{4,3,2,1,0:T(8,128)(2,1)S(1)} collective-permute-done((bf16[2,1,2,512,128]{4,3,2,1,0:T(8,128)(2,1)}, bf16[2,1,2,512,128]{4,3,2,1,0:T(8,128)(2,1)S(1)}, u32[]{:S(2)}, u32[]{:S(2)}) %collective-permute-start) | collective-permute-done | bytes 524320 | tf_op jit(solution)/shard_map/ppermute | solution.py:439
  32.2 1.9 %shard_map.61 = bf16[2,160,128]{2,1,0:T(8,128)(2,1)S(1)} custom-call(s32[2,2]{1,0:T(2,128)S(1)} %copy-done.1, bf16[2,32,2,512,128]{4,3,2,1,0:T(8,128)(2,1)} %chan.9, bf16[2,32,14,2,512]{4,3,2,1,0:T(2,128)(2,1)S(1)} %bitcast.18, bf16[2,1,2,512,128]{4,3,2,1,0:T(8,128)(2,1)S(1)} %collective-permute-done.near_ref, ...), custom_call_target="tpu_custom_call" | custom-call | flops 150994944 | bytes 1572864 | tf_op jit(solution)/shard_map/pallas_call | solution.py:261
  34.2 0.9 %collective-permute-start.4 = (bf16[2,160,128]{2,1,0:T(8,128)(2,1)S(1)}, bf16[2,160,128]{2,1,0:T(8,128)(2,1)S(1)}, u32[]{:S(2)}, u32[]{:S(2)}) collective-permute-start(bf16[2,160,128]{2,1,0:T(8,128)(2,1)S(1)} %shard_map.61), channel_id=1, source_target_pairs={{0,8},{8,0},{1,9},{9,1},{2,10},{10,2},{3,11},{11,3},{4,12},{12,4},... | collective-permute-start | bytes 245768 | tf_op jit(solution)/shard_map/ppermute | solution.py:449
  35.3 2.0 %shard_map.59.edge_own_ref = f32[2,160,128]{2,1,0:T(8,128)S(1)} custom-call(s32[2,2]{1,0:T(2,128)S(1)} %copy-done.1, bf16[2,32,2,512,128]{4,3,2,1,0:T(8,128)(2,1)} %chan.9, bf16[2,32,14,2,512]{4,3,2,1,0:T(2,128)(2,1)S(1)} %bitcast.19, bf16[2,1,2,512,128]{4,3,2,1,0:T(8,128)(2,1)S(1)} %collective-permute-done.near_ref, ...), custom_call_target="tpu_custom_call" | custom-call | flops 150994944 | bytes 1572864 | tf_op jit(solution)/shard_map/pallas_call | solution.py:261
  37.3 2.2 %shard_map.62.state_ref = f32[2,512,128]{2,1,0:T(8,128)S(1)} custom-call(f32[2]{0:T(128)S(1)} %copy-done.2, f32[2,15,160,128]{3,2,1,0:T(8,128)S(1)} %shard_map.57.own_ref, bf16[2,9,160,128]{3,2,1,0:T(8,128)(2,1)} %collective-permute-done.3.peer_ref, f32[2,512,128]{2,1,0:T(8,128)S(1)} %shard_map.58.refs_0_), custom_call_target="tpu_custom_call" | custom-call | flops 75497472 | bytes 3686400 | tf_op jit(solution)/shard_map/pallas_call | solution.py:326
  39.6 1.5 %shard_map.63 = (bf16[448,128]{1,0:T(8,128)(2,1)S(1)}, bf16[448,128]{1,0:T(8,128)(2,1)S(1)}, bf16[448,128]{1,0:T(8,128)(2,1)S(1)}, bf16[448,128]{1,0:T(8,128)(2,1)S(1)}) custom-call(f32[2]{0:T(128)S(1)} %copy-done.2, f32[2,160,128]{2,1,0:T(8,128)S(1)} %shard_map.59.edge_own_ref, bf16[2,160,128]{2,1,0:T(8,128)(2,1)S(1)} %collective-permute-done.4.edge_peer_ref, ...), custom_call_target="tpu_custom_call" | custom-call | flops 234881024 | bytes 524288 | tf_op jit(solution)/shard_map/pallas_call | solution.py:367
  41.1 4.0 %collective-permute-start.8 = (bf16[448,128]{1,0:T(8,128)(2,1)S(1)}, bf16[448,128]{1,0:T(8,128)(2,1)S(1)}, u32[]{:S(2)}, u32[]{:S(2)}) collective-permute-start(bf16[448,128]{1,0:T(8,128)(2,1)S(1)} %get-tuple-element.36), channel_id=1, source_target_pairs={{0,3},{1,0},{2,1},{3,2},{4,19},{5,16},{6,17},{7,18},{16,7},{17,4},... | collective-permute-start | bytes 344072 | tf_op jit(solution)/shard_map/ppermute | solution.py:475
  46.4 2.2 %collective-permute-done.8 = bf16[448,128]{1,0:T(8,128)(2,1)S(1)} collective-permute-done((bf16[448,128]{1,0:T(8,128)(2,1)S(1)}, bf16[448,128]{1,0:T(8,128)(2,1)S(1)}, u32[]{:S(2)}, u32[]{:S(2)}) %collective-permute-start.8) | collective-permute-done | bytes 114720 | tf_op jit(solution)/shard_map/ppermute | solution.py:475
  48.7 2.5 %collective-permute-done.7 = bf16[448,128]{1,0:T(8,128)(2,1)S(1)} collective-permute-done((bf16[448,128]{1,0:T(8,128)(2,1)S(1)}, bf16[448,128]{1,0:T(8,128)(2,1)S(1)}, u32[]{:S(2)}, u32[]{:S(2)}) %collective-permute-start.7) | collective-permute-done | bytes 114720 | tf_op jit(solution)/shard_map/ppermute | solution.py:475
  51.6 2.2 %collective-permute-done.6 = bf16[448,128]{1,0:T(8,128)(2,1)S(1)} collective-permute-done((bf16[448,128]{1,0:T(8,128)(2,1)S(1)}, bf16[448,128]{1,0:T(8,128)(2,1)S(1)}, u32[]{:S(2)}, u32[]{:S(2)}) %collective-permute-start.6) | collective-permute-done | bytes 114720 | tf_op jit(solution)/shard_map/ppermute | solution.py:475
  53.8 0.7 collective-permute-start.9
  54.5 3.2 %collective-permute-start.11 = (bf16[4,224,128]{2,1,0:T(8,128)(2,1)S(1)}, bf16[4,224,128]{2,1,0:T(8,128)(2,1)S(1)}, u32[]{:S(2)}, u32[]{:S(2)}) collective-permute-start(bf16[4,224,128]{2,1,0:T(8,128)(2,1)S(1)} %pad_maximum_fusion.2), channel_id=1, source_target_pairs={{0,16},{16,0},{1,17},{17,1},{2,18},{18,2},{3,19},{19,3},{4,20},{20... | collective-permute-start | bytes 688136 | tf_op jit(solution)/shard_map/ppermute | solution.py:481
  57.8 2.0 %collective-permute-done.10.refs_3_ = bf16[2,448,128]{2,1,0:T(8,128)(2,1)S(1)} collective-permute-done((bf16[2,448,128]{2,1,0:T(8,128)(2,1)S(1)}, bf16[2,448,128]{2,1,0:T(8,128)(2,1)S(1)}, u32[]{:S(2)}, u32[]{:S(2)}) %collective-permute-start.10) | collective-permute-done | bytes 229408 | tf_op jit(solution)/shard_map/ppermute | solution.py:480
  59.8 4.7 %collective-permute-done.9.refs_2_ = bf16[2,448,128]{2,1,0:T(8,128)(2,1)S(1)} collective-permute-done((bf16[2,448,128]{2,1,0:T(8,128)(2,1)S(1)}, bf16[2,448,128]{2,1,0:T(8,128)(2,1)S(1)}, u32[]{:S(2)}, u32[]{:S(2)}) %collective-permute-start.9) | collective-permute-done | bytes 229408 | tf_op jit(solution)/shard_map/ppermute | solution.py:480
  64.7 1.2 %collective-permute-done.12.refs_5_ = bf16[2,224,128]{2,1,0:T(8,128)(2,1)S(1)} collective-permute-done((bf16[2,224,128]{2,1,0:T(8,128)(2,1)S(1)}, bf16[2,224,128]{2,1,0:T(8,128)(2,1)S(1)}, u32[]{:S(2)}, u32[]{:S(2)}) %collective-permute-start.12) | collective-permute-done | bytes 114720 | tf_op jit(solution)/shard_map/ppermute | solution.py:482
  65.9 1.9 %shard_map.64 = bf16[2,32,14,2,256]{4,3,2,1,0:T(2,128)(2,1)} custom-call(s32[8]{0:T(128)S(1)} %pad_add_fusion.1.source_ref, bf16[2,448,128]{2,1,0:T(8,128)(2,1)S(1)} %pad_maximum_fusion.refs_0_, bf16[2,448,128]{2,1,0:T(8,128)(2,1)S(1)} %pad_maximum_fusion.1.refs_1_, bf16[2,448,128]{2,1,0:T(8,128)(2,1)S(1)} %collective-permute-done.9.refs_2_, ...), custom_call_target="tpu_custom_call" | custom-call | tf_op jit(solution)/shard_map/pallas_call | solution.py:413
  (37 shorter events, 3.1 us)
Async XLA Ops:
  5.2 15.0 %collective-permute-start.2 = (bf16[2,6,160,128]{3,2,1,0:T(8,128)(2,1)}, bf16[2,6,160,128]{3,2,1,0:T(8,128)(2,1)S(1)}, u32[]{:S(2)}, u32[]{:S(2)}) collective-permute-start(bf16[2,6,160,128]{3,2,1,0:T(8,128)(2,1)} %get-tuple-element.25), channel_id=1, source_target_pairs={{0,8},{8,0},{1,9},{9,1},{2,10},{10,2},{3,11},{11,3},{4,12},{12,4},... | collective-permute-start | bytes 1474568 | tf_op jit(solution)/shard_map/ppermute | solution.py:437
  8.3 24.0 %collective-permute-start = (bf16[2,1,2,512,128]{4,3,2,1,0:T(8,128)(2,1)}, bf16[2,1,2,512,128]{4,3,2,1,0:T(8,128)(2,1)S(1)}, u32[]{:S(2)}, u32[]{:S(2)}) collective-permute-start(bf16[2,1,2,512,128]{4,3,2,1,0:T(8,128)(2,1)} %get-tuple-element.23), channel_id=1, source_target_pairs={{0,1},{1,0},{2,3},{3,2},{4,5},{5,4},{6,7},{7,6},{8,9},{9,8},{10,11... | collective-permute-start | bytes 1572872 | tf_op jit(solution)/shard_map/ppermute | solution.py:439
  9.8 8.2 %copy-start.3 = (s32[2,128,1]{1,2,0:T(1,128)S(1)}, s32[2,128,1]{1,2,0:T(1,128)}, u32[]{:S(2)}) copy-start(s32[2,128,1]{1,2,0:T(1,128)} %param.9) | copy-start | bytes 3076
  9.8 10.4 %copy-start = (bf16[2,32,2,14,512]{4,2,3,1,0:T(2,128)(2,1)S(1)}, bf16[2,32,2,14,512]{4,2,3,1,0:T(2,128)(2,1)}, u32[]{:S(2)}) copy-start(bf16[2,32,2,14,512]{4,2,3,1,0:T(2,128)(2,1)} %param.6) | copy-start | bytes 5505028
  9.8 10.4 %copy-start.1 = (s32[2,2]{1,0:T(2,128)S(1)}, s32[2,2]{1,0:T(2,128)}, u32[]{:S(2)}) copy-start(s32[2,2]{1,0:T(2,128)} %counts_hbm.8) | copy-start | bytes 52
  9.8 22.4 %collective-permute-start.1 = (bf16[2,1,2,512,128]{4,3,2,1,0:T(8,128)(2,1)}, bf16[2,1,2,512,128]{4,3,2,1,0:T(8,128)(2,1)S(1)}, u32[]{:S(2)}, u32[]{:S(2)}) collective-permute-start(bf16[2,1,2,512,128]{4,3,2,1,0:T(8,128)(2,1)} %get-tuple-element.24), channel_id=1, source_target_pairs={{1,2},{2,1},{3,4},{4,3},{5,6},{6,5},{9,10},{10,9},{11,12},{12,11},... | collective-permute-start | bytes 1572872 | tf_op jit(solution)/shard_map/ppermute | solution.py:440
  17.4 19.9 %collective-permute-start.3 = (bf16[2,9,160,128]{3,2,1,0:T(8,128)(2,1)}, bf16[2,9,160,128]{3,2,1,0:T(8,128)(2,1)}, u32[]{:S(2)}, u32[]{:S(2)}) collective-permute-start(bf16[2,9,160,128]{3,2,1,0:T(8,128)(2,1)} %shard_map.60), channel_id=1, source_target_pairs={{0,8},{8,0},{1,9},{9,1},{2,10},{10,2},{3,11},{11,3},{4,12},{12,4},... | collective-permute-start | bytes 2211848 | tf_op jit(solution)/shard_map/ppermute | solution.py:444
  18.2 11.0 %copy-start.2 = (f32[2]{0:T(128)S(1)}, f32[2]{0:T(128)}, u32[]{:S(2)}) copy-start(f32[2]{0:T(128)} %noise_ref.5) | copy-start | bytes 28
  34.2 5.4 %collective-permute-start.4 = (bf16[2,160,128]{2,1,0:T(8,128)(2,1)S(1)}, bf16[2,160,128]{2,1,0:T(8,128)(2,1)S(1)}, u32[]{:S(2)}, u32[]{:S(2)}) collective-permute-start(bf16[2,160,128]{2,1,0:T(8,128)(2,1)S(1)} %shard_map.61), channel_id=1, source_target_pairs={{0,8},{8,0},{1,9},{9,1},{2,10},{10,2},{3,11},{11,3},{4,12},{12,4},... | collective-permute-start | bytes 245768 | tf_op jit(solution)/shard_map/ppermute | solution.py:449
  41.1 7.6 %collective-permute-start.8 = (bf16[448,128]{1,0:T(8,128)(2,1)S(1)}, bf16[448,128]{1,0:T(8,128)(2,1)S(1)}, u32[]{:S(2)}, u32[]{:S(2)}) collective-permute-start(bf16[448,128]{1,0:T(8,128)(2,1)S(1)} %get-tuple-element.36), channel_id=1, source_target_pairs={{0,3},{1,0},{2,1},{3,2},{4,19},{5,16},{6,17},{7,18},{16,7},{17,4},... | collective-permute-start | bytes 344072 | tf_op jit(solution)/shard_map/ppermute | solution.py:475
  45.1 6.0 %collective-permute-start.7 = (bf16[448,128]{1,0:T(8,128)(2,1)S(1)}, bf16[448,128]{1,0:T(8,128)(2,1)S(1)}, u32[]{:S(2)}, u32[]{:S(2)}) collective-permute-start(bf16[448,128]{1,0:T(8,128)(2,1)S(1)} %get-tuple-element.35), channel_id=1, source_target_pairs={{0,2},{1,3},{2,0},{3,1},{4,18},{5,19},{6,16},{7,17},{16,6},{17,7},... | collective-permute-start | bytes 344072 | tf_op jit(solution)/shard_map/ppermute | solution.py:475
  45.6 8.1 %collective-permute-start.6 = (bf16[448,128]{1,0:T(8,128)(2,1)S(1)}, bf16[448,128]{1,0:T(8,128)(2,1)S(1)}, u32[]{:S(2)}, u32[]{:S(2)}) collective-permute-start(bf16[448,128]{1,0:T(8,128)(2,1)S(1)} %get-tuple-element.34), channel_id=1, source_target_pairs={{0,1},{1,2},{2,3},{3,0},{4,17},{5,18},{6,19},{7,16},{16,5},{17,6},... | collective-permute-start | bytes 344072 | tf_op jit(solution)/shard_map/ppermute | solution.py:475
  45.8 8.0 %collective-permute-start.5 = (bf16[448,128]{1,0:T(8,128)(2,1)S(1)}, bf16[448,128]{1,0:T(8,128)(2,1)S(1)}, u32[]{:S(2)}, u32[]{:S(2)}) collective-permute-start(bf16[448,128]{1,0:T(8,128)(2,1)S(1)} %get-tuple-element.33), channel_id=1, source_target_pairs={{0,0},{1,1},{2,2},{3,3},{4,16},{5,17},{6,18},{7,19},{16,4},{17,5},... | collective-permute-start | bytes 344072 | tf_op jit(solution)/shard_map/ppermute | solution.py:475
  51.2 8.5 %collective-permute-start.10 = (bf16[2,448,128]{2,1,0:T(8,128)(2,1)S(1)}, bf16[2,448,128]{2,1,0:T(8,128)(2,1)S(1)}, u32[]{:S(2)}, u32[]{:S(2)}) collective-permute-start(bf16[2,448,128]{2,1,0:T(8,128)(2,1)S(1)} %pad_maximum_fusion.1.refs_1_), channel_id=1, source_target_pairs={{0,8},{8,0},{1,9},{9,1},{2,10},{10,2},{3,11},{11,3},{4,12},{12,4},... | collective-permute-start | bytes 688136 | tf_op jit(solution)/shard_map/ppermute | solution.py:480
  53.8 10.7 %collective-permute-start.9 = (bf16[2,448,128]{2,1,0:T(8,128)(2,1)S(1)}, bf16[2,448,128]{2,1,0:T(8,128)(2,1)S(1)}, u32[]{:S(2)}, u32[]{:S(2)}) collective-permute-start(bf16[2,448,128]{2,1,0:T(8,128)(2,1)S(1)} %pad_maximum_fusion.refs_0_), channel_id=1, source_target_pairs={{0,8},{8,0},{1,9},{9,1},{2,10},{10,2},{3,11},{11,3},{4,12},{12,4},... | collective-permute-start | bytes 688136 | tf_op jit(solution)/shard_map/ppermute | solution.py:480
  54.5 10.2 %collective-permute-start.11 = (bf16[4,224,128]{2,1,0:T(8,128)(2,1)S(1)}, bf16[4,224,128]{2,1,0:T(8,128)(2,1)S(1)}, u32[]{:S(2)}, u32[]{:S(2)}) collective-permute-start(bf16[4,224,128]{2,1,0:T(8,128)(2,1)S(1)} %pad_maximum_fusion.2), channel_id=1, source_target_pairs={{0,16},{16,0},{1,17},{17,1},{2,18},{18,2},{3,19},{19,3},{4,20},{20... | collective-permute-start | bytes 688136 | tf_op jit(solution)/shard_map/ppermute | solution.py:481
  59.7 5.0 %collective-permute-start.13 = (bf16[2,224,128]{2,1,0:T(8,128)(2,1)S(1)}, bf16[2,224,128]{2,1,0:T(8,128)(2,1)S(1)}, u32[]{:S(2)}, u32[]{:S(2)}) collective-permute-start(bf16[2,224,128]{2,1,0:T(8,128)(2,1)S(1)} %slice.29), channel_id=1, source_target_pairs={{0,16},{16,0},{1,17},{17,1},{2,18},{18,2},{3,19},{19,3},{4,20},{20... | collective-permute-start | bytes 344072 | tf_op jit(solution)/shard_map/ppermute | solution.py:482
  64.5 1.4 %collective-permute-start.12 = (bf16[2,224,128]{2,1,0:T(8,128)(2,1)S(1)}, bf16[2,224,128]{2,1,0:T(8,128)(2,1)S(1)}, u32[]{:S(2)}, u32[]{:S(2)}) collective-permute-start(bf16[2,224,128]{2,1,0:T(8,128)(2,1)S(1)} %slice.28), channel_id=1, source_target_pairs={{0,16},{16,0},{1,17},{17,1},{2,18},{18,2},{3,19},{19,3},{4,20},{20... | collective-permute-start | bytes 344072 | tf_op jit(solution)/shard_map/ppermute | solution.py:482

commit v13 on v12

--- a/solution.py
+++ b/solution.py
@@ -248,13 +248,13 @@
     return fetch, work
 
 
-def edge_gram(counts, channel, received, near, far, peer, dtype):
+def edge_gram(counts, channel, received, near, far):
     cells, _, _, antennas, users = channel.shape
     symbols = received.shape[2]
 
     def kernel(counts_hbm, chan, samp, near_ref, far_ref, out, *scratch):
         panel = lax.axis_index("panel")
-        fetch, work = edge_work(1 - panel if peer else panel, counts_hbm, chan, samp, near_ref, far_ref, out, scratch)
+        fetch, work = edge_work(1 - panel, counts_hbm, chan, samp, near_ref, far_ref, out, scratch)
         fetch()
         work()
 
@@ -262,7 +262,7 @@
         kernel,
         in_specs=[HBM_SPEC] * 5,
         out_specs=VMEM_SPEC,
-        out_shape=jax.ShapeDtypeStruct((cells, users + 2 * SPAD, users), dtype),
+        out_shape=jax.ShapeDtypeStruct((cells, users + 2 * SPAD, users), BF16),
         scratch_shapes=edge_scratch(counts, symbols, antennas, users),
         compiler_params=pltpu.CompilerParams(vmem_limit_bytes=VMEM_LIMIT),
         cost_estimate=pl.CostEstimate(
@@ -308,33 +308,45 @@
     return [e + a * d for e, a, d in zip(estimate, alpha, direction)]
 
 
-def detect_inner(noise_power, own, peer, first, state):
+def detect_inner(noise_power, own, peer, first, state, edge):
     cells, inner, rows, users = own.shape
     half, number = inner + 1, peer.shape[1]
 
     def kernel(noise_ref, own_ref, peer_ref, *refs):
-        out = refs[-1]
+        panel = lax.axis_index("panel")
+        state_refs, edge_refs = refs[: len(state)], refs[len(state) : len(state) + len(edge)]
+        out, *refs = refs[len(state) + len(edge) :]
+        if edge:
+            fetch, work = edge_work(panel, *edge_refs, refs[0], refs[1:])
+            fetch()
         if state:
-            out[...] = refs[0][...]
-        panel = lax.axis_index("panel")
+            out[...] = state_refs[0][...]
         spots = [(c, i) for c in range(cells) for i in range(number)]
         sums = [own_ref[c, first + i] + peer_ref[c, i].astype(F32) for c, i in spots]
         values = conjugate_gradient(sums, [noise_ref[c] for c, _ in spots], users)
         for (c, i), value in zip(spots, values):
             out[c, pl.ds(first + i + 1 - panel, 2 * SPAD, stride=half), :] = value
-
+        if edge:
+            work()
+
+    outs = [jax.ShapeDtypeStruct((cells, 2 * SPAD * half, users), F32)]
+    scratch = []
+    if edge:
+        outs.append(jax.ShapeDtypeStruct((cells, rows, users), F32))
+        scratch = edge_scratch(edge[0], edge[2].shape[2], edge[1].shape[3], users)
     return pl.pallas_call(
         kernel,
-        in_specs=[SMEM_SPEC] + [VMEM_SPEC] * (2 + len(state)),
-        out_specs=VMEM_SPEC,
-        out_shape=jax.ShapeDtypeStruct((cells, 2 * SPAD * half, users), F32),
+        in_specs=[SMEM_SPEC] + [VMEM_SPEC] * (2 + len(state)) + [HBM_SPEC] * len(edge),
+        out_specs=[VMEM_SPEC] * len(outs),
+        out_shape=outs,
+        scratch_shapes=scratch,
         compiler_params=pltpu.CompilerParams(vmem_limit_bytes=VMEM_LIMIT),
         cost_estimate=pl.CostEstimate(
             flops=cells * number * 2 * 2 * 2 * SPAD * users * 2 * users,
             bytes_accessed=cells * inner * rows * users * 6,
             transcendentals=0,
         ),
-    )(noise_power, own, peer, *state)
+    )(noise_power, own, peer, *state, *edge)
 
 
 def detect_edge(noise_power, edge_own, edge_peer, state, onehot, symbols, rounds):
@@ -444,12 +456,11 @@
     second_peer = lax.ppermute(second, "panel", SWAP)
     counts, first_peer = lax.optimization_barrier((user_count, first_peer))
     (own,) = inner_gram(counts, channel, samples, False, (1, half), inner, F32)
-    state = detect_inner(noise_power, own, first_peer, 0, ())
+    (state,) = detect_inner(noise_power, own, first_peer, 0, (), ())
     near, far, state = lax.optimization_barrier((near, far, state))
-    edge_peer = lax.ppermute(edge_gram(user_count, channel, samples, near, far, True, BF16), "panel", SWAP)
-    edge_own = edge_gram(user_count, channel, samples, near, far, False, F32)
-    edge_own, second_peer = lax.optimization_barrier((edge_own, second_peer))
-    state = detect_inner(noise_power, own, second_peer, count, (state,))
+    edge_peer = lax.ppermute(edge_gram(user_count, channel, samples, near, far), "panel", SWAP)
+    edge_inputs = (user_count, channel, samples, near, far)
+    state, edge_own = detect_inner(noise_power, own, second_peer, count, (state,), edge_inputs)
 
     capacity = cells * users // n_cell
     per_device = n_cell * capacity // n_sc
@@ -458,7 +469,7 @@
     position = lax.iota(jnp.int32, cells * users)
     earlier = (keys[:, None] == keys[None, :]) & (position[None, :] < position[:, None])
     rank = jnp.sum(earlier.astype(jnp.int32), axis=1)
-    turn = (rank // per_device - sc % reach) % reach * 2 + (keys // cells == sc // reach).astype(jnp.int32)
+    turn = (rank // per_device - sc % reach - reach // 2) % reach * 2 + (keys // cells == sc // reach).astype(jnp.int32)
     column = ((turn * cells + keys % cells) * per_device + rank % per_device) * 2
     column = jnp.concatenate([column, column + 1])
     width = 2 * cells * per_device
@@ -466,14 +477,14 @@
 
     messages = detect_edge(noise_power, edge_own, edge_peer, state, onehot, symbols, reach)
     arrived = []
-    for b in range(reach):
+    for b in [(n + reach // 2) % reach for n in range(reach)]:
         pairs = [
             (s * n_sc + j, j // reach * n_sc + s * reach + (j % reach + b) % reach)
             for s in range(n_cell)
             for j in range(n_sc)
         ]
-        arrived.append(lax.ppermute(messages[b], ("cell", "sc"), pairs))
-    turns = (sc % reach - lax.iota(jnp.int32, reach)) % reach
+        arrived.append(lax.ppermute(messages[len(arrived)], ("cell", "sc"), pairs))
+    turns = (sc % reach - lax.iota(jnp.int32, reach) - reach // 2) % reach
     sources = jnp.concatenate([cell * reach + turns, (1 - cell) * reach + turns])
     keep = symbols * half
     mine = [jnp.stack(arrived[: reach // 2]), jnp.stack(arrived[reach // 2 :])]

time: 68 us -> 67.6 us (level)
  starting transfers between devices: 16.6 us -> 25.3 us
  waiting for transfers between devices: 18.3 us -> 10.1 us
  Pallas kernels: 32 us -> 31.2 us
    ppermute x2, waiting for transfers between devices: 6.65 us -> 0.01 us  [body(): theirs = [lax.ppermute(group, 'panel', SWAP) for group in mine]]
    ppermute x2, starting transfers between devices: 0.14 us -> 5.66 us  [body(): others += [lax.ppermute(group[:, :keep], 'cell', SWAP) for group in theirs]]
    pallas_call x2 -> x1, Pallas kernels: 3.94 us -> 1.95 us  [edge_gram(): pl.pallas_call(kernel, in_specs=[HBM_SPEC] * 5, out_specs=VMEM_SPEC, out_...]
    ppermute x1, starting transfers between devices: 3.23 us -> 5.12 us  [body(): lax.ppermute(jnp.stack([block[:keep] for block in arrived]), 'cell', SWAP)]
    ppermute x5, starting transfers between devices: 6.22 us -> 7.88 us  [the longest x4 6.99 us: body(): arrived.append(lax.ppermute(messages[len(arrived)], ('cell', 'sc'), pairs))]
    ppermute x5, waiting for transfers between devices: 6.87 us -> 5.27 us  [the longest x4 5.27 us: body(): arrived.append(lax.ppermute(messages[len(arrived)], ('cell', 'sc'), pairs))]
    pallas_call x2, Pallas kernels: 3.59 us -> 4.77 us  [detect_inner(): pl.pallas_call(kernel, in_specs=[SMEM_SPEC] + [VMEM_SPEC] * (2 + len(stat...]
  transfers between devices with their start and end apart: 14 -> 14, of which waited for: 8 -> 7; matrix products, arithmetic and copies ran while one was open for 1% -> 1% of each run, Pallas kernels for 34% -> 33%
where the time goes in v13:
time: 67.6 us; the launch traced here: 67.4 us
  Pallas kernels  31.2 us (46%)
  starting transfers between devices  25.3 us (37%)
  waiting for transfers between devices  10.1 us (15%)
    pallas_call x3, Pallas kernels, inner_gram(): pl.pallas_call(kernel, in_specs=[HBM_SPEC] * 3, out_specs=[VMEM_SPEC] + [...  21 us
    ppermute x4, starting transfers between devices, body(): arrived.append(lax.ppermute(messages[len(arrived)], ('cell', 'sc'), pairs))  6.99 us
    ppermute x2, starting transfers between devices, body(): others += [lax.ppermute(group[:, :keep], 'cell', SWAP) for group in theirs]  5.66 us
    ppermute x4, waiting for transfers between devices, body(): arrived.append(lax.ppermute(messages[len(arrived)], ('cell', 'sc'), pairs))  5.27 us
    ppermute x1, starting transfers between devices, body(): lax.ppermute(jnp.stack([block[:keep] for block in arrived]), 'cell', SWAP)  5.12 us
    pallas_call x2, Pallas kernels, detect_inner(): pl.pallas_call(kernel, in_specs=[SMEM_SPEC] + [VMEM_SPEC] * (2 + len(stat...  4.77 us
    ppermute x1, starting transfers between devices, body(): first_peer = lax.ppermute(first, 'panel', SWAP)  3.01 us
    ppermute x1, waiting for transfers between devices, body(): first_peer = lax.ppermute(first, 'panel', SWAP)  1.96 us
  transfers between devices with their start and end apart: 14, of which 7 were waited for; matrix products, arithmetic and copies ran while one was open for 1% of the time, Pallas kernels for 33%

profile of v13, /device:TPU:0, one launch (start us, length us, event | category | flops | bytes accessed | tf_op | source)
XLA Modules:
  0.0 67.4 jit_solution(3865915451156902085)
XLA Ops:
  0.0 5.2 %shard_map.55 = (bf16[2,6,160,128]{3,2,1,0:T(8,128)(2,1)}, bf16[2,1,2,512,128]{4,3,2,1,0:T(8,128)(2,1)}, bf16[2,1,2,512,128]{4,3,2,1,0:T(8,128)(2,1)}) custom-call(s32[2,2]{1,0:T(2,128)} %counts_hbm.6, bf16[2,32,2,512,128]{4,3,2,1,0:T(8,128)(2,1)} %chan.7, bf16[2,32,14,2,512]{4,3,2,1,0:T(2,128)(2,1)} %bitcast.15), custom_call_target="tpu_custom_call" | custom-call | flops 905969664 | bytes 4194304 | tf_op jit(solution)/shard_map/pallas_call | solution.py:149
  5.2 3.0 %collective-permute-start = (bf16[2,6,160,128]{3,2,1,0:T(8,128)(2,1)}, bf16[2,6,160,128]{3,2,1,0:T(8,128)(2,1)S(1)}, u32[]{:S(2)}, u32[]{:S(2)}) collective-permute-start(bf16[2,6,160,128]{3,2,1,0:T(8,128)(2,1)} %get-tuple-element.21), channel_id=1, source_target_pairs={{0,8},{8,0},{1,9},{9,1},{2,10},{10,2},{3,11},{11,3},{4,12},{12,4},... | collective-permute-start | bytes 1474568 | tf_op jit(solution)/shard_map/ppermute | solution.py:449
  8.2 1.5 %collective-permute-start.2 = (bf16[2,1,2,512,128]{4,3,2,1,0:T(8,128)(2,1)}, bf16[2,1,2,512,128]{4,3,2,1,0:T(8,128)(2,1)S(1)}, u32[]{:S(2)}, u32[]{:S(2)}) collective-permute-start(bf16[2,1,2,512,128]{4,3,2,1,0:T(8,128)(2,1)} %get-tuple-element.25), channel_id=1, source_target_pairs={{0,1},{1,0},{2,3},{3,2},{4,5},{5,4},{6,7},{7,6},{8,9},{9,8},{10,11... | collective-permute-start | bytes 1572872 | tf_op jit(solution)/shard_map/ppermute | solution.py:451
  9.8 0.8 %collective-permute-start.3 = (bf16[2,1,2,512,128]{4,3,2,1,0:T(8,128)(2,1)}, bf16[2,1,2,512,128]{4,3,2,1,0:T(8,128)(2,1)S(1)}, u32[]{:S(2)}, u32[]{:S(2)}) collective-permute-start(bf16[2,1,2,512,128]{4,3,2,1,0:T(8,128)(2,1)} %get-tuple-element.26), channel_id=1, source_target_pairs={{1,2},{2,1},{3,4},{4,3},{5,6},{6,5},{9,10},{10,9},{11,12},{12,11},... | collective-permute-start | bytes 1572872 | tf_op jit(solution)/shard_map/ppermute | solution.py:452
  10.6 6.8 %shard_map.57 = bf16[2,9,160,128]{3,2,1,0:T(8,128)(2,1)} custom-call(s32[2,2]{1,0:T(2,128)} %counts_hbm.6, bf16[2,32,2,512,128]{4,3,2,1,0:T(8,128)(2,1)} %chan.7, bf16[2,32,14,2,512]{4,3,2,1,0:T(2,128)(2,1)} %bitcast.16), custom_call_target="tpu_custom_call" | custom-call | flops 1358954496 | bytes 5767168 | tf_op jit(solution)/shard_map/pallas_call | solution.py:149
  18.2 2.0 %collective-permute-done.peer_ref = bf16[2,6,160,128]{3,2,1,0:T(8,128)(2,1)S(1)} collective-permute-done((bf16[2,6,160,128]{3,2,1,0:T(8,128)(2,1)}, bf16[2,6,160,128]{3,2,1,0:T(8,128)(2,1)S(1)}, u32[]{:S(2)}, u32[]{:S(2)}) %collective-permute-start) | collective-permute-done | bytes 491552 | tf_op jit(solution)/shard_map/ppermute | solution.py:449
  20.2 9.0 %shard_map.56.own_ref = f32[2,15,160,128]{3,2,1,0:T(8,128)S(1)} custom-call(s32[2,2]{1,0:T(2,128)S(1)} %copy-done.1, bf16[2,32,2,512,128]{4,3,2,1,0:T(8,128)(2,1)} %chan.7, bf16[2,32,14,2,512]{4,3,2,1,0:T(2,128)(2,1)S(1)} %bitcast.17), custom_call_target="tpu_custom_call" | custom-call | flops 141557760 | bytes 557056 | tf_op jit(solution)/shard_map/pallas_call | solution.py:149
  29.2 1.4 %shard_map.59.refs_0_ = f32[2,512,128]{2,1,0:T(8,128)S(1)} custom-call(f32[2]{0:T(128)S(1)} %copy-done.2, f32[2,15,160,128]{3,2,1,0:T(8,128)S(1)} %shard_map.56.own_ref, bf16[2,6,160,128]{3,2,1,0:T(8,128)(2,1)S(1)} %collective-permute-done.peer_ref), custom_call_target="tpu_custom_call" | custom-call | flops 50331648 | bytes 3686400 | tf_op jit(solution)/shard_map/pallas_call | solution.py:337
  30.6 1.6 %collective-permute-done.2.refs_4_.near_ref = bf16[2,1,2,512,128]{4,3,2,1,0:T(8,128)(2,1)S(1)} collective-permute-done((bf16[2,1,2,512,128]{4,3,2,1,0:T(8,128)(2,1)}, bf16[2,1,2,512,128]{4,3,2,1,0:T(8,128)(2,1)S(1)}, u32[]{:S(2)}, u32[]{:S(2)}) %collective-permute-start.2) | collective-permute-done | bytes 524320 | tf_op jit(solution)/shard_map/ppermute | solution.py:451
  32.2 1.9 %shard_map.61 = bf16[2,160,128]{2,1,0:T(8,128)(2,1)S(1)} custom-call(s32[2,2]{1,0:T(2,128)S(1)} %copy-done.1, bf16[2,32,2,512,128]{4,3,2,1,0:T(8,128)(2,1)} %chan.7, bf16[2,32,14,2,512]{4,3,2,1,0:T(2,128)(2,1)S(1)} %bitcast.18, bf16[2,1,2,512,128]{4,3,2,1,0:T(8,128)(2,1)S(1)} %collective-permute-done.2.refs_4_.near_ref, ...), custom_call_target="tpu_custom_call" | custom-call | flops 150994944 | bytes 1572864 | tf_op jit(solution)/shard_map/pallas_call | solution.py:261
  34.2 0.9 %collective-permute-start.4 = (bf16[2,160,128]{2,1,0:T(8,128)(2,1)S(1)}, bf16[2,160,128]{2,1,0:T(8,128)(2,1)S(1)}, u32[]{:S(2)}, u32[]{:S(2)}) collective-permute-start(bf16[2,160,128]{2,1,0:T(8,128)(2,1)S(1)} %shard_map.61), channel_id=1, source_target_pairs={{0,8},{8,0},{1,9},{9,1},{2,10},{10,2},{3,11},{11,3},{4,12},{12,4},... | collective-permute-start | bytes 245768 | tf_op jit(solution)/shard_map/ppermute | solution.py:461
  35.7 3.4 %shard_map.60 = (f32[2,512,128]{2,1,0:T(8,128)S(1)}, f32[2,160,128]{2,1,0:T(8,128)S(1)}) custom-call(f32[2]{0:T(128)S(1)} %copy-done.2, f32[2,15,160,128]{3,2,1,0:T(8,128)S(1)} %shard_map.56.own_ref, bf16[2,9,160,128]{3,2,1,0:T(8,128)(2,1)} %collective-permute-done.1.peer_ref, f32[2,512,128]{2,1,0:T(8,128)S(1)} %shard_map.59.refs_0_, s32[2,2]{1,0:T(2,128)S(1)} %copy-done.1, ...), custom_call_target="tpu_custom_call" | custom-call | flops 75497472 | bytes 3686400 | tf_op jit(solution)/shard_map/pallas_call | solution.py:337
  39.1 1.5 %shard_map.62 = (bf16[448,128]{1,0:T(8,128)(2,1)S(1)}, bf16[448,128]{1,0:T(8,128)(2,1)S(1)}, bf16[448,128]{1,0:T(8,128)(2,1)S(1)}, bf16[448,128]{1,0:T(8,128)(2,1)S(1)}) custom-call(f32[2]{0:T(128)S(1)} %copy-done.2, f32[2,160,128]{2,1,0:T(8,128)S(1)} %get-tuple-element.31.edge_own_ref, bf16[2,160,128]{2,1,0:T(8,128)(2,1)S(1)} %collective-permute-done.4.edge_peer_ref, ...), custom_call_target="tpu_custom_call" | custom-call | flops 234881024 | bytes 524288 | tf_op jit(solution)/shard_map/pallas_call | solution.py:379
  40.7 4.6 %collective-permute-start.8 = (bf16[448,128]{1,0:T(8,128)(2,1)S(1)}, bf16[448,128]{1,0:T(8,128)(2,1)S(1)}, u32[]{:S(2)}, u32[]{:S(2)}) collective-permute-start(bf16[448,128]{1,0:T(8,128)(2,1)S(1)} %get-tuple-element.36), channel_id=1, source_target_pairs={{0,1},{1,2},{2,3},{3,0},{4,17},{5,18},{6,19},{7,16},{16,5},{17,6},... | collective-permute-start | bytes 344072 | tf_op jit(solution)/shard_map/ppermute | solution.py:486
  45.3 0.7 collective-permute-start.7
  46.0 1.1 %collective-permute-start.6 = (bf16[448,128]{1,0:T(8,128)(2,1)S(1)}, bf16[448,128]{1,0:T(8,128)(2,1)S(1)}, u32[]{:S(2)}, u32[]{:S(2)}) collective-permute-start(bf16[448,128]{1,0:T(8,128)(2,1)S(1)} %get-tuple-element.34), channel_id=1, source_target_pairs={{0,3},{1,0},{2,1},{3,2},{4,19},{5,16},{6,17},{7,18},{16,7},{17,4},... | collective-permute-start | bytes 344072 | tf_op jit(solution)/shard_map/ppermute | solution.py:486
  47.7 2.7 %collective-permute-done.8 = bf16[448,128]{1,0:T(8,128)(2,1)S(1)} collective-permute-done((bf16[448,128]{1,0:T(8,128)(2,1)S(1)}, bf16[448,128]{1,0:T(8,128)(2,1)S(1)}, u32[]{:S(2)}, u32[]{:S(2)}) %collective-permute-start.8) | collective-permute-done | bytes 114720 | tf_op jit(solution)/shard_map/ppermute | solution.py:486
  50.5 1.0 %collective-permute-done.6 = bf16[448,128]{1,0:T(8,128)(2,1)S(1)} collective-permute-done((bf16[448,128]{1,0:T(8,128)(2,1)S(1)}, bf16[448,128]{1,0:T(8,128)(2,1)S(1)}, u32[]{:S(2)}, u32[]{:S(2)}) %collective-permute-start.6) | collective-permute-done | bytes 114720 | tf_op jit(solution)/shard_map/ppermute | solution.py:486
  51.5 1.6 %collective-permute-done.5 = bf16[448,128]{1,0:T(8,128)(2,1)S(1)} collective-permute-done((bf16[448,128]{1,0:T(8,128)(2,1)S(1)}, bf16[448,128]{1,0:T(8,128)(2,1)S(1)}, u32[]{:S(2)}, u32[]{:S(2)}) %collective-permute-start.5) | collective-permute-done | bytes 114720 | tf_op jit(solution)/shard_map/ppermute | solution.py:486
  53.8 5.1 %collective-permute-start.11 = (bf16[4,224,128]{2,1,0:T(8,128)(2,1)S(1)}, bf16[4,224,128]{2,1,0:T(8,128)(2,1)S(1)}, u32[]{:S(2)}, u32[]{:S(2)}) collective-permute-start(bf16[4,224,128]{2,1,0:T(8,128)(2,1)S(1)} %pad_maximum_fusion.2), channel_id=1, source_target_pairs={{0,16},{16,0},{1,17},{17,1},{2,18},{18,2},{3,19},{19,3},{4,20},{20... | collective-permute-start | bytes 688136 | tf_op jit(solution)/shard_map/ppermute | solution.py:492
  58.9 3.2 %collective-permute-start.13 = (bf16[2,224,128]{2,1,0:T(8,128)(2,1)S(1)}, bf16[2,224,128]{2,1,0:T(8,128)(2,1)S(1)}, u32[]{:S(2)}, u32[]{:S(2)}) collective-permute-start(bf16[2,224,128]{2,1,0:T(8,128)(2,1)S(1)} %slice.29), channel_id=1, source_target_pairs={{0,16},{16,0},{1,17},{17,1},{2,18},{18,2},{3,19},{19,3},{4,20},{20... | collective-permute-start | bytes 344072 | tf_op jit(solution)/shard_map/ppermute | solution.py:493
  62.1 2.4 %collective-permute-start.12 = (bf16[2,224,128]{2,1,0:T(8,128)(2,1)S(1)}, bf16[2,224,128]{2,1,0:T(8,128)(2,1)S(1)}, u32[]{:S(2)}, u32[]{:S(2)}) collective-permute-start(bf16[2,224,128]{2,1,0:T(8,128)(2,1)S(1)} %slice.28), channel_id=1, source_target_pairs={{0,16},{16,0},{1,17},{17,1},{2,18},{18,2},{3,19},{19,3},{4,20},{20... | collective-permute-start | bytes 344072 | tf_op jit(solution)/shard_map/ppermute | solution.py:493
  64.7 0.9 %collective-permute-done.12.refs_5_ = bf16[2,224,128]{2,1,0:T(8,128)(2,1)S(1)} collective-permute-done((bf16[2,224,128]{2,1,0:T(8,128)(2,1)S(1)}, bf16[2,224,128]{2,1,0:T(8,128)(2,1)S(1)}, u32[]{:S(2)}, u32[]{:S(2)}) %collective-permute-start.12) | collective-permute-done | bytes 114720 | tf_op jit(solution)/shard_map/ppermute | solution.py:493
  65.5 1.9 %shard_map.63 = bf16[2,32,14,2,256]{4,3,2,1,0:T(2,128)(2,1)} custom-call(s32[8]{0:T(128)S(1)} %pad_add_fusion.1.source_ref, bf16[2,448,128]{2,1,0:T(8,128)(2,1)S(1)} %pad_maximum_fusion.refs_0_, bf16[2,448,128]{2,1,0:T(8,128)(2,1)S(1)} %pad_maximum_fusion.1.refs_1_, bf16[2,448,128]{2,1,0:T(8,128)(2,1)S(1)} %collective-permute-done.9.refs_2_, ...), custom_call_target="tpu_custom_call" | custom-call | tf_op jit(solution)/shard_map/pallas_call | solution.py:425
  (36 shorter events, 3.0 us)
Async XLA Ops:
  5.2 15.0 %collective-permute-start = (bf16[2,6,160,128]{3,2,1,0:T(8,128)(2,1)}, bf16[2,6,160,128]{3,2,1,0:T(8,128)(2,1)S(1)}, u32[]{:S(2)}, u32[]{:S(2)}) collective-permute-start(bf16[2,6,160,128]{3,2,1,0:T(8,128)(2,1)} %get-tuple-element.21), channel_id=1, source_target_pairs={{0,8},{8,0},{1,9},{9,1},{2,10},{10,2},{3,11},{11,3},{4,12},{12,4},... | collective-permute-start | bytes 1474568 | tf_op jit(solution)/shard_map/ppermute | solution.py:449
  8.2 24.0 %collective-permute-start.2 = (bf16[2,1,2,512,128]{4,3,2,1,0:T(8,128)(2,1)}, bf16[2,1,2,512,128]{4,3,2,1,0:T(8,128)(2,1)S(1)}, u32[]{:S(2)}, u32[]{:S(2)}) collective-permute-start(bf16[2,1,2,512,128]{4,3,2,1,0:T(8,128)(2,1)} %get-tuple-element.25), channel_id=1, source_target_pairs={{0,1},{1,0},{2,3},{3,2},{4,5},{5,4},{6,7},{7,6},{8,9},{9,8},{10,11... | collective-permute-start | bytes 1572872 | tf_op jit(solution)/shard_map/ppermute | solution.py:451
  9.8 8.2 %copy-start.3 = (s32[2,128,1]{1,2,0:T(1,128)S(1)}, s32[2,128,1]{1,2,0:T(1,128)}, u32[]{:S(2)}) copy-start(s32[2,128,1]{1,2,0:T(1,128)} %param.9) | copy-start | bytes 3076
  9.8 10.4 %copy-start = (bf16[2,32,2,14,512]{4,2,3,1,0:T(2,128)(2,1)S(1)}, bf16[2,32,2,14,512]{4,2,3,1,0:T(2,128)(2,1)}, u32[]{:S(2)}) copy-start(bf16[2,32,2,14,512]{4,2,3,1,0:T(2,128)(2,1)} %param.6) | copy-start | bytes 5505028
  9.8 10.4 %copy-start.1 = (s32[2,2]{1,0:T(2,128)S(1)}, s32[2,2]{1,0:T(2,128)}, u32[]{:S(2)}) copy-start(s32[2,2]{1,0:T(2,128)} %counts_hbm.6) | copy-start | bytes 52
  9.8 22.4 %collective-permute-start.3 = (bf16[2,1,2,512,128]{4,3,2,1,0:T(8,128)(2,1)}, bf16[2,1,2,512,128]{4,3,2,1,0:T(8,128)(2,1)S(1)}, u32[]{:S(2)}, u32[]{:S(2)}) collective-permute-start(bf16[2,1,2,512,128]{4,3,2,1,0:T(8,128)(2,1)} %get-tuple-element.26), channel_id=1, source_target_pairs={{1,2},{2,1},{3,4},{4,3},{5,6},{6,5},{9,10},{10,9},{11,12},{12,11},... | collective-permute-start | bytes 1572872 | tf_op jit(solution)/shard_map/ppermute | solution.py:452
  17.4 18.3 %collective-permute-start.1 = (bf16[2,9,160,128]{3,2,1,0:T(8,128)(2,1)}, bf16[2,9,160,128]{3,2,1,0:T(8,128)(2,1)}, u32[]{:S(2)}, u32[]{:S(2)}) collective-permute-start(bf16[2,9,160,128]{3,2,1,0:T(8,128)(2,1)} %shard_map.57), channel_id=1, source_target_pairs={{0,8},{8,0},{1,9},{9,1},{2,10},{10,2},{3,11},{11,3},{4,12},{12,4},... | collective-permute-start | bytes 2211848 | tf_op jit(solution)/shard_map/ppermute | solution.py:456
  18.2 11.0 %copy-start.2 = (f32[2]{0:T(128)S(1)}, f32[2]{0:T(128)}, u32[]{:S(2)}) copy-start(f32[2]{0:T(128)} %noise_ref.5) | copy-start | bytes 28
  34.2 5.0 %collective-permute-start.4 = (bf16[2,160,128]{2,1,0:T(8,128)(2,1)S(1)}, bf16[2,160,128]{2,1,0:T(8,128)(2,1)S(1)}, u32[]{:S(2)}, u32[]{:S(2)}) collective-permute-start(bf16[2,160,128]{2,1,0:T(8,128)(2,1)S(1)} %shard_map.61), channel_id=1, source_target_pairs={{0,8},{8,0},{1,9},{9,1},{2,10},{10,2},{3,11},{11,3},{4,12},{12,4},... | collective-permute-start | bytes 245768 | tf_op jit(solution)/shard_map/ppermute | solution.py:461
  40.7 9.7 %collective-permute-start.8 = (bf16[448,128]{1,0:T(8,128)(2,1)S(1)}, bf16[448,128]{1,0:T(8,128)(2,1)S(1)}, u32[]{:S(2)}, u32[]{:S(2)}) collective-permute-start(bf16[448,128]{1,0:T(8,128)(2,1)S(1)} %get-tuple-element.36), channel_id=1, source_target_pairs={{0,1},{1,2},{2,3},{3,0},{4,17},{5,18},{6,19},{7,16},{16,5},{17,6},... | collective-permute-start | bytes 344072 | tf_op jit(solution)/shard_map/ppermute | solution.py:486
  45.3 5.0 %collective-permute-start.7 = (bf16[448,128]{1,0:T(8,128)(2,1)S(1)}, bf16[448,128]{1,0:T(8,128)(2,1)S(1)}, u32[]{:S(2)}, u32[]{:S(2)}) collective-permute-start(bf16[448,128]{1,0:T(8,128)(2,1)S(1)} %get-tuple-element.35), channel_id=1, source_target_pairs={{0,0},{1,1},{2,2},{3,3},{4,16},{5,17},{6,18},{7,19},{16,4},{17,5},... | collective-permute-start | bytes 344072 | tf_op jit(solution)/shard_map/ppermute | solution.py:486
  46.0 5.5 %collective-permute-start.6 = (bf16[448,128]{1,0:T(8,128)(2,1)S(1)}, bf16[448,128]{1,0:T(8,128)(2,1)S(1)}, u32[]{:S(2)}, u32[]{:S(2)}) collective-permute-start(bf16[448,128]{1,0:T(8,128)(2,1)S(1)} %get-tuple-element.34), channel_id=1, source_target_pairs={{0,3},{1,0},{2,1},{3,2},{4,19},{5,16},{6,17},{7,18},{16,7},{17,4},... | collective-permute-start | bytes 344072 | tf_op jit(solution)/shard_map/ppermute | solution.py:486
  47.1 6.0 %collective-permute-start.5 = (bf16[448,128]{1,0:T(8,128)(2,1)S(1)}, bf16[448,128]{1,0:T(8,128)(2,1)S(1)}, u32[]{:S(2)}, u32[]{:S(2)}) collective-permute-start(bf16[448,128]{1,0:T(8,128)(2,1)S(1)} %get-tuple-element.33), channel_id=1, source_target_pairs={{0,2},{1,3},{2,0},{3,1},{4,18},{5,19},{6,16},{7,17},{16,6},{17,7},... | collective-permute-start | bytes 344072 | tf_op jit(solution)/shard_map/ppermute | solution.py:486
  50.4 8.5 %collective-permute-start.10 = (bf16[2,448,128]{2,1,0:T(8,128)(2,1)S(1)}, bf16[2,448,128]{2,1,0:T(8,128)(2,1)S(1)}, u32[]{:S(2)}, u32[]{:S(2)}) collective-permute-start(bf16[2,448,128]{2,1,0:T(8,128)(2,1)S(1)} %pad_maximum_fusion.1.refs_1_), channel_id=1, source_target_pairs={{0,8},{8,0},{1,9},{9,1},{2,10},{10,2},{3,11},{11,3},{4,12},{12,4},... | collective-permute-start | bytes 688136 | tf_op jit(solution)/shard_map/ppermute | solution.py:491
  53.1 9.0 %collective-permute-start.9 = (bf16[2,448,128]{2,1,0:T(8,128)(2,1)S(1)}, bf16[2,448,128]{2,1,0:T(8,128)(2,1)S(1)}, u32[]{:S(2)}, u32[]{:S(2)}) collective-permute-start(bf16[2,448,128]{2,1,0:T(8,128)(2,1)S(1)} %pad_maximum_fusion.refs_0_), channel_id=1, source_target_pairs={{0,8},{8,0},{1,9},{9,1},{2,10},{10,2},{3,11},{11,3},{4,12},{12,4},... | collective-permute-start | bytes 688136 | tf_op jit(solution)/shard_map/ppermute | solution.py:491
  53.8 10.9 %collective-permute-start.11 = (bf16[4,224,128]{2,1,0:T(8,128)(2,1)S(1)}, bf16[4,224,128]{2,1,0:T(8,128)(2,1)S(1)}, u32[]{:S(2)}, u32[]{:S(2)}) collective-permute-start(bf16[4,224,128]{2,1,0:T(8,128)(2,1)S(1)} %pad_maximum_fusion.2), channel_id=1, source_target_pairs={{0,16},{16,0},{1,17},{17,1},{2,18},{18,2},{3,19},{19,3},{4,20},{20... | collective-permute-start | bytes 688136 | tf_op jit(solution)/shard_map/ppermute | solution.py:492
  58.9 5.8 %collective-permute-start.13 = (bf16[2,224,128]{2,1,0:T(8,128)(2,1)S(1)}, bf16[2,224,128]{2,1,0:T(8,128)(2,1)S(1)}, u32[]{:S(2)}, u32[]{:S(2)}) collective-permute-start(bf16[2,224,128]{2,1,0:T(8,128)(2,1)S(1)} %slice.29), channel_id=1, source_target_pairs={{0,16},{16,0},{1,17},{17,1},{2,18},{18,2},{3,19},{19,3},{4,20},{20... | collective-permute-start | bytes 344072 | tf_op jit(solution)/shard_map/ppermute | solution.py:493
  62.1 3.4 %collective-permute-start.12 = (bf16[2,224,128]{2,1,0:T(8,128)(2,1)S(1)}, bf16[2,224,128]{2,1,0:T(8,128)(2,1)S(1)}, u32[]{:S(2)}, u32[]{:S(2)}) collective-permute-start(bf16[2,224,128]{2,1,0:T(8,128)(2,1)S(1)} %slice.28), channel_id=1, source_target_pairs={{0,16},{16,0},{1,17},{17,1},{2,18},{18,2},{3,19},{19,3},{4,20},{20... | collective-permute-start | bytes 344072 | tf_op jit(solution)/shard_map/ppermute | solution.py:493

commit v14 on v12

--- a/solution.py
+++ b/solution.py
@@ -430,7 +430,7 @@
     samples = jnp.transpose(received, (0, 1, 3, 2, 4))
 
     inner = half - 1
-    count = inner * 2 // 5
+    count = inner // 2
     first, near, far = inner_gram(
         user_count, channel, samples, True, (1, half), count, BF16, limit=56 << 20, ends=True
     )
@@ -458,7 +458,7 @@
     position = lax.iota(jnp.int32, cells * users)
     earlier = (keys[:, None] == keys[None, :]) & (position[None, :] < position[:, None])
     rank = jnp.sum(earlier.astype(jnp.int32), axis=1)
-    turn = (rank // per_device - sc % reach) % reach * 2 + (keys // cells == sc // reach).astype(jnp.int32)
+    turn = (rank // per_device - sc % reach - reach // 2) % reach * 2 + (keys // cells == sc // reach).astype(jnp.int32)
     column = ((turn * cells + keys % cells) * per_device + rank % per_device) * 2
     column = jnp.concatenate([column, column + 1])
     width = 2 * cells * per_device
@@ -466,14 +466,14 @@
 
     messages = detect_edge(noise_power, edge_own, edge_peer, state, onehot, symbols, reach)
     arrived = []
-    for b in range(reach):
+    for b in [(n + reach // 2) % reach for n in range(reach)]:
         pairs = [
             (s * n_sc + j, j // reach * n_sc + s * reach + (j % reach + b) % reach)
             for s in range(n_cell)
             for j in range(n_sc)
         ]
-        arrived.append(lax.ppermute(messages[b], ("cell", "sc"), pairs))
-    turns = (sc % reach - lax.iota(jnp.int32, reach)) % reach
+        arrived.append(lax.ppermute(messages[len(arrived)], ("cell", "sc"), pairs))
+    turns = (sc % reach - lax.iota(jnp.int32, reach) - reach // 2) % reach
     sources = jnp.concatenate([cell * reach + turns, (1 - cell) * reach + turns])
     keep = symbols * half
     mine = [jnp.stack(arrived[: reach // 2]), jnp.stack(arrived[reach // 2 :])]

time: 68 us -> 68.4 us (level)
  starting transfers between devices: 16.6 us -> 26.5 us
  waiting for transfers between devices: 18.3 us -> 8.9 us
    ppermute x2, waiting for transfers between devices: 6.65 us -> 0.01 us  [body(): theirs = [lax.ppermute(group, 'panel', SWAP) for group in mine]]
    ppermute x2, starting transfers between devices: 0.14 us -> 5.66 us  [body(): others += [lax.ppermute(group[:, :keep], 'cell', SWAP) for group in theirs]]
    ppermute x4, waiting for transfers between devices: 6.87 us -> 3.32 us  [body(): arrived.append(lax.ppermute(messages[len(arrived)], ('cell', 'sc'), pairs))]
    ppermute x1, starting transfers between devices: 3.23 us -> 6.09 us  [body(): lax.ppermute(jnp.stack([block[:keep] for block in arrived]), 'cell', SWAP)]
    ppermute x1, waiting for transfers between devices: 1.96 us -> 4.69 us  [body(): first_peer = lax.ppermute(first, 'panel', SWAP)]
    ppermute x1, waiting for transfers between devices: 1.61 us -> 0.01 us  [body(): near = lax.ppermute(near, 'sc', [(i, i ^ 1) for i in range(n_sc)])]
    ppermute x1, starting transfers between devices: 0.89 us -> 2.13 us  [body(): lax.ppermute(edge_gram(user_count, channel, samples, near, far, True, BF1...]
  transfers between devices with their start and end apart: 14 -> 14, of which waited for: 8 -> 5; matrix products, arithmetic and copies ran while one was open for 1% -> 1% of each run, Pallas kernels for 34% -> 33%
where the time goes in v14:
time: 68.4 us; the launch traced here: 68.2 us
  Pallas kernels  31.9 us (47%)
  starting transfers between devices  26.5 us (39%)
  waiting for transfers between devices  8.9 us (13%)
    pallas_call x3, Pallas kernels, inner_gram(): pl.pallas_call(kernel, in_specs=[HBM_SPEC] * 3, out_specs=[VMEM_SPEC] + [...  21 us
    ppermute x1, starting transfers between devices, body(): lax.ppermute(jnp.stack([block[:keep] for block in arrived]), 'cell', SWAP)  6.09 us
    ppermute x2, starting transfers between devices, body(): others += [lax.ppermute(group[:, :keep], 'cell', SWAP) for group in theirs]  5.66 us
    ppermute x4, starting transfers between devices, body(): arrived.append(lax.ppermute(messages[len(arrived)], ('cell', 'sc'), pairs))  5.26 us
    ppermute x1, waiting for transfers between devices, body(): first_peer = lax.ppermute(first, 'panel', SWAP)  4.69 us
    pallas_call x2, Pallas kernels, edge_gram(): pl.pallas_call(kernel, in_specs=[HBM_SPEC] * 5, out_specs=VMEM_SPEC, out_...  3.96 us
    pallas_call x2, Pallas kernels, detect_inner(): pl.pallas_call(kernel, in_specs=[SMEM_SPEC] + [VMEM_SPEC] * (2 + len(stat...  3.53 us
    ppermute x4, waiting for transfers between devices, body(): arrived.append(lax.ppermute(messages[len(arrived)], ('cell', 'sc'), pairs))  3.32 us
  transfers between devices with their start and end apart: 14, of which 5 were waited for; matrix products, arithmetic and copies ran while one was open for 1% of the time, Pallas kernels for 33%

profile of v14, /device:TPU:0, one launch (start us, length us, event | category | flops | bytes accessed | tf_op | source)
XLA Modules:
  0.0 68.2 jit_solution(13240289334592927615)
XLA Ops:
  0.0 5.8 %shard_map.55 = (bf16[2,7,160,128]{3,2,1,0:T(8,128)(2,1)}, bf16[2,1,2,512,128]{4,3,2,1,0:T(8,128)(2,1)}, bf16[2,1,2,512,128]{4,3,2,1,0:T(8,128)(2,1)}) custom-call(s32[2,2]{1,0:T(2,128)} %counts_hbm.8, bf16[2,32,2,512,128]{4,3,2,1,0:T(8,128)(2,1)} %chan.9, bf16[2,32,14,2,512]{4,3,2,1,0:T(2,128)(2,1)} %bitcast.15), custom_call_target="tpu_custom_call" | custom-call | flops 1056964608 | bytes 4718592 | tf_op jit(solution)/shard_map/pallas_call | solution.py:149
  5.8 3.0 %collective-permute-start.2 = (bf16[2,7,160,128]{3,2,1,0:T(8,128)(2,1)}, bf16[2,7,160,128]{3,2,1,0:T(8,128)(2,1)}, u32[]{:S(2)}, u32[]{:S(2)}) collective-permute-start(bf16[2,7,160,128]{3,2,1,0:T(8,128)(2,1)} %get-tuple-element.25), channel_id=1, source_target_pairs={{0,8},{8,0},{1,9},{9,1},{2,10},{10,2},{3,11},{11,3},{4,12},{12,4},... | collective-permute-start | bytes 1720328 | tf_op jit(solution)/shard_map/ppermute | solution.py:437
  8.8 1.5 %collective-permute-start = (bf16[2,1,2,512,128]{4,3,2,1,0:T(8,128)(2,1)}, bf16[2,1,2,512,128]{4,3,2,1,0:T(8,128)(2,1)S(1)}, u32[]{:S(2)}, u32[]{:S(2)}) collective-permute-start(bf16[2,1,2,512,128]{4,3,2,1,0:T(8,128)(2,1)} %get-tuple-element.23), channel_id=1, source_target_pairs={{0,1},{1,0},{2,3},{3,2},{4,5},{5,4},{6,7},{7,6},{8,9},{9,8},{10,11... | collective-permute-start | bytes 1572872 | tf_op jit(solution)/shard_map/ppermute | solution.py:439
  10.3 0.8 %collective-permute-start.1 = (bf16[2,1,2,512,128]{4,3,2,1,0:T(8,128)(2,1)}, bf16[2,1,2,512,128]{4,3,2,1,0:T(8,128)(2,1)S(1)}, u32[]{:S(2)}, u32[]{:S(2)}) collective-permute-start(bf16[2,1,2,512,128]{4,3,2,1,0:T(8,128)(2,1)} %get-tuple-element.24), channel_id=1, source_target_pairs={{1,2},{2,1},{3,4},{4,3},{5,6},{6,5},{9,10},{10,9},{11,12},{12,11},... | collective-permute-start | bytes 1572872 | tf_op jit(solution)/shard_map/ppermute | solution.py:440
  11.1 6.2 %shard_map.60 = bf16[2,8,160,128]{3,2,1,0:T(8,128)(2,1)} custom-call(s32[2,2]{1,0:T(2,128)} %counts_hbm.8, bf16[2,32,2,512,128]{4,3,2,1,0:T(8,128)(2,1)} %chan.9, bf16[2,32,14,2,512]{4,3,2,1,0:T(2,128)(2,1)} %bitcast.16), custom_call_target="tpu_custom_call" | custom-call | flops 1207959552 | bytes 5242880 | tf_op jit(solution)/shard_map/pallas_call | solution.py:149
  18.2 4.7 %collective-permute-done.2.peer_ref = bf16[2,7,160,128]{3,2,1,0:T(8,128)(2,1)} collective-permute-done((bf16[2,7,160,128]{3,2,1,0:T(8,128)(2,1)}, bf16[2,7,160,128]{3,2,1,0:T(8,128)(2,1)}, u32[]{:S(2)}, u32[]{:S(2)}) %collective-permute-start.2) | collective-permute-done | bytes 573472 | tf_op jit(solution)/shard_map/ppermute | solution.py:437
  22.9 9.0 %shard_map.57.own_ref = f32[2,15,160,128]{3,2,1,0:T(8,128)S(1)} custom-call(s32[2,2]{1,0:T(2,128)S(1)} %copy-done.1, bf16[2,32,2,512,128]{4,3,2,1,0:T(8,128)(2,1)} %chan.9, bf16[2,32,14,2,512]{4,3,2,1,0:T(2,128)(2,1)S(1)} %bitcast.17), custom_call_target="tpu_custom_call" | custom-call | flops 141557760 | bytes 557056 | tf_op jit(solution)/shard_map/pallas_call | solution.py:149
  32.0 2.0 %shard_map.58.refs_0_ = f32[2,512,128]{2,1,0:T(8,128)S(1)} custom-call(f32[2]{0:T(128)S(1)} %copy-done.2, f32[2,15,160,128]{3,2,1,0:T(8,128)S(1)} %shard_map.57.own_ref, bf16[2,7,160,128]{3,2,1,0:T(8,128)(2,1)} %collective-permute-done.2.peer_ref), custom_call_target="tpu_custom_call" | custom-call | flops 58720256 | bytes 3686400 | tf_op jit(solution)/shard_map/pallas_call | solution.py:326
  34.0 2.0 %shard_map.61 = bf16[2,160,128]{2,1,0:T(8,128)(2,1)S(1)} custom-call(s32[2,2]{1,0:T(2,128)S(1)} %copy-done.1, bf16[2,32,2,512,128]{4,3,2,1,0:T(8,128)(2,1)} %chan.9, bf16[2,32,14,2,512]{4,3,2,1,0:T(2,128)(2,1)S(1)} %bitcast.18, bf16[2,1,2,512,128]{4,3,2,1,0:T(8,128)(2,1)S(1)} %collective-permute-done.near_ref, ...), custom_call_target="tpu_custom_call" | custom-call | flops 150994944 | bytes 1572864 | tf_op jit(solution)/shard_map/pallas_call | solution.py:261
  36.0 2.1 %collective-permute-start.4 = (bf16[2,160,128]{2,1,0:T(8,128)(2,1)S(1)}, bf16[2,160,128]{2,1,0:T(8,128)(2,1)S(1)}, u32[]{:S(2)}, u32[]{:S(2)}) collective-permute-start(bf16[2,160,128]{2,1,0:T(8,128)(2,1)S(1)} %shard_map.61), channel_id=1, source_target_pairs={{0,8},{8,0},{1,9},{9,1},{2,10},{10,2},{3,11},{11,3},{4,12},{12,4},... | collective-permute-start | bytes 245768 | tf_op jit(solution)/shard_map/ppermute | solution.py:449
  38.3 2.0 %shard_map.59.edge_own_ref = f32[2,160,128]{2,1,0:T(8,128)S(1)} custom-call(s32[2,2]{1,0:T(2,128)S(1)} %copy-done.1, bf16[2,32,2,512,128]{4,3,2,1,0:T(8,128)(2,1)} %chan.9, bf16[2,32,14,2,512]{4,3,2,1,0:T(2,128)(2,1)S(1)} %bitcast.19, bf16[2,1,2,512,128]{4,3,2,1,0:T(8,128)(2,1)S(1)} %collective-permute-done.near_ref, ...), custom_call_target="tpu_custom_call" | custom-call | flops 150994944 | bytes 1572864 | tf_op jit(solution)/shard_map/pallas_call | solution.py:261
  40.3 1.6 %shard_map.62.state_ref = f32[2,512,128]{2,1,0:T(8,128)S(1)} custom-call(f32[2]{0:T(128)S(1)} %copy-done.2, f32[2,15,160,128]{3,2,1,0:T(8,128)S(1)} %shard_map.57.own_ref, bf16[2,8,160,128]{3,2,1,0:T(8,128)(2,1)S(1)} %collective-permute-done.3.peer_ref, f32[2,512,128]{2,1,0:T(8,128)S(1)} %shard_map.58.refs_0_), custom_call_target="tpu_custom_call" | custom-call | flops 67108864 | bytes 3686400 | tf_op jit(solution)/shard_map/pallas_call | solution.py:326
  41.9 1.5 %shard_map.63 = (bf16[448,128]{1,0:T(8,128)(2,1)S(1)}, bf16[448,128]{1,0:T(8,128)(2,1)S(1)}, bf16[448,128]{1,0:T(8,128)(2,1)S(1)}, bf16[448,128]{1,0:T(8,128)(2,1)S(1)}) custom-call(f32[2]{0:T(128)S(1)} %copy-done.2, f32[2,160,128]{2,1,0:T(8,128)S(1)} %shard_map.59.edge_own_ref, bf16[2,160,128]{2,1,0:T(8,128)(2,1)S(1)} %collective-permute-done.4.edge_peer_ref, ...), custom_call_target="tpu_custom_call" | custom-call | flops 234881024 | bytes 524288 | tf_op jit(solution)/shard_map/pallas_call | solution.py:367
  43.4 1.6 %collective-permute-start.8 = (bf16[448,128]{1,0:T(8,128)(2,1)S(1)}, bf16[448,128]{1,0:T(8,128)(2,1)S(1)}, u32[]{:S(2)}, u32[]{:S(2)}) collective-permute-start(bf16[448,128]{1,0:T(8,128)(2,1)S(1)} %get-tuple-element.36), channel_id=1, source_target_pairs={{0,1},{1,2},{2,3},{3,0},{4,17},{5,18},{6,19},{7,16},{16,5},{17,6},... | collective-permute-start | bytes 344072 | tf_op jit(solution)/shard_map/ppermute | solution.py:475
  45.7 1.5 %collective-permute-start.6 = (bf16[448,128]{1,0:T(8,128)(2,1)S(1)}, bf16[448,128]{1,0:T(8,128)(2,1)S(1)}, u32[]{:S(2)}, u32[]{:S(2)}) collective-permute-start(bf16[448,128]{1,0:T(8,128)(2,1)S(1)} %get-tuple-element.34), channel_id=1, source_target_pairs={{0,3},{1,0},{2,1},{3,2},{4,19},{5,16},{6,17},{7,18},{16,7},{17,4},... | collective-permute-start | bytes 344072 | tf_op jit(solution)/shard_map/ppermute | solution.py:475
  47.1 1.6 %collective-permute-start.5 = (bf16[448,128]{1,0:T(8,128)(2,1)S(1)}, bf16[448,128]{1,0:T(8,128)(2,1)S(1)}, u32[]{:S(2)}, u32[]{:S(2)}) collective-permute-start(bf16[448,128]{1,0:T(8,128)(2,1)S(1)} %get-tuple-element.33), channel_id=1, source_target_pairs={{0,2},{1,3},{2,0},{3,1},{4,18},{5,19},{6,16},{7,17},{16,6},{17,7},... | collective-permute-start | bytes 344072 | tf_op jit(solution)/shard_map/ppermute | solution.py:475
  49.9 1.8 %collective-permute-done.6 = bf16[448,128]{1,0:T(8,128)(2,1)S(1)} collective-permute-done((bf16[448,128]{1,0:T(8,128)(2,1)S(1)}, bf16[448,128]{1,0:T(8,128)(2,1)S(1)}, u32[]{:S(2)}, u32[]{:S(2)}) %collective-permute-start.6) | collective-permute-done | bytes 114720 | tf_op jit(solution)/shard_map/ppermute | solution.py:475
  51.8 1.0 %collective-permute-done.5 = bf16[448,128]{1,0:T(8,128)(2,1)S(1)} collective-permute-done((bf16[448,128]{1,0:T(8,128)(2,1)S(1)}, bf16[448,128]{1,0:T(8,128)(2,1)S(1)}, u32[]{:S(2)}, u32[]{:S(2)}) %collective-permute-start.5) | collective-permute-done | bytes 114720 | tf_op jit(solution)/shard_map/ppermute | solution.py:475
  52.8 0.7 %collective-permute-start.9 = (bf16[2,448,128]{2,1,0:T(8,128)(2,1)S(1)}, bf16[2,448,128]{2,1,0:T(8,128)(2,1)S(1)}, u32[]{:S(2)}, u32[]{:S(2)}) collective-permute-start(bf16[2,448,128]{2,1,0:T(8,128)(2,1)S(1)} %pad_maximum_fusion.refs_0_), channel_id=1, source_target_pairs={{0,8},{8,0},{1,9},{9,1},{2,10},{10,2},{3,11},{11,3},{4,12},{12,4},... | collective-permute-start | bytes 688136 | tf_op jit(solution)/shard_map/ppermute | solution.py:480
  53.6 6.1 %collective-permute-start.11 = (bf16[4,224,128]{2,1,0:T(8,128)(2,1)S(1)}, bf16[4,224,128]{2,1,0:T(8,128)(2,1)S(1)}, u32[]{:S(2)}, u32[]{:S(2)}) collective-permute-start(bf16[4,224,128]{2,1,0:T(8,128)(2,1)S(1)} %pad_maximum_fusion.2), channel_id=1, source_target_pairs={{0,16},{16,0},{1,17},{17,1},{2,18},{18,2},{3,19},{19,3},{4,20},{20... | collective-permute-start | bytes 688136 | tf_op jit(solution)/shard_map/ppermute | solution.py:481
  59.7 3.2 %collective-permute-start.13 = (bf16[2,224,128]{2,1,0:T(8,128)(2,1)S(1)}, bf16[2,224,128]{2,1,0:T(8,128)(2,1)S(1)}, u32[]{:S(2)}, u32[]{:S(2)}) collective-permute-start(bf16[2,224,128]{2,1,0:T(8,128)(2,1)S(1)} %slice.29), channel_id=1, source_target_pairs={{0,16},{16,0},{1,17},{17,1},{2,18},{18,2},{3,19},{19,3},{4,20},{20... | collective-permute-start | bytes 344072 | tf_op jit(solution)/shard_map/ppermute | solution.py:482
  62.9 2.4 %collective-permute-start.12 = (bf16[2,224,128]{2,1,0:T(8,128)(2,1)S(1)}, bf16[2,224,128]{2,1,0:T(8,128)(2,1)S(1)}, u32[]{:S(2)}, u32[]{:S(2)}) collective-permute-start(bf16[2,224,128]{2,1,0:T(8,128)(2,1)S(1)} %slice.28), channel_id=1, source_target_pairs={{0,16},{16,0},{1,17},{17,1},{2,18},{18,2},{3,19},{19,3},{4,20},{20... | collective-permute-start | bytes 344072 | tf_op jit(solution)/shard_map/ppermute | solution.py:482
  65.4 0.9 %collective-permute-done.12.refs_5_ = bf16[2,224,128]{2,1,0:T(8,128)(2,1)S(1)} collective-permute-done((bf16[2,224,128]{2,1,0:T(8,128)(2,1)S(1)}, bf16[2,224,128]{2,1,0:T(8,128)(2,1)S(1)}, u32[]{:S(2)}, u32[]{:S(2)}) %collective-permute-start.12) | collective-permute-done | bytes 114720 | tf_op jit(solution)/shard_map/ppermute | solution.py:482
  66.3 1.9 %shard_map.64 = bf16[2,32,14,2,256]{4,3,2,1,0:T(2,128)(2,1)} custom-call(s32[8]{0:T(128)S(1)} %pad_add_fusion.1.source_ref, bf16[2,448,128]{2,1,0:T(8,128)(2,1)S(1)} %pad_maximum_fusion.refs_0_, bf16[2,448,128]{2,1,0:T(8,128)(2,1)S(1)} %pad_maximum_fusion.1.refs_1_, bf16[2,448,128]{2,1,0:T(8,128)(2,1)S(1)} %collective-permute-done.9.refs_2_, ...), custom_call_target="tpu_custom_call" | custom-call | tf_op jit(solution)/shard_map/pallas_call | solution.py:413
  (37 shorter events, 3.2 us)
Async XLA Ops:
  5.8 17.1 %collective-permute-start.2 = (bf16[2,7,160,128]{3,2,1,0:T(8,128)(2,1)}, bf16[2,7,160,128]{3,2,1,0:T(8,128)(2,1)}, u32[]{:S(2)}, u32[]{:S(2)}) collective-permute-start(bf16[2,7,160,128]{3,2,1,0:T(8,128)(2,1)} %get-tuple-element.25), channel_id=1, source_target_pairs={{0,8},{8,0},{1,9},{9,1},{2,10},{10,2},{3,11},{11,3},{4,12},{12,4},... | collective-permute-start | bytes 1720328 | tf_op jit(solution)/shard_map/ppermute | solution.py:437
  8.8 25.2 %collective-permute-start = (bf16[2,1,2,512,128]{4,3,2,1,0:T(8,128)(2,1)}, bf16[2,1,2,512,128]{4,3,2,1,0:T(8,128)(2,1)S(1)}, u32[]{:S(2)}, u32[]{:S(2)}) collective-permute-start(bf16[2,1,2,512,128]{4,3,2,1,0:T(8,128)(2,1)} %get-tuple-element.23), channel_id=1, source_target_pairs={{0,1},{1,0},{2,3},{3,2},{4,5},{5,4},{6,7},{7,6},{8,9},{9,8},{10,11... | collective-permute-start | bytes 1572872 | tf_op jit(solution)/shard_map/ppermute | solution.py:439
  10.3 7.7 %copy-start.3 = (s32[2,128,1]{1,2,0:T(1,128)S(1)}, s32[2,128,1]{1,2,0:T(1,128)}, u32[]{:S(2)}) copy-start(s32[2,128,1]{1,2,0:T(1,128)} %param.9) | copy-start | bytes 3076
  10.3 12.6 %copy-start = (bf16[2,32,2,14,512]{4,2,3,1,0:T(2,128)(2,1)S(1)}, bf16[2,32,2,14,512]{4,2,3,1,0:T(2,128)(2,1)}, u32[]{:S(2)}) copy-start(bf16[2,32,2,14,512]{4,2,3,1,0:T(2,128)(2,1)} %param.6) | copy-start | bytes 5505028
  10.3 12.6 %copy-start.1 = (s32[2,2]{1,0:T(2,128)S(1)}, s32[2,2]{1,0:T(2,128)}, u32[]{:S(2)}) copy-start(s32[2,2]{1,0:T(2,128)} %counts_hbm.8) | copy-start | bytes 52
  10.3 23.6 %collective-permute-start.1 = (bf16[2,1,2,512,128]{4,3,2,1,0:T(8,128)(2,1)}, bf16[2,1,2,512,128]{4,3,2,1,0:T(8,128)(2,1)S(1)}, u32[]{:S(2)}, u32[]{:S(2)}) collective-permute-start(bf16[2,1,2,512,128]{4,3,2,1,0:T(8,128)(2,1)} %get-tuple-element.24), channel_id=1, source_target_pairs={{1,2},{2,1},{3,4},{4,3},{5,6},{6,5},{9,10},{10,9},{11,12},{12,11},... | collective-permute-start | bytes 1572872 | tf_op jit(solution)/shard_map/ppermute | solution.py:440
  17.3 23.0 %collective-permute-start.3 = (bf16[2,8,160,128]{3,2,1,0:T(8,128)(2,1)}, bf16[2,8,160,128]{3,2,1,0:T(8,128)(2,1)S(1)}, u32[]{:S(2)}, u32[]{:S(2)}) collective-permute-start(bf16[2,8,160,128]{3,2,1,0:T(8,128)(2,1)} %shard_map.60), channel_id=1, source_target_pairs={{0,8},{8,0},{1,9},{9,1},{2,10},{10,2},{3,11},{11,3},{4,12},{12,4},... | collective-permute-start | bytes 1966088 | tf_op jit(solution)/shard_map/ppermute | solution.py:444
  18.2 13.8 %copy-start.2 = (f32[2]{0:T(128)S(1)}, f32[2]{0:T(128)}, u32[]{:S(2)}) copy-start(f32[2]{0:T(128)} %noise_ref.5) | copy-start | bytes 28
  36.0 5.9 %collective-permute-start.4 = (bf16[2,160,128]{2,1,0:T(8,128)(2,1)S(1)}, bf16[2,160,128]{2,1,0:T(8,128)(2,1)S(1)}, u32[]{:S(2)}, u32[]{:S(2)}) collective-permute-start(bf16[2,160,128]{2,1,0:T(8,128)(2,1)S(1)} %shard_map.61), channel_id=1, source_target_pairs={{0,8},{8,0},{1,9},{9,1},{2,10},{10,2},{3,11},{11,3},{4,12},{12,4},... | collective-permute-start | bytes 245768 | tf_op jit(solution)/shard_map/ppermute | solution.py:449
  43.4 5.7 %collective-permute-start.8 = (bf16[448,128]{1,0:T(8,128)(2,1)S(1)}, bf16[448,128]{1,0:T(8,128)(2,1)S(1)}, u32[]{:S(2)}, u32[]{:S(2)}) collective-permute-start(bf16[448,128]{1,0:T(8,128)(2,1)S(1)} %get-tuple-element.36), channel_id=1, source_target_pairs={{0,1},{1,2},{2,3},{3,0},{4,17},{5,18},{6,19},{7,16},{16,5},{17,6},... | collective-permute-start | bytes 344072 | tf_op jit(solution)/shard_map/ppermute | solution.py:475
  45.0 4.2 %collective-permute-start.7 = (bf16[448,128]{1,0:T(8,128)(2,1)S(1)}, bf16[448,128]{1,0:T(8,128)(2,1)S(1)}, u32[]{:S(2)}, u32[]{:S(2)}) collective-permute-start(bf16[448,128]{1,0:T(8,128)(2,1)S(1)} %get-tuple-element.35), channel_id=1, source_target_pairs={{0,0},{1,1},{2,2},{3,3},{4,16},{5,17},{6,18},{7,19},{16,4},{17,5},... | collective-permute-start | bytes 344072 | tf_op jit(solution)/shard_map/ppermute | solution.py:475
  45.7 6.1 %collective-permute-start.6 = (bf16[448,128]{1,0:T(8,128)(2,1)S(1)}, bf16[448,128]{1,0:T(8,128)(2,1)S(1)}, u32[]{:S(2)}, u32[]{:S(2)}) collective-permute-start(bf16[448,128]{1,0:T(8,128)(2,1)S(1)} %get-tuple-element.34), channel_id=1, source_target_pairs={{0,3},{1,0},{2,1},{3,2},{4,19},{5,16},{6,17},{7,18},{16,7},{17,4},... | collective-permute-start | bytes 344072 | tf_op jit(solution)/shard_map/ppermute | solution.py:475
  47.1 5.6 %collective-permute-start.5 = (bf16[448,128]{1,0:T(8,128)(2,1)S(1)}, bf16[448,128]{1,0:T(8,128)(2,1)S(1)}, u32[]{:S(2)}, u32[]{:S(2)}) collective-permute-start(bf16[448,128]{1,0:T(8,128)(2,1)S(1)} %get-tuple-element.33), channel_id=1, source_target_pairs={{0,2},{1,3},{2,0},{3,1},{4,18},{5,19},{6,16},{7,17},{16,6},{17,7},... | collective-permute-start | bytes 344072 | tf_op jit(solution)/shard_map/ppermute | solution.py:475
  49.2 10.4 %collective-permute-start.10 = (bf16[2,448,128]{2,1,0:T(8,128)(2,1)S(1)}, bf16[2,448,128]{2,1,0:T(8,128)(2,1)S(1)}, u32[]{:S(2)}, u32[]{:S(2)}) collective-permute-start(bf16[2,448,128]{2,1,0:T(8,128)(2,1)S(1)} %pad_maximum_fusion.1.refs_1_), channel_id=1, source_target_pairs={{0,8},{8,0},{1,9},{9,1},{2,10},{10,2},{3,11},{11,3},{4,12},{12,4},... | collective-permute-start | bytes 688136 | tf_op jit(solution)/shard_map/ppermute | solution.py:480
  52.8 10.1 %collective-permute-start.9 = (bf16[2,448,128]{2,1,0:T(8,128)(2,1)S(1)}, bf16[2,448,128]{2,1,0:T(8,128)(2,1)S(1)}, u32[]{:S(2)}, u32[]{:S(2)}) collective-permute-start(bf16[2,448,128]{2,1,0:T(8,128)(2,1)S(1)} %pad_maximum_fusion.refs_0_), channel_id=1, source_target_pairs={{0,8},{8,0},{1,9},{9,1},{2,10},{10,2},{3,11},{11,3},{4,12},{12,4},... | collective-permute-start | bytes 688136 | tf_op jit(solution)/shard_map/ppermute | solution.py:480
  53.6 11.9 %collective-permute-start.11 = (bf16[4,224,128]{2,1,0:T(8,128)(2,1)S(1)}, bf16[4,224,128]{2,1,0:T(8,128)(2,1)S(1)}, u32[]{:S(2)}, u32[]{:S(2)}) collective-permute-start(bf16[4,224,128]{2,1,0:T(8,128)(2,1)S(1)} %pad_maximum_fusion.2), channel_id=1, source_target_pairs={{0,16},{16,0},{1,17},{17,1},{2,18},{18,2},{3,19},{19,3},{4,20},{20... | collective-permute-start | bytes 688136 | tf_op jit(solution)/shard_map/ppermute | solution.py:481
  59.7 5.8 %collective-permute-start.13 = (bf16[2,224,128]{2,1,0:T(8,128)(2,1)S(1)}, bf16[2,224,128]{2,1,0:T(8,128)(2,1)S(1)}, u32[]{:S(2)}, u32[]{:S(2)}) collective-permute-start(bf16[2,224,128]{2,1,0:T(8,128)(2,1)S(1)} %slice.29), channel_id=1, source_target_pairs={{0,16},{16,0},{1,17},{17,1},{2,18},{18,2},{3,19},{19,3},{4,20},{20... | collective-permute-start | bytes 344072 | tf_op jit(solution)/shard_map/ppermute | solution.py:482
  62.9 3.4 %collective-permute-start.12 = (bf16[2,224,128]{2,1,0:T(8,128)(2,1)S(1)}, bf16[2,224,128]{2,1,0:T(8,128)(2,1)S(1)}, u32[]{:S(2)}, u32[]{:S(2)}) collective-permute-start(bf16[2,224,128]{2,1,0:T(8,128)(2,1)S(1)} %slice.28), channel_id=1, source_target_pairs={{0,16},{16,0},{1,17},{17,1},{2,18},{18,2},{3,19},{19,3},{4,20},{20... | collective-permute-start | bytes 344072 | tf_op jit(solution)/shard_map/ppermute | solution.py:482

commit v15 on v14

--- a/solution.py
+++ b/solution.py
@@ -430,7 +430,7 @@
     samples = jnp.transpose(received, (0, 1, 3, 2, 4))
 
     inner = half - 1
-    count = inner // 2
+    count = inner * 2 // 5
     first, near, far = inner_gram(
         user_count, channel, samples, True, (1, half), count, BF16, limit=56 << 20, ends=True
     )

time: 68.4 us -> 67.1 us (0.981)
  starting transfers between devices: 26.5 us -> 24.7 us
    ppermute x1, waiting for transfers between devices: 4.69 us -> 1.96 us  [body(): first_peer = lax.ppermute(first, 'panel', SWAP)]
    ppermute x1, waiting for transfers between devices: 0.01 us -> 1.61 us  [body(): near = lax.ppermute(near, 'sc', [(i, i ^ 1) for i in range(n_sc)])]
    ppermute x4, waiting for transfers between devices: 3.32 us -> 4.82 us  [body(): arrived.append(lax.ppermute(messages[len(arrived)], ('cell', 'sc'), pairs))]
    ppermute x1, starting transfers between devices: 2.13 us -> 0.89 us  [body(): lax.ppermute(edge_gram(user_count, channel, samples, near, far, True, BF1...]
  transfers between devices with their start and end apart: 14 -> 14, of which waited for: 5 -> 6; matrix products, arithmetic and copies ran while one was open for 1% -> 1% of each run, Pallas kernels for 33% -> 35%
where the time goes in v15:
time: 67.1 us; the launch traced here: 66.8 us
  Pallas kernels  32 us (48%)
  starting transfers between devices  24.7 us (37%)
  waiting for transfers between devices  9.28 us (14%)
    pallas_call x3, Pallas kernels, inner_gram(): pl.pallas_call(kernel, in_specs=[HBM_SPEC] * 3, out_specs=[VMEM_SPEC] + [...  21.1 us
    ppermute x1, starting transfers between devices, body(): lax.ppermute(jnp.stack([block[:keep] for block in arrived]), 'cell', SWAP)  6.03 us
    ppermute x4, starting transfers between devices, body(): arrived.append(lax.ppermute(messages[len(arrived)], ('cell', 'sc'), pairs))  5.84 us
    ppermute x2, starting transfers between devices, body(): others += [lax.ppermute(group[:, :keep], 'cell', SWAP) for group in theirs]  5.28 us
    ppermute x4, waiting for transfers between devices, body(): arrived.append(lax.ppermute(messages[len(arrived)], ('cell', 'sc'), pairs))  4.82 us
    pallas_call x2, Pallas kernels, edge_gram(): pl.pallas_call(kernel, in_specs=[HBM_SPEC] * 5, out_specs=VMEM_SPEC, out_...  3.94 us
    pallas_call x2, Pallas kernels, detect_inner(): pl.pallas_call(kernel, in_specs=[SMEM_SPEC] + [VMEM_SPEC] * (2 + len(stat...  3.59 us
    ppermute x1, starting transfers between devices, body(): first_peer = lax.ppermute(first, 'panel', SWAP)  3.01 us
  transfers between devices with their start and end apart: 14, of which 6 were waited for; matrix products, arithmetic and copies ran while one was open for 1% of the time, Pallas kernels for 35%

profile of v15, /device:TPU:0, one launch (start us, length us, event | category | flops | bytes accessed | tf_op | source)
XLA Modules:
  0.0 66.8 jit_solution(13034066714870736759)
XLA Ops:
  0.0 5.2 %shard_map.55 = (bf16[2,6,160,128]{3,2,1,0:T(8,128)(2,1)}, bf16[2,1,2,512,128]{4,3,2,1,0:T(8,128)(2,1)}, bf16[2,1,2,512,128]{4,3,2,1,0:T(8,128)(2,1)}) custom-call(s32[2,2]{1,0:T(2,128)} %counts_hbm.8, bf16[2,32,2,512,128]{4,3,2,1,0:T(8,128)(2,1)} %chan.9, bf16[2,32,14,2,512]{4,3,2,1,0:T(2,128)(2,1)} %bitcast.15), custom_call_target="tpu_custom_call" | custom-call | flops 905969664 | bytes 4194304 | tf_op jit(solution)/shard_map/pallas_call | solution.py:149
  5.2 3.0 %collective-permute-start.2 = (bf16[2,6,160,128]{3,2,1,0:T(8,128)(2,1)}, bf16[2,6,160,128]{3,2,1,0:T(8,128)(2,1)S(1)}, u32[]{:S(2)}, u32[]{:S(2)}) collective-permute-start(bf16[2,6,160,128]{3,2,1,0:T(8,128)(2,1)} %get-tuple-element.25), channel_id=1, source_target_pairs={{0,8},{8,0},{1,9},{9,1},{2,10},{10,2},{3,11},{11,3},{4,12},{12,4},... | collective-permute-start | bytes 1474568 | tf_op jit(solution)/shard_map/ppermute | solution.py:437
  8.3 1.5 %collective-permute-start = (bf16[2,1,2,512,128]{4,3,2,1,0:T(8,128)(2,1)}, bf16[2,1,2,512,128]{4,3,2,1,0:T(8,128)(2,1)S(1)}, u32[]{:S(2)}, u32[]{:S(2)}) collective-permute-start(bf16[2,1,2,512,128]{4,3,2,1,0:T(8,128)(2,1)} %get-tuple-element.23), channel_id=1, source_target_pairs={{0,1},{1,0},{2,3},{3,2},{4,5},{5,4},{6,7},{7,6},{8,9},{9,8},{10,11... | collective-permute-start | bytes 1572872 | tf_op jit(solution)/shard_map/ppermute | solution.py:439
  10.6 6.8 %shard_map.60 = bf16[2,9,160,128]{3,2,1,0:T(8,128)(2,1)} custom-call(s32[2,2]{1,0:T(2,128)} %counts_hbm.8, bf16[2,32,2,512,128]{4,3,2,1,0:T(8,128)(2,1)} %chan.9, bf16[2,32,14,2,512]{4,3,2,1,0:T(2,128)(2,1)} %bitcast.16), custom_call_target="tpu_custom_call" | custom-call | flops 1358954496 | bytes 5767168 | tf_op jit(solution)/shard_map/pallas_call | solution.py:149
  18.2 2.0 %collective-permute-done.2.peer_ref = bf16[2,6,160,128]{3,2,1,0:T(8,128)(2,1)S(1)} collective-permute-done((bf16[2,6,160,128]{3,2,1,0:T(8,128)(2,1)}, bf16[2,6,160,128]{3,2,1,0:T(8,128)(2,1)S(1)}, u32[]{:S(2)}, u32[]{:S(2)}) %collective-permute-start.2) | collective-permute-done | bytes 491552 | tf_op jit(solution)/shard_map/ppermute | solution.py:437
  20.2 9.0 %shard_map.57.own_ref = f32[2,15,160,128]{3,2,1,0:T(8,128)S(1)} custom-call(s32[2,2]{1,0:T(2,128)S(1)} %copy-done.1, bf16[2,32,2,512,128]{4,3,2,1,0:T(8,128)(2,1)} %chan.9, bf16[2,32,14,2,512]{4,3,2,1,0:T(2,128)(2,1)S(1)} %bitcast.17), custom_call_target="tpu_custom_call" | custom-call | flops 141557760 | bytes 557056 | tf_op jit(solution)/shard_map/pallas_call | solution.py:149
  29.3 1.4 %shard_map.58.refs_0_ = f32[2,512,128]{2,1,0:T(8,128)S(1)} custom-call(f32[2]{0:T(128)S(1)} %copy-done.2, f32[2,15,160,128]{3,2,1,0:T(8,128)S(1)} %shard_map.57.own_ref, bf16[2,6,160,128]{3,2,1,0:T(8,128)(2,1)S(1)} %collective-permute-done.2.peer_ref), custom_call_target="tpu_custom_call" | custom-call | flops 50331648 | bytes 3686400 | tf_op jit(solution)/shard_map/pallas_call | solution.py:326
  30.6 1.6 %collective-permute-done.near_ref = bf16[2,1,2,512,128]{4,3,2,1,0:T(8,128)(2,1)S(1)} collective-permute-done((bf16[2,1,2,512,128]{4,3,2,1,0:T(8,128)(2,1)}, bf16[2,1,2,512,128]{4,3,2,1,0:T(8,128)(2,1)S(1)}, u32[]{:S(2)}, u32[]{:S(2)}) %collective-permute-start) | collective-permute-done | bytes 524320 | tf_op jit(solution)/shard_map/ppermute | solution.py:439
  32.2 1.9 %shard_map.61 = bf16[2,160,128]{2,1,0:T(8,128)(2,1)S(1)} custom-call(s32[2,2]{1,0:T(2,128)S(1)} %copy-done.1, bf16[2,32,2,512,128]{4,3,2,1,0:T(8,128)(2,1)} %chan.9, bf16[2,32,14,2,512]{4,3,2,1,0:T(2,128)(2,1)S(1)} %bitcast.18, bf16[2,1,2,512,128]{4,3,2,1,0:T(8,128)(2,1)S(1)} %collective-permute-done.near_ref, ...), custom_call_target="tpu_custom_call" | custom-call | flops 150994944 | bytes 1572864 | tf_op jit(solution)/shard_map/pallas_call | solution.py:261
  34.2 0.9 %collective-permute-start.4 = (bf16[2,160,128]{2,1,0:T(8,128)(2,1)S(1)}, bf16[2,160,128]{2,1,0:T(8,128)(2,1)S(1)}, u32[]{:S(2)}, u32[]{:S(2)}) collective-permute-start(bf16[2,160,128]{2,1,0:T(8,128)(2,1)S(1)} %shard_map.61), channel_id=1, source_target_pairs={{0,8},{8,0},{1,9},{9,1},{2,10},{10,2},{3,11},{11,3},{4,12},{12,4},... | collective-permute-start | bytes 245768 | tf_op jit(solution)/shard_map/ppermute | solution.py:449
  35.3 2.0 %shard_map.59.edge_own_ref = f32[2,160,128]{2,1,0:T(8,128)S(1)} custom-call(s32[2,2]{1,0:T(2,128)S(1)} %copy-done.1, bf16[2,32,2,512,128]{4,3,2,1,0:T(8,128)(2,1)} %chan.9, bf16[2,32,14,2,512]{4,3,2,1,0:T(2,128)(2,1)S(1)} %bitcast.19, bf16[2,1,2,512,128]{4,3,2,1,0:T(8,128)(2,1)S(1)} %collective-permute-done.near_ref, ...), custom_call_target="tpu_custom_call" | custom-call | flops 150994944 | bytes 1572864 | tf_op jit(solution)/shard_map/pallas_call | solution.py:261
  37.3 2.2 %shard_map.62.state_ref = f32[2,512,128]{2,1,0:T(8,128)S(1)} custom-call(f32[2]{0:T(128)S(1)} %copy-done.2, f32[2,15,160,128]{3,2,1,0:T(8,128)S(1)} %shard_map.57.own_ref, bf16[2,9,160,128]{3,2,1,0:T(8,128)(2,1)} %collective-permute-done.3.peer_ref, f32[2,512,128]{2,1,0:T(8,128)S(1)} %shard_map.58.refs_0_), custom_call_target="tpu_custom_call" | custom-call | flops 75497472 | bytes 3686400 | tf_op jit(solution)/shard_map/pallas_call | solution.py:326
  39.6 1.5 %shard_map.63 = (bf16[448,128]{1,0:T(8,128)(2,1)S(1)}, bf16[448,128]{1,0:T(8,128)(2,1)S(1)}, bf16[448,128]{1,0:T(8,128)(2,1)S(1)}, bf16[448,128]{1,0:T(8,128)(2,1)S(1)}) custom-call(f32[2]{0:T(128)S(1)} %copy-done.2, f32[2,160,128]{2,1,0:T(8,128)S(1)} %shard_map.59.edge_own_ref, bf16[2,160,128]{2,1,0:T(8,128)(2,1)S(1)} %collective-permute-done.4.edge_peer_ref, ...), custom_call_target="tpu_custom_call" | custom-call | flops 234881024 | bytes 524288 | tf_op jit(solution)/shard_map/pallas_call | solution.py:367
  41.1 3.0 %collective-permute-start.8 = (bf16[448,128]{1,0:T(8,128)(2,1)S(1)}, bf16[448,128]{1,0:T(8,128)(2,1)S(1)}, u32[]{:S(2)}, u32[]{:S(2)}) collective-permute-start(bf16[448,128]{1,0:T(8,128)(2,1)S(1)} %get-tuple-element.36), channel_id=1, source_target_pairs={{0,1},{1,2},{2,3},{3,0},{4,17},{5,18},{6,19},{7,16},{16,5},{17,6},... | collective-permute-start | bytes 344072 | tf_op jit(solution)/shard_map/ppermute | solution.py:475
  44.8 1.1 %collective-permute-start.6 = (bf16[448,128]{1,0:T(8,128)(2,1)S(1)}, bf16[448,128]{1,0:T(8,128)(2,1)S(1)}, u32[]{:S(2)}, u32[]{:S(2)}) collective-permute-start(bf16[448,128]{1,0:T(8,128)(2,1)S(1)} %get-tuple-element.34), channel_id=1, source_target_pairs={{0,3},{1,0},{2,1},{3,2},{4,19},{5,16},{6,17},{7,18},{16,7},{17,4},... | collective-permute-start | bytes 344072 | tf_op jit(solution)/shard_map/ppermute | solution.py:475
  45.9 1.1 %collective-permute-start.5 = (bf16[448,128]{1,0:T(8,128)(2,1)S(1)}, bf16[448,128]{1,0:T(8,128)(2,1)S(1)}, u32[]{:S(2)}, u32[]{:S(2)}) collective-permute-start(bf16[448,128]{1,0:T(8,128)(2,1)S(1)} %get-tuple-element.33), channel_id=1, source_target_pairs={{0,2},{1,3},{2,0},{3,1},{4,18},{5,19},{6,16},{7,17},{16,6},{17,7},... | collective-permute-start | bytes 344072 | tf_op jit(solution)/shard_map/ppermute | solution.py:475
  47.0 2.3 %collective-permute-done.8 = bf16[448,128]{1,0:T(8,128)(2,1)S(1)} collective-permute-done((bf16[448,128]{1,0:T(8,128)(2,1)S(1)}, bf16[448,128]{1,0:T(8,128)(2,1)S(1)}, u32[]{:S(2)}, u32[]{:S(2)}) %collective-permute-start.8) | collective-permute-done | bytes 114720 | tf_op jit(solution)/shard_map/ppermute | solution.py:475
  49.3 1.0 %collective-permute-done.6 = bf16[448,128]{1,0:T(8,128)(2,1)S(1)} collective-permute-done((bf16[448,128]{1,0:T(8,128)(2,1)S(1)}, bf16[448,128]{1,0:T(8,128)(2,1)S(1)}, u32[]{:S(2)}, u32[]{:S(2)}) %collective-permute-start.6) | collective-permute-done | bytes 114720 | tf_op jit(solution)/shard_map/ppermute | solution.py:475
  50.4 1.5 %collective-permute-done.5 = bf16[448,128]{1,0:T(8,128)(2,1)S(1)} collective-permute-done((bf16[448,128]{1,0:T(8,128)(2,1)S(1)}, bf16[448,128]{1,0:T(8,128)(2,1)S(1)}, u32[]{:S(2)}, u32[]{:S(2)}) %collective-permute-start.5) | collective-permute-done | bytes 114720 | tf_op jit(solution)/shard_map/ppermute | solution.py:475
  52.7 6.0 %collective-permute-start.11 = (bf16[4,224,128]{2,1,0:T(8,128)(2,1)S(1)}, bf16[4,224,128]{2,1,0:T(8,128)(2,1)S(1)}, u32[]{:S(2)}, u32[]{:S(2)}) collective-permute-start(bf16[4,224,128]{2,1,0:T(8,128)(2,1)S(1)} %pad_maximum_fusion.2), channel_id=1, source_target_pairs={{0,16},{16,0},{1,17},{17,1},{2,18},{18,2},{3,19},{19,3},{4,20},{20... | collective-permute-start | bytes 688136 | tf_op jit(solution)/shard_map/ppermute | solution.py:481
  58.7 2.8 %collective-permute-start.13 = (bf16[2,224,128]{2,1,0:T(8,128)(2,1)S(1)}, bf16[2,224,128]{2,1,0:T(8,128)(2,1)S(1)}, u32[]{:S(2)}, u32[]{:S(2)}) collective-permute-start(bf16[2,224,128]{2,1,0:T(8,128)(2,1)S(1)} %slice.29), channel_id=1, source_target_pairs={{0,16},{16,0},{1,17},{17,1},{2,18},{18,2},{3,19},{19,3},{4,20},{20... | collective-permute-start | bytes 344072 | tf_op jit(solution)/shard_map/ppermute | solution.py:482
  61.6 2.4 %collective-permute-start.12 = (bf16[2,224,128]{2,1,0:T(8,128)(2,1)S(1)}, bf16[2,224,128]{2,1,0:T(8,128)(2,1)S(1)}, u32[]{:S(2)}, u32[]{:S(2)}) collective-permute-start(bf16[2,224,128]{2,1,0:T(8,128)(2,1)S(1)} %slice.28), channel_id=1, source_target_pairs={{0,16},{16,0},{1,17},{17,1},{2,18},{18,2},{3,19},{19,3},{4,20},{20... | collective-permute-start | bytes 344072 | tf_op jit(solution)/shard_map/ppermute | solution.py:482
  64.1 0.9 %collective-permute-done.12.refs_5_ = bf16[2,224,128]{2,1,0:T(8,128)(2,1)S(1)} collective-permute-done((bf16[2,224,128]{2,1,0:T(8,128)(2,1)S(1)}, bf16[2,224,128]{2,1,0:T(8,128)(2,1)S(1)}, u32[]{:S(2)}, u32[]{:S(2)}) %collective-permute-start.12) | collective-permute-done | bytes 114720 | tf_op jit(solution)/shard_map/ppermute | solution.py:482
  65.0 1.9 %shard_map.64 = bf16[2,32,14,2,256]{4,3,2,1,0:T(2,128)(2,1)} custom-call(s32[8]{0:T(128)S(1)} %pad_add_fusion.1.source_ref, bf16[2,448,128]{2,1,0:T(8,128)(2,1)S(1)} %pad_maximum_fusion.refs_0_, bf16[2,448,128]{2,1,0:T(8,128)(2,1)S(1)} %pad_maximum_fusion.1.refs_1_, bf16[2,448,128]{2,1,0:T(8,128)(2,1)S(1)} %collective-permute-done.9.refs_2_, ...), custom_call_target="tpu_custom_call" | custom-call | tf_op jit(solution)/shard_map/pallas_call | solution.py:413
  (37 shorter events, 3.5 us)
Async XLA Ops:
  5.2 15.0 %collective-permute-start.2 = (bf16[2,6,160,128]{3,2,1,0:T(8,128)(2,1)}, bf16[2,6,160,128]{3,2,1,0:T(8,128)(2,1)S(1)}, u32[]{:S(2)}, u32[]{:S(2)}) collective-permute-start(bf16[2,6,160,128]{3,2,1,0:T(8,128)(2,1)} %get-tuple-element.25), channel_id=1, source_target_pairs={{0,8},{8,0},{1,9},{9,1},{2,10},{10,2},{3,11},{11,3},{4,12},{12,4},... | collective-permute-start | bytes 1474568 | tf_op jit(solution)/shard_map/ppermute | solution.py:437
  8.3 24.0 %collective-permute-start = (bf16[2,1,2,512,128]{4,3,2,1,0:T(8,128)(2,1)}, bf16[2,1,2,512,128]{4,3,2,1,0:T(8,128)(2,1)S(1)}, u32[]{:S(2)}, u32[]{:S(2)}) collective-permute-start(bf16[2,1,2,512,128]{4,3,2,1,0:T(8,128)(2,1)} %get-tuple-element.23), channel_id=1, source_target_pairs={{0,1},{1,0},{2,3},{3,2},{4,5},{5,4},{6,7},{7,6},{8,9},{9,8},{10,11... | collective-permute-start | bytes 1572872 | tf_op jit(solution)/shard_map/ppermute | solution.py:439
  9.8 8.2 %copy-start.3 = (s32[2,128,1]{1,2,0:T(1,128)S(1)}, s32[2,128,1]{1,2,0:T(1,128)}, u32[]{:S(2)}) copy-start(s32[2,128,1]{1,2,0:T(1,128)} %param.9) | copy-start | bytes 3076
  9.8 10.4 %copy-start = (bf16[2,32,2,14,512]{4,2,3,1,0:T(2,128)(2,1)S(1)}, bf16[2,32,2,14,512]{4,2,3,1,0:T(2,128)(2,1)}, u32[]{:S(2)}) copy-start(bf16[2,32,2,14,512]{4,2,3,1,0:T(2,128)(2,1)} %param.6) | copy-start | bytes 5505028
  9.8 10.4 %copy-start.1 = (s32[2,2]{1,0:T(2,128)S(1)}, s32[2,2]{1,0:T(2,128)}, u32[]{:S(2)}) copy-start(s32[2,2]{1,0:T(2,128)} %counts_hbm.8) | copy-start | bytes 52
  9.8 22.4 %collective-permute-start.1 = (bf16[2,1,2,512,128]{4,3,2,1,0:T(8,128)(2,1)}, bf16[2,1,2,512,128]{4,3,2,1,0:T(8,128)(2,1)S(1)}, u32[]{:S(2)}, u32[]{:S(2)}) collective-permute-start(bf16[2,1,2,512,128]{4,3,2,1,0:T(8,128)(2,1)} %get-tuple-element.24), channel_id=1, source_target_pairs={{1,2},{2,1},{3,4},{4,3},{5,6},{6,5},{9,10},{10,9},{11,12},{12,11},... | collective-permute-start | bytes 1572872 | tf_op jit(solution)/shard_map/ppermute | solution.py:440
  17.4 19.9 %collective-permute-start.3 = (bf16[2,9,160,128]{3,2,1,0:T(8,128)(2,1)}, bf16[2,9,160,128]{3,2,1,0:T(8,128)(2,1)}, u32[]{:S(2)}, u32[]{:S(2)}) collective-permute-start(bf16[2,9,160,128]{3,2,1,0:T(8,128)(2,1)} %shard_map.60), channel_id=1, source_target_pairs={{0,8},{8,0},{1,9},{9,1},{2,10},{10,2},{3,11},{11,3},{4,12},{12,4},... | collective-permute-start | bytes 2211848 | tf_op jit(solution)/shard_map/ppermute | solution.py:444
  18.2 11.0 %copy-start.2 = (f32[2]{0:T(128)S(1)}, f32[2]{0:T(128)}, u32[]{:S(2)}) copy-start(f32[2]{0:T(128)} %noise_ref.5) | copy-start | bytes 28
  34.2 5.4 %collective-permute-start.4 = (bf16[2,160,128]{2,1,0:T(8,128)(2,1)S(1)}, bf16[2,160,128]{2,1,0:T(8,128)(2,1)S(1)}, u32[]{:S(2)}, u32[]{:S(2)}) collective-permute-start(bf16[2,160,128]{2,1,0:T(8,128)(2,1)S(1)} %shard_map.61), channel_id=1, source_target_pairs={{0,8},{8,0},{1,9},{9,1},{2,10},{10,2},{3,11},{11,3},{4,12},{12,4},... | collective-permute-start | bytes 245768 | tf_op jit(solution)/shard_map/ppermute | solution.py:449
  41.1 8.1 %collective-permute-start.8 = (bf16[448,128]{1,0:T(8,128)(2,1)S(1)}, bf16[448,128]{1,0:T(8,128)(2,1)S(1)}, u32[]{:S(2)}, u32[]{:S(2)}) collective-permute-start(bf16[448,128]{1,0:T(8,128)(2,1)S(1)} %get-tuple-element.36), channel_id=1, source_target_pairs={{0,1},{1,2},{2,3},{3,0},{4,17},{5,18},{6,19},{7,16},{16,5},{17,6},... | collective-permute-start | bytes 344072 | tf_op jit(solution)/shard_map/ppermute | solution.py:475
  44.1 5.1 %collective-permute-start.7 = (bf16[448,128]{1,0:T(8,128)(2,1)S(1)}, bf16[448,128]{1,0:T(8,128)(2,1)S(1)}, u32[]{:S(2)}, u32[]{:S(2)}) collective-permute-start(bf16[448,128]{1,0:T(8,128)(2,1)S(1)} %get-tuple-element.35), channel_id=1, source_target_pairs={{0,0},{1,1},{2,2},{3,3},{4,16},{5,17},{6,18},{7,19},{16,4},{17,5},... | collective-permute-start | bytes 344072 | tf_op jit(solution)/shard_map/ppermute | solution.py:475
  44.8 5.6 %collective-permute-start.6 = (bf16[448,128]{1,0:T(8,128)(2,1)S(1)}, bf16[448,128]{1,0:T(8,128)(2,1)S(1)}, u32[]{:S(2)}, u32[]{:S(2)}) collective-permute-start(bf16[448,128]{1,0:T(8,128)(2,1)S(1)} %get-tuple-element.34), channel_id=1, source_target_pairs={{0,3},{1,0},{2,1},{3,2},{4,19},{5,16},{6,17},{7,18},{16,7},{17,4},... | collective-permute-start | bytes 344072 | tf_op jit(solution)/shard_map/ppermute | solution.py:475
  45.9 6.0 %collective-permute-start.5 = (bf16[448,128]{1,0:T(8,128)(2,1)S(1)}, bf16[448,128]{1,0:T(8,128)(2,1)S(1)}, u32[]{:S(2)}, u32[]{:S(2)}) collective-permute-start(bf16[448,128]{1,0:T(8,128)(2,1)S(1)} %get-tuple-element.33), channel_id=1, source_target_pairs={{0,2},{1,3},{2,0},{3,1},{4,18},{5,19},{6,16},{7,17},{16,6},{17,7},... | collective-permute-start | bytes 344072 | tf_op jit(solution)/shard_map/ppermute | solution.py:475
  49.2 9.4 %collective-permute-start.10 = (bf16[2,448,128]{2,1,0:T(8,128)(2,1)S(1)}, bf16[2,448,128]{2,1,0:T(8,128)(2,1)S(1)}, u32[]{:S(2)}, u32[]{:S(2)}) collective-permute-start(bf16[2,448,128]{2,1,0:T(8,128)(2,1)S(1)} %pad_maximum_fusion.1.refs_1_), channel_id=1, source_target_pairs={{0,8},{8,0},{1,9},{9,1},{2,10},{10,2},{3,11},{11,3},{4,12},{12,4},... | collective-permute-start | bytes 688136 | tf_op jit(solution)/shard_map/ppermute | solution.py:480
  51.9 9.6 %collective-permute-start.9 = (bf16[2,448,128]{2,1,0:T(8,128)(2,1)S(1)}, bf16[2,448,128]{2,1,0:T(8,128)(2,1)S(1)}, u32[]{:S(2)}, u32[]{:S(2)}) collective-permute-start(bf16[2,448,128]{2,1,0:T(8,128)(2,1)S(1)} %pad_maximum_fusion.refs_0_), channel_id=1, source_target_pairs={{0,8},{8,0},{1,9},{9,1},{2,10},{10,2},{3,11},{11,3},{4,12},{12,4},... | collective-permute-start | bytes 688136 | tf_op jit(solution)/shard_map/ppermute | solution.py:480
  52.7 11.4 %collective-permute-start.11 = (bf16[4,224,128]{2,1,0:T(8,128)(2,1)S(1)}, bf16[4,224,128]{2,1,0:T(8,128)(2,1)S(1)}, u32[]{:S(2)}, u32[]{:S(2)}) collective-permute-start(bf16[4,224,128]{2,1,0:T(8,128)(2,1)S(1)} %pad_maximum_fusion.2), channel_id=1, source_target_pairs={{0,16},{16,0},{1,17},{17,1},{2,18},{18,2},{3,19},{19,3},{4,20},{20... | collective-permute-start | bytes 688136 | tf_op jit(solution)/shard_map/ppermute | solution.py:481
  58.7 5.4 %collective-permute-start.13 = (bf16[2,224,128]{2,1,0:T(8,128)(2,1)S(1)}, bf16[2,224,128]{2,1,0:T(8,128)(2,1)S(1)}, u32[]{:S(2)}, u32[]{:S(2)}) collective-permute-start(bf16[2,224,128]{2,1,0:T(8,128)(2,1)S(1)} %slice.29), channel_id=1, source_target_pairs={{0,16},{16,0},{1,17},{17,1},{2,18},{18,2},{3,19},{19,3},{4,20},{20... | collective-permute-start | bytes 344072 | tf_op jit(solution)/shard_map/ppermute | solution.py:482
  61.6 3.4 %collective-permute-start.12 = (bf16[2,224,128]{2,1,0:T(8,128)(2,1)S(1)}, bf16[2,224,128]{2,1,0:T(8,128)(2,1)S(1)}, u32[]{:S(2)}, u32[]{:S(2)}) collective-permute-start(bf16[2,224,128]{2,1,0:T(8,128)(2,1)S(1)} %slice.28), channel_id=1, source_target_pairs={{0,16},{16,0},{1,17},{17,1},{2,18},{18,2},{3,19},{19,3},{4,20},{20... | collective-permute-start | bytes 344072 | tf_op jit(solution)/shard_map/ppermute | solution.py:482

commit v16 on v12

--- a/solution.py
+++ b/solution.py
@@ -472,7 +472,10 @@
             for s in range(n_cell)
             for j in range(n_sc)
         ]
-        arrived.append(lax.ppermute(messages[b], ("cell", "sc"), pairs))
+        message, before = messages[b], b - reach // 2
+        if before >= 0:
+            message, arrived[before] = lax.optimization_barrier((message, arrived[before]))
+        arrived.append(lax.ppermute(message, ("cell", "sc"), pairs))
     turns = (sc % reach - lax.iota(jnp.int32, reach)) % reach
     sources = jnp.concatenate([cell * reach + turns, (1 - cell) * reach + turns])
     keep = symbols * half

time: 68 us -> 71.9 us (1.057)
  starting transfers between devices: 16.6 us -> 27.6 us
  waiting for transfers between devices: 18.3 us -> 11.3 us
    ppermute x2, waiting for transfers between devices: 6.65 us -> 0.01 us  [body(): theirs = [lax.ppermute(group, 'panel', SWAP) for group in mine]]
    ppermute x1, starting transfers between devices: 3.23 us -> 8.03 us  [body(): lax.ppermute(jnp.stack([block[:keep] for block in arrived]), 'cell', SWAP)]
    ppermute x2, starting transfers between devices: 0.14 us -> 4.35 us  [body(): others += [lax.ppermute(group[:, :keep], 'cell', SWAP) for group in theirs]]
    ppermute x2, starting transfers between devices: 1.07 us -> 2.2 us  [body(): theirs = [lax.ppermute(group, 'panel', SWAP) for group in mine]]
    ppermute x4, starting transfers between devices: 5.34 us -> 6.16 us  [body(): arrived.append(lax.ppermute(message, ('cell', 'sc'), pairs))]
  transfers between devices with their start and end apart: 14 -> 14, of which waited for: 8 -> 6; matrix products, arithmetic and copies ran while one was open for 1% -> 1% of each run, Pallas kernels for 34% -> 33%
where the time goes in v16:
time: 71.9 us; the launch traced here: 71.7 us
  Pallas kernels  32 us (45%)
  starting transfers between devices  27.6 us (38%)
  waiting for transfers between devices  11.3 us (16%)
    pallas_call x3, Pallas kernels, inner_gram(): pl.pallas_call(kernel, in_specs=[HBM_SPEC] * 3, out_specs=[VMEM_SPEC] + [...  21 us
    ppermute x1, starting transfers between devices, body(): lax.ppermute(jnp.stack([block[:keep] for block in arrived]), 'cell', SWAP)  8.03 us
    ppermute x4, waiting for transfers between devices, body(): arrived.append(lax.ppermute(message, ('cell', 'sc'), pairs))  6.84 us
    ppermute x4, starting transfers between devices, body(): arrived.append(lax.ppermute(message, ('cell', 'sc'), pairs))  6.16 us
    ppermute x2, starting transfers between devices, body(): others += [lax.ppermute(group[:, :keep], 'cell', SWAP) for group in theirs]  4.35 us
    pallas_call x2, Pallas kernels, edge_gram(): pl.pallas_call(kernel, in_specs=[HBM_SPEC] * 5, out_specs=VMEM_SPEC, out_...  3.94 us
    pallas_call x2, Pallas kernels, detect_inner(): pl.pallas_call(kernel, in_specs=[SMEM_SPEC] + [VMEM_SPEC] * (2 + len(stat...  3.59 us
    ppermute x1, starting transfers between devices, body(): first_peer = lax.ppermute(first, 'panel', SWAP)  3.01 us
  transfers between devices with their start and end apart: 14, of which 6 were waited for; matrix products, arithmetic and copies ran while one was open for 1% of the time, Pallas kernels for 33%

profile of v16, /device:TPU:0, one launch (start us, length us, event | category | flops | bytes accessed | tf_op | source)
XLA Modules:
  0.0 71.7 jit_solution(3489016552706629345)
XLA Ops:
  0.0 5.2 %shard_map.55 = (bf16[2,6,160,128]{3,2,1,0:T(8,128)(2,1)}, bf16[2,1,2,512,128]{4,3,2,1,0:T(8,128)(2,1)}, bf16[2,1,2,512,128]{4,3,2,1,0:T(8,128)(2,1)}) custom-call(s32[2,2]{1,0:T(2,128)} %counts_hbm.8, bf16[2,32,2,512,128]{4,3,2,1,0:T(8,128)(2,1)} %chan.9, bf16[2,32,14,2,512]{4,3,2,1,0:T(2,128)(2,1)} %bitcast.15), custom_call_target="tpu_custom_call" | custom-call | flops 905969664 | bytes 4194304 | tf_op jit(solution)/shard_map/pallas_call | solution.py:149
  5.2 3.0 %collective-permute-start.2 = (bf16[2,6,160,128]{3,2,1,0:T(8,128)(2,1)}, bf16[2,6,160,128]{3,2,1,0:T(8,128)(2,1)S(1)}, u32[]{:S(2)}, u32[]{:S(2)}) collective-permute-start(bf16[2,6,160,128]{3,2,1,0:T(8,128)(2,1)} %get-tuple-element.29), channel_id=1, source_target_pairs={{0,8},{8,0},{1,9},{9,1},{2,10},{10,2},{3,11},{11,3},{4,12},{12,4},... | collective-permute-start | bytes 1474568 | tf_op jit(solution)/shard_map/ppermute | solution.py:437
  8.2 1.5 %collective-permute-start = (bf16[2,1,2,512,128]{4,3,2,1,0:T(8,128)(2,1)}, bf16[2,1,2,512,128]{4,3,2,1,0:T(8,128)(2,1)S(1)}, u32[]{:S(2)}, u32[]{:S(2)}) collective-permute-start(bf16[2,1,2,512,128]{4,3,2,1,0:T(8,128)(2,1)} %get-tuple-element.27), channel_id=1, source_target_pairs={{0,1},{1,0},{2,3},{3,2},{4,5},{5,4},{6,7},{7,6},{8,9},{9,8},{10,11... | collective-permute-start | bytes 1572872 | tf_op jit(solution)/shard_map/ppermute | solution.py:439
  10.6 6.8 %shard_map.60 = bf16[2,9,160,128]{3,2,1,0:T(8,128)(2,1)} custom-call(s32[2,2]{1,0:T(2,128)} %counts_hbm.8, bf16[2,32,2,512,128]{4,3,2,1,0:T(8,128)(2,1)} %chan.9, bf16[2,32,14,2,512]{4,3,2,1,0:T(2,128)(2,1)} %bitcast.16), custom_call_target="tpu_custom_call" | custom-call | flops 1358954496 | bytes 5767168 | tf_op jit(solution)/shard_map/pallas_call | solution.py:149
  18.2 2.0 %collective-permute-done.2.peer_ref = bf16[2,6,160,128]{3,2,1,0:T(8,128)(2,1)S(1)} collective-permute-done((bf16[2,6,160,128]{3,2,1,0:T(8,128)(2,1)}, bf16[2,6,160,128]{3,2,1,0:T(8,128)(2,1)S(1)}, u32[]{:S(2)}, u32[]{:S(2)}) %collective-permute-start.2) | collective-permute-done | bytes 491552 | tf_op jit(solution)/shard_map/ppermute | solution.py:437
  20.2 9.0 %shard_map.57.own_ref = f32[2,15,160,128]{3,2,1,0:T(8,128)S(1)} custom-call(s32[2,2]{1,0:T(2,128)S(1)} %copy-done.1, bf16[2,32,2,512,128]{4,3,2,1,0:T(8,128)(2,1)} %chan.9, bf16[2,32,14,2,512]{4,3,2,1,0:T(2,128)(2,1)S(1)} %bitcast.17), custom_call_target="tpu_custom_call" | custom-call | flops 141557760 | bytes 557056 | tf_op jit(solution)/shard_map/pallas_call | solution.py:149
  29.2 1.4 %shard_map.58.refs_0_ = f32[2,512,128]{2,1,0:T(8,128)S(1)} custom-call(f32[2]{0:T(128)S(1)} %copy-done.2, f32[2,15,160,128]{3,2,1,0:T(8,128)S(1)} %shard_map.57.own_ref, bf16[2,6,160,128]{3,2,1,0:T(8,128)(2,1)S(1)} %collective-permute-done.2.peer_ref), custom_call_target="tpu_custom_call" | custom-call | flops 50331648 | bytes 3686400 | tf_op jit(solution)/shard_map/pallas_call | solution.py:326
  30.6 1.6 %collective-permute-done.near_ref = bf16[2,1,2,512,128]{4,3,2,1,0:T(8,128)(2,1)S(1)} collective-permute-done((bf16[2,1,2,512,128]{4,3,2,1,0:T(8,128)(2,1)}, bf16[2,1,2,512,128]{4,3,2,1,0:T(8,128)(2,1)S(1)}, u32[]{:S(2)}, u32[]{:S(2)}) %collective-permute-start) | collective-permute-done | bytes 524320 | tf_op jit(solution)/shard_map/ppermute | solution.py:439
  32.2 1.9 %shard_map.61 = bf16[2,160,128]{2,1,0:T(8,128)(2,1)S(1)} custom-call(s32[2,2]{1,0:T(2,128)S(1)} %copy-done.1, bf16[2,32,2,512,128]{4,3,2,1,0:T(8,128)(2,1)} %chan.9, bf16[2,32,14,2,512]{4,3,2,1,0:T(2,128)(2,1)S(1)} %bitcast.18, bf16[2,1,2,512,128]{4,3,2,1,0:T(8,128)(2,1)S(1)} %collective-permute-done.near_ref, ...), custom_call_target="tpu_custom_call" | custom-call | flops 150994944 | bytes 1572864 | tf_op jit(solution)/shard_map/pallas_call | solution.py:261
  34.2 0.9 %collective-permute-start.4 = (bf16[2,160,128]{2,1,0:T(8,128)(2,1)S(1)}, bf16[2,160,128]{2,1,0:T(8,128)(2,1)S(1)}, u32[]{:S(2)}, u32[]{:S(2)}) collective-permute-start(bf16[2,160,128]{2,1,0:T(8,128)(2,1)S(1)} %shard_map.61), channel_id=1, source_target_pairs={{0,8},{8,0},{1,9},{9,1},{2,10},{10,2},{3,11},{11,3},{4,12},{12,4},... | collective-permute-start | bytes 245768 | tf_op jit(solution)/shard_map/ppermute | solution.py:449
  35.3 2.0 %shard_map.59.edge_own_ref = f32[2,160,128]{2,1,0:T(8,128)S(1)} custom-call(s32[2,2]{1,0:T(2,128)S(1)} %copy-done.1, bf16[2,32,2,512,128]{4,3,2,1,0:T(8,128)(2,1)} %chan.9, bf16[2,32,14,2,512]{4,3,2,1,0:T(2,128)(2,1)S(1)} %bitcast.19, bf16[2,1,2,512,128]{4,3,2,1,0:T(8,128)(2,1)S(1)} %collective-permute-done.near_ref, ...), custom_call_target="tpu_custom_call" | custom-call | flops 150994944 | bytes 1572864 | tf_op jit(solution)/shard_map/pallas_call | solution.py:261
  37.3 2.2 %shard_map.62.state_ref = f32[2,512,128]{2,1,0:T(8,128)S(1)} custom-call(f32[2]{0:T(128)S(1)} %copy-done.2, f32[2,15,160,128]{3,2,1,0:T(8,128)S(1)} %shard_map.57.own_ref, bf16[2,9,160,128]{3,2,1,0:T(8,128)(2,1)} %collective-permute-done.3.peer_ref, f32[2,512,128]{2,1,0:T(8,128)S(1)} %shard_map.58.refs_0_), custom_call_target="tpu_custom_call" | custom-call | flops 75497472 | bytes 3686400 | tf_op jit(solution)/shard_map/pallas_call | solution.py:326
  39.6 1.5 %shard_map.63 = (bf16[448,128]{1,0:T(8,128)(2,1)S(1)}, bf16[448,128]{1,0:T(8,128)(2,1)S(1)}, bf16[448,128]{1,0:T(8,128)(2,1)S(1)}, bf16[448,128]{1,0:T(8,128)(2,1)S(1)}) custom-call(f32[2]{0:T(128)S(1)} %copy-done.2, f32[2,160,128]{2,1,0:T(8,128)S(1)} %shard_map.59.edge_own_ref, bf16[2,160,128]{2,1,0:T(8,128)(2,1)S(1)} %collective-permute-done.4.edge_peer_ref, ...), custom_call_target="tpu_custom_call" | custom-call | flops 234881024 | bytes 524288 | tf_op jit(solution)/shard_map/pallas_call | solution.py:367
  41.8 3.0 %collective-permute-start.6 = (bf16[448,128]{1,0:T(8,128)(2,1)S(1)}, bf16[448,128]{1,0:T(8,128)(2,1)S(1)}, u32[]{:S(2)}, u32[]{:S(2)}) collective-permute-start(bf16[448,128]{1,0:T(8,128)(2,1)S(1)} %get-tuple-element.41), channel_id=1, source_target_pairs={{0,1},{1,2},{2,3},{3,0},{4,17},{5,18},{6,19},{7,16},{16,5},{17,6},... | collective-permute-start | bytes 344072 | tf_op jit(solution)/shard_map/ppermute | solution.py:478
  44.8 3.8 %collective-permute-done.6 = bf16[448,128]{1,0:T(8,128)(2,1)S(1)} collective-permute-done((bf16[448,128]{1,0:T(8,128)(2,1)S(1)}, bf16[448,128]{1,0:T(8,128)(2,1)S(1)}, u32[]{:S(2)}, u32[]{:S(2)}) %collective-permute-start.6) | collective-permute-done | bytes 114720 | tf_op jit(solution)/shard_map/ppermute | solution.py:478
  48.6 1.1 %collective-permute-start.7 = (bf16[448,128]{1,0:T(8,128)(2,1)S(1)}, bf16[448,128]{1,0:T(8,128)(2,1)S(1)}, u32[]{:S(2)}, u32[]{:S(2)}) collective-permute-start(bf16[448,128]{1,0:T(8,128)(2,1)S(1)} %get-tuple-element.43), channel_id=1, source_target_pairs={{0,2},{1,3},{2,0},{3,1},{4,18},{5,19},{6,16},{7,17},{16,6},{17,7},... | collective-permute-start | bytes 344072 | tf_op jit(solution)/shard_map/ppermute | solution.py:478
  49.7 1.4 %collective-permute-start.8 = (bf16[448,128]{1,0:T(8,128)(2,1)S(1)}, bf16[448,128]{1,0:T(8,128)(2,1)S(1)}, u32[]{:S(2)}, u32[]{:S(2)}) collective-permute-start(bf16[448,128]{1,0:T(8,128)(2,1)S(1)} %get-tuple-element.44), channel_id=1, source_target_pairs={{0,3},{1,0},{2,1},{3,2},{4,19},{5,16},{6,17},{7,18},{16,7},{17,4},... | collective-permute-start | bytes 344072 | tf_op jit(solution)/shard_map/ppermute | solution.py:478
  51.8 2.2 %collective-permute-done.7 = bf16[448,128]{1,0:T(8,128)(2,1)S(1)} collective-permute-done((bf16[448,128]{1,0:T(8,128)(2,1)S(1)}, bf16[448,128]{1,0:T(8,128)(2,1)S(1)}, u32[]{:S(2)}, u32[]{:S(2)}) %collective-permute-start.7) | collective-permute-done | bytes 114720 | tf_op jit(solution)/shard_map/ppermute | solution.py:478
  53.9 0.9 %collective-permute-done.8 = bf16[448,128]{1,0:T(8,128)(2,1)S(1)} collective-permute-done((bf16[448,128]{1,0:T(8,128)(2,1)S(1)}, bf16[448,128]{1,0:T(8,128)(2,1)S(1)}, u32[]{:S(2)}, u32[]{:S(2)}) %collective-permute-start.8) | collective-permute-done | bytes 114720 | tf_op jit(solution)/shard_map/ppermute | solution.py:478
  54.9 1.5 %collective-permute-start.10 = (bf16[2,448,128]{2,1,0:T(8,128)(2,1)S(1)}, bf16[2,448,128]{2,1,0:T(8,128)(2,1)S(1)}, u32[]{:S(2)}, u32[]{:S(2)}) collective-permute-start(bf16[2,448,128]{2,1,0:T(8,128)(2,1)S(1)} %pad_maximum_fusion.1.refs_1_), channel_id=1, source_target_pairs={{0,8},{8,0},{1,9},{9,1},{2,10},{10,2},{3,11},{11,3},{4,12},{12,4},... | collective-permute-start | bytes 688136 | tf_op jit(solution)/shard_map/ppermute | solution.py:483
  56.4 8.0 %collective-permute-start.11 = (bf16[4,224,128]{2,1,0:T(8,128)(2,1)S(1)}, bf16[4,224,128]{2,1,0:T(8,128)(2,1)S(1)}, u32[]{:S(2)}, u32[]{:S(2)}) collective-permute-start(bf16[4,224,128]{2,1,0:T(8,128)(2,1)S(1)} %pad_maximum_fusion.2), channel_id=1, source_target_pairs={{0,16},{16,0},{1,17},{17,1},{2,18},{18,2},{3,19},{19,3},{4,20},{20... | collective-permute-start | bytes 688136 | tf_op jit(solution)/shard_map/ppermute | solution.py:484
  64.6 4.2 %collective-permute-start.13 = (bf16[2,224,128]{2,1,0:T(8,128)(2,1)S(1)}, bf16[2,224,128]{2,1,0:T(8,128)(2,1)S(1)}, u32[]{:S(2)}, u32[]{:S(2)}) collective-permute-start(bf16[2,224,128]{2,1,0:T(8,128)(2,1)S(1)} %slice.27), channel_id=1, source_target_pairs={{0,16},{16,0},{1,17},{17,1},{2,18},{18,2},{3,19},{19,3},{4,20},{20... | collective-permute-start | bytes 344072 | tf_op jit(solution)/shard_map/ppermute | solution.py:485
  68.9 0.9 %collective-permute-done.13.refs_6_ = bf16[2,224,128]{2,1,0:T(8,128)(2,1)S(1)} collective-permute-done((bf16[2,224,128]{2,1,0:T(8,128)(2,1)S(1)}, bf16[2,224,128]{2,1,0:T(8,128)(2,1)S(1)}, u32[]{:S(2)}, u32[]{:S(2)}) %collective-permute-start.13) | collective-permute-done | bytes 114720 | tf_op jit(solution)/shard_map/ppermute | solution.py:485
  69.8 1.9 %shard_map.64 = bf16[2,32,14,2,256]{4,3,2,1,0:T(2,128)(2,1)} custom-call(s32[8]{0:T(128)S(1)} %pad_add_fusion.1.source_ref, bf16[2,448,128]{2,1,0:T(8,128)(2,1)S(1)} %pad_maximum_fusion.refs_0_, bf16[2,448,128]{2,1,0:T(8,128)(2,1)S(1)} %pad_maximum_fusion.1.refs_1_, bf16[2,448,128]{2,1,0:T(8,128)(2,1)S(1)} %collective-permute-done.9.refs_2_, ...), custom_call_target="tpu_custom_call" | custom-call | tf_op jit(solution)/shard_map/pallas_call | solution.py:413
  (36 shorter events, 3.5 us)
Async XLA Ops:
  5.2 15.0 %collective-permute-start.2 = (bf16[2,6,160,128]{3,2,1,0:T(8,128)(2,1)}, bf16[2,6,160,128]{3,2,1,0:T(8,128)(2,1)S(1)}, u32[]{:S(2)}, u32[]{:S(2)}) collective-permute-start(bf16[2,6,160,128]{3,2,1,0:T(8,128)(2,1)} %get-tuple-element.29), channel_id=1, source_target_pairs={{0,8},{8,0},{1,9},{9,1},{2,10},{10,2},{3,11},{11,3},{4,12},{12,4},... | collective-permute-start | bytes 1474568 | tf_op jit(solution)/shard_map/ppermute | solution.py:437
  8.2 24.0 %collective-permute-start = (bf16[2,1,2,512,128]{4,3,2,1,0:T(8,128)(2,1)}, bf16[2,1,2,512,128]{4,3,2,1,0:T(8,128)(2,1)S(1)}, u32[]{:S(2)}, u32[]{:S(2)}) collective-permute-start(bf16[2,1,2,512,128]{4,3,2,1,0:T(8,128)(2,1)} %get-tuple-element.27), channel_id=1, source_target_pairs={{0,1},{1,0},{2,3},{3,2},{4,5},{5,4},{6,7},{7,6},{8,9},{9,8},{10,11... | collective-permute-start | bytes 1572872 | tf_op jit(solution)/shard_map/ppermute | solution.py:439
  9.8 8.2 %copy-start.3 = (s32[2,128,1]{1,2,0:T(1,128)S(1)}, s32[2,128,1]{1,2,0:T(1,128)}, u32[]{:S(2)}) copy-start(s32[2,128,1]{1,2,0:T(1,128)} %param.9) | copy-start | bytes 3076
  9.8 10.4 %copy-start = (bf16[2,32,2,14,512]{4,2,3,1,0:T(2,128)(2,1)S(1)}, bf16[2,32,2,14,512]{4,2,3,1,0:T(2,128)(2,1)}, u32[]{:S(2)}) copy-start(bf16[2,32,2,14,512]{4,2,3,1,0:T(2,128)(2,1)} %param.6) | copy-start | bytes 5505028
  9.8 10.4 %copy-start.1 = (s32[2,2]{1,0:T(2,128)S(1)}, s32[2,2]{1,0:T(2,128)}, u32[]{:S(2)}) copy-start(s32[2,2]{1,0:T(2,128)} %counts_hbm.8) | copy-start | bytes 52
  9.8 22.4 %collective-permute-start.1 = (bf16[2,1,2,512,128]{4,3,2,1,0:T(8,128)(2,1)}, bf16[2,1,2,512,128]{4,3,2,1,0:T(8,128)(2,1)S(1)}, u32[]{:S(2)}, u32[]{:S(2)}) collective-permute-start(bf16[2,1,2,512,128]{4,3,2,1,0:T(8,128)(2,1)} %get-tuple-element.28), channel_id=1, source_target_pairs={{1,2},{2,1},{3,4},{4,3},{5,6},{6,5},{9,10},{10,9},{11,12},{12,11},... | collective-permute-start | bytes 1572872 | tf_op jit(solution)/shard_map/ppermute | solution.py:440
  17.4 19.9 %collective-permute-start.3 = (bf16[2,9,160,128]{3,2,1,0:T(8,128)(2,1)}, bf16[2,9,160,128]{3,2,1,0:T(8,128)(2,1)}, u32[]{:S(2)}, u32[]{:S(2)}) collective-permute-start(bf16[2,9,160,128]{3,2,1,0:T(8,128)(2,1)} %shard_map.60), channel_id=1, source_target_pairs={{0,8},{8,0},{1,9},{9,1},{2,10},{10,2},{3,11},{11,3},{4,12},{12,4},... | collective-permute-start | bytes 2211848 | tf_op jit(solution)/shard_map/ppermute | solution.py:444
  18.2 11.0 %copy-start.2 = (f32[2]{0:T(128)S(1)}, f32[2]{0:T(128)}, u32[]{:S(2)}) copy-start(f32[2]{0:T(128)} %noise_ref.5) | copy-start | bytes 28
  34.2 5.4 %collective-permute-start.4 = (bf16[2,160,128]{2,1,0:T(8,128)(2,1)S(1)}, bf16[2,160,128]{2,1,0:T(8,128)(2,1)S(1)}, u32[]{:S(2)}, u32[]{:S(2)}) collective-permute-start(bf16[2,160,128]{2,1,0:T(8,128)(2,1)S(1)} %shard_map.61), channel_id=1, source_target_pairs={{0,8},{8,0},{1,9},{9,1},{2,10},{10,2},{3,11},{11,3},{4,12},{12,4},... | collective-permute-start | bytes 245768 | tf_op jit(solution)/shard_map/ppermute | solution.py:449
  41.1 3.7 %collective-permute-start.5 = (bf16[448,128]{1,0:T(8,128)(2,1)S(1)}, bf16[448,128]{1,0:T(8,128)(2,1)S(1)}, u32[]{:S(2)}, u32[]{:S(2)}) collective-permute-start(bf16[448,128]{1,0:T(8,128)(2,1)S(1)} %get-tuple-element.38), channel_id=1, source_target_pairs={{0,0},{1,1},{2,2},{3,3},{4,16},{5,17},{6,18},{7,19},{16,4},{17,5},... | collective-permute-start | bytes 344072 | tf_op jit(solution)/shard_map/ppermute | solution.py:478
  41.8 6.8 %collective-permute-start.6 = (bf16[448,128]{1,0:T(8,128)(2,1)S(1)}, bf16[448,128]{1,0:T(8,128)(2,1)S(1)}, u32[]{:S(2)}, u32[]{:S(2)}) collective-permute-start(bf16[448,128]{1,0:T(8,128)(2,1)S(1)} %get-tuple-element.41), channel_id=1, source_target_pairs={{0,1},{1,2},{2,3},{3,0},{4,17},{5,18},{6,19},{7,16},{16,5},{17,6},... | collective-permute-start | bytes 344072 | tf_op jit(solution)/shard_map/ppermute | solution.py:478
  48.6 5.3 %collective-permute-start.7 = (bf16[448,128]{1,0:T(8,128)(2,1)S(1)}, bf16[448,128]{1,0:T(8,128)(2,1)S(1)}, u32[]{:S(2)}, u32[]{:S(2)}) collective-permute-start(bf16[448,128]{1,0:T(8,128)(2,1)S(1)} %get-tuple-element.43), channel_id=1, source_target_pairs={{0,2},{1,3},{2,0},{3,1},{4,18},{5,19},{6,16},{7,17},{16,6},{17,7},... | collective-permute-start | bytes 344072 | tf_op jit(solution)/shard_map/ppermute | solution.py:478
  49.7 5.2 %collective-permute-start.8 = (bf16[448,128]{1,0:T(8,128)(2,1)S(1)}, bf16[448,128]{1,0:T(8,128)(2,1)S(1)}, u32[]{:S(2)}, u32[]{:S(2)}) collective-permute-start(bf16[448,128]{1,0:T(8,128)(2,1)S(1)} %get-tuple-element.44), channel_id=1, source_target_pairs={{0,3},{1,0},{2,1},{3,2},{4,19},{5,16},{6,17},{7,18},{16,7},{17,4},... | collective-permute-start | bytes 344072 | tf_op jit(solution)/shard_map/ppermute | solution.py:478
  51.1 13.4 %collective-permute-start.9 = (bf16[2,448,128]{2,1,0:T(8,128)(2,1)S(1)}, bf16[2,448,128]{2,1,0:T(8,128)(2,1)S(1)}, u32[]{:S(2)}, u32[]{:S(2)}) collective-permute-start(bf16[2,448,128]{2,1,0:T(8,128)(2,1)S(1)} %pad_maximum_fusion.refs_0_), channel_id=1, source_target_pairs={{0,8},{8,0},{1,9},{9,1},{2,10},{10,2},{3,11},{11,3},{4,12},{12,4},... | collective-permute-start | bytes 688136 | tf_op jit(solution)/shard_map/ppermute | solution.py:483
  54.9 9.7 %collective-permute-start.10 = (bf16[2,448,128]{2,1,0:T(8,128)(2,1)S(1)}, bf16[2,448,128]{2,1,0:T(8,128)(2,1)S(1)}, u32[]{:S(2)}, u32[]{:S(2)}) collective-permute-start(bf16[2,448,128]{2,1,0:T(8,128)(2,1)S(1)} %pad_maximum_fusion.1.refs_1_), channel_id=1, source_target_pairs={{0,8},{8,0},{1,9},{9,1},{2,10},{10,2},{3,11},{11,3},{4,12},{12,4},... | collective-permute-start | bytes 688136 | tf_op jit(solution)/shard_map/ppermute | solution.py:483
  56.4 12.5 %collective-permute-start.11 = (bf16[4,224,128]{2,1,0:T(8,128)(2,1)S(1)}, bf16[4,224,128]{2,1,0:T(8,128)(2,1)S(1)}, u32[]{:S(2)}, u32[]{:S(2)}) collective-permute-start(bf16[4,224,128]{2,1,0:T(8,128)(2,1)S(1)} %pad_maximum_fusion.2), channel_id=1, source_target_pairs={{0,16},{16,0},{1,17},{17,1},{2,18},{18,2},{3,19},{19,3},{4,20},{20... | collective-permute-start | bytes 688136 | tf_op jit(solution)/shard_map/ppermute | solution.py:484
  64.5 4.5 %collective-permute-start.12 = (bf16[2,224,128]{2,1,0:T(8,128)(2,1)S(1)}, bf16[2,224,128]{2,1,0:T(8,128)(2,1)S(1)}, u32[]{:S(2)}, u32[]{:S(2)}) collective-permute-start(bf16[2,224,128]{2,1,0:T(8,128)(2,1)S(1)} %slice.26), channel_id=1, source_target_pairs={{0,16},{16,0},{1,17},{17,1},{2,18},{18,2},{3,19},{19,3},{4,20},{20... | collective-permute-start | bytes 344072 | tf_op jit(solution)/shard_map/ppermute | solution.py:485
  64.6 5.2 %collective-permute-start.13 = (bf16[2,224,128]{2,1,0:T(8,128)(2,1)S(1)}, bf16[2,224,128]{2,1,0:T(8,128)(2,1)S(1)}, u32[]{:S(2)}, u32[]{:S(2)}) collective-permute-start(bf16[2,224,128]{2,1,0:T(8,128)(2,1)S(1)} %slice.27), channel_id=1, source_target_pairs={{0,16},{16,0},{1,17},{17,1},{2,18},{18,2},{3,19},{19,3},{4,20},{20... | collective-permute-start | bytes 344072 | tf_op jit(solution)/shard_map/ppermute | solution.py:485

commit v17 on v11

--- a/solution.py
+++ b/solution.py
@@ -402,7 +402,7 @@
             n = 0
             for ref in group:
                 for i in range(ref.shape[0]):
-                    place(ref, i, keep, source_ref[n], side)
+                    place(ref, i, ref.shape[1] - keep, source_ref[n], side)
                     n += 1
         for side, group in ((panel, (own_other,)), (1 - panel, peer_others)):
             n = rounds
@@ -477,10 +477,14 @@
     turns = (sc % reach - lax.iota(jnp.int32, reach)) % reach
     sources = jnp.concatenate([cell * reach + turns, (1 - cell) * reach + turns])
     keep = symbols * half
-    mine = [jnp.stack(arrived[: reach // 2]), jnp.stack(arrived[reach // 2 :])]
-    theirs = [lax.ppermute(group, "panel", SWAP) for group in mine]
-    others = [lax.ppermute(jnp.stack([block[:keep] for block in arrived]), "cell", SWAP)]
-    others += [lax.ppermute(group[:, :keep], "cell", SWAP) for group in theirs]
+    cut = reach // 2
+    mine = [jnp.stack(arrived[:cut]), jnp.stack(arrived[cut:])]
+    gives = jnp.stack([block[:keep] for block in arrived])
+    theirs = [lax.ppermute(mine[0], "panel", SWAP)]
+    theirs.append(lax.ppermute(jnp.stack([block[keep:] for block in arrived[cut:]]), "panel", SWAP))
+    across = lax.ppermute(gives[cut:], ("cell", "panel"), [(i, 3 - i) for i in range(4)])
+    gifts = lax.ppermute(jnp.concatenate([gives, theirs[0][:, :keep]]), "cell", SWAP)
+    others = [gifts[:reach], gifts[reach:], across]
     routed = assemble(sources, mine, theirs, others, cells, per_device, symbols, half)
     return jnp.transpose(routed, (0, 1, 3, 2, 4))
 

time: 66 us -> 71.8 us (1.088)
  waiting for transfers between devices: 9.87 us -> 12.7 us
  local copies, waits for them, and re-layouts: 0.06 us -> 1.98 us
  Pallas kernels: 30.9 us -> 31.8 us
    ppermute x5 -> x4, waiting for transfers between devices: 0.88 us -> 7.18 us  [the longest x1 4.48 us: body(): lax.ppermute(jnp.stack([block[keep:] for block in arrived[cut:]]), 'panel...]
    unnamed x8 -> x24, local copies, waits for them, and re-layouts: 0.02 us -> 1.91 us
    ppermute x1, waiting for transfers between devices: 1.42 us -> 0.01 us  [body(): lax.ppermute(edge_gram(user_count, channel, samples, near, far, True, BF1...]
    ppermute x4, waiting for transfers between devices: 3.99 us -> 2.73 us  [body(): arrived.append(lax.ppermute(messages[b], ('cell', 'sc'), pairs))]
    pallas_call x2, Pallas kernels: 3.85 us -> 4.77 us  [edge_gram(): pl.pallas_call(kernel, in_specs=[HBM_SPEC] * 5, out_specs=VMEM_SPEC, out_...]
    ppermute x1, waiting for transfers between devices: 1.61 us -> 0.78 us  [body(): near = lax.ppermute(near, 'sc', [(i, i ^ 1) for i in range(n_sc)])]
    ppermute x1, starting transfers between devices: 0.89 us -> 1.67 us  [body(): lax.ppermute(edge_gram(user_count, channel, samples, near, far, True, BF1...]
    ppermute x5 -> x4, starting transfers between devices: 11.3 us -> 10.6 us  [the longest x1 7.94 us: body(): lax.ppermute(jnp.concatenate([gives, theirs[0][:, :keep]]), 'cell', SWAP)]
  transfers between devices with their start and end apart: 14 -> 13, of which waited for: 7 -> 7; matrix products, arithmetic and copies ran while one was open for 1% -> 1% of each run, Pallas kernels for 32% -> 31%
where the time goes in v17:
time: 71.8 us; the launch traced here: 71.3 us
  Pallas kernels  31.8 us (44%)
  starting transfers between devices  24 us (33%)
  waiting for transfers between devices  12.7 us (18%)
  local copies, waits for them, and re-layouts  1.98 us (3%)
    pallas_call x3, Pallas kernels, inner_gram(): pl.pallas_call(kernel, in_specs=[HBM_SPEC] * 3, out_specs=[VMEM_SPEC] + [...  21.1 us
    ppermute x1, starting transfers between devices, body(): lax.ppermute(jnp.concatenate([gives, theirs[0][:, :keep]]), 'cell', SWAP)  7.94 us
    ppermute x4, starting transfers between devices, body(): arrived.append(lax.ppermute(messages[b], ('cell', 'sc'), pairs))  5.71 us
    pallas_call x2, Pallas kernels, edge_gram(): pl.pallas_call(kernel, in_specs=[HBM_SPEC] * 5, out_specs=VMEM_SPEC, out_...  4.77 us
    ppermute x1, waiting for transfers between devices, body(): lax.ppermute(jnp.stack([block[keep:] for block in arrived[cut:]]), 'panel...  4.48 us
    ppermute x1, starting transfers between devices, body(): first_peer = lax.ppermute(first, 'panel', SWAP)  3.01 us
    ppermute x4, waiting for transfers between devices, body(): arrived.append(lax.ppermute(messages[b], ('cell', 'sc'), pairs))  2.73 us
    pallas_call x1, Pallas kernels, detect_last(): pl.pallas_call(kernel, in_specs=[SMEM_SPEC] + [VMEM_SPEC] * 6, out_specs=...  2.7 us
  transfers between devices with their start and end apart: 13, of which 7 were waited for; matrix products, arithmetic and copies ran while one was open for 1% of the time, Pallas kernels for 31%

profile of v17, /device:TPU:0, one launch (start us, length us, event | category | flops | bytes accessed | tf_op | source)
XLA Modules:
  0.0 71.3 jit_solution(3128046552049253748)
XLA Ops:
  0.0 5.2 %shard_map.55 = (bf16[2,6,160,128]{3,2,1,0:T(8,128)(2,1)}, bf16[2,1,2,512,128]{4,3,2,1,0:T(8,128)(2,1)}, bf16[2,1,2,512,128]{4,3,2,1,0:T(8,128)(2,1)}) custom-call(s32[2,2]{1,0:T(2,128)} %counts_hbm.8, bf16[2,32,2,512,128]{4,3,2,1,0:T(8,128)(2,1)} %chan.9, bf16[2,32,14,2,512]{4,3,2,1,0:T(2,128)(2,1)} %bitcast.27), custom_call_target="tpu_custom_call" | custom-call | flops 905969664 | bytes 4194304 | tf_op jit(solution)/shard_map/pallas_call | solution.py:149
  5.2 3.0 %collective-permute-start = (bf16[2,6,160,128]{3,2,1,0:T(8,128)(2,1)}, bf16[2,6,160,128]{3,2,1,0:T(8,128)(2,1)S(1)}, u32[]{:S(2)}, u32[]{:S(2)}) collective-permute-start(bf16[2,6,160,128]{3,2,1,0:T(8,128)(2,1)} %get-tuple-element.19), channel_id=1, source_target_pairs={{0,8},{8,0},{1,9},{9,1},{2,10},{10,2},{3,11},{11,3},{4,12},{12,4},... | collective-permute-start | bytes 1474568 | tf_op jit(solution)/shard_map/ppermute | solution.py:440
  8.3 1.5 %collective-permute-start.2 = (bf16[2,1,2,512,128]{4,3,2,1,0:T(8,128)(2,1)}, bf16[2,1,2,512,128]{4,3,2,1,0:T(8,128)(2,1)S(1)}, u32[]{:S(2)}, u32[]{:S(2)}) collective-permute-start(bf16[2,1,2,512,128]{4,3,2,1,0:T(8,128)(2,1)} %get-tuple-element.23), channel_id=1, source_target_pairs={{0,1},{1,0},{2,3},{3,2},{4,5},{5,4},{6,7},{7,6},{8,9},{9,8},{10,11... | collective-permute-start | bytes 1572872 | tf_op jit(solution)/shard_map/ppermute | solution.py:442
  9.8 0.8 %collective-permute-start.3 = (bf16[2,1,2,512,128]{4,3,2,1,0:T(8,128)(2,1)}, bf16[2,1,2,512,128]{4,3,2,1,0:T(8,128)(2,1)S(1)}, u32[]{:S(2)}, u32[]{:S(2)}) collective-permute-start(bf16[2,1,2,512,128]{4,3,2,1,0:T(8,128)(2,1)} %get-tuple-element.24), channel_id=1, source_target_pairs={{1,2},{2,1},{3,4},{4,3},{5,6},{6,5},{9,10},{10,9},{11,12},{12,11},... | collective-permute-start | bytes 1572872 | tf_op jit(solution)/shard_map/ppermute | solution.py:443
  10.6 6.8 %shard_map.57 = bf16[2,9,160,128]{3,2,1,0:T(8,128)(2,1)} custom-call(s32[2,2]{1,0:T(2,128)} %counts_hbm.8, bf16[2,32,2,512,128]{4,3,2,1,0:T(8,128)(2,1)} %chan.9, bf16[2,32,14,2,512]{4,3,2,1,0:T(2,128)(2,1)} %bitcast.28), custom_call_target="tpu_custom_call" | custom-call | flops 1358954496 | bytes 5767168 | tf_op jit(solution)/shard_map/pallas_call | solution.py:149
  18.2 2.0 %collective-permute-done.peer_ref = bf16[2,6,160,128]{3,2,1,0:T(8,128)(2,1)S(1)} collective-permute-done((bf16[2,6,160,128]{3,2,1,0:T(8,128)(2,1)}, bf16[2,6,160,128]{3,2,1,0:T(8,128)(2,1)S(1)}, u32[]{:S(2)}, u32[]{:S(2)}) %collective-permute-start) | collective-permute-done | bytes 491552 | tf_op jit(solution)/shard_map/ppermute | solution.py:440
  20.2 9.0 %shard_map.56.own_ref = f32[2,15,160,128]{3,2,1,0:T(8,128)S(1)} custom-call(s32[2,2]{1,0:T(2,128)S(1)} %copy-done.7, bf16[2,32,2,512,128]{4,3,2,1,0:T(8,128)(2,1)} %chan.9, bf16[2,32,14,2,512]{4,3,2,1,0:T(2,128)(2,1)S(1)} %bitcast.29), custom_call_target="tpu_custom_call" | custom-call | flops 141557760 | bytes 557056 | tf_op jit(solution)/shard_map/pallas_call | solution.py:149
  29.3 1.4 %shard_map.59.state_ref = f32[2,512,128]{2,1,0:T(8,128)S(1)} custom-call(f32[2]{0:T(128)S(1)} %copy-done.8, f32[2,15,160,128]{3,2,1,0:T(8,128)S(1)} %shard_map.56.own_ref, bf16[2,6,160,128]{3,2,1,0:T(8,128)(2,1)S(1)} %collective-permute-done.peer_ref), custom_call_target="tpu_custom_call" | custom-call | flops 50331648 | bytes 3686400 | tf_op jit(solution)/shard_map/pallas_call | solution.py:324
  32.2 2.7 %shard_map.61 = bf16[2,160,128]{2,1,0:T(8,128)(2,1)} custom-call(s32[2,2]{1,0:T(2,128)S(1)} %copy-done.7, bf16[2,32,2,512,128]{4,3,2,1,0:T(8,128)(2,1)} %chan.9, bf16[2,32,14,2,512]{4,3,2,1,0:T(2,128)(2,1)S(1)} %bitcast.30, bf16[2,1,2,512,128]{4,3,2,1,0:T(8,128)(2,1)S(1)} %collective-permute-done.2.near_ref, ...), custom_call_target="tpu_custom_call" | custom-call | flops 150994944 | bytes 1572864 | tf_op jit(solution)/shard_map/pallas_call | solution.py:262
  35.0 1.7 %collective-permute-start.4 = (bf16[2,160,128]{2,1,0:T(8,128)(2,1)}, bf16[2,160,128]{2,1,0:T(8,128)(2,1)S(1)}, u32[]{:S(2)}, u32[]{:S(2)}) collective-permute-start(bf16[2,160,128]{2,1,0:T(8,128)(2,1)} %shard_map.61), channel_id=1, source_target_pairs={{0,8},{8,0},{1,9},{9,1},{2,10},{10,2},{3,11},{11,3},{4,12},{12,4},... | collective-permute-start | bytes 245768 | tf_op jit(solution)/shard_map/ppermute | solution.py:452
  36.9 1.0 %copy-done.4 = bf16[2,1,2,512,128]{4,3,2,1,0:T(8,128)(2,1)S(1)} copy-done((bf16[2,1,2,512,128]{4,3,2,1,0:T(8,128)(2,1)S(1)}, bf16[2,1,2,512,128]{4,3,2,1,0:T(8,128)(2,1)}, u32[]{:S(2)}) %copy-start.4) | copy-done | bytes 524312
  37.9 2.1 %shard_map.60.edge_own_ref = f32[2,160,128]{2,1,0:T(8,128)S(1)} custom-call(s32[2,2]{1,0:T(2,128)S(1)} %copy-done.7, bf16[2,32,2,512,128]{4,3,2,1,0:T(8,128)(2,1)} %chan.9, bf16[2,32,14,2,512]{4,3,2,1,0:T(2,128)(2,1)S(1)} %bitcast.31, bf16[2,1,2,512,128]{4,3,2,1,0:T(8,128)(2,1)S(1)} %collective-permute-done.2.near_ref, bf16[2,1,2,512,128]{4,3,2,1,0:T(8,128)(2,1)S(1)} %copy-done.4), custom_call_target="tpu_custom_call" | custom-call | flops 150994944 | bytes 1572864 | tf_op jit(solution)/shard_map/pallas_call | solution.py:262
  40.1 2.7 %shard_map.62 = (bf16[448,128]{1,0:T(8,128)(2,1)S(1)}, bf16[448,128]{1,0:T(8,128)(2,1)S(1)}, bf16[448,128]{1,0:T(8,128)(2,1)S(1)}, bf16[448,128]{1,0:T(8,128)(2,1)S(1)}) custom-call(f32[2]{0:T(128)S(1)} %copy-done.8, f32[2,15,160,128]{3,2,1,0:T(8,128)S(1)} %copy-done.2, bf16[2,9,160,128]{3,2,1,0:T(8,128)(2,1)} %collective-permute-done.1.peer_ref, ...), custom_call_target="tpu_custom_call" | custom-call | flops 234881024 | bytes 524288 | tf_op jit(solution)/shard_map/pallas_call | solution.py:370
  42.8 2.1 %collective-permute-start.6 = (bf16[448,128]{1,0:T(8,128)(2,1)S(1)}, bf16[448,128]{1,0:T(8,128)(2,1)S(1)}, u32[]{:S(2)}, u32[]{:S(2)}) collective-permute-start(bf16[448,128]{1,0:T(8,128)(2,1)S(1)} %get-tuple-element.30), channel_id=1, source_target_pairs={{0,1},{1,2},{2,3},{3,0},{4,17},{5,18},{6,19},{7,16},{16,5},{17,6},... | collective-permute-start | bytes 344072 | tf_op jit(solution)/shard_map/ppermute | solution.py:476
  45.6 1.0 %collective-permute-start.8 = (bf16[448,128]{1,0:T(8,128)(2,1)S(1)}, bf16[448,128]{1,0:T(8,128)(2,1)S(1)}, u32[]{:S(2)}, u32[]{:S(2)}) collective-permute-start(bf16[448,128]{1,0:T(8,128)(2,1)S(1)} %get-tuple-element.32), channel_id=1, source_target_pairs={{0,3},{1,0},{2,1},{3,2},{4,19},{5,16},{6,17},{7,18},{16,7},{17,4},... | collective-permute-start | bytes 344072 | tf_op jit(solution)/shard_map/ppermute | solution.py:476
  46.6 1.9 %collective-permute-start.7 = (bf16[448,128]{1,0:T(8,128)(2,1)S(1)}, bf16[448,128]{1,0:T(8,128)(2,1)S(1)}, u32[]{:S(2)}, u32[]{:S(2)}) collective-permute-start(bf16[448,128]{1,0:T(8,128)(2,1)S(1)} %get-tuple-element.31), channel_id=1, source_target_pairs={{0,2},{1,3},{2,0},{3,1},{4,18},{5,19},{6,16},{7,17},{16,6},{17,7},... | collective-permute-start | bytes 344072 | tf_op jit(solution)/shard_map/ppermute | solution.py:476
  48.7 1.2 %collective-permute-start.9 = (bf16[2,448,128]{2,1,0:T(8,128)(2,1)S(1)}, bf16[2,448,128]{2,1,0:T(8,128)(2,1)S(1)}, u32[]{:S(2)}, u32[]{:S(2)}) collective-permute-start(bf16[2,448,128]{2,1,0:T(8,128)(2,1)S(1)} %pad_maximum_fusion.refs_0_), channel_id=1, source_target_pairs={{0,8},{8,0},{1,9},{9,1},{2,10},{10,2},{3,11},{11,3},{4,12},{12,4},... | collective-permute-start | bytes 688136 | tf_op jit(solution)/shard_map/ppermute | solution.py:483
  49.9 1.6 %collective-permute-done.8 = bf16[448,128]{1,0:T(8,128)(2,1)S(1)} collective-permute-done((bf16[448,128]{1,0:T(8,128)(2,1)S(1)}, bf16[448,128]{1,0:T(8,128)(2,1)S(1)}, u32[]{:S(2)}, u32[]{:S(2)}) %collective-permute-start.8) | collective-permute-done | bytes 114720 | tf_op jit(solution)/shard_map/ppermute | solution.py:476
  51.5 1.1 %collective-permute-done.7 = bf16[448,128]{1,0:T(8,128)(2,1)S(1)} collective-permute-done((bf16[448,128]{1,0:T(8,128)(2,1)S(1)}, bf16[448,128]{1,0:T(8,128)(2,1)S(1)}, u32[]{:S(2)}, u32[]{:S(2)}) %collective-permute-start.7) | collective-permute-done | bytes 114720 | tf_op jit(solution)/shard_map/ppermute | solution.py:476
  52.6 2.1 %collective-permute-done.9.refs_2_ = bf16[2,448,128]{2,1,0:T(8,128)(2,1)S(1)} collective-permute-done((bf16[2,448,128]{2,1,0:T(8,128)(2,1)S(1)}, bf16[2,448,128]{2,1,0:T(8,128)(2,1)S(1)}, u32[]{:S(2)}, u32[]{:S(2)}) %collective-permute-start.9) | collective-permute-done | bytes 229408 | tf_op jit(solution)/shard_map/ppermute | solution.py:483
  54.8 7.9 %collective-permute-start.11 = (bf16[6,224,128]{2,1,0:T(8,128)(2,1)S(1)}, bf16[6,224,128]{2,1,0:T(8,128)(2,1)S(1)}, u32[]{:S(2)}, u32[]{:S(2)}) collective-permute-start(bf16[6,224,128]{2,1,0:T(8,128)(2,1)S(1)} %slice_dynamic-update-slice_fusion), channel_id=1, source_target_pairs={{0,16},{16,0},{1,17},{17,1},{2,18},{18,2},{3,19},{19,3},{4,20},{20... | collective-permute-start | bytes 1032200 | tf_op jit(solution)/shard_map/ppermute | solution.py:486
  62.7 0.8 %collective-permute-start.10 = (bf16[2,224,128]{2,1,0:T(8,128)(2,1)S(1)}, bf16[2,224,128]{2,1,0:T(8,128)(2,1)S(1)}, u32[]{:S(2)}, u32[]{:S(2)}) collective-permute-start(bf16[2,224,128]{2,1,0:T(8,128)(2,1)S(1)} %pad_maximum_fusion.2), channel_id=1, source_target_pairs={{0,8},{8,0},{1,9},{9,1},{2,10},{10,2},{3,11},{11,3},{4,12},{12,4},... | collective-permute-start | bytes 344072 | tf_op jit(solution)/shard_map/ppermute | solution.py:484
  64.3 4.5 %collective-permute-done.10.refs_3_ = bf16[2,224,128]{2,1,0:T(8,128)(2,1)S(1)} collective-permute-done((bf16[2,224,128]{2,1,0:T(8,128)(2,1)S(1)}, bf16[2,224,128]{2,1,0:T(8,128)(2,1)S(1)}, u32[]{:S(2)}, u32[]{:S(2)}) %collective-permute-start.10) | collective-permute-done | bytes 114720 | tf_op jit(solution)/shard_map/ppermute | solution.py:484
  69.4 1.9 %shard_map.63 = bf16[2,32,14,2,256]{4,3,2,1,0:T(2,128)(2,1)} custom-call(s32[8]{0:T(128)S(1)} %pad_add_fusion.1.source_ref, bf16[2,448,128]{2,1,0:T(8,128)(2,1)S(1)} %pad_maximum_fusion.refs_0_, bf16[2,448,128]{2,1,0:T(8,128)(2,1)S(1)} %pad_maximum_fusion.1.refs_1_, bf16[2,448,128]{2,1,0:T(8,128)(2,1)S(1)} %collective-permute-done.9.refs_2_, ...), custom_call_target="tpu_custom_call" | custom-call | tf_op jit(solution)/shard_map/pallas_call | solution.py:416
  (50 shorter events, 4.9 us)
Async XLA Ops:
  5.2 15.0 %collective-permute-start = (bf16[2,6,160,128]{3,2,1,0:T(8,128)(2,1)}, bf16[2,6,160,128]{3,2,1,0:T(8,128)(2,1)S(1)}, u32[]{:S(2)}, u32[]{:S(2)}) collective-permute-start(bf16[2,6,160,128]{3,2,1,0:T(8,128)(2,1)} %get-tuple-element.19), channel_id=1, source_target_pairs={{0,8},{8,0},{1,9},{9,1},{2,10},{10,2},{3,11},{11,3},{4,12},{12,4},... | collective-permute-start | bytes 1474568 | tf_op jit(solution)/shard_map/ppermute | solution.py:440
  8.3 24.0 %collective-permute-start.2 = (bf16[2,1,2,512,128]{4,3,2,1,0:T(8,128)(2,1)}, bf16[2,1,2,512,128]{4,3,2,1,0:T(8,128)(2,1)S(1)}, u32[]{:S(2)}, u32[]{:S(2)}) collective-permute-start(bf16[2,1,2,512,128]{4,3,2,1,0:T(8,128)(2,1)} %get-tuple-element.23), channel_id=1, source_target_pairs={{0,1},{1,0},{2,3},{3,2},{4,5},{5,4},{6,7},{7,6},{8,9},{9,8},{10,11... | collective-permute-start | bytes 1572872 | tf_op jit(solution)/shard_map/ppermute | solution.py:442
  9.8 8.2 %copy-start.9 = (s32[2,128,1]{1,2,0:T(1,128)S(1)}, s32[2,128,1]{1,2,0:T(1,128)}, u32[]{:S(2)}) copy-start(s32[2,128,1]{1,2,0:T(1,128)} %param.9) | copy-start | bytes 3076
  9.8 10.4 %copy-start = (bf16[2,32,2,14,512]{4,2,3,1,0:T(2,128)(2,1)S(1)}, bf16[2,32,2,14,512]{4,2,3,1,0:T(2,128)(2,1)}, u32[]{:S(2)}) copy-start(bf16[2,32,2,14,512]{4,2,3,1,0:T(2,128)(2,1)} %param.6) | copy-start | bytes 5505028
  9.8 10.4 %copy-start.7 = (s32[2,2]{1,0:T(2,128)S(1)}, s32[2,2]{1,0:T(2,128)}, u32[]{:S(2)}) copy-start(s32[2,2]{1,0:T(2,128)} %counts_hbm.8) | copy-start | bytes 52
  9.8 22.4 %collective-permute-start.3 = (bf16[2,1,2,512,128]{4,3,2,1,0:T(8,128)(2,1)}, bf16[2,1,2,512,128]{4,3,2,1,0:T(8,128)(2,1)S(1)}, u32[]{:S(2)}, u32[]{:S(2)}) collective-permute-start(bf16[2,1,2,512,128]{4,3,2,1,0:T(8,128)(2,1)} %get-tuple-element.24), channel_id=1, source_target_pairs={{1,2},{2,1},{3,4},{4,3},{5,6},{6,5},{9,10},{10,9},{11,12},{12,11},... | collective-permute-start | bytes 1572872 | tf_op jit(solution)/shard_map/ppermute | solution.py:443
  17.4 22.6 %collective-permute-start.1 = (bf16[2,9,160,128]{3,2,1,0:T(8,128)(2,1)}, bf16[2,9,160,128]{3,2,1,0:T(8,128)(2,1)}, u32[]{:S(2)}, u32[]{:S(2)}) collective-permute-start(bf16[2,9,160,128]{3,2,1,0:T(8,128)(2,1)} %shard_map.57), channel_id=1, source_target_pairs={{0,8},{8,0},{1,9},{9,1},{2,10},{10,2},{3,11},{11,3},{4,12},{12,4},... | collective-permute-start | bytes 2211848 | tf_op jit(solution)/shard_map/ppermute | solution.py:447
  18.2 11.0 %copy-start.8 = (f32[2]{0:T(128)S(1)}, f32[2]{0:T(128)}, u32[]{:S(2)}) copy-start(f32[2]{0:T(128)} %noise_ref.3) | copy-start | bytes 28
  29.3 5.7 %copy-start.1 = (f32[2,15,160,128]{3,2,1,0:T(8,128)}, f32[2,15,160,128]{3,2,1,0:T(8,128)S(1)}, u32[]{:S(2)}) copy-start(f32[2,15,160,128]{3,2,1,0:T(8,128)S(1)} %shard_map.56.own_ref) | copy-start | bytes 7372804
  30.6 0.8 %copy-start.5 = (f32[2,512,128]{2,1,0:T(8,128)}, f32[2,512,128]{2,1,0:T(8,128)S(1)}, u32[]{:S(2)}) copy-start(f32[2,512,128]{2,1,0:T(8,128)S(1)} %shard_map.59.state_ref) | copy-start | bytes 1572868
  32.2 2.7 %copy-start.3 = (bf16[2,1,2,512,128]{4,3,2,1,0:T(8,128)(2,1)}, bf16[2,1,2,512,128]{4,3,2,1,0:T(8,128)(2,1)S(1)}, u32[]{:S(2)}) copy-start(bf16[2,1,2,512,128]{4,3,2,1,0:T(8,128)(2,1)S(1)} %collective-permute-done.3.far_ref) | copy-start | bytes 1572868
  35.0 5.0 %collective-permute-start.4 = (bf16[2,160,128]{2,1,0:T(8,128)(2,1)}, bf16[2,160,128]{2,1,0:T(8,128)(2,1)S(1)}, u32[]{:S(2)}, u32[]{:S(2)}) collective-permute-start(bf16[2,160,128]{2,1,0:T(8,128)(2,1)} %shard_map.61), channel_id=1, source_target_pairs={{0,8},{8,0},{1,9},{9,1},{2,10},{10,2},{3,11},{11,3},{4,12},{12,4},... | collective-permute-start | bytes 245768 | tf_op jit(solution)/shard_map/ppermute | solution.py:452
  36.9 1.0 %copy-start.4 = (bf16[2,1,2,512,128]{4,3,2,1,0:T(8,128)(2,1)S(1)}, bf16[2,1,2,512,128]{4,3,2,1,0:T(8,128)(2,1)}, u32[]{:S(2)}) copy-start(bf16[2,1,2,512,128]{4,3,2,1,0:T(8,128)(2,1)} %copy-done.3) | copy-start | bytes 1572868
  37.9 2.1 %copy-start.2 = (f32[2,15,160,128]{3,2,1,0:T(8,128)S(1)}, f32[2,15,160,128]{3,2,1,0:T(8,128)}, u32[]{:S(2)}) copy-start(f32[2,15,160,128]{3,2,1,0:T(8,128)} %copy-done.1) | copy-start | bytes 7372804
  37.9 2.1 %copy-start.6 = (f32[2,512,128]{2,1,0:T(8,128)S(1)}, f32[2,512,128]{2,1,0:T(8,128)}, u32[]{:S(2)}) copy-start(f32[2,512,128]{2,1,0:T(8,128)} %copy-done.5) | copy-start | bytes 1572868
  42.8 5.9 %collective-permute-start.6 = (bf16[448,128]{1,0:T(8,128)(2,1)S(1)}, bf16[448,128]{1,0:T(8,128)(2,1)S(1)}, u32[]{:S(2)}, u32[]{:S(2)}) collective-permute-start(bf16[448,128]{1,0:T(8,128)(2,1)S(1)} %get-tuple-element.30), channel_id=1, source_target_pairs={{0,1},{1,2},{2,3},{3,0},{4,17},{5,18},{6,19},{7,16},{16,5},{17,6},... | collective-permute-start | bytes 344072 | tf_op jit(solution)/shard_map/ppermute | solution.py:476
  44.8 3.8 %collective-permute-start.5 = (bf16[448,128]{1,0:T(8,128)(2,1)S(1)}, bf16[448,128]{1,0:T(8,128)(2,1)S(1)}, u32[]{:S(2)}, u32[]{:S(2)}) collective-permute-start(bf16[448,128]{1,0:T(8,128)(2,1)S(1)} %get-tuple-element.29), channel_id=1, source_target_pairs={{0,0},{1,1},{2,2},{3,3},{4,16},{5,17},{6,18},{7,19},{16,4},{17,5},... | collective-permute-start | bytes 344072 | tf_op jit(solution)/shard_map/ppermute | solution.py:476
  45.6 5.9 %collective-permute-start.8 = (bf16[448,128]{1,0:T(8,128)(2,1)S(1)}, bf16[448,128]{1,0:T(8,128)(2,1)S(1)}, u32[]{:S(2)}, u32[]{:S(2)}) collective-permute-start(bf16[448,128]{1,0:T(8,128)(2,1)S(1)} %get-tuple-element.32), channel_id=1, source_target_pairs={{0,3},{1,0},{2,1},{3,2},{4,19},{5,16},{6,17},{7,18},{16,7},{17,4},... | collective-permute-start | bytes 344072 | tf_op jit(solution)/shard_map/ppermute | solution.py:476
  46.6 5.9 %collective-permute-start.7 = (bf16[448,128]{1,0:T(8,128)(2,1)S(1)}, bf16[448,128]{1,0:T(8,128)(2,1)S(1)}, u32[]{:S(2)}, u32[]{:S(2)}) collective-permute-start(bf16[448,128]{1,0:T(8,128)(2,1)S(1)} %get-tuple-element.31), channel_id=1, source_target_pairs={{0,2},{1,3},{2,0},{3,1},{4,18},{5,19},{6,16},{7,17},{16,6},{17,7},... | collective-permute-start | bytes 344072 | tf_op jit(solution)/shard_map/ppermute | solution.py:476
  48.7 6.1 %collective-permute-start.9 = (bf16[2,448,128]{2,1,0:T(8,128)(2,1)S(1)}, bf16[2,448,128]{2,1,0:T(8,128)(2,1)S(1)}, u32[]{:S(2)}, u32[]{:S(2)}) collective-permute-start(bf16[2,448,128]{2,1,0:T(8,128)(2,1)S(1)} %pad_maximum_fusion.refs_0_), channel_id=1, source_target_pairs={{0,8},{8,0},{1,9},{9,1},{2,10},{10,2},{3,11},{11,3},{4,12},{12,4},... | collective-permute-start | bytes 688136 | tf_op jit(solution)/shard_map/ppermute | solution.py:483
  54.8 9.5 %collective-permute-start.11 = (bf16[6,224,128]{2,1,0:T(8,128)(2,1)S(1)}, bf16[6,224,128]{2,1,0:T(8,128)(2,1)S(1)}, u32[]{:S(2)}, u32[]{:S(2)}) collective-permute-start(bf16[6,224,128]{2,1,0:T(8,128)(2,1)S(1)} %slice_dynamic-update-slice_fusion), channel_id=1, source_target_pairs={{0,16},{16,0},{1,17},{17,1},{2,18},{18,2},{3,19},{19,3},{4,20},{20... | collective-permute-start | bytes 1032200 | tf_op jit(solution)/shard_map/ppermute | solution.py:486
  62.7 6.1 %collective-permute-start.10 = (bf16[2,224,128]{2,1,0:T(8,128)(2,1)S(1)}, bf16[2,224,128]{2,1,0:T(8,128)(2,1)S(1)}, u32[]{:S(2)}, u32[]{:S(2)}) collective-permute-start(bf16[2,224,128]{2,1,0:T(8,128)(2,1)S(1)} %pad_maximum_fusion.2), channel_id=1, source_target_pairs={{0,8},{8,0},{1,9},{9,1},{2,10},{10,2},{3,11},{11,3},{4,12},{12,4},... | collective-permute-start | bytes 344072 | tf_op jit(solution)/shard_map/ppermute | solution.py:484
  63.6 5.8 %collective-permute-start.12 = (bf16[2,224,128]{2,1,0:T(8,128)(2,1)S(1)}, bf16[2,224,128]{2,1,0:T(8,128)(2,1)S(1)}, u32[]{:S(2)}, u32[]{:S(2)}) collective-permute-start(bf16[2,224,128]{2,1,0:T(8,128)(2,1)S(1)} %pad_maximum_fusion.3), channel_id=1, source_target_pairs={{0,24},{8,16},{16,8},{24,0},{1,25},{9,17},{17,9},{25,1},{2,26},{10... | collective-permute-start | bytes 344072 | tf_op jit(solution)/shard_map/ppermute | solution.py:485

commit v18 on v11

--- a/solution.py
+++ b/solution.py
@@ -97,8 +97,8 @@
                     fetch_samples(c, i - 2).start()
         for copy in end_copies:
             copy.start()
-        lhs_a[...] = jnp.zeros_like(lhs_a)
-        lhs_b[...] = jnp.zeros_like(lhs_b)
+        for lhs in (lhs_a, lhs_b):
+            lhs[2 * users :, :] = jnp.zeros((2 * SPAD, lhs.shape[1]), BF16)
 
         def wait(item):
             c, i = item // number, item % number
@@ -233,8 +233,8 @@
     def fetch():
         count_copy.start()
         each_copy(lambda copy: copy.start())
-        lhs_a[...] = jnp.zeros_like(lhs_a)
-        lhs_b[...] = jnp.zeros_like(lhs_b)
+        for lhs in (lhs_a, lhs_b):
+            lhs[2 * users :, :] = jnp.zeros((2 * SPAD, lhs.shape[1]), BF16)
 
     def work():
         each_copy(lambda copy: copy.wait())
@@ -390,7 +390,7 @@
     def kernel(source_ref, *refs):
         mine_refs, theirs_refs = refs[:number], refs[number : 2 * number]
         own_other, peer_others = refs[2 * number], refs[2 * number + 1 : 3 * number + 1]
-        out, gathered = refs[3 * number + 1 :]
+        out, gathered, turned, sems = refs[3 * number + 1 :]
         panel = lax.axis_index("panel")
 
         def place(ref, i, first, source, side):
@@ -410,15 +410,26 @@
                 for i in range(ref.shape[0]):
                     place(ref, i, 0, source_ref[n], side)
                     n += 1
-        for s in range(symbols):
-            out[:, :, s] = gathered[s].T.reshape(cells, per_device, 2, total)
+        copies = []
+        for n, (first, last) in enumerate(((0, symbols // 2), (symbols // 2, symbols))):
+            for s in range(first, last):
+                turned[:, :, s] = gathered[s].T.reshape(cells, per_device, 2, total)
+            part = (slice(None), slice(None), pl.ds(first, last - first))
+            copies.append(pltpu.make_async_copy(turned.at[part], out.at[part], sems.at[n]))
+            copies[-1].start()
+        for copy in copies:
+            copy.wait()
 
     return pl.pallas_call(
         kernel,
         in_specs=[SMEM_SPEC] + [VMEM_SPEC] * (3 * number + 1),
-        out_specs=VMEM_SPEC,
+        out_specs=HBM_SPEC,
         out_shape=jax.ShapeDtypeStruct((cells, per_device, symbols, 2, total), BF16),
-        scratch_shapes=[pltpu.VMEM((symbols, total, lanes), BF16)],
+        scratch_shapes=[
+            pltpu.VMEM((symbols, total, lanes), BF16),
+            pltpu.VMEM((cells, per_device, symbols, 2, total), BF16),
+            pltpu.SemaphoreType.DMA((2,)),
+        ],
         compiler_params=pltpu.CompilerParams(vmem_limit_bytes=VMEM_LIMIT),
     )(sources, *mine, *theirs, *others)
 

time: 66 us -> 65.9 us (level)
  no operation moved by 1% of the time
where the time goes in v18:
time: 65.9 us; the launch traced here: 65.7 us
  Pallas kernels  30.7 us (47%)
  starting transfers between devices  24.2 us (37%)
  waiting for transfers between devices  9.93 us (15%)
    pallas_call x3, Pallas kernels, inner_gram(): pl.pallas_call(kernel, in_specs=[HBM_SPEC] * 3, out_specs=[VMEM_SPEC] + [...  21 us
    ppermute x4, starting transfers between devices, body(): arrived.append(lax.ppermute(messages[b], ('cell', 'sc'), pairs))  6.12 us
    ppermute x1, starting transfers between devices, body(): lax.ppermute(jnp.stack([block[:keep] for block in arrived]), 'cell', SWAP)  6.01 us
    ppermute x2, starting transfers between devices, body(): others += [lax.ppermute(group[:, :keep], 'cell', SWAP) for group in theirs]  4.62 us
    ppermute x4, waiting for transfers between devices, body(): arrived.append(lax.ppermute(messages[b], ('cell', 'sc'), pairs))  3.99 us
    pallas_call x2, Pallas kernels, edge_gram(): pl.pallas_call(kernel, in_specs=[HBM_SPEC] * 5, out_specs=VMEM_SPEC, out_...  3.86 us
    ppermute x1, starting transfers between devices, body(): first_peer = lax.ppermute(first, 'panel', SWAP)  3.01 us
    pallas_call x1, Pallas kernels, detect_last(): pl.pallas_call(kernel, in_specs=[SMEM_SPEC] + [VMEM_SPEC] * 6, out_specs=...  2.71 us
  transfers between devices with their start and end apart: 14, of which 7 were waited for; matrix products, arithmetic and copies ran while one was open for 1% of the time, Pallas kernels for 32%

profile of v18, /device:TPU:0, one launch (start us, length us, event | category | flops | bytes accessed | tf_op | source)
XLA Modules:
  0.0 65.7 jit_solution(17142687527958852367)
XLA Ops:
  0.0 5.2 %shard_map.55 = (bf16[2,6,160,128]{3,2,1,0:T(8,128)(2,1)}, bf16[2,1,2,512,128]{4,3,2,1,0:T(8,128)(2,1)}, bf16[2,1,2,512,128]{4,3,2,1,0:T(8,128)(2,1)}) custom-call(s32[2,2]{1,0:T(2,128)} %counts_hbm.8, bf16[2,32,2,512,128]{4,3,2,1,0:T(8,128)(2,1)} %chan.9, bf16[2,32,14,2,512]{4,3,2,1,0:T(2,128)(2,1)} %bitcast.15), custom_call_target="tpu_custom_call" | custom-call | flops 905969664 | bytes 4194304 | tf_op jit(solution)/shard_map/pallas_call | solution.py:149
  5.2 3.0 %collective-permute-start = (bf16[2,6,160,128]{3,2,1,0:T(8,128)(2,1)}, bf16[2,6,160,128]{3,2,1,0:T(8,128)(2,1)S(1)}, u32[]{:S(2)}, u32[]{:S(2)}) collective-permute-start(bf16[2,6,160,128]{3,2,1,0:T(8,128)(2,1)} %get-tuple-element.19), channel_id=1, source_target_pairs={{0,8},{8,0},{1,9},{9,1},{2,10},{10,2},{3,11},{11,3},{4,12},{12,4},... | collective-permute-start | bytes 1474568 | tf_op jit(solution)/shard_map/ppermute | solution.py:451
  8.2 1.5 %collective-permute-start.2 = (bf16[2,1,2,512,128]{4,3,2,1,0:T(8,128)(2,1)}, bf16[2,1,2,512,128]{4,3,2,1,0:T(8,128)(2,1)S(1)}, u32[]{:S(2)}, u32[]{:S(2)}) collective-permute-start(bf16[2,1,2,512,128]{4,3,2,1,0:T(8,128)(2,1)} %get-tuple-element.23), channel_id=1, source_target_pairs={{0,1},{1,0},{2,3},{3,2},{4,5},{5,4},{6,7},{7,6},{8,9},{9,8},{10,11... | collective-permute-start | bytes 1572872 | tf_op jit(solution)/shard_map/ppermute | solution.py:453
  10.6 6.8 %shard_map.57 = bf16[2,9,160,128]{3,2,1,0:T(8,128)(2,1)} custom-call(s32[2,2]{1,0:T(2,128)} %counts_hbm.8, bf16[2,32,2,512,128]{4,3,2,1,0:T(8,128)(2,1)} %chan.9, bf16[2,32,14,2,512]{4,3,2,1,0:T(2,128)(2,1)} %bitcast.16), custom_call_target="tpu_custom_call" | custom-call | flops 1358954496 | bytes 5767168 | tf_op jit(solution)/shard_map/pallas_call | solution.py:149
  18.2 2.0 %collective-permute-done.peer_ref = bf16[2,6,160,128]{3,2,1,0:T(8,128)(2,1)S(1)} collective-permute-done((bf16[2,6,160,128]{3,2,1,0:T(8,128)(2,1)}, bf16[2,6,160,128]{3,2,1,0:T(8,128)(2,1)S(1)}, u32[]{:S(2)}, u32[]{:S(2)}) %collective-permute-start) | collective-permute-done | bytes 491552 | tf_op jit(solution)/shard_map/ppermute | solution.py:451
  20.2 9.0 %shard_map.56.own_ref = f32[2,15,160,128]{3,2,1,0:T(8,128)S(1)} custom-call(s32[2,2]{1,0:T(2,128)S(1)} %copy-done.1, bf16[2,32,2,512,128]{4,3,2,1,0:T(8,128)(2,1)} %chan.9, bf16[2,32,14,2,512]{4,3,2,1,0:T(2,128)(2,1)S(1)} %bitcast.17), custom_call_target="tpu_custom_call" | custom-call | flops 141557760 | bytes 557056 | tf_op jit(solution)/shard_map/pallas_call | solution.py:149
  29.2 1.4 %shard_map.59.state_ref = f32[2,512,128]{2,1,0:T(8,128)S(1)} custom-call(f32[2]{0:T(128)S(1)} %copy-done.2, f32[2,15,160,128]{3,2,1,0:T(8,128)S(1)} %shard_map.56.own_ref, bf16[2,6,160,128]{3,2,1,0:T(8,128)(2,1)S(1)} %collective-permute-done.peer_ref), custom_call_target="tpu_custom_call" | custom-call | flops 50331648 | bytes 3686400 | tf_op jit(solution)/shard_map/pallas_call | solution.py:324
  30.6 1.6 %collective-permute-done.2.near_ref = bf16[2,1,2,512,128]{4,3,2,1,0:T(8,128)(2,1)S(1)} collective-permute-done((bf16[2,1,2,512,128]{4,3,2,1,0:T(8,128)(2,1)}, bf16[2,1,2,512,128]{4,3,2,1,0:T(8,128)(2,1)S(1)}, u32[]{:S(2)}, u32[]{:S(2)}) %collective-permute-start.2) | collective-permute-done | bytes 524320 | tf_op jit(solution)/shard_map/ppermute | solution.py:453
  32.2 1.9 %shard_map.61 = bf16[2,160,128]{2,1,0:T(8,128)(2,1)S(1)} custom-call(s32[2,2]{1,0:T(2,128)S(1)} %copy-done.1, bf16[2,32,2,512,128]{4,3,2,1,0:T(8,128)(2,1)} %chan.9, bf16[2,32,14,2,512]{4,3,2,1,0:T(2,128)(2,1)S(1)} %bitcast.18, bf16[2,1,2,512,128]{4,3,2,1,0:T(8,128)(2,1)S(1)} %collective-permute-done.2.near_ref, ...), custom_call_target="tpu_custom_call" | custom-call | flops 150994944 | bytes 1572864 | tf_op jit(solution)/shard_map/pallas_call | solution.py:262
  34.1 0.9 %collective-permute-start.4 = (bf16[2,160,128]{2,1,0:T(8,128)(2,1)S(1)}, bf16[2,160,128]{2,1,0:T(8,128)(2,1)S(1)}, u32[]{:S(2)}, u32[]{:S(2)}) collective-permute-start(bf16[2,160,128]{2,1,0:T(8,128)(2,1)S(1)} %shard_map.61), channel_id=1, source_target_pairs={{0,8},{8,0},{1,9},{9,1},{2,10},{10,2},{3,11},{11,3},{4,12},{12,4},... | collective-permute-start | bytes 245768 | tf_op jit(solution)/shard_map/ppermute | solution.py:463
  35.2 1.9 %shard_map.60.edge_own_ref = f32[2,160,128]{2,1,0:T(8,128)S(1)} custom-call(s32[2,2]{1,0:T(2,128)S(1)} %copy-done.1, bf16[2,32,2,512,128]{4,3,2,1,0:T(8,128)(2,1)} %chan.9, bf16[2,32,14,2,512]{4,3,2,1,0:T(2,128)(2,1)S(1)} %bitcast.19, bf16[2,1,2,512,128]{4,3,2,1,0:T(8,128)(2,1)S(1)} %collective-permute-done.2.near_ref, ...), custom_call_target="tpu_custom_call" | custom-call | flops 150994944 | bytes 1572864 | tf_op jit(solution)/shard_map/pallas_call | solution.py:262
  37.2 1.4 %collective-permute-done.4.edge_peer_ref = bf16[2,160,128]{2,1,0:T(8,128)(2,1)S(1)} collective-permute-done((bf16[2,160,128]{2,1,0:T(8,128)(2,1)S(1)}, bf16[2,160,128]{2,1,0:T(8,128)(2,1)S(1)}, u32[]{:S(2)}, u32[]{:S(2)}) %collective-permute-start.4) | collective-permute-done | bytes 81952 | tf_op jit(solution)/shard_map/ppermute | solution.py:463
  38.6 2.7 %shard_map.62 = (bf16[448,128]{1,0:T(8,128)(2,1)S(1)}, bf16[448,128]{1,0:T(8,128)(2,1)S(1)}, bf16[448,128]{1,0:T(8,128)(2,1)S(1)}, bf16[448,128]{1,0:T(8,128)(2,1)S(1)}) custom-call(f32[2]{0:T(128)S(1)} %copy-done.2, f32[2,15,160,128]{3,2,1,0:T(8,128)S(1)} %shard_map.56.own_ref, bf16[2,9,160,128]{3,2,1,0:T(8,128)(2,1)} %collective-permute-done.1.peer_ref, ...), custom_call_target="tpu_custom_call" | custom-call | flops 234881024 | bytes 524288 | tf_op jit(solution)/shard_map/pallas_call | solution.py:370
  41.4 2.5 %collective-permute-start.6 = (bf16[448,128]{1,0:T(8,128)(2,1)S(1)}, bf16[448,128]{1,0:T(8,128)(2,1)S(1)}, u32[]{:S(2)}, u32[]{:S(2)}) collective-permute-start(bf16[448,128]{1,0:T(8,128)(2,1)S(1)} %get-tuple-element.30), channel_id=1, source_target_pairs={{0,1},{1,2},{2,3},{3,0},{4,17},{5,18},{6,19},{7,16},{16,5},{17,6},... | collective-permute-start | bytes 344072 | tf_op jit(solution)/shard_map/ppermute | solution.py:487
  44.5 1.1 %collective-permute-start.8 = (bf16[448,128]{1,0:T(8,128)(2,1)S(1)}, bf16[448,128]{1,0:T(8,128)(2,1)S(1)}, u32[]{:S(2)}, u32[]{:S(2)}) collective-permute-start(bf16[448,128]{1,0:T(8,128)(2,1)S(1)} %get-tuple-element.32), channel_id=1, source_target_pairs={{0,3},{1,0},{2,1},{3,2},{4,19},{5,16},{6,17},{7,18},{16,7},{17,4},... | collective-permute-start | bytes 344072 | tf_op jit(solution)/shard_map/ppermute | solution.py:487
  45.6 1.9 %collective-permute-start.7 = (bf16[448,128]{1,0:T(8,128)(2,1)S(1)}, bf16[448,128]{1,0:T(8,128)(2,1)S(1)}, u32[]{:S(2)}, u32[]{:S(2)}) collective-permute-start(bf16[448,128]{1,0:T(8,128)(2,1)S(1)} %get-tuple-element.31), channel_id=1, source_target_pairs={{0,2},{1,3},{2,0},{3,1},{4,18},{5,19},{6,16},{7,17},{16,6},{17,7},... | collective-permute-start | bytes 344072 | tf_op jit(solution)/shard_map/ppermute | solution.py:487
  47.5 1.4 %collective-permute-done.6 = bf16[448,128]{1,0:T(8,128)(2,1)S(1)} collective-permute-done((bf16[448,128]{1,0:T(8,128)(2,1)S(1)}, bf16[448,128]{1,0:T(8,128)(2,1)S(1)}, u32[]{:S(2)}, u32[]{:S(2)}) %collective-permute-start.6) | collective-permute-done | bytes 114720 | tf_op jit(solution)/shard_map/ppermute | solution.py:487
  49.0 1.0 %collective-permute-done.8 = bf16[448,128]{1,0:T(8,128)(2,1)S(1)} collective-permute-done((bf16[448,128]{1,0:T(8,128)(2,1)S(1)}, bf16[448,128]{1,0:T(8,128)(2,1)S(1)}, u32[]{:S(2)}, u32[]{:S(2)}) %collective-permute-start.8) | collective-permute-done | bytes 114720 | tf_op jit(solution)/shard_map/ppermute | solution.py:487
  50.1 1.5 %collective-permute-done.7 = bf16[448,128]{1,0:T(8,128)(2,1)S(1)} collective-permute-done((bf16[448,128]{1,0:T(8,128)(2,1)S(1)}, bf16[448,128]{1,0:T(8,128)(2,1)S(1)}, u32[]{:S(2)}, u32[]{:S(2)}) %collective-permute-start.7) | collective-permute-done | bytes 114720 | tf_op jit(solution)/shard_map/ppermute | solution.py:487
  52.3 6.0 %collective-permute-start.11 = (bf16[4,224,128]{2,1,0:T(8,128)(2,1)S(1)}, bf16[4,224,128]{2,1,0:T(8,128)(2,1)S(1)}, u32[]{:S(2)}, u32[]{:S(2)}) collective-permute-start(bf16[4,224,128]{2,1,0:T(8,128)(2,1)S(1)} %pad_maximum_fusion.2), channel_id=1, source_target_pairs={{0,16},{16,0},{1,17},{17,1},{2,18},{18,2},{3,19},{19,3},{4,20},{20... | collective-permute-start | bytes 688136 | tf_op jit(solution)/shard_map/ppermute | solution.py:493
  58.3 2.2 %collective-permute-start.12 = (bf16[2,224,128]{2,1,0:T(8,128)(2,1)S(1)}, bf16[2,224,128]{2,1,0:T(8,128)(2,1)S(1)}, u32[]{:S(2)}, u32[]{:S(2)}) collective-permute-start(bf16[2,224,128]{2,1,0:T(8,128)(2,1)S(1)} %slice.28), channel_id=1, source_target_pairs={{0,16},{16,0},{1,17},{17,1},{2,18},{18,2},{3,19},{19,3},{4,20},{20... | collective-permute-start | bytes 344072 | tf_op jit(solution)/shard_map/ppermute | solution.py:494
  60.5 2.4 %collective-permute-start.13 = (bf16[2,224,128]{2,1,0:T(8,128)(2,1)S(1)}, bf16[2,224,128]{2,1,0:T(8,128)(2,1)S(1)}, u32[]{:S(2)}, u32[]{:S(2)}) collective-permute-start(bf16[2,224,128]{2,1,0:T(8,128)(2,1)S(1)} %slice.29), channel_id=1, source_target_pairs={{0,16},{16,0},{1,17},{17,1},{2,18},{18,2},{3,19},{19,3},{4,20},{20... | collective-permute-start | bytes 344072 | tf_op jit(solution)/shard_map/ppermute | solution.py:494
  63.0 0.9 %collective-permute-done.13.refs_6_ = bf16[2,224,128]{2,1,0:T(8,128)(2,1)S(1)} collective-permute-done((bf16[2,224,128]{2,1,0:T(8,128)(2,1)S(1)}, bf16[2,224,128]{2,1,0:T(8,128)(2,1)S(1)}, u32[]{:S(2)}, u32[]{:S(2)}) %collective-permute-start.13) | collective-permute-done | bytes 114720 | tf_op jit(solution)/shard_map/ppermute | solution.py:494
  63.9 1.8 %shard_map.63 = bf16[2,32,14,2,256]{4,3,2,1,0:T(2,128)(2,1)} custom-call(s32[8]{0:T(128)S(1)} %pad_add_fusion.1.source_ref, bf16[2,448,128]{2,1,0:T(8,128)(2,1)S(1)} %pad_maximum_fusion.refs_0_, bf16[2,448,128]{2,1,0:T(8,128)(2,1)S(1)} %pad_maximum_fusion.1.refs_1_, bf16[2,448,128]{2,1,0:T(8,128)(2,1)S(1)} %collective-permute-done.9.refs_2_, ...), custom_call_target="tpu_custom_call" | custom-call | tf_op jit(solution)/shard_map/pallas_call | solution.py:423
  (36 shorter events, 3.4 us)
Async XLA Ops:
  5.2 15.0 %collective-permute-start = (bf16[2,6,160,128]{3,2,1,0:T(8,128)(2,1)}, bf16[2,6,160,128]{3,2,1,0:T(8,128)(2,1)S(1)}, u32[]{:S(2)}, u32[]{:S(2)}) collective-permute-start(bf16[2,6,160,128]{3,2,1,0:T(8,128)(2,1)} %get-tuple-element.19), channel_id=1, source_target_pairs={{0,8},{8,0},{1,9},{9,1},{2,10},{10,2},{3,11},{11,3},{4,12},{12,4},... | collective-permute-start | bytes 1474568 | tf_op jit(solution)/shard_map/ppermute | solution.py:451
  8.2 24.0 %collective-permute-start.2 = (bf16[2,1,2,512,128]{4,3,2,1,0:T(8,128)(2,1)}, bf16[2,1,2,512,128]{4,3,2,1,0:T(8,128)(2,1)S(1)}, u32[]{:S(2)}, u32[]{:S(2)}) collective-permute-start(bf16[2,1,2,512,128]{4,3,2,1,0:T(8,128)(2,1)} %get-tuple-element.23), channel_id=1, source_target_pairs={{0,1},{1,0},{2,3},{3,2},{4,5},{5,4},{6,7},{7,6},{8,9},{9,8},{10,11... | collective-permute-start | bytes 1572872 | tf_op jit(solution)/shard_map/ppermute | solution.py:453
  9.8 8.2 %copy-start.3 = (s32[2,128,1]{1,2,0:T(1,128)S(1)}, s32[2,128,1]{1,2,0:T(1,128)}, u32[]{:S(2)}) copy-start(s32[2,128,1]{1,2,0:T(1,128)} %param.9) | copy-start | bytes 3076
  9.8 10.4 %copy-start = (bf16[2,32,2,14,512]{4,2,3,1,0:T(2,128)(2,1)S(1)}, bf16[2,32,2,14,512]{4,2,3,1,0:T(2,128)(2,1)}, u32[]{:S(2)}) copy-start(bf16[2,32,2,14,512]{4,2,3,1,0:T(2,128)(2,1)} %param.6) | copy-start | bytes 5505028
  9.8 10.4 %copy-start.1 = (s32[2,2]{1,0:T(2,128)S(1)}, s32[2,2]{1,0:T(2,128)}, u32[]{:S(2)}) copy-start(s32[2,2]{1,0:T(2,128)} %counts_hbm.8) | copy-start | bytes 52
  9.8 22.4 %collective-permute-start.3 = (bf16[2,1,2,512,128]{4,3,2,1,0:T(8,128)(2,1)}, bf16[2,1,2,512,128]{4,3,2,1,0:T(8,128)(2,1)S(1)}, u32[]{:S(2)}, u32[]{:S(2)}) collective-permute-start(bf16[2,1,2,512,128]{4,3,2,1,0:T(8,128)(2,1)} %get-tuple-element.24), channel_id=1, source_target_pairs={{1,2},{2,1},{3,4},{4,3},{5,6},{6,5},{9,10},{10,9},{11,12},{12,11},... | collective-permute-start | bytes 1572872 | tf_op jit(solution)/shard_map/ppermute | solution.py:454
  17.4 21.3 %collective-permute-start.1 = (bf16[2,9,160,128]{3,2,1,0:T(8,128)(2,1)}, bf16[2,9,160,128]{3,2,1,0:T(8,128)(2,1)}, u32[]{:S(2)}, u32[]{:S(2)}) collective-permute-start(bf16[2,9,160,128]{3,2,1,0:T(8,128)(2,1)} %shard_map.57), channel_id=1, source_target_pairs={{0,8},{8,0},{1,9},{9,1},{2,10},{10,2},{3,11},{11,3},{4,12},{12,4},... | collective-permute-start | bytes 2211848 | tf_op jit(solution)/shard_map/ppermute | solution.py:458
  18.2 11.0 %copy-start.2 = (f32[2]{0:T(128)S(1)}, f32[2]{0:T(128)}, u32[]{:S(2)}) copy-start(f32[2]{0:T(128)} %noise_ref.3) | copy-start | bytes 28
  34.1 4.5 %collective-permute-start.4 = (bf16[2,160,128]{2,1,0:T(8,128)(2,1)S(1)}, bf16[2,160,128]{2,1,0:T(8,128)(2,1)S(1)}, u32[]{:S(2)}, u32[]{:S(2)}) collective-permute-start(bf16[2,160,128]{2,1,0:T(8,128)(2,1)S(1)} %shard_map.61), channel_id=1, source_target_pairs={{0,8},{8,0},{1,9},{9,1},{2,10},{10,2},{3,11},{11,3},{4,12},{12,4},... | collective-permute-start | bytes 245768 | tf_op jit(solution)/shard_map/ppermute | solution.py:463
  41.4 7.6 %collective-permute-start.6 = (bf16[448,128]{1,0:T(8,128)(2,1)S(1)}, bf16[448,128]{1,0:T(8,128)(2,1)S(1)}, u32[]{:S(2)}, u32[]{:S(2)}) collective-permute-start(bf16[448,128]{1,0:T(8,128)(2,1)S(1)} %get-tuple-element.30), channel_id=1, source_target_pairs={{0,1},{1,2},{2,3},{3,0},{4,17},{5,18},{6,19},{7,16},{16,5},{17,6},... | collective-permute-start | bytes 344072 | tf_op jit(solution)/shard_map/ppermute | solution.py:487
  43.8 5.1 %collective-permute-start.5 = (bf16[448,128]{1,0:T(8,128)(2,1)S(1)}, bf16[448,128]{1,0:T(8,128)(2,1)S(1)}, u32[]{:S(2)}, u32[]{:S(2)}) collective-permute-start(bf16[448,128]{1,0:T(8,128)(2,1)S(1)} %get-tuple-element.29), channel_id=1, source_target_pairs={{0,0},{1,1},{2,2},{3,3},{4,16},{5,17},{6,18},{7,19},{16,4},{17,5},... | collective-permute-start | bytes 344072 | tf_op jit(solution)/shard_map/ppermute | solution.py:487
  44.5 5.6 %collective-permute-start.8 = (bf16[448,128]{1,0:T(8,128)(2,1)S(1)}, bf16[448,128]{1,0:T(8,128)(2,1)S(1)}, u32[]{:S(2)}, u32[]{:S(2)}) collective-permute-start(bf16[448,128]{1,0:T(8,128)(2,1)S(1)} %get-tuple-element.32), channel_id=1, source_target_pairs={{0,3},{1,0},{2,1},{3,2},{4,19},{5,16},{6,17},{7,18},{16,7},{17,4},... | collective-permute-start | bytes 344072 | tf_op jit(solution)/shard_map/ppermute | solution.py:487
  45.6 6.0 %collective-permute-start.7 = (bf16[448,128]{1,0:T(8,128)(2,1)S(1)}, bf16[448,128]{1,0:T(8,128)(2,1)S(1)}, u32[]{:S(2)}, u32[]{:S(2)}) collective-permute-start(bf16[448,128]{1,0:T(8,128)(2,1)S(1)} %get-tuple-element.31), channel_id=1, source_target_pairs={{0,2},{1,3},{2,0},{3,1},{4,18},{5,19},{6,16},{7,17},{16,6},{17,7},... | collective-permute-start | bytes 344072 | tf_op jit(solution)/shard_map/ppermute | solution.py:487
  49.0 9.3 %collective-permute-start.9 = (bf16[2,448,128]{2,1,0:T(8,128)(2,1)S(1)}, bf16[2,448,128]{2,1,0:T(8,128)(2,1)S(1)}, u32[]{:S(2)}, u32[]{:S(2)}) collective-permute-start(bf16[2,448,128]{2,1,0:T(8,128)(2,1)S(1)} %pad_maximum_fusion.refs_0_), channel_id=1, source_target_pairs={{0,8},{8,0},{1,9},{9,1},{2,10},{10,2},{3,11},{11,3},{4,12},{12,4},... | collective-permute-start | bytes 688136 | tf_op jit(solution)/shard_map/ppermute | solution.py:492
  51.6 8.9 %collective-permute-start.10 = (bf16[2,448,128]{2,1,0:T(8,128)(2,1)S(1)}, bf16[2,448,128]{2,1,0:T(8,128)(2,1)S(1)}, u32[]{:S(2)}, u32[]{:S(2)}) collective-permute-start(bf16[2,448,128]{2,1,0:T(8,128)(2,1)S(1)} %pad_maximum_fusion.1.refs_1_), channel_id=1, source_target_pairs={{0,8},{8,0},{1,9},{9,1},{2,10},{10,2},{3,11},{11,3},{4,12},{12,4},... | collective-permute-start | bytes 688136 | tf_op jit(solution)/shard_map/ppermute | solution.py:492
  52.3 10.8 %collective-permute-start.11 = (bf16[4,224,128]{2,1,0:T(8,128)(2,1)S(1)}, bf16[4,224,128]{2,1,0:T(8,128)(2,1)S(1)}, u32[]{:S(2)}, u32[]{:S(2)}) collective-permute-start(bf16[4,224,128]{2,1,0:T(8,128)(2,1)S(1)} %pad_maximum_fusion.2), channel_id=1, source_target_pairs={{0,16},{16,0},{1,17},{17,1},{2,18},{18,2},{3,19},{19,3},{4,20},{20... | collective-permute-start | bytes 688136 | tf_op jit(solution)/shard_map/ppermute | solution.py:493
  58.3 4.7 %collective-permute-start.12 = (bf16[2,224,128]{2,1,0:T(8,128)(2,1)S(1)}, bf16[2,224,128]{2,1,0:T(8,128)(2,1)S(1)}, u32[]{:S(2)}, u32[]{:S(2)}) collective-permute-start(bf16[2,224,128]{2,1,0:T(8,128)(2,1)S(1)} %slice.28), channel_id=1, source_target_pairs={{0,16},{16,0},{1,17},{17,1},{2,18},{18,2},{3,19},{19,3},{4,20},{20... | collective-permute-start | bytes 344072 | tf_op jit(solution)/shard_map/ppermute | solution.py:494
  60.5 3.4 %collective-permute-start.13 = (bf16[2,224,128]{2,1,0:T(8,128)(2,1)S(1)}, bf16[2,224,128]{2,1,0:T(8,128)(2,1)S(1)}, u32[]{:S(2)}, u32[]{:S(2)}) collective-permute-start(bf16[2,224,128]{2,1,0:T(8,128)(2,1)S(1)} %slice.29), channel_id=1, source_target_pairs={{0,16},{16,0},{1,17},{17,1},{2,18},{18,2},{3,19},{19,3},{4,20},{20... | collective-permute-start | bytes 344072 | tf_op jit(solution)/shard_map/ppermute | solution.py:494
